TPU v7x, 128 devices: a whole 4x4x4 slice. The times are simulated.
128 devices in a mesh: segment: 2 (over core), seq: 16 (over y, x), tp: 4 (over z).
Axes of the slice: x: 4, y: 4, z: 4, core: 2. Of those that a mesh axis runs over, the one named last changes fastest.
Arguments:
- latents: bfloat16 [8, 1024, 3072], P(None, 'seq', 'tp'), may hold values from -6 to 6
- w_qkv: bfloat16 [2, 3072, 3, 1536], P('segment', None, None, 'tp'), may hold values from -0.109375 to 0.109375
- w_out: bfloat16 [2, 1536, 3072], P('segment', 'tp'), may hold values from -0.15625 to 0.15625
- modulation: float32 [2, 3, 3072], P('segment'), may hold values from -3 to 3
- qk_gain: float32 [2, 2, 128], P('segment'), may hold values from 0.5 to 2
- stale_cache: bfloat16 [2, 2, 8, 1024, 1536], P('segment', None, None, 'seq', 'tp'), may hold values from -70 to 70
- kv_tiles: int32 [2, 128, 8], P('segment'), may hold values from 0 to 127, as said below
- tile_counts: int32 [2, 128], P('segment'), may hold values from 2 to 8, as said below
- patch_order: int32 [8], replicated, may hold values from 0 to 7, each once
Outputs:
- handed: bfloat16 [2, 8, 1024, 3072], P('segment', None, 'seq', 'tp')
- new_cache: bfloat16 [2, 2, 8, 1024, 1536], P('segment', None, None, 'seq', 'tp')
Inputs may be any that keep to these rules, and one draw needn't show every extreme that they name: `kv_tiles`: slot 0 of a row is the query tile itself; slot 1 is the tile 8192 // 128 + 1024 // 128 tiles further round; the other slots lie within (6) // 2 tiles of the query tile, counting cyclically over the 128 tiles. Tiles of a row may repeat; slots past the row's count are padding. `tile_counts`: how many leading slots of a row are live. `patch_order`: each patch once.
All inputs are finite; a program needn't handle non-finite values.
Results may differ from a plain program's by a relative error of at most 0.029.
Values may be sent and summed in bfloat16 or wider, within the bound.
No kernel may reach another device: no remote copies, remote signals or barrier semaphores. Data moves between devices by JAX's collectives and lax.ppermute only.
A program may use at most 192 MiB of HBM per device.

v0:
```python
import jax
import jax.numpy as jnp
from jax import lax
from jax.sharding import PartitionSpec as P

TILE = 64


def passed_along(block, axis, distance):
    devices = range(lax.axis_size(axis))
    route = [((i - distance) % len(devices), i) for i in devices]
    return lax.ppermute(block, axis, route)


def norm_heads(values, norm_gain):
    return values * lax.rsqrt(jnp.mean(values * values, axis=-1, keepdims=True) + 1e-06) * norm_gain


def masked_scores(q_tiles, key_tiles, live_mask):
    score_scale = q_tiles.shape[-1] ** (-0.5)
    scores = (
        jnp.einsum("iqhe,ikthe->ihqkt", q_tiles, key_tiles, preferred_element_type=jnp.float32)
        * score_scale
    )
    return jnp.where(live_mask[:, None, None, :, None], scores, -1e30)


def weigh_values(scores, row_peak, value_tiles):
    weights_raw = jnp.exp(scores - row_peak[..., None, None])
    totals = jnp.sum(weights_raw, axis=(3, 4))
    summed = jnp.einsum(
        "ihqkt,ikthe->iqhe",
        weights_raw.astype(jnp.bfloat16),
        value_tiles,
        preferred_element_type=jnp.float32,
    )
    return (summed, totals)


def local(
    latents, w_qkv, w_out, modulation, qk_gain, stale_cache, kv_tiles, tile_counts, patch_order
):
    segments = lax.axis_size("segment")
    seq_size = lax.axis_size("seq")
    segment_pos = lax.axis_index("segment")
    seq_pos = lax.axis_index("seq")
    tp_pos = lax.axis_index("tp")
    patches, patch_rows, part_cols = latents.shape
    weights = w_qkv[0]
    out_weight = w_out[0]
    modul = modulation[0]
    norm_gain = qk_gain[0]
    tile_table = kv_tiles[0]
    counts = tile_counts[0]
    model_width = weights.shape[0]
    width_dev = out_weight.shape[0]
    head_dim = norm_gain.shape[-1]
    heads_dev = width_dev // head_dim
    tiles_dev = patch_rows // TILE
    tiles_patch = tiles_dev * seq_size
    slots = tile_table.shape[1]
    flat_weights = weights.reshape(model_width, 3 * width_dev)
    gate_cols = lax.dynamic_slice_in_dim(modul[2], tp_pos * part_cols, part_cols)
    local_cache = stale_cache[0]
    buffer = lax.all_gather(local_cache, "seq", axis=2, tiled=True)
    inflow = jnp.zeros((patch_rows, part_cols), jnp.bfloat16)
    entering = jnp.zeros((patches, patch_rows, part_cols), jnp.bfloat16)

    def tick(tick_id, state_in):
        local_cache, buffer, inflow, entering = state_in
        micro_id = tick_id - segment_pos
        is_live = (micro_id >= 0) & (micro_id < patches)
        patch_id = patch_order[jnp.clip(micro_id, 0, patches - 1)]
        own_rows = lax.dynamic_index_in_dim(latents, patch_id, 0, keepdims=False)
        inputs_now = jnp.where(segment_pos == 0, own_rows, inflow)
        full_rows = lax.all_gather(inputs_now, "tp", axis=1, tiled=True)
        xf = full_rows.astype(jnp.float32)
        centred = xf - jnp.mean(xf, axis=-1, keepdims=True)
        normed = centred * lax.rsqrt(jnp.mean(centred * centred, axis=-1, keepdims=True) + 1e-06)
        modded = (normed * (1.0 + modul[1]) + modul[0]).astype(jnp.bfloat16)
        projected = jnp.dot(modded, flat_weights, preferred_element_type=jnp.float32)
        projected = projected.reshape(patch_rows, 3, heads_dev, head_dim)
        queries = norm_heads(projected[:, 0], norm_gain[0]).astype(jnp.bfloat16)
        keys_new = norm_heads(projected[:, 1], norm_gain[1]).astype(jnp.bfloat16)
        values_new = projected[:, 2].astype(jnp.bfloat16)
        fresh_kv = jnp.stack(
            [keys_new.reshape(patch_rows, width_dev), values_new.reshape(patch_rows, width_dev)]
        )
        current = lax.dynamic_index_in_dim(local_cache, patch_id, 1, keepdims=False)
        local_cache = lax.dynamic_update_index_in_dim(
            local_cache, jnp.where(is_live, fresh_kv, current), patch_id, 1
        )
        query_tiles = (
            patch_id * tiles_patch + seq_pos * tiles_dev + jnp.arange(tiles_dev, dtype=jnp.int32)
        )
        chosen = tile_table[query_tiles]
        live_mask = jnp.arange(slots, dtype=jnp.int32)[None, :] < counts[query_tiles][:, None]
        fresh_all = lax.all_gather(fresh_kv, "seq", axis=1, tiled=True)
        current_all = lax.dynamic_index_in_dim(buffer, patch_id, 1, keepdims=False)
        buffer = lax.dynamic_update_index_in_dim(
            buffer, jnp.where(is_live, fresh_all, current_all), patch_id, 1
        )
        tile_pool = buffer.reshape(2, patches * tiles_patch, TILE, heads_dev, head_dim)
        key_tiles = tile_pool[0][chosen]
        value_tiles = tile_pool[1][chosen]
        scores = masked_scores(
            queries.reshape(tiles_dev, TILE, heads_dev, head_dim), key_tiles, live_mask
        )
        row_peak = jnp.max(scores, axis=(3, 4))
        summed, totals = weigh_values(scores, row_peak, value_tiles)
        attended = summed / jnp.transpose(totals, (0, 2, 1))[..., None]
        attended = attended.reshape(patch_rows, width_dev).astype(jnp.bfloat16)
        partial_value = jnp.dot(attended, out_weight, preferred_element_type=jnp.float32)
        head_sum = lax.psum_scatter(
            partial_value.astype(jnp.bfloat16), "tp", scatter_dimension=1, tiled=True
        ).astype(jnp.float32)
        mixed_out = (inputs_now.astype(jnp.float32) + gate_cols * head_sum).astype(jnp.bfloat16)
        received = passed_along(mixed_out, "segment", 1)
        sender = (segment_pos + segments - 1) % segments
        arrived = tick_id - sender
        landed = (arrived >= 0) & (arrived < patches)
        target = patch_order[jnp.clip(arrived, 0, patches - 1)]
        current_out = lax.dynamic_index_in_dim(entering, target, 0, keepdims=False)
        entering = lax.dynamic_update_index_in_dim(
            entering, jnp.where(landed, received, current_out), target, 0
        )
        return (local_cache, buffer, received, entering)

    state_out = lax.fori_loop(
        0, patches + segments - 1, tick, (local_cache, buffer, inflow, entering)
    )
    return (state_out[3][None], state_out[0][None])


def solution(mesh):
    in_specs = (
        P(None, "seq", "tp"),
        P("segment", None, None, "tp"),
        P("segment", "tp", None),
        P("segment", None, None),
        P("segment", None, None),
        P("segment", None, None, "seq", "tp"),
        P("segment", None, None),
        P("segment", None),
        P(),
    )
    out_specs = (P("segment", None, "seq", "tp"), P("segment", None, None, "seq", "tp"))
    return jax.shard_map(local, mesh=mesh, in_specs=in_specs, out_specs=out_specs, check_vma=False)
```

profile of v0, /device:TPU:1, one launch (start us, length us, event | category | flops | bytes accessed | tf_op | source)
XLA Modules:
  0.0 1596.5 jit_solution(14872052790657232163)
XLA Ops:
  32.9 70.9 %all-gather.4.cloned.1.call-done = bf16[1,2,8,1024,384]{4,3,2,1,0:T(8,128)(2,1)} async-done(((bf16[1,2,8,64,384]{4,3,2,1,0:T(8,128)(2,1)}), bf16[1,2,8,1024,384]{4,3,2,1,0:T(8,128)(2,1)}) %all-gather.4.cloned.1.call-update) | async-done | bytes 12582928 | tf_op jit(solution)/shard_map/all_gather | solution.py:65
  104.8 1485.2 %while.23 = (s32[]{:T(128)}, bf16[2,8,64,384]{3,2,1,0:T(8,128)(2,1)}, bf16[2,8,1024,384]{3,2,1,0:T(8,128)(2,1)}, bf16[64,768]{1,0:T(8,128)(2,1)S(1)}, bf16[8,64,...) while((s32[]{:T(128)}, ...), condition=%wide.region_8.9_spmd, body=%wide.region_0.8_spmd.sunk | while | flops 659452032 | bytes 120859384 | solution.py:129
  133.5 37.9 %all-gather.6.cloned.1.call-done = bf16[2,1024,384]{2,1,0:T(8,128)(2,1)} async-done(((bf16[2,64,384]{2,1,0:T(8,128)(2,1)}), bf16[2,1024,384]{2,1,0:T(8,128)(2,1)}) %all-gather.6.cloned.1.call-update) | async-done | bytes 1572880 | tf_op jit(solution)/shard_map/while/body/eval_jaxpr/all_gather | solution.py:98
  183.3 16.6 %squeeze.131 = bf16[128,64,3,128]{3,2,1,0:T(4,128)(2,1)} reshape(bf16[1,8,1024,384]{3,2,1,0:T(8,128)(2,1)} %get-tuple-element.638) | data formatting | bytes 12582912 | tf_op jit(solution)/shard_map/while/body/eval_jaxpr/squeeze | solution.py:105
  246.2 18.1 %reduce-scatter.2.cloned.1.call-done = bf16[64,768]{1,0:T(8,128)(2,1)} async-done(((bf16[64,3072]{1,0:T(8,128)(2,1)}), bf16[64,768]{1,0:T(8,128)(2,1)}) %reduce-scatter.2.cloned.1.call-update) | async-done | bytes 98320 | tf_op jit(solution)/shard_map/while/body/eval_jaxpr/reduce_scatter | solution.py:114
  297.9 38.6 %all-gather.6.cloned.1.call-done = bf16[2,1024,384]{2,1,0:T(8,128)(2,1)} async-done(((bf16[2,64,384]{2,1,0:T(8,128)(2,1)}), bf16[2,1024,384]{2,1,0:T(8,128)(2,1)}) %all-gather.6.cloned.1.call-update) | async-done | bytes 1572880 | tf_op jit(solution)/shard_map/while/body/eval_jaxpr/all_gather | solution.py:98
  349.8 16.6 %squeeze.131 = bf16[128,64,3,128]{3,2,1,0:T(4,128)(2,1)} reshape(bf16[1,8,1024,384]{3,2,1,0:T(8,128)(2,1)} %get-tuple-element.638) | data formatting | bytes 12582912 | tf_op jit(solution)/shard_map/while/body/eval_jaxpr/squeeze | solution.py:105
  412.7 16.8 %reduce-scatter.2.cloned.1.call-done = bf16[64,768]{1,0:T(8,128)(2,1)} async-done(((bf16[64,3072]{1,0:T(8,128)(2,1)}), bf16[64,768]{1,0:T(8,128)(2,1)}) %reduce-scatter.2.cloned.1.call-update) | async-done | bytes 98320 | tf_op jit(solution)/shard_map/while/body/eval_jaxpr/reduce_scatter | solution.py:114
  463.1 38.6 %all-gather.6.cloned.1.call-done = bf16[2,1024,384]{2,1,0:T(8,128)(2,1)} async-done(((bf16[2,64,384]{2,1,0:T(8,128)(2,1)}), bf16[2,1024,384]{2,1,0:T(8,128)(2,1)}) %all-gather.6.cloned.1.call-update) | async-done | bytes 1572880 | tf_op jit(solution)/shard_map/while/body/eval_jaxpr/all_gather | solution.py:98
  515.0 16.6 %squeeze.131 = bf16[128,64,3,128]{3,2,1,0:T(4,128)(2,1)} reshape(bf16[1,8,1024,384]{3,2,1,0:T(8,128)(2,1)} %get-tuple-element.638) | data formatting | bytes 12582912 | tf_op jit(solution)/shard_map/while/body/eval_jaxpr/squeeze | solution.py:105
  577.9 16.6 %reduce-scatter.2.cloned.1.call-done = bf16[64,768]{1,0:T(8,128)(2,1)} async-done(((bf16[64,3072]{1,0:T(8,128)(2,1)}), bf16[64,768]{1,0:T(8,128)(2,1)}) %reduce-scatter.2.cloned.1.call-update) | async-done | bytes 98320 | tf_op jit(solution)/shard_map/while/body/eval_jaxpr/reduce_scatter | solution.py:114
  628.2 38.6 %all-gather.6.cloned.1.call-done = bf16[2,1024,384]{2,1,0:T(8,128)(2,1)} async-done(((bf16[2,64,384]{2,1,0:T(8,128)(2,1)}), bf16[2,1024,384]{2,1,0:T(8,128)(2,1)}) %all-gather.6.cloned.1.call-update) | async-done | bytes 1572880 | tf_op jit(solution)/shard_map/while/body/eval_jaxpr/all_gather | solution.py:98
  680.1 16.6 %squeeze.131 = bf16[128,64,3,128]{3,2,1,0:T(4,128)(2,1)} reshape(bf16[1,8,1024,384]{3,2,1,0:T(8,128)(2,1)} %get-tuple-element.638) | data formatting | bytes 12582912 | tf_op jit(solution)/shard_map/while/body/eval_jaxpr/squeeze | solution.py:105
  743.0 16.6 %reduce-scatter.2.cloned.1.call-done = bf16[64,768]{1,0:T(8,128)(2,1)} async-done(((bf16[64,3072]{1,0:T(8,128)(2,1)}), bf16[64,768]{1,0:T(8,128)(2,1)}) %reduce-scatter.2.cloned.1.call-update) | async-done | bytes 98320 | tf_op jit(solution)/shard_map/while/body/eval_jaxpr/reduce_scatter | solution.py:114
  793.3 38.5 %all-gather.6.cloned.1.call-done = bf16[2,1024,384]{2,1,0:T(8,128)(2,1)} async-done(((bf16[2,64,384]{2,1,0:T(8,128)(2,1)}), bf16[2,1024,384]{2,1,0:T(8,128)(2,1)}) %all-gather.6.cloned.1.call-update) | async-done | bytes 1572880 | tf_op jit(solution)/shard_map/while/body/eval_jaxpr/all_gather | solution.py:98
  845.1 16.6 %squeeze.131 = bf16[128,64,3,128]{3,2,1,0:T(4,128)(2,1)} reshape(bf16[1,8,1024,384]{3,2,1,0:T(8,128)(2,1)} %get-tuple-element.638) | data formatting | bytes 12582912 | tf_op jit(solution)/shard_map/while/body/eval_jaxpr/squeeze | solution.py:105
  908.0 16.7 %reduce-scatter.2.cloned.1.call-done = bf16[64,768]{1,0:T(8,128)(2,1)} async-done(((bf16[64,3072]{1,0:T(8,128)(2,1)}), bf16[64,768]{1,0:T(8,128)(2,1)}) %reduce-scatter.2.cloned.1.call-update) | async-done | bytes 98320 | tf_op jit(solution)/shard_map/while/body/eval_jaxpr/reduce_scatter | solution.py:114
  958.4 38.6 %all-gather.6.cloned.1.call-done = bf16[2,1024,384]{2,1,0:T(8,128)(2,1)} async-done(((bf16[2,64,384]{2,1,0:T(8,128)(2,1)}), bf16[2,1024,384]{2,1,0:T(8,128)(2,1)}) %all-gather.6.cloned.1.call-update) | async-done | bytes 1572880 | tf_op jit(solution)/shard_map/while/body/eval_jaxpr/all_gather | solution.py:98
  1073.2 16.7 %reduce-scatter.2.cloned.1.call-done = bf16[64,768]{1,0:T(8,128)(2,1)} async-done(((bf16[64,3072]{1,0:T(8,128)(2,1)}), bf16[64,768]{1,0:T(8,128)(2,1)}) %reduce-scatter.2.cloned.1.call-update) | async-done | bytes 98320 | tf_op jit(solution)/shard_map/while/body/eval_jaxpr/reduce_scatter | solution.py:114
  1123.5 38.5 %all-gather.6.cloned.1.call-done = bf16[2,1024,384]{2,1,0:T(8,128)(2,1)} async-done(((bf16[2,64,384]{2,1,0:T(8,128)(2,1)}), bf16[2,1024,384]{2,1,0:T(8,128)(2,1)}) %all-gather.6.cloned.1.call-update) | async-done | bytes 1572880 | tf_op jit(solution)/shard_map/while/body/eval_jaxpr/all_gather | solution.py:98
  1238.3 16.7 %reduce-scatter.2.cloned.1.call-done = bf16[64,768]{1,0:T(8,128)(2,1)} async-done(((bf16[64,3072]{1,0:T(8,128)(2,1)}), bf16[64,768]{1,0:T(8,128)(2,1)}) %reduce-scatter.2.cloned.1.call-update) | async-done | bytes 98320 | tf_op jit(solution)/shard_map/while/body/eval_jaxpr/reduce_scatter | solution.py:114
  1288.6 38.5 %all-gather.6.cloned.1.call-done = bf16[2,1024,384]{2,1,0:T(8,128)(2,1)} async-done(((bf16[2,64,384]{2,1,0:T(8,128)(2,1)}), bf16[2,1024,384]{2,1,0:T(8,128)(2,1)}) %all-gather.6.cloned.1.call-update) | async-done | bytes 1572880 | tf_op jit(solution)/shard_map/while/body/eval_jaxpr/all_gather | solution.py:98
  1403.4 16.8 %reduce-scatter.2.cloned.1.call-done = bf16[64,768]{1,0:T(8,128)(2,1)} async-done(((bf16[64,3072]{1,0:T(8,128)(2,1)}), bf16[64,768]{1,0:T(8,128)(2,1)}) %reduce-scatter.2.cloned.1.call-update) | async-done | bytes 98320 | tf_op jit(solution)/shard_map/while/body/eval_jaxpr/reduce_scatter | solution.py:114
  1453.8 38.5 %all-gather.6.cloned.1.call-done = bf16[2,1024,384]{2,1,0:T(8,128)(2,1)} async-done(((bf16[2,64,384]{2,1,0:T(8,128)(2,1)}), bf16[2,1024,384]{2,1,0:T(8,128)(2,1)}) %all-gather.6.cloned.1.call-update) | async-done | bytes 1572880 | tf_op jit(solution)/shard_map/while/body/eval_jaxpr/all_gather | solution.py:98
  (647 shorter events, 907.4 us)
Async XLA Ops:
  7.2 96.7 %all-gather.4.cloned.1.call-start = ((), (), s32[]{:S(2)}) async-start(), calls=%async_computation.1 | async-start | bytes 13369344 | tf_op jit(solution)/shard_map/all_gather | solution.py:65
  104.8 66.6 %all-gather.6.cloned.1.call-start = ((), (), s32[]{:S(2)}) async-start(), calls=%async_computation.2 | async-start | bytes 1671168 | tf_op jit(solution)/shard_map/while/body/eval_jaxpr/all_gather | solution.py:98
  127.1 137.2 %reduce-scatter.2.cloned.1.call-start = ((), (), s32[]{:S(2)}) async-start(), calls=%async_computation.3 | async-start | bytes 491520 | tf_op jit(solution)/shard_map/while/body/eval_jaxpr/reduce_scatter | solution.py:114
  265.2 4.5 collective-permute-start
  270.4 66.1 %all-gather.6.cloned.1.call-start = ((), (), s32[]{:S(2)}) async-start(), calls=%async_computation.2 | async-start | bytes 1671168 | tf_op jit(solution)/shard_map/while/body/eval_jaxpr/all_gather | solution.py:98
  291.5 137.9 %reduce-scatter.2.cloned.1.call-start = ((), (), s32[]{:S(2)}) async-start(), calls=%async_computation.3 | async-start | bytes 491520 | tf_op jit(solution)/shard_map/while/body/eval_jaxpr/reduce_scatter | solution.py:114
  435.5 66.1 %all-gather.6.cloned.1.call-start = ((), (), s32[]{:S(2)}) async-start(), calls=%async_computation.2 | async-start | bytes 1671168 | tf_op jit(solution)/shard_map/while/body/eval_jaxpr/all_gather | solution.py:98
  456.7 137.9 %reduce-scatter.2.cloned.1.call-start = ((), (), s32[]{:S(2)}) async-start(), calls=%async_computation.3 | async-start | bytes 491520 | tf_op jit(solution)/shard_map/while/body/eval_jaxpr/reduce_scatter | solution.py:114
  600.7 66.1 %all-gather.6.cloned.1.call-start = ((), (), s32[]{:S(2)}) async-start(), calls=%async_computation.2 | async-start | bytes 1671168 | tf_op jit(solution)/shard_map/while/body/eval_jaxpr/all_gather | solution.py:98
  621.8 137.8 %reduce-scatter.2.cloned.1.call-start = ((), (), s32[]{:S(2)}) async-start(), calls=%async_computation.3 | async-start | bytes 491520 | tf_op jit(solution)/shard_map/while/body/eval_jaxpr/reduce_scatter | solution.py:114
  760.6 4.5 collective-permute-start
  765.8 66.1 %all-gather.6.cloned.1.call-start = ((), (), s32[]{:S(2)}) async-start(), calls=%async_computation.2 | async-start | bytes 1671168 | tf_op jit(solution)/shard_map/while/body/eval_jaxpr/all_gather | solution.py:98
  786.9 137.8 %reduce-scatter.2.cloned.1.call-start = ((), (), s32[]{:S(2)}) async-start(), calls=%async_computation.3 | async-start | bytes 491520 | tf_op jit(solution)/shard_map/while/body/eval_jaxpr/reduce_scatter | solution.py:114
  925.7 4.5 collective-permute-start
  930.8 66.1 %all-gather.6.cloned.1.call-start = ((), (), s32[]{:S(2)}) async-start(), calls=%async_computation.2 | async-start | bytes 1671168 | tf_op jit(solution)/shard_map/while/body/eval_jaxpr/all_gather | solution.py:98
  952.0 137.9 %reduce-scatter.2.cloned.1.call-start = ((), (), s32[]{:S(2)}) async-start(), calls=%async_computation.3 | async-start | bytes 491520 | tf_op jit(solution)/shard_map/while/body/eval_jaxpr/reduce_scatter | solution.py:114
  1096.0 66.1 %all-gather.6.cloned.1.call-start = ((), (), s32[]{:S(2)}) async-start(), calls=%async_computation.2 | async-start | bytes 1671168 | tf_op jit(solution)/shard_map/while/body/eval_jaxpr/all_gather | solution.py:98
  1117.1 137.8 %reduce-scatter.2.cloned.1.call-start = ((), (), s32[]{:S(2)}) async-start(), calls=%async_computation.3 | async-start | bytes 491520 | tf_op jit(solution)/shard_map/while/body/eval_jaxpr/reduce_scatter | solution.py:114
  1255.9 4.5 collective-permute-start
  1261.1 66.1 %all-gather.6.cloned.1.call-start = ((), (), s32[]{:S(2)}) async-start(), calls=%async_computation.2 | async-start | bytes 1671168 | tf_op jit(solution)/shard_map/while/body/eval_jaxpr/all_gather | solution.py:98
  1282.2 137.9 %reduce-scatter.2.cloned.1.call-start = ((), (), s32[]{:S(2)}) async-start(), calls=%async_computation.3 | async-start | bytes 491520 | tf_op jit(solution)/shard_map/while/body/eval_jaxpr/reduce_scatter | solution.py:114
  1421.1 4.5 collective-permute-start
  1426.2 66.1 %all-gather.6.cloned.1.call-start = ((), (), s32[]{:S(2)}) async-start(), calls=%async_computation.2 | async-start | bytes 1671168 | tf_op jit(solution)/shard_map/while/body/eval_jaxpr/all_gather | solution.py:98
  1447.4 136.5 %reduce-scatter.2.cloned.1.call-start = ((), (), s32[]{:S(2)}) async-start(), calls=%async_computation.3 | async-start | bytes 491520 | tf_op jit(solution)/shard_map/while/body/eval_jaxpr/reduce_scatter | solution.py:114
  (68 other events, 1898.1 us)
Sparse Core Ops, SparseCore 0:
  10.7 93.0 all-gather.3
  127.2 44.1 all-gather.5
  243.5 20.7 reduce-scatter.1
  291.7 44.7 all-gather.5
  410.0 19.4 reduce-scatter.1
  456.8 44.8 all-gather.5
  575.2 19.2 reduce-scatter.1
  621.9 44.8 all-gather.5
  740.3 19.2 reduce-scatter.1
  787.1 44.7 all-gather.5
  905.4 19.3 reduce-scatter.1
  952.1 44.7 all-gather.5
  1070.5 19.3 reduce-scatter.1
  1117.3 44.7 all-gather.5
  1235.6 19.3 reduce-scatter.1
  1282.4 44.7 all-gather.5
  1400.7 19.4 reduce-scatter.1
  1447.5 44.7 all-gather.5
  1565.9 17.9 reduce-scatter.1
where the time goes:
time: 1610 us; the launch traced here: 1600 us
  local copies, waits for them, and re-layouts  685 us (43%)
  waiting for transfers between devices  568 us (35%)
  other arithmetic  107 us (7%)
  blocking collectives  91.5 us (6%)
  matrix products  64.3 us (4%)
  loops' own time  39.9 us (2%)
  starting transfers between devices  26.8 us (2%)
    all_gather x9, waiting for transfers between devices, tick(): fresh_all = lax.all_gather(fresh_kv, 'seq', axis=1, tiled=True)  346 us
    squeeze x18, local copies, waits for them, and re-layouts, tick(): key_tiles = tile_pool[0][chosen]  221 us
    squeeze x18, local copies, waits for them, and re-layouts, tick(): value_tiles = tile_pool[1][chosen]  221 us
    reduce_scatter x9, waiting for transfers between devices, tick(): lax.psum_scatter(partial_value.astype(jnp.bfloat16), 'tp', scatter_dimens...  150 us
    slice x9, local copies, waits for them, and re-layouts, tick(): key_tiles = tile_pool[0][chosen]  93.2 us
    all_gather x9, blocking collectives, tick(): full_rows = lax.all_gather(inputs_now, 'tp', axis=1, tiled=True)  91.5 us
    all_gather x1, waiting for transfers between devices, local(): buffer = lax.all_gather(local_cache, 'seq', axis=2, tiled=True)  70.9 us
    another operation x1, loops' own time, local(): lax.fori_loop(0, patches + segments - 1, tick, (local_cache, buffer, infl...  39.9 us
  transfers between devices with their start and end apart: 28, of which 19 were waited for; matrix products, arithmetic and copies ran while one was open for 6% of the time, Pallas kernels for 0%

commit v1 on v0

v1 whole, which is shorter than its diff:
```python
import jax
import jax.numpy as jnp
from jax import lax
from jax.experimental import pallas as pl
from jax.experimental.pallas import tpu as pltpu
from jax.sharding import PartitionSpec as P

TILE = 64
EPS = 1e-06
NEAR = (0, 1, -1, 2, -2, 3, -3)
VMEM_BYTES = 48 * 1024 * 1024


def shifted(block, axis, distance):
    devices = range(lax.axis_size(axis))
    route = [((i - distance) % len(devices), i) for i in devices]
    return lax.ppermute(block, axis, route)


def params():
    return pltpu.CompilerParams(vmem_limit_bytes=VMEM_BYTES)


def project_kernel(
    meta,
    x_own,
    x_next,
    x_far_a,
    x_far_b,
    x_prev,
    shift,
    scale,
    gain,
    w_own,
    w_other,
    stale,
    q_out,
    kv_out,
    *rest,
):
    *payloads, xs, acc, stat = rest
    step = pl.program_id(0)
    rows, cols = x_own.shape
    width = cols * 4
    half = rows // 2

    @pl.when(step == 0)
    def _():
        xs[0] = x_own[...]
        xs[1] = x_next[...]
        xs[2, :half] = x_far_a[...]
        xs[2, half:] = x_far_b[...]
        xs[3] = x_prev[...]
        total = jnp.zeros((rows, 1), jnp.float32)
        for part in range(4):
            total += jnp.sum(xs[part].astype(jnp.float32), axis=-1, keepdims=True)
        mean = total / width
        square = jnp.zeros((rows, 1), jnp.float32)
        for part in range(4):
            centred = xs[part].astype(jnp.float32) - mean
            square += jnp.sum(centred * centred, axis=-1, keepdims=True)
        stat[0] = mean
        stat[1] = lax.rsqrt(square / width + EPS)
        acc[...] = jnp.zeros_like(acc)

    normed = (xs[step].astype(jnp.float32) - stat[0]) * stat[1]
    modded = (normed * (1.0 + scale[0]) + shift[0]).astype(jnp.bfloat16)

    @pl.when(meta[1] == 1)
    def _():
        for part in range(3):
            acc[part] += jnp.dot(modded, w_own[part], preferred_element_type=jnp.float32)

    @pl.when(meta[1] == 0)
    def _():
        for part in range(3):
            acc[part] += jnp.dot(modded, w_other[part], preferred_element_type=jnp.float32)

    @pl.when(step == 3)
    def _():
        patches, rows_patch, heads_cols = kv_out.shape[1:]
        head_dim = gain.shape[-1]
        for head in range(heads_cols // head_dim):
            cut = slice(head * head_dim, (head + 1) * head_dim)
            for part in range(2):
                vec = acc[part, :, cut]
                mean_sq = jnp.mean(vec * vec, axis=-1, keepdims=True)
                vec = vec * lax.rsqrt(mean_sq + EPS) * gain[part : part + 1]
                vec = vec.astype(jnp.bfloat16).reshape(patches, rows_patch, head_dim)
                if part == 0:
                    q_out[:, :, cut] = vec
                else:
                    kv_out[0, :, :, cut] = vec
        kv_out[1] = acc[2].astype(jnp.bfloat16).reshape(patches, rows_patch, heads_cols)
        for which, out in enumerate(payloads):
            for patch in range(patches):
                place = 2 + which * patches + patch
                source = meta[place]
                fresh = meta[place + len(payloads) * patches]

                @pl.when(fresh == 1)
                def _():
                    out[:, patch] = kv_out[:, source]

                @pl.when(fresh == 0)
                def _():
                    out[:, patch] = stale[:, source]


def project(meta, blocks, shift, scale, gain, w_own, w_other, stale, count):
    rows, cols = blocks[0].shape
    heads_cols = w_own.shape[-1]
    kv_shape = stale.shape

    def whole(shape):
        return pl.BlockSpec(shape, lambda j, meta: (0,) * len(shape))

    def feature(j, meta):
        return lax.rem(meta[0] + j, 4)

    w_block = (3, cols, heads_cols)
    kv_struct = jax.ShapeDtypeStruct(kv_shape, jnp.bfloat16)
    q_struct = jax.ShapeDtypeStruct(kv_shape[1:], jnp.bfloat16)
    return pl.pallas_call(
        project_kernel,
        grid_spec=pltpu.PrefetchScalarGridSpec(
            num_scalar_prefetch=1,
            grid=(4,),
            in_specs=[whole(b.shape) for b in blocks]
            + [pl.BlockSpec((1, 1, cols), lambda j, meta: (feature(j, meta), 0, 0))] * 2
            + [
                whole(gain.shape),
                pl.BlockSpec(
                    w_block, lambda j, meta: (0, jnp.where(meta[1] == 1, feature(j, meta), 0), 0)
                ),
                pl.BlockSpec(
                    w_block, lambda j, meta: (0, jnp.where(meta[1] == 1, 0, feature(j, meta)), 0)
                ),
                whole(kv_shape),
            ],
            out_specs=[whole(q_struct.shape)] + [whole(kv_shape)] * (1 + count),
            scratch_shapes=[
                pltpu.VMEM((4, rows, cols), jnp.bfloat16),
                pltpu.VMEM((3, rows, heads_cols), jnp.float32),
                pltpu.VMEM((2, rows, 1), jnp.float32),
            ],
        ),
        out_shape=[q_struct] + [kv_struct] * (1 + count),
        compiler_params=params(),
        name="project",
    )(meta, *blocks, shift, scale, gain, w_own, w_other, stale)


def attend_kernel(
    edge, q_own, q_other, own, up1, down1, up2, down2, edge2, up3, down3, far, multiple, *rest
):
    out_own, out_other, qs, kvs = rest
    rows = own.shape[2]
    head_dim = 128
    heads = own.shape[-1] // head_dim
    qs[:rows] = q_own[0]
    qs[rows:] = q_other[0]
    for place, ref in enumerate((own, up1, down1, up2, down2, up3, down3, far)):
        kvs[:, place * rows : (place + 1) * rows] = ref[:, 0]

    @pl.when(edge[0] == 1)
    def _():
        kvs[:, 3 * rows : 4 * rows] = edge2[:, 0]

    @pl.when(edge[1] == 1)
    def _():
        kvs[:, 4 * rows : 5 * rows] = edge2[:, 0]

    times = multiple[0]
    lane = lax.broadcasted_iota(jnp.int32, (2 * rows, head_dim), 1)
    extra = jnp.zeros((2 * rows, head_dim), jnp.float32)
    for head in range(heads):
        cut = slice(head * head_dim, (head + 1) * head_dim)
        scores = lax.dot_general(
            qs[:, cut], kvs[0, :, cut], (((1,), (1,)), ((), ())), preferred_element_type=jnp.float32
        )
        scores = jnp.where(times > 0.0, scores * head_dim ** (-0.5), -1e30)
        peak = jnp.max(scores, axis=-1, keepdims=True)
        weights = jnp.exp(scores - peak) * times
        total = jnp.sum(weights, axis=-1, keepdims=True)
        summed = jnp.dot(
            weights.astype(jnp.bfloat16), kvs[1, :, cut], preferred_element_type=jnp.float32
        )
        out_own[0, :, cut] = summed[:rows]
        out_other[0, :, cut] = summed[rows:]
        extra = jnp.where(lane == head, peak, extra)
        extra = jnp.where(lane == 64 + head, total, extra)
    out_own[0, :, heads * head_dim :] = extra[:rows]
    out_other[0, :, heads * head_dim :] = extra[rows:]


def attend(edge, q_own, q_other, kvs, multiple):
    _, patches, rows, heads_cols = kvs[0].shape
    keys = multiple.shape[-1]
    out_cols = heads_cols + 128
    q_spec = pl.BlockSpec((1, rows, heads_cols), lambda p, edge: (p, 0, 0))
    kv_spec = pl.BlockSpec((2, 1, rows, heads_cols), lambda p, edge: (0, p, 0, 0))
    out_spec = pl.BlockSpec((1, rows, out_cols), lambda p, edge: (p, 0, 0))
    out_struct = jax.ShapeDtypeStruct((patches, rows, out_cols), jnp.float32)
    return pl.pallas_call(
        attend_kernel,
        grid_spec=pltpu.PrefetchScalarGridSpec(
            num_scalar_prefetch=1,
            grid=(patches,),
            in_specs=[q_spec] * 2
            + [kv_spec] * len(kvs)
            + [pl.BlockSpec((1, 1, keys), lambda p, edge: (p, 0, 0))],
            out_specs=[out_spec] * 2,
            scratch_shapes=[
                pltpu.VMEM((2 * rows, heads_cols), jnp.bfloat16),
                pltpu.VMEM((2, keys, heads_cols), jnp.bfloat16),
            ],
        ),
        out_shape=[out_struct] * 2,
        compiler_params=params(),
        name="attend",
    )(edge, q_own, q_other, *kvs, multiple)


def merge_kernel(meta, part_a, part_b, w_own, w_other, att, y_a, y_b):
    head_dim = 128
    heads = att.shape[-1] // head_dim
    half = y_a.shape[0]
    extra_a = part_a[:, heads * head_dim :]
    extra_b = part_b[:, heads * head_dim :]
    for head in range(heads):
        cut = slice(head * head_dim, (head + 1) * head_dim)
        peak_a, total_a = extra_a[:, head : head + 1], extra_a[:, 64 + head : 65 + head]
        peak_b, total_b = extra_b[:, head : head + 1], extra_b[:, 64 + head : 65 + head]
        peak = jnp.maximum(peak_a, peak_b)
        grow_a, grow_b = jnp.exp(peak_a - peak), jnp.exp(peak_b - peak)
        total = total_a * grow_a + total_b * grow_b
        summed = part_a[:, cut] * grow_a + part_b[:, cut] * grow_b
        att[:, cut] = (summed / total).astype(jnp.bfloat16)

    def finish(weight):
        product = jnp.dot(att[...], weight[...], preferred_element_type=jnp.float32)
        y_a[...] = product[:half].astype(jnp.bfloat16)
        y_b[...] = product[half:].astype(jnp.bfloat16)

    @pl.when(meta[1] == 1)
    def _():
        finish(w_own)

    @pl.when(meta[1] == 0)
    def _():
        finish(w_other)


def out_weight_specs(rows, cols, place):
    def chosen(j, meta):
        return (0, jnp.where(meta[1] == 1, lax.rem(meta[0] + place(j), 4), 0))

    def spare(j, meta):
        return (0, jnp.where(meta[1] == 1, 0, lax.rem(meta[0] + place(j), 4)))

    return [pl.BlockSpec((rows, cols), chosen), pl.BlockSpec((rows, cols), spare)]


def merge(meta, part_a, part_b, w_own, w_other):
    rows = part_a.shape[0]
    heads_cols, width = w_own.shape
    cols = width // 4

    def whole(shape):
        return pl.BlockSpec(shape, lambda j, meta: (0,) * len(shape))

    return pl.pallas_call(
        merge_kernel,
        grid_spec=pltpu.PrefetchScalarGridSpec(
            num_scalar_prefetch=1,
            grid=(1,),
            in_specs=[whole(part_a.shape)] * 2
            + out_weight_specs(heads_cols, cols, lambda j: 2),
            out_specs=[whole((rows, heads_cols))] + [whole((rows // 2, cols))] * 2,
        ),
        out_shape=[jax.ShapeDtypeStruct((rows, heads_cols), jnp.bfloat16)]
        + [jax.ShapeDtypeStruct((rows // 2, cols), jnp.bfloat16)] * 2,
        compiler_params=params(),
        name="merge",
    )(meta, part_a, part_b, w_own, w_other)


def spread_kernel(meta, att, from_prev, from_next, w_own, w_other, to_next, to_prev, keep):
    step = pl.program_id(0)
    half = from_prev.shape[0]

    def finish(weight):
        product = jnp.dot(att[...], weight[...], preferred_element_type=jnp.float32)

        @pl.when(step == 0)
        def _():
            to_next[:half] = (product[:half] + from_prev[...].astype(jnp.float32)).astype(
                jnp.bfloat16
            )
            to_next[half:] = product[half:].astype(jnp.bfloat16)

        @pl.when(step == 1)
        def _():
            to_prev[:half] = product[:half].astype(jnp.bfloat16)
            to_prev[half:] = (product[half:] + from_next[...].astype(jnp.float32)).astype(
                jnp.bfloat16
            )

        @pl.when(step == 2)
        def _():
            keep[...] = product

    @pl.when(meta[1] == 1)
    def _():
        finish(w_own)

    @pl.when(meta[1] == 0)
    def _():
        finish(w_other)


def spread(meta, att, from_prev, from_next, w_own, w_other):
    rows, heads_cols = att.shape
    cols = w_own.shape[1] // 4

    def whole(shape):
        return pl.BlockSpec(shape, lambda j, meta: (0,) * len(shape))

    return pl.pallas_call(
        spread_kernel,
        grid_spec=pltpu.PrefetchScalarGridSpec(
            num_scalar_prefetch=1,
            grid=(3,),
            in_specs=[whole(att.shape), whole(from_prev.shape), whole(from_next.shape)]
            + out_weight_specs(
                heads_cols, cols, lambda j: jnp.where(j == 0, 1, jnp.where(j == 1, 3, 0))
            ),
            out_specs=[whole((rows, cols))] * 3,
        ),
        out_shape=[
            jax.ShapeDtypeStruct((rows, cols), jnp.bfloat16),
            jax.ShapeDtypeStruct((rows, cols), jnp.bfloat16),
            jax.ShapeDtypeStruct((rows, cols), jnp.float32),
        ],
        compiler_params=params(),
        name="spread",
    )(meta, att, from_prev, from_next, w_own, w_other)


def local(
    latents, w_qkv, w_out, modulation, qk_gain, stale_cache, kv_tiles, tile_counts, patch_order
):
    core = lax.axis_index("segment")
    seq_size = lax.axis_size("seq")
    seq_pos = lax.axis_index("seq")
    tp_pos = lax.axis_index("tp")
    patches, patch_rows, part_cols = latents.shape
    rows_core = patch_rows // 2
    rows = patches * rows_core
    w_own = jnp.transpose(w_qkv[0], (1, 0, 2))
    wo_own = w_out[0]
    heads_cols = wo_own.shape[0]
    width = wo_own.shape[1]
    head_dim = qk_gain.shape[-1]
    tiles = patches * seq_size

    mine = lax.dynamic_slice_in_dim(latents, core * rows_core, rows_core, 1)
    x_own = mine.reshape(rows, part_cols)

    patch_ids = jnp.arange(patches, dtype=jnp.int32)
    query_tiles = patch_ids * seq_size + seq_pos
    table = lax.dynamic_index_in_dim(
        kv_tiles[0].reshape(patches, seq_size, -1), seq_pos, 1, keepdims=False
    )
    counts = lax.dynamic_index_in_dim(
        tile_counts[0].reshape(patches, seq_size), seq_pos, 1, keepdims=False
    )
    slots = table.shape[1]
    far = tiles // 2 + seq_size // 2
    reach = jnp.array([d % tiles for d in NEAR] + [far], jnp.int32)
    relative = (table - query_tiles[:, None]) % tiles
    live = jnp.arange(slots, dtype=jnp.int32)[None] < counts[:, None]
    hits = (relative[:, :, None] == reach[None, None, :]) & live[:, :, None]
    multiple_own = jnp.sum(hits.astype(jnp.float32), axis=1)

    small_own = jnp.concatenate(
        [modulation[0].reshape(-1), qk_gain[0].reshape(-1), multiple_own.reshape(-1)]
    )
    small_other = shifted(small_own, "segment", 1)
    w_other = shifted(w_own, "segment", 1)
    wo_other = shifted(wo_own, "segment", 1)
    stale_all = stale_cache[0]
    stale_own = lax.dynamic_slice_in_dim(stale_all, core * rows_core, rows_core, 2)
    stale_other = shifted(
        lax.dynamic_slice_in_dim(stale_all, (1 - core) * rows_core, rows_core, 2), "segment", 1
    )

    patch_shift = jnp.stack(
        [
            jnp.where(seq_pos < 1, 1, 0),
            jnp.where(seq_pos >= seq_size - 1, -1, 0),
            jnp.where(seq_pos < 3, 1, 0),
            jnp.where(seq_pos >= seq_size - 3, -1, 0),
            jnp.where(seq_pos < seq_size // 2, patches // 2 + 1, patches // 2),
            jnp.where(seq_pos == 1, 1, jnp.where(seq_pos == seq_size - 2, -1, 0)),
        ]
    ).astype(jnp.int32)
    key_patch = (patch_ids[None] + patch_shift[:, None]) % patches
    turns = jnp.arange(patches, dtype=jnp.int32)
    rank = jnp.sum(jnp.where(patch_order[None] == patch_ids[:, None], turns[None], 0), axis=-1)
    key_rank = jnp.sum(
        jnp.where(patch_order[None, None] == key_patch[..., None], turns[None, None], 0), axis=-1
    )
    fresh = (key_rank <= rank[None]).astype(jnp.int32)
    pairs = patch_shift.shape[0]
    plan = jnp.concatenate([key_patch.reshape(-1), fresh.reshape(-1)])
    edge = jnp.stack([seq_pos == seq_size - 1, seq_pos == 0]).astype(jnp.int32)
    ends = [(1, seq_size - 1), (seq_size - 2, 0)]

    hidden = x_own
    hiddens, caches = [], []
    for section in range(2):
        is_own = core == section
        meta = jnp.concatenate(
            [jnp.stack([tp_pos, is_own.astype(tp_pos.dtype)]).astype(jnp.int32), plan]
        )
        small = jnp.where(is_own, small_own, small_other)
        modul = small[: 3 * width].reshape(3, 4, 1, part_cols)
        gain = small[3 * width : 3 * width + 2 * head_dim].reshape(2, head_dim)
        multiple = small[3 * width + 2 * head_dim :].reshape(patches, -1)
        multiple = jnp.repeat(multiple, rows_core, axis=1)[:, None]
        gate = lax.dynamic_index_in_dim(modul[2], tp_pos, 0, keepdims=False)
        stale = jnp.where(is_own, stale_own, stale_other)

        half = rows // 2
        x_prev = shifted(hidden, "tp", 1)
        x_next = shifted(hidden, "tp", -1)
        far_a = shifted(x_prev[:half], "tp", 1)
        far_b = shifted(x_next[half:], "tp", -1)
        q_own, kv, up1, down1, up3, down3, across, ended = project(
            meta,
            (hidden, x_next, far_a, far_b, x_prev),
            modul[0],
            modul[1],
            gain,
            w_own,
            w_other,
            stale,
            pairs,
        )
        up1 = shifted(up1, "seq", -1)
        down1 = shifted(down1, "seq", 1)
        across = shifted(across, "seq", -(seq_size // 2))
        up3 = shifted(up3, "seq", -3)
        down3 = shifted(down3, "seq", 3)
        up2 = shifted(up1, "seq", -1)
        down2 = shifted(down1, "seq", 1)
        edge2 = lax.ppermute(ended, "seq", ends)
        q_other = shifted(q_own, "segment", 1)
        kv_other = shifted(kv, "segment", 1)
        part_own, part_other = attend(
            edge,
            q_own,
            q_other,
            (kv, up1, down1, up2, down2, edge2, up3, down3, across),
            multiple,
        )
        part_back = shifted(part_other, "segment", 1)
        att, y_a, y_b = merge(
            meta,
            part_own.reshape(rows, -1),
            part_back.reshape(rows, -1),
            wo_own,
            wo_other,
        )
        from_prev = shifted(y_a, "tp", 1)
        from_next = shifted(y_b, "tp", -1)
        to_next, to_prev, keep = spread(meta, att, from_prev, from_next, wo_own, wo_other)
        got_prev = shifted(to_next, "tp", 1)
        got_next = shifted(to_prev, "tp", -1)
        head_sum = keep + got_prev.astype(jnp.float32) + got_next.astype(jnp.float32)
        hidden = (hidden.astype(jnp.float32) + gate * head_sum).astype(jnp.bfloat16)
        hiddens.append((hidden, shifted(hidden, "segment", 1)))
        caches.append((kv, kv_other))

    first = core == 0
    h_shape = (patches, rows_core, part_cols)
    upper = jnp.where(first, hiddens[1][0], hiddens[0][1]).reshape(h_shape)
    lower = jnp.where(first, hiddens[1][1], hiddens[0][0]).reshape(h_shape)
    handed = jnp.concatenate([upper, lower], axis=1)
    cache_upper = jnp.where(first, caches[0][0], caches[1][1])
    cache_lower = jnp.where(first, caches[0][1], caches[1][0])
    new_cache = jnp.concatenate([cache_upper, cache_lower], axis=2)
    return (handed[None], new_cache[None])


def solution(mesh):
    in_specs = (
        P(None, "seq", "tp"),
        P("segment", None, None, "tp"),
        P("segment", "tp", None),
        P("segment", None, None),
        P("segment", None, None),
        P("segment", None, None, "seq", "tp"),
        P("segment", None, None),
        P("segment", None),
        P(),
    )
    out_specs = (P("segment", None, "seq", "tp"), P("segment", None, None, "seq", "tp"))
    return jax.shard_map(local, mesh=mesh, in_specs=in_specs, out_specs=out_specs, check_vma=False)
```

time: 1610 us -> 270 us (0.17)
  local copies, waits for them, and re-layouts: 685 us -> 40.9 us
  waiting for transfers between devices: 568 us -> 99.5 us
  other arithmetic: 107 us -> 12.5 us
  blocking collectives: 91.5 us -> 0 us
  matrix products: 64.3 us -> 0 us
  Pallas kernels: 0 us -> 50.8 us
  loops' own time: 39.9 us -> 0 us
  starting transfers between devices: 26.8 us -> 63.7 us
    squeeze x54 -> x0, local copies, waits for them, and re-layouts: 443 us -> none  [the longest x18 221 us: tick(): key_tiles = tile_pool[0][chosen]]
    all_gather x10 -> x0, waiting for transfers between devices: 417 us -> none  [the longest x9 346 us: tick(): fresh_all = lax.all_gather(fresh_kv, 'seq', axis=1, tiled=True)]
    reduce_scatter x9 -> x0, waiting for transfers between devices: 150 us -> none  [tick(): lax.psum_scatter(partial_value.astype(jnp.bfloat16), 'tp', scatter_dimens...]
    ppermute x9 -> x44, waiting for transfers between devices: 0.02 us -> 99.5 us  [the longest x42 99.5 us: shifted(): return lax.ppermute(block, axis, route)]
    all_gather x9 -> x0, blocking collectives: 91.5 us -> none  [tick(): full_rows = lax.all_gather(inputs_now, 'tp', axis=1, tiled=True)]
    slice x20 -> x9, local copies, waits for them, and re-layouts: 93.5 us -> 4.07 us  [the longest x4 3.37 us: local(): multiple = small[3 * width + 2 * head_dim:].reshape(patches, -1)]
    gather x36 -> x0, local copies, waits for them, and re-layouts: 75.8 us -> none  [the longest x18 32 us: tick(): key_tiles = tile_pool[0][chosen]]
    dot_general x27 -> x0, matrix products: 54.2 us -> none  [the longest x9 39.8 us: tick(): jnp.dot(modded, flat_weights, preferred_element_type=jnp.float32)]
  transfers between devices with their start and end apart: 28 -> 44, of which waited for: 19 -> 18; matrix products, arithmetic and copies ran while one was open for 6% -> 9% of each run, Pallas kernels for 0% -> 8%
where the time goes in v1:
time: 270 us; the launch traced here: 268 us
  waiting for transfers between devices  99.5 us (37%)
  starting transfers between devices  63.7 us (24%)
  Pallas kernels  50.8 us (19%)
  local copies, waits for them, and re-layouts  40.9 us (15%)
  other arithmetic  12.5 us (5%)
    ppermute x42, waiting for transfers between devices, shifted(): return lax.ppermute(block, axis, route)  99.5 us
    ppermute x42, starting transfers between devices, shifted(): return lax.ppermute(block, axis, route)  61.2 us
    unnamed x93, local copies, waits for them, and re-layouts  27.2 us
    pallas_call x2, Pallas kernels, project(): pl.pallas_call(project_kernel, grid_spec=pltpu.PrefetchScalarGridSpec(num...  20.5 us
    pallas_call x2, Pallas kernels, attend(): pl.pallas_call(attend_kernel, grid_spec=pltpu.PrefetchScalarGridSpec(num_...  17.6 us
    pallas_call x2, Pallas kernels, spread(): pl.pallas_call(spread_kernel, grid_spec=pltpu.PrefetchScalarGridSpec(num_...  7.53 us
  transfers between devices with their start and end apart: 44, of which 18 were waited for; matrix products, arithmetic and copies ran while one was open for 9% of the time, Pallas kernels for 8%

profile of v1, /device:TPU:1, one launch (start us, length us, event | category | flops | bytes accessed | tf_op | source)
XLA Modules:
  0.0 268.5 jit_solution(13098982596819420268)
XLA Ops:
  23.3 4.0 %collective-permute-done.3.x_far_a = bf16[128,768]{1,0:T(8,128)(2,1)S(1)} collective-permute-done((bf16[128,768]{1,0:T(8,128)(2,1)S(1)}, bf16[128,768]{1,0:T(8,128)(2,1)S(1)}, u32[]{:S(2)}, u32[]{:S(2)}) %collective-permute-start.3) | collective-permute-done | bytes 196640 | tf_op jit(solution)/shard_map/ppermute | solution.py:17
  27.3 10.2 %project.2 = (bf16[8,32,384]{2,1,0:T(8,128)(2,1)S(1)}, bf16[2,8,32,384]{3,2,1,0:T(8,128)(2,1)S(1)}, bf16[2,8,32,384]{3,2,1,0:T(8,128)(2,1)S(1)}, bf16[2,8,32,384...) custom-call(s32[98]{0:T(128)S(1)} %get-tuple-element.79.meta, ...), custom_call_target="tpu_custom_call" | custom-call | tf_op jit(solution)/shard_map/project/pallas_call | solution.py:124
  39.0 4.9 %collective-permute-start.8 = (bf16[2,8,32,384]{3,2,1,0:T(8,128)(2,1)S(1)}, bf16[2,8,32,384]{3,2,1,0:T(8,128)(2,1)S(1)}, u32[]{:S(2)}, u32[]{:S(2)}) collective-permute-start(bf16[2,8,32,384]{3,2,1,0:T(8,128)(2,1)S(1)} %get-tuple-element.36), channel_id=1, source_target_pairs={{4,0},{8,4},{12,8},{16,12},{20,16},{24,20},{28,24},{32,28},{36,32}... | collective-permute-start | bytes 1179656 | tf_op jit(solution)/shard_map/ppermute | solution.py:17
  45.9 20.0 %collective-permute-done.8.up1 = bf16[2,8,32,384]{3,2,1,0:T(8,128)(2,1)S(1)} collective-permute-done((bf16[2,8,32,384]{3,2,1,0:T(8,128)(2,1)S(1)}, bf16[2,8,32,384]{3,2,1,0:T(8,128)(2,1)S(1)}, u32[]{:S(2)}, u32[]{:S(2)}) %collective-permute-start.8) | collective-permute-done | bytes 393248 | tf_op jit(solution)/shard_map/ppermute | solution.py:17
  66.8 7.0 %collective-permute-start.10 = (bf16[2,8,32,384]{3,2,1,0:T(8,128)(2,1)S(1)}, bf16[2,8,32,384]{3,2,1,0:T(8,128)(2,1)S(1)}, u32[]{:S(2)}, u32[]{:S(2)}) collective-permute-start(bf16[2,8,32,384]{3,2,1,0:T(8,128)(2,1)S(1)} %collective-permute-done.8.up1), channel_id=1, source_target_pairs={{4,0},{8,4},{12,8},{16,12},{20,16},{24,20},{28,24},{32,28},{36,32}... | collective-permute-start | bytes 1179656 | tf_op jit(solution)/shard_map/ppermute | solution.py:17
  85.4 5.1 %collective-permute-done.15.far = bf16[2,8,32,384]{3,2,1,0:T(8,128)(2,1)S(1)} collective-permute-done((bf16[2,8,32,384]{3,2,1,0:T(8,128)(2,1)}, bf16[2,8,32,384]{3,2,1,0:T(8,128)(2,1)S(1)}, u32[]{:S(2)}, u32[]{:S(2)}) %collective-permute-start.15) | collective-permute-done | bytes 393248 | tf_op jit(solution)/shard_map/ppermute | solution.py:17
  103.9 8.4 %attend.2 = (f32[8,32,512]{2,1,0:T(8,128)S(1)}, f32[8,32,512]{2,1,0:T(8,128)S(1)}) custom-call(s32[2]{0:T(128)S(1)} %copy-done.40, bf16[8,32,384]{2,1,0:T(8,128)(2,1)S(1)} %copy-done.29, bf16[8,32,384]{2,1,0:T(8,128)(2,1)S(1)} %copy-done.33, bf16[2,8,32,384]{3,2,1,0:T(8,128)(2,1)S(1)} %get-tuple-element.35.own, bf16[2,8,32,384]{3,2,1,0:T(8,128)(2,1)S(1)} %copy-done.11, ...), custom_call_target="tpu_custom_call" | custom-call | tf_op jit(solution)/shard_map/attend/pallas_call | solution.py:205
  112.3 5.7 %collective-permute-start.16 = (f32[8,32,512]{2,1,0:T(8,128)S(1)}, f32[8,32,512]{2,1,0:T(8,128)S(1)}, u32[]{:S(2)}, u32[]{:S(2)}) collective-permute-start(f32[8,32,512]{2,1,0:T(8,128)S(1)} %get-tuple-element.43), channel_id=1, source_target_pairs={{64,0},{0,64},{65,1},{1,65},{66,2},{2,66},{67,3},{3,67},{68,4},{4,... | collective-permute-start | bytes 1572872 | tf_op jit(solution)/shard_map/ppermute | solution.py:17
  122.4 2.8 %collective-permute-start.19 = (bf16[128,768]{1,0:T(8,128)(2,1)S(1)}, bf16[128,768]{1,0:T(8,128)(2,1)S(1)}, u32[]{:S(2)}, u32[]{:S(2)}) collective-permute-start(bf16[128,768]{1,0:T(8,128)(2,1)S(1)} %get-tuple-element.46), channel_id=1, source_target_pairs={{1,0},{2,1},{3,2},{0,3},{5,4},{6,5},{7,6},{4,7},{9,8},{10,9},{11,1... | collective-permute-start | bytes 589832 | tf_op jit(solution)/shard_map/ppermute | solution.py:17
  125.1 4.7 %collective-permute-done.18.from_prev = bf16[128,768]{1,0:T(8,128)(2,1)S(1)} collective-permute-done((bf16[128,768]{1,0:T(8,128)(2,1)S(1)}, bf16[128,768]{1,0:T(8,128)(2,1)S(1)}, u32[]{:S(2)}, u32[]{:S(2)}) %collective-permute-start.18) | collective-permute-done | bytes 196640 | tf_op jit(solution)/shard_map/ppermute | solution.py:17
  129.8 4.4 %spread.2 = (bf16[256,768]{1,0:T(8,128)(2,1)}, bf16[256,768]{1,0:T(8,128)(2,1)S(1)}, f32[256,768]{1,0:T(8,128)S(1)}) custom-call(s32[98]{0:T(128)S(1)} %copy-done.39, bf16[256,384]{1,0:T(8,128)(2,1)S(1)} %get-tuple-element.44.att, bf16[128,768]{1,0:T(8,128)(2,1)S(1)} %collective-permute-done.18.from_prev, ...), custom_call_target="tpu_custom_call" | custom-call | tf_op jit(solution)/shard_map/spread/pallas_call | solution.py:330
  138.4 8.2 %collective-permute-done.20 = bf16[256,768]{1,0:T(8,128)(2,1)} collective-permute-done((bf16[256,768]{1,0:T(8,128)(2,1)}, bf16[256,768]{1,0:T(8,128)(2,1)}, u32[]{:S(2)}, u32[]{:S(2)}) %collective-permute-start.20) | collective-permute-done | bytes 393248 | tf_op jit(solution)/shard_map/ppermute | solution.py:17
  151.2 7.7 %collective-permute-done.23.x_prev = bf16[256,768]{1,0:T(8,128)(2,1)S(1)} collective-permute-done((bf16[256,768]{1,0:T(8,128)(2,1)S(1)}, bf16[256,768]{1,0:T(8,128)(2,1)S(1)}, u32[]{:S(2)}, u32[]{:S(2)}) %collective-permute-start.23) | collective-permute-done | bytes 393248 | tf_op jit(solution)/shard_map/ppermute | solution.py:17
  159.0 2.7 %collective-permute-start.25 = (bf16[128,768]{1,0:T(8,128)(2,1)S(1)}, bf16[128,768]{1,0:T(8,128)(2,1)S(1)}, u32[]{:S(2)}, u32[]{:S(2)}) collective-permute-start(bf16[128,768]{1,0:T(8,128)(2,1)S(1)} %slice.131), channel_id=1, source_target_pairs={{1,0},{2,1},{3,2},{0,3},{5,4},{6,5},{7,6},{4,7},{9,8},{10,9},{11,1... | collective-permute-start | bytes 589832 | tf_op jit(solution)/shard_map/ppermute | solution.py:17
  164.7 10.3 %project.3 = (bf16[8,32,384]{2,1,0:T(8,128)(2,1)S(1)}, bf16[2,8,32,384]{3,2,1,0:T(8,128)(2,1)S(1)}, bf16[2,8,32,384]{3,2,1,0:T(8,128)(2,1)S(1)}, bf16[2,8,32,384...) custom-call(s32[98]{0:T(128)S(1)} %get-tuple-element.78.meta, ...), custom_call_target="tpu_custom_call" | custom-call | tf_op jit(solution)/shard_map/project/pallas_call | solution.py:124
  178.5 4.2 %collective-permute-start.26 = (bf16[8,32,384]{2,1,0:T(8,128)(2,1)S(1)}, bf16[8,32,384]{2,1,0:T(8,128)(2,1)S(1)}, u32[]{:S(2)}, u32[]{:S(2)}) collective-permute-start(bf16[8,32,384]{2,1,0:T(8,128)(2,1)S(1)} %get-tuple-element.50.q_own), channel_id=1, source_target_pairs={{64,0},{0,64},{65,1},{1,65},{66,2},{2,66},{67,3},{3,67},{68,4},{4,... | collective-permute-start | bytes 589832 | tf_op jit(solution)/shard_map/ppermute | solution.py:17
  186.7 8.9 %collective-permute-done.28.down1 = bf16[2,8,32,384]{3,2,1,0:T(8,128)(2,1)} collective-permute-done((bf16[2,8,32,384]{3,2,1,0:T(8,128)(2,1)S(1)}, bf16[2,8,32,384]{3,2,1,0:T(8,128)(2,1)}, u32[]{:S(2)}, u32[]{:S(2)}) %collective-permute-start.28) | collective-permute-done | bytes 393248 | tf_op jit(solution)/shard_map/ppermute | solution.py:17
  200.1 8.9 %collective-permute-done.33.down3 = bf16[2,8,32,384]{3,2,1,0:T(8,128)(2,1)} collective-permute-done((bf16[2,8,32,384]{3,2,1,0:T(8,128)(2,1)}, bf16[2,8,32,384]{3,2,1,0:T(8,128)(2,1)}, u32[]{:S(2)}, u32[]{:S(2)}) %collective-permute-start.33) | collective-permute-done | bytes 393248 | tf_op jit(solution)/shard_map/ppermute | solution.py:17
  209.0 14.9 %collective-permute-done.34.far = bf16[2,8,32,384]{3,2,1,0:T(8,128)(2,1)} collective-permute-done((bf16[2,8,32,384]{3,2,1,0:T(8,128)(2,1)}, bf16[2,8,32,384]{3,2,1,0:T(8,128)(2,1)}, u32[]{:S(2)}, u32[]{:S(2)}) %collective-permute-start.34) | collective-permute-done | bytes 393248 | tf_op jit(solution)/shard_map/ppermute | solution.py:17
  228.3 9.2 %attend.3 = (f32[8,32,512]{2,1,0:T(8,128)S(1)}, f32[8,32,512]{2,1,0:T(8,128)S(1)}) custom-call(s32[2]{0:T(128)S(1)} %copy-done.41, bf16[8,32,384]{2,1,0:T(8,128)(2,1)S(1)} %copy-done.31, bf16[8,32,384]{2,1,0:T(8,128)(2,1)S(1)} %copy-done.35, bf16[2,8,32,384]{3,2,1,0:T(8,128)(2,1)S(1)} %copy-done.6, bf16[2,8,32,384]{3,2,1,0:T(8,128)(2,1)} %collective-permute-done.27.up1, ...), custom_call_target="tpu_custom_call" | custom-call | tf_op jit(solution)/shard_map/attend/pallas_call | solution.py:205
  242.3 2.8 %collective-permute-start.37 = (bf16[128,768]{1,0:T(8,128)(2,1)S(1)}, bf16[128,768]{1,0:T(8,128)(2,1)S(1)}, u32[]{:S(2)}, u32[]{:S(2)}) collective-permute-start(bf16[128,768]{1,0:T(8,128)(2,1)S(1)} %get-tuple-element.62), channel_id=1, source_target_pairs={{1,0},{2,1},{3,2},{0,3},{5,4},{6,5},{7,6},{4,7},{9,8},{10,9},{11,1... | collective-permute-start | bytes 589832 | tf_op jit(solution)/shard_map/ppermute | solution.py:17
  245.9 3.9 %collective-permute-done.36.from_prev = bf16[128,768]{1,0:T(8,128)(2,1)S(1)} collective-permute-done((bf16[128,768]{1,0:T(8,128)(2,1)S(1)}, bf16[128,768]{1,0:T(8,128)(2,1)S(1)}, u32[]{:S(2)}, u32[]{:S(2)}) %collective-permute-start.36) | collective-permute-done | bytes 196640 | tf_op jit(solution)/shard_map/ppermute | solution.py:17
  249.8 3.1 %spread.3 = (bf16[256,768]{1,0:T(8,128)(2,1)S(1)}, bf16[256,768]{1,0:T(8,128)(2,1)S(1)}, f32[256,768]{1,0:T(8,128)S(1)}) custom-call(s32[98]{0:T(128)S(1)} %get-tuple-element.78.meta, bf16[256,384]{1,0:T(8,128)(2,1)S(1)} %get-tuple-element.60.att, bf16[128,768]{1,0:T(8,128)(2,1)S(1)} %collective-permute-done.36.from_prev, ...), custom_call_target="tpu_custom_call" | custom-call | tf_op jit(solution)/shard_map/spread/pallas_call | solution.py:330
  258.7 4.5 %collective-permute-done.38 = bf16[256,768]{1,0:T(8,128)(2,1)S(1)} collective-permute-done((bf16[256,768]{1,0:T(8,128)(2,1)S(1)}, bf16[256,768]{1,0:T(8,128)(2,1)S(1)}, u32[]{:S(2)}, u32[]{:S(2)}) %collective-permute-start.38) | collective-permute-done | bytes 393248 | tf_op jit(solution)/shard_map/ppermute | solution.py:17
  (215 shorter events, 100.9 us)
Async XLA Ops:
  0.7 26.6 %collective-permute-start.5 = (bf16[3,3072,384]{2,1,0:T(8,128)(2,1)}, bf16[3,3072,384]{2,1,0:T(8,128)(2,1)}, u32[]{:S(2)}, u32[]{:S(2)}) collective-permute-start(bf16[3,3072,384]{2,1,0:T(8,128)(2,1)} %bitcast.68), channel_id=1, source_target_pairs={{64,0},{0,64},{65,1},{1,65},{66,2},{2,66},{67,3},{3,67},{68,4},{4,... | collective-permute-start | bytes 21233672 | tf_op jit(solution)/shard_map/ppermute | solution.py:17
  2.2 17.3 %collective-permute-start.2 = (bf16[256,768]{1,0:T(8,128)(2,1)S(1)}, bf16[256,768]{1,0:T(8,128)(2,1)S(1)}, u32[]{:S(2)}, u32[]{:S(2)}) collective-permute-start(bf16[256,768]{1,0:T(8,128)(2,1)S(1)} %bitcast.57), channel_id=1, source_target_pairs={{3,0},{0,1},{1,2},{2,3},{7,4},{4,5},{5,6},{6,7},{11,8},{8,9},{9,10... | collective-permute-start | bytes 1179656 | tf_op jit(solution)/shard_map/ppermute | solution.py:17
  4.3 15.3 %collective-permute-start.1 = (bf16[256,768]{1,0:T(8,128)(2,1)S(1)}, bf16[256,768]{1,0:T(8,128)(2,1)S(1)}, u32[]{:S(2)}, u32[]{:S(2)}) collective-permute-start(bf16[256,768]{1,0:T(8,128)(2,1)S(1)} %bitcast.58), channel_id=1, source_target_pairs={{1,0},{2,1},{3,2},{0,3},{5,4},{6,5},{7,6},{4,7},{9,8},{10,9},{11,1... | collective-permute-start | bytes 1179656 | tf_op jit(solution)/shard_map/ppermute | solution.py:17
  17.5 100.5 %collective-permute-start.17 = (bf16[384,3072]{1,0:T(8,128)(2,1)}, bf16[384,3072]{1,0:T(8,128)(2,1)}, u32[]{:S(2)}, u32[]{:S(2)}) collective-permute-start(bf16[384,3072]{1,0:T(8,128)(2,1)} %bitcast.52), channel_id=1, source_target_pairs={{64,0},{0,64},{65,1},{1,65},{66,2},{2,66},{67,3},{3,67},{68,4},{4,... | collective-permute-start | bytes 7077896 | tf_op jit(solution)/shard_map/ppermute | solution.py:17
  39.0 26.9 %collective-permute-start.8 = (bf16[2,8,32,384]{3,2,1,0:T(8,128)(2,1)S(1)}, bf16[2,8,32,384]{3,2,1,0:T(8,128)(2,1)S(1)}, u32[]{:S(2)}, u32[]{:S(2)}) collective-permute-start(bf16[2,8,32,384]{3,2,1,0:T(8,128)(2,1)S(1)} %get-tuple-element.36), channel_id=1, source_target_pairs={{4,0},{8,4},{12,8},{16,12},{20,16},{24,20},{28,24},{32,28},{36,32}... | collective-permute-start | bytes 1179656 | tf_op jit(solution)/shard_map/ppermute | solution.py:17
  44.0 22.1 %collective-permute-start.9 = (bf16[2,8,32,384]{3,2,1,0:T(8,128)(2,1)S(1)}, bf16[2,8,32,384]{3,2,1,0:T(8,128)(2,1)S(1)}, u32[]{:S(2)}, u32[]{:S(2)}) collective-permute-start(bf16[2,8,32,384]{3,2,1,0:T(8,128)(2,1)S(1)} %get-tuple-element.37), channel_id=1, source_target_pairs={{60,0},{0,4},{4,8},{8,12},{12,16},{16,20},{20,24},{24,28},{28,32},... | collective-permute-start | bytes 1179656 | tf_op jit(solution)/shard_map/ppermute | solution.py:17
  44.0 22.1 %collective-permute-start.12 = (bf16[2,8,32,384]{3,2,1,0:T(8,128)(2,1)S(1)}, bf16[2,8,32,384]{3,2,1,0:T(8,128)(2,1)S(1)}, u32[]{:S(2)}, u32[]{:S(2)}) collective-permute-start(bf16[2,8,32,384]{3,2,1,0:T(8,128)(2,1)S(1)} %get-tuple-element.38), channel_id=1, source_target_pairs={{4,60},{56,0},{5,61},{57,1},{6,62},{58,2},{7,63},{59,3},{68,124},{... | collective-permute-start | bytes 1179656 | tf_op jit(solution)/shard_map/ppermute | solution.py:459
  45.9 28.6 %collective-permute-start.13 = (bf16[2,8,32,384]{3,2,1,0:T(8,128)(2,1)S(1)}, bf16[2,8,32,384]{3,2,1,0:T(8,128)(2,1)S(1)}, u32[]{:S(2)}, u32[]{:S(2)}) collective-permute-start(bf16[2,8,32,384]{3,2,1,0:T(8,128)(2,1)S(1)} %get-tuple-element.39), channel_id=1, source_target_pairs={{12,0},{16,4},{20,8},{24,12},{28,16},{32,20},{36,24},{40,28},{44,3... | collective-permute-start | bytes 1179656 | tf_op jit(solution)/shard_map/ppermute | solution.py:17
  65.9 18.7 %collective-permute-start.14 = (bf16[2,8,32,384]{3,2,1,0:T(8,128)(2,1)}, bf16[2,8,32,384]{3,2,1,0:T(8,128)(2,1)S(1)}, u32[]{:S(2)}, u32[]{:S(2)}) collective-permute-start(bf16[2,8,32,384]{3,2,1,0:T(8,128)(2,1)} %get-tuple-element.40), channel_id=1, source_target_pairs={{52,0},{56,4},{60,8},{0,12},{4,16},{8,20},{12,24},{16,28},{20,32},... | collective-permute-start | bytes 1179656 | tf_op jit(solution)/shard_map/ppermute | solution.py:17
  66.1 24.5 %collective-permute-start.15 = (bf16[2,8,32,384]{3,2,1,0:T(8,128)(2,1)}, bf16[2,8,32,384]{3,2,1,0:T(8,128)(2,1)S(1)}, u32[]{:S(2)}, u32[]{:S(2)}) collective-permute-start(bf16[2,8,32,384]{3,2,1,0:T(8,128)(2,1)} %get-tuple-element.41), channel_id=1, source_target_pairs={{32,0},{36,4},{40,8},{44,12},{48,16},{52,20},{56,24},{60,28},{0,32... | collective-permute-start | bytes 1179656 | tf_op jit(solution)/shard_map/ppermute | solution.py:17
  66.8 24.5 %collective-permute-start.10 = (bf16[2,8,32,384]{3,2,1,0:T(8,128)(2,1)S(1)}, bf16[2,8,32,384]{3,2,1,0:T(8,128)(2,1)S(1)}, u32[]{:S(2)}, u32[]{:S(2)}) collective-permute-start(bf16[2,8,32,384]{3,2,1,0:T(8,128)(2,1)S(1)} %collective-permute-done.8.up1), channel_id=1, source_target_pairs={{4,0},{8,4},{12,8},{16,12},{20,16},{24,20},{28,24},{32,28},{36,32}... | collective-permute-start | bytes 1179656 | tf_op jit(solution)/shard_map/ppermute | solution.py:17
  75.3 16.7 %collective-permute-start.11 = (bf16[2,8,32,384]{3,2,1,0:T(8,128)(2,1)S(1)}, bf16[2,8,32,384]{3,2,1,0:T(8,128)(2,1)S(1)}, u32[]{:S(2)}, u32[]{:S(2)}) collective-permute-start(bf16[2,8,32,384]{3,2,1,0:T(8,128)(2,1)S(1)} %collective-permute-done.9.down1), channel_id=1, source_target_pairs={{60,0},{0,4},{4,8},{8,12},{12,16},{16,20},{20,24},{24,28},{28,32},... | collective-permute-start | bytes 1179656 | tf_op jit(solution)/shard_map/ppermute | solution.py:17
  135.1 11.6 %collective-permute-start.20 = (bf16[256,768]{1,0:T(8,128)(2,1)}, bf16[256,768]{1,0:T(8,128)(2,1)}, u32[]{:S(2)}, u32[]{:S(2)}) collective-permute-start(bf16[256,768]{1,0:T(8,128)(2,1)} %get-tuple-element.48), channel_id=1, source_target_pairs={{3,0},{0,1},{1,2},{2,3},{7,4},{4,5},{5,6},{6,7},{11,8},{8,9},{9,10... | collective-permute-start | bytes 1179656 | tf_op jit(solution)/shard_map/ppermute | solution.py:17
  135.8 10.8 %collective-permute-start.21 = (bf16[256,768]{1,0:T(8,128)(2,1)S(1)}, bf16[256,768]{1,0:T(8,128)(2,1)}, u32[]{:S(2)}, u32[]{:S(2)}) collective-permute-start(bf16[256,768]{1,0:T(8,128)(2,1)S(1)} %get-tuple-element.49), channel_id=1, source_target_pairs={{1,0},{2,1},{3,2},{0,3},{5,4},{6,5},{7,6},{4,7},{9,8},{10,9},{11,1... | collective-permute-start | bytes 1179656 | tf_op jit(solution)/shard_map/ppermute | solution.py:17
  148.5 10.5 %collective-permute-start.22 = (bf16[256,768]{1,0:T(8,128)(2,1)S(1)}, bf16[256,768]{1,0:T(8,128)(2,1)S(1)}, u32[]{:S(2)}, u32[]{:S(2)}) collective-permute-start(bf16[256,768]{1,0:T(8,128)(2,1)S(1)} %add_convert_fusion.1.x_own), channel_id=1, source_target_pairs={{1,0},{2,1},{3,2},{0,3},{5,4},{6,5},{7,6},{4,7},{9,8},{10,9},{11,1... | collective-permute-start | bytes 1179656 | tf_op jit(solution)/shard_map/ppermute | solution.py:17
  175.8 11.0 %collective-permute-start.27 = (bf16[2,8,32,384]{3,2,1,0:T(8,128)(2,1)S(1)}, bf16[2,8,32,384]{3,2,1,0:T(8,128)(2,1)}, u32[]{:S(2)}, u32[]{:S(2)}) collective-permute-start(bf16[2,8,32,384]{3,2,1,0:T(8,128)(2,1)S(1)} %get-tuple-element.52), channel_id=1, source_target_pairs={{4,0},{8,4},{12,8},{16,12},{20,16},{24,20},{28,24},{32,28},{36,32}... | collective-permute-start | bytes 1179656 | tf_op jit(solution)/shard_map/ppermute | solution.py:17
  175.8 19.8 %collective-permute-start.28 = (bf16[2,8,32,384]{3,2,1,0:T(8,128)(2,1)S(1)}, bf16[2,8,32,384]{3,2,1,0:T(8,128)(2,1)}, u32[]{:S(2)}, u32[]{:S(2)}) collective-permute-start(bf16[2,8,32,384]{3,2,1,0:T(8,128)(2,1)S(1)} %get-tuple-element.53), channel_id=1, source_target_pairs={{60,0},{0,4},{4,8},{8,12},{12,16},{16,20},{20,24},{24,28},{28,32},... | collective-permute-start | bytes 1179656 | tf_op jit(solution)/shard_map/ppermute | solution.py:17
  177.2 18.4 %collective-permute-start.31 = (bf16[2,8,32,384]{3,2,1,0:T(8,128)(2,1)S(1)}, bf16[2,8,32,384]{3,2,1,0:T(8,128)(2,1)S(1)}, u32[]{:S(2)}, u32[]{:S(2)}) collective-permute-start(bf16[2,8,32,384]{3,2,1,0:T(8,128)(2,1)S(1)} %get-tuple-element.54), channel_id=1, source_target_pairs={{4,60},{56,0},{5,61},{57,1},{6,62},{58,2},{7,63},{59,3},{68,124},{... | collective-permute-start | bytes 1179656 | tf_op jit(solution)/shard_map/ppermute | solution.py:459
  183.4 16.7 %collective-permute-start.32 = (bf16[2,8,32,384]{3,2,1,0:T(8,128)(2,1)}, bf16[2,8,32,384]{3,2,1,0:T(8,128)(2,1)}, u32[]{:S(2)}, u32[]{:S(2)}) collective-permute-start(bf16[2,8,32,384]{3,2,1,0:T(8,128)(2,1)} %get-tuple-element.55), channel_id=1, source_target_pairs={{12,0},{16,4},{20,8},{24,12},{28,16},{32,20},{36,24},{40,28},{44,3... | collective-permute-start | bytes 1179656 | tf_op jit(solution)/shard_map/ppermute | solution.py:17
  184.4 24.5 %collective-permute-start.33 = (bf16[2,8,32,384]{3,2,1,0:T(8,128)(2,1)}, bf16[2,8,32,384]{3,2,1,0:T(8,128)(2,1)}, u32[]{:S(2)}, u32[]{:S(2)}) collective-permute-start(bf16[2,8,32,384]{3,2,1,0:T(8,128)(2,1)} %get-tuple-element.56), channel_id=1, source_target_pairs={{52,0},{56,4},{60,8},{0,12},{4,16},{8,20},{12,24},{16,28},{20,32},... | collective-permute-start | bytes 1179656 | tf_op jit(solution)/shard_map/ppermute | solution.py:17
  186.7 37.1 %collective-permute-start.34 = (bf16[2,8,32,384]{3,2,1,0:T(8,128)(2,1)}, bf16[2,8,32,384]{3,2,1,0:T(8,128)(2,1)}, u32[]{:S(2)}, u32[]{:S(2)}) collective-permute-start(bf16[2,8,32,384]{3,2,1,0:T(8,128)(2,1)} %get-tuple-element.57), channel_id=1, source_target_pairs={{32,0},{36,4},{40,8},{44,12},{48,16},{52,20},{56,24},{60,28},{0,32... | collective-permute-start | bytes 1179656 | tf_op jit(solution)/shard_map/ppermute | solution.py:17
  195.6 28.3 %collective-permute-start.29 = (bf16[2,8,32,384]{3,2,1,0:T(8,128)(2,1)}, bf16[2,8,32,384]{3,2,1,0:T(8,128)(2,1)}, u32[]{:S(2)}, u32[]{:S(2)}) collective-permute-start(bf16[2,8,32,384]{3,2,1,0:T(8,128)(2,1)} %collective-permute-done.27.up1), channel_id=1, source_target_pairs={{4,0},{8,4},{12,8},{16,12},{20,16},{24,20},{28,24},{32,28},{36,32}... | collective-permute-start | bytes 1179656 | tf_op jit(solution)/shard_map/ppermute | solution.py:17
  196.4 27.5 %collective-permute-start.30 = (bf16[2,8,32,384]{3,2,1,0:T(8,128)(2,1)}, bf16[2,8,32,384]{3,2,1,0:T(8,128)(2,1)}, u32[]{:S(2)}, u32[]{:S(2)}) collective-permute-start(bf16[2,8,32,384]{3,2,1,0:T(8,128)(2,1)} %collective-permute-done.28.down1), channel_id=1, source_target_pairs={{60,0},{0,4},{4,8},{8,12},{12,16},{16,20},{20,24},{24,28},{28,32},... | collective-permute-start | bytes 1179656 | tf_op jit(solution)/shard_map/ppermute | solution.py:17
  245.1 13.6 %collective-permute-start.40 = (bf16[256,768]{1,0:T(8,128)(2,1)S(1)}, bf16[256,768]{1,0:T(8,128)(2,1)S(1)}, u32[]{:S(2)}, u32[]{:S(2)}) collective-permute-start(bf16[256,768]{1,0:T(8,128)(2,1)S(1)} %add_convert_fusion.1.x_own), channel_id=1, source_target_pairs={{64,0},{0,64},{65,1},{1,65},{66,2},{2,66},{67,3},{3,67},{68,4},{4,... | collective-permute-start | bytes 1179656 | tf_op jit(solution)/shard_map/ppermute | solution.py:17
  (66 other events, 415.9 us)

commit v2 on v0

v2 whole, which is shorter than its diff:
```python
import jax
import jax.numpy as jnp
from jax import lax
from jax.experimental import pallas as pl
from jax.experimental.pallas import tpu as pltpu
from jax.sharding import PartitionSpec as P

EPS = 1e-06
HEAD_DIM = 128
REACH = 3
MIB = 1024 * 1024
ON_CHIP = pl.BlockSpec(memory_space=pltpu.VMEM)
SCALARS = pl.BlockSpec(memory_space=pltpu.SMEM)


def shifted(block, axis, distance):
    devices = range(lax.axis_size(axis))
    route = [((i - distance) % len(devices), i) for i in devices]
    return lax.ppermute(block, axis, route)


def after(values, *gates):
    return lax.optimization_barrier((values, gates))[0]


def params(mib):
    return pltpu.CompilerParams(vmem_limit_bytes=mib * MIB)


def struct(shape, dtype=jnp.bfloat16):
    return jax.ShapeDtypeStruct(shape, dtype)


def to_work(blocks):
    rounds, size = len(blocks), lax.axis_size("seq")
    share = size // rounds
    out = []
    for r, block in enumerate(blocks):
        route = [
            (s, share * ((s % rounds - r) % rounds) + s // rounds) for s in range(size)
        ]
        out.append(lax.ppermute(block, "seq", route))
    return out


def to_home(blocks):
    rounds, size = len(blocks), lax.axis_size("seq")
    share = size // rounds
    out = []
    for r, block in enumerate(blocks):
        route = [
            (i, rounds * (i % share) + (i // share + r) % rounds) for i in range(size)
        ]
        out.append(lax.ppermute(block, "seq", route))
    return out


def deal_latents_kernel(meta, latents, *outs):
    rounds, rows = len(outs), outs[0].shape[0]
    first = pl.multiple_of(meta[0] * rows, rows)
    for r, out in enumerate(outs):
        patch = lax.rem(meta[1] + rounds - r, rounds)
        out[...] = latents[patch, pl.ds(first, rows)]


def deal_latents(meta, latents):
    patches, rows, cols = latents.shape
    return pl.pallas_call(
        deal_latents_kernel,
        in_specs=[SCALARS, ON_CHIP],
        out_specs=[ON_CHIP] * patches,
        out_shape=[struct((rows // 2, cols))] * patches,
        compiler_params=params(8),
        name="deal_latents",
    )(meta, latents)


def halve_stale_kernel(meta, stale, mine, theirs):
    rows, cols = mine.shape[1], stale.shape[-1]
    for which, out in enumerate((mine, theirs)):
        first = meta[0] if which == 0 else 1 - meta[0]
        first = pl.multiple_of(first * rows, rows)
        for half in range(2):
            out[:, :, half * cols : (half + 1) * cols] = stale[half, :, pl.ds(first, rows)]


def halve_stale(meta, stale):
    _, patches, rows, cols = stale.shape
    out = struct((patches, rows // 2, 2 * cols))
    return pl.pallas_call(
        halve_stale_kernel,
        in_specs=[SCALARS, ON_CHIP],
        out_specs=[ON_CHIP] * 2,
        out_shape=[out] * 2,
        compiler_params=params(8),
        name="halve_stale",
    )(meta, stale)


def deal_stale_kernel(meta, own, other, *outs):
    rounds, rows = len(outs), own.shape[1]
    for r, out in enumerate(outs):
        patch = lax.rem(meta[1] + rounds - r, rounds)
        out[:rows] = own[patch]
        out[rows:] = other[patch]


def deal_stale(meta, own, other):
    patches, rows, cols = own.shape
    return pl.pallas_call(
        deal_stale_kernel,
        in_specs=[SCALARS] + [ON_CHIP] * 2,
        out_specs=[ON_CHIP] * patches,
        out_shape=[struct((2 * rows, cols))] * patches,
        compiler_params=params(8),
        name="deal_stale",
    )(meta, own, other)


def sort_stale_kernel(meta, *refs):
    *blocks, out = refs
    rounds, rows = len(blocks), out.shape[1]
    first = pl.multiple_of((1 - meta[0]) * rows, rows)
    for r, block in enumerate(blocks):
        out[lax.rem(meta[2] + r, rounds)] = block[pl.ds(first, rows)]


def sort_stale(meta, blocks):
    rows, cols = blocks[0].shape
    return pl.pallas_call(
        sort_stale_kernel,
        in_specs=[SCALARS] + [ON_CHIP] * len(blocks),
        out_specs=ON_CHIP,
        out_shape=struct((len(blocks), rows // 2, cols)),
        compiler_params=params(8),
        name="sort_stale",
    )(meta, *blocks)


def deal_results_kernel(meta, for_first, for_second, got, *outs):
    rounds, rows = len(outs), got.shape[1]

    def deal(upper, lower):
        for r, out in enumerate(outs):
            tile = lax.rem(meta[2] + r, rounds)
            out[:rows] = upper[tile]
            out[rows:] = lower[tile]

    @pl.when(meta[0] == 0)
    def _():
        deal(for_first, got)

    @pl.when(meta[0] == 1)
    def _():
        deal(got, for_second)


def deal_results(meta, for_first, for_second, got):
    tiles, rows, cols = got.shape
    return pl.pallas_call(
        deal_results_kernel,
        in_specs=[SCALARS] + [ON_CHIP] * 3,
        out_specs=[ON_CHIP] * tiles,
        out_shape=[struct((2 * rows, cols))] * tiles,
        compiler_params=params(8),
        name="deal_results",
    )(meta, for_first, for_second, got)


def collect_kernel(meta, *refs):
    *blocks, handed, cache = refs
    rounds = len(blocks) // 2
    cols = cache.shape[-1]

    def collect(features, keys):
        for r in range(rounds):
            patch = lax.rem(meta[1] + rounds - r, rounds)
            handed[patch] = features[r][...]
            cache[0, patch] = keys[r][:, :cols]
            cache[1, patch] = keys[r][:, cols:]

    @pl.when(meta[0] == 0)
    def _():
        collect(blocks[rounds:], blocks[:rounds])

    @pl.when(meta[0] == 1)
    def _():
        collect(blocks[:rounds], blocks[rounds:])


def collect(meta, early, late):
    rows, cols = early[0].shape
    rounds = len(early)
    return pl.pallas_call(
        collect_kernel,
        in_specs=[SCALARS] + [ON_CHIP] * (2 * rounds),
        out_specs=[ON_CHIP] * 2,
        out_shape=[struct((rounds, rows, cols)), struct((2, rounds, rows, cols // 2))],
        compiler_params=params(8),
        name="collect",
    )(meta, *early, *late)


def choose(meta, kv, stale, outs):
    tiles = kv.shape[0]
    for place, out in enumerate(outs):
        first = tiles - REACH if place == 1 else 0
        cut = slice(first, first + out.shape[0])

        @pl.when(meta[3 + place] == 1)
        def _():
            out[...] = kv[cut]

        @pl.when(meta[3 + place] == 0)
        def _():
            out[...] = stale[cut]


def choose_kernel(meta, kv, *refs):
    *blocks, lo_out, hi_out, far_out = refs
    rounds, rows, _ = kv.shape
    first = pl.multiple_of((1 - meta[1]) * rows, rows)
    for place, out in enumerate((lo_out, hi_out, far_out)):
        start = rounds - REACH if place == 1 else 0

        @pl.when(meta[3 + place] == 1)
        def _():
            out[...] = kv[start : start + out.shape[0]]

        @pl.when(meta[3 + place] == 0)
        def _():
            for r, block in enumerate(blocks):
                tile = lax.rem(meta[2] + r, rounds) - start

                @pl.when((tile >= 0) & (tile < out.shape[0]))
                def _():
                    out[tile] = block[pl.ds(first, rows)]


def payloads(kv_shape):
    edge = struct((REACH,) + kv_shape[1:])
    return [edge, edge, struct(kv_shape)]


def choose_alone(meta, kv, blocks):
    return pl.pallas_call(
        choose_kernel,
        in_specs=[SCALARS] + [ON_CHIP] * (1 + len(blocks)),
        out_specs=[ON_CHIP] * 3,
        out_shape=payloads(kv.shape),
        compiler_params=params(8),
        name="choose",
    )(meta, kv, *blocks)


def project_kernel(meta, *refs, with_stale):
    blocks = refs[:7]
    shift, scale, gain, w_own, w_other = refs[7:12]
    refs = refs[12:]
    if with_stale:
        stale, x_out, q_out, kv_out, *outs = refs[:-4]
    else:
        x_out, q_out, kv_out = refs[:-4]
    xs, modded, weights, sems = refs[-4:]
    rows, cols = x_out.shape
    tiles, rows_tile, kv_cols = kv_out.shape
    heads_cols = kv_cols // 2
    parts = shift.shape[0]
    width = cols * parts
    features = [lax.rem(meta[0] + j, parts) for j in range(parts)]

    def fetch(j, source):
        first = pl.multiple_of(features[j] * cols, cols)
        return pltpu.make_async_copy(
            source.at[:, pl.ds(first, cols)],
            weights.at[:, j * cols : (j + 1) * cols],
            sems.at[j],
        )

    for chosen, source in enumerate((w_other, w_own)):

        @pl.when(meta[1] == chosen)
        def _():
            for j in range(parts):
                fetch(j, source).start()

    own, next_a, next_b, far_a, far_b, prev_a, prev_b = blocks
    for r in range(tiles):
        tile = lax.rem(meta[2] + r, tiles)
        place = pl.ds(pl.multiple_of(tile * rows_tile, rows_tile), rows_tile)
        here = slice(r * rows_tile, (r + 1) * rows_tile)
        late = r >= tiles // 2
        there = slice((r % (tiles // 2)) * rows_tile, (r % (tiles // 2) + 1) * rows_tile)
        xs[0, place] = own[here]
        xs[1, place] = (next_b if late else next_a)[there]
        xs[2, place] = (far_b if late else far_a)[there]
        xs[3, place] = (prev_b if late else prev_a)[there]
    x_out[...] = xs[0]
    total = jnp.zeros((rows, 1), jnp.float32)
    for j in range(parts):
        total += jnp.sum(xs[j].astype(jnp.float32), axis=-1, keepdims=True)
    mean = total / width
    square = jnp.zeros((rows, 1), jnp.float32)
    for j in range(parts):
        centred = xs[j].astype(jnp.float32) - mean
        square += jnp.sum(centred * centred, axis=-1, keepdims=True)
    spread = lax.rsqrt(square / width + EPS)
    for j in range(parts):
        normed = (xs[j].astype(jnp.float32) - mean) * spread
        modded[:, j * cols : (j + 1) * cols] = (
            normed * (1.0 + scale[features[j]]) + shift[features[j]]
        ).astype(jnp.bfloat16)
    for j in range(parts):
        fetch(j, w_own).wait()

    for part in (1, 2, 0):
        product = jnp.dot(modded[...], weights[part], preferred_element_type=jnp.float32)
        if part == 2:
            kv_out[:, :, heads_cols:] = product.astype(jnp.bfloat16).reshape(
                tiles, rows_tile, heads_cols
            )
            continue
        for head in range(heads_cols // HEAD_DIM):
            cut = slice(head * HEAD_DIM, (head + 1) * HEAD_DIM)
            vec = product[:, cut]
            mean_sq = jnp.mean(vec * vec, axis=-1, keepdims=True)
            vec = vec * lax.rsqrt(mean_sq + EPS) * gain[part : part + 1]
            vec = vec.astype(jnp.bfloat16).reshape(tiles, rows_tile, HEAD_DIM)
            if part == 0:
                q_out[:, :, cut] = vec
            else:
                kv_out[:, :, cut] = vec
    if with_stale:
        choose(meta, kv_out, stale, outs)


def project(meta, blocks, shift, scale, gain, w_own, w_other, stale, kv_shape):
    rows, cols = blocks[0].shape
    tiles, rows_tile, kv_cols = kv_shape
    heads_cols = kv_cols // 2
    parts = shift.shape[0]
    shapes = [struct((rows, cols)), struct((tiles, rows_tile, heads_cols)), struct(kv_shape)]
    extra = []
    if stale is not None:
        shapes += payloads(kv_shape)
        extra = [stale]

    def kernel(*refs):
        project_kernel(*refs, with_stale=stale is not None)

    return pl.pallas_call(
        kernel,
        in_specs=[SCALARS]
        + [ON_CHIP] * (len(blocks) + 3)
        + [pl.BlockSpec(memory_space=pltpu.HBM)] * 2
        + [ON_CHIP] * len(extra),
        out_specs=[ON_CHIP] * len(shapes),
        out_shape=shapes,
        scratch_shapes=[
            pltpu.VMEM((parts, rows, cols), jnp.bfloat16),
            pltpu.VMEM((rows, parts * cols), jnp.bfloat16),
            pltpu.VMEM((3, parts * cols, heads_cols), jnp.bfloat16),
            pltpu.SemaphoreType.DMA((parts,)),
        ],
        compiler_params=params(46),
        name="project",
    )(meta, *blocks, shift, scale, gain, w_own, w_other, *extra)


def soften(queries, keys, values, times, floor):
    scores = lax.dot_general(
        queries, keys, (((1,), (1,)), ((), ())), preferred_element_type=jnp.float32
    )
    scores = jnp.where(times > 0.0, scores * HEAD_DIM ** (-0.5), -1e30)
    peak = jnp.max(scores, axis=-1, keepdims=True)
    if floor is not None:
        peak = jnp.maximum(peak, floor)
    weights = jnp.exp(scores - peak) * times
    total = jnp.sum(weights, axis=-1, keepdims=True)
    summed = jnp.dot(weights.astype(jnp.bfloat16), values, preferred_element_type=jnp.float32)
    return peak, total, summed


def attend_near_kernel(q_own, q_other, below, own, above, multiple, out, window):
    tiles, rows, heads_cols = q_own.shape
    window[: REACH * rows] = below[...].reshape(REACH * rows, 2 * heads_cols)
    window[REACH * rows : (REACH + tiles) * rows] = own[...].reshape(tiles * rows, 2 * heads_cols)
    window[(REACH + tiles) * rows :] = above[...].reshape(REACH * rows, 2 * heads_cols)
    lane = lax.broadcasted_iota(jnp.int32, (2 * rows, HEAD_DIM), 1)
    for tile in range(tiles):
        times = multiple[tile]
        span = slice(tile * rows, tile * rows + times.shape[-1])
        extra = jnp.zeros((2 * rows, HEAD_DIM), jnp.float32)
        for head in range(heads_cols // HEAD_DIM):
            first = head * HEAD_DIM
            cut = slice(first, first + HEAD_DIM)
            queries = jnp.concatenate([q_own[tile, :, cut], q_other[tile, :, cut]], axis=0)
            peak, total, summed = soften(
                queries,
                window[span, cut],
                window[span, heads_cols + first : heads_cols + first + HEAD_DIM],
                times,
                None,
            )
            out[tile, :, cut] = summed
            extra = jnp.where(lane == head, peak, extra)
            extra = jnp.where(lane == 64 + head, total, extra)
        out[tile, :, heads_cols:] = extra


def attend_near(q_own, q_other, below, own, above, multiple):
    tiles, rows, heads_cols = q_own.shape
    return pl.pallas_call(
        attend_near_kernel,
        in_specs=[ON_CHIP] * 6,
        out_specs=ON_CHIP,
        out_shape=struct((tiles, 2 * rows, heads_cols + HEAD_DIM), jnp.float32),
        scratch_shapes=[pltpu.VMEM(((tiles + 2 * REACH) * rows, 2 * heads_cols), jnp.bfloat16)],
        compiler_params=params(8),
        name="attend_near",
    )(q_own, q_other, below, own, above, multiple)


def attend_far_kernel(q_own, q_other, far, multiple, before, out_own, out_other):
    tiles, rows, heads_cols = q_own.shape
    lane = lax.broadcasted_iota(jnp.int32, (2 * rows, HEAD_DIM), 1)
    for tile in range(tiles):
        extra = jnp.zeros((2 * rows, HEAD_DIM), jnp.float32)
        for head in range(heads_cols // HEAD_DIM):
            first = head * HEAD_DIM
            cut = slice(first, first + HEAD_DIM)
            queries = jnp.concatenate([q_own[tile, :, cut], q_other[tile, :, cut]], axis=0)
            peak_before = before[tile, :, heads_cols + head : heads_cols + head + 1]
            total_before = before[tile, :, heads_cols + 64 + head : heads_cols + 65 + head]
            peak, total, summed = soften(
                queries,
                far[tile, :, cut],
                far[tile, :, heads_cols + first : heads_cols + first + HEAD_DIM],
                multiple[tile],
                peak_before,
            )
            shrink = jnp.exp(peak_before - peak)
            total += total_before * shrink
            summed += before[tile, :, cut] * shrink
            out_own[tile, :, cut] = summed[:rows]
            out_other[tile, :, cut] = summed[rows:]
            extra = jnp.where(lane == head, peak, extra)
            extra = jnp.where(lane == 64 + head, total, extra)
        out_own[tile, :, heads_cols:] = extra[:rows]
        out_other[tile, :, heads_cols:] = extra[rows:]


def attend_far(q_own, q_other, far, multiple, before):
    tiles, rows, heads_cols = q_own.shape
    return pl.pallas_call(
        attend_far_kernel,
        in_specs=[ON_CHIP] * 5,
        out_specs=[ON_CHIP] * 2,
        out_shape=[struct((tiles, rows, heads_cols + HEAD_DIM), jnp.float32)] * 2,
        compiler_params=params(8),
        name="attend_far",
    )(q_own, q_other, far, multiple, before)


def merge_kernel(part_a, part_b, att):
    tiles, rows, _ = part_a.shape
    heads_cols = att.shape[-1]
    for tile in range(tiles):
        extra_a = part_a[tile, :, heads_cols:]
        extra_b = part_b[tile, :, heads_cols:]
        for head in range(heads_cols // HEAD_DIM):
            cut = slice(head * HEAD_DIM, (head + 1) * HEAD_DIM)
            peak_a, total_a = extra_a[:, head : head + 1], extra_a[:, 64 + head : 65 + head]
            peak_b, total_b = extra_b[:, head : head + 1], extra_b[:, 64 + head : 65 + head]
            peak = jnp.maximum(peak_a, peak_b)
            grow_a, grow_b = jnp.exp(peak_a - peak), jnp.exp(peak_b - peak)
            total = total_a * grow_a + total_b * grow_b
            summed = part_a[tile, :, cut] * grow_a + part_b[tile, :, cut] * grow_b
            att[tile * rows : (tile + 1) * rows, cut] = (summed / total).astype(jnp.bfloat16)


def merge(part_a, part_b):
    tiles, rows, cols = part_a.shape
    return pl.pallas_call(
        merge_kernel,
        in_specs=[ON_CHIP] * 2,
        out_specs=ON_CHIP,
        out_shape=struct((tiles * rows, cols - HEAD_DIM)),
        compiler_params=params(8),
        name="merge",
    )(part_a, part_b)


def output_kernel(meta, att0, att1, att2, att3, wo_own, wo_other, hidden, gate, out):
    def finish(weight):
        product = jnp.zeros(out.shape, jnp.float32)
        for place, att in enumerate((att0, att1, att2, att3)):
            product += jnp.dot(att[...], weight[place], preferred_element_type=jnp.float32)
        out[...] = (hidden[...].astype(jnp.float32) + gate[...] * product).astype(out.dtype)

    @pl.when(meta[1] == 1)
    def _():
        finish(wo_own)

    @pl.when(meta[1] == 0)
    def _():
        finish(wo_other)


def output(meta, atts, wo_own, wo_other, hidden, gate):
    return pl.pallas_call(
        output_kernel,
        in_specs=[SCALARS] + [ON_CHIP] * 8,
        out_specs=ON_CHIP,
        out_shape=struct(hidden.shape),
        compiler_params=params(8),
        name="output",
    )(meta, *atts, wo_own, wo_other, hidden, gate)


def count_tiles(table, counts, chip, per_chip, repeat):
    tiles, slots = table.shape
    table = lax.dynamic_slice_in_dim(table, chip * per_chip, per_chip, 0)
    counts = lax.dynamic_slice_in_dim(counts, chip * per_chip, per_chip, 0)
    query_tiles = jnp.arange(per_chip, dtype=jnp.int32) + chip * per_chip
    across = tiles // 2 + (tiles // per_chip) // 2
    distances = list(range(-REACH, REACH + 1)) + [across]
    reach = jnp.repeat(jnp.array([d % tiles for d in distances], jnp.int32), repeat)
    relative = (table - query_tiles[:, None]) % tiles
    live = jnp.arange(slots, dtype=jnp.int32)[None] < counts[:, None]
    hits = (relative[:, :, None] == reach[None, None]) & live[:, :, None]
    return jnp.sum(hits.astype(jnp.float32), axis=1)[:, None]


def gather_features(hidden):
    half = hidden.shape[0] // 2
    halves = (hidden[:half], hidden[half:])
    prev_a = shifted(halves[0], "tp", 1)
    next_b = shifted(halves[1], "tp", -1)
    prev_b = shifted(halves[1], "tp", 1)
    next_a = shifted(halves[0], "tp", -1)
    prev_a, next_b = lax.optimization_barrier((prev_a, next_b))
    far_a = shifted(prev_a, "tp", 1)
    far_b = shifted(next_b, "tp", -1)
    return hidden, next_a, next_b, far_a, far_b, prev_a, prev_b


def local(
    latents, w_qkv, w_out, modulation, qk_gain, stale_cache, kv_tiles, tile_counts, patch_order
):
    core = lax.axis_index("segment")
    seq_size = lax.axis_size("seq")
    chip = lax.axis_index("seq")
    tp_size = lax.axis_size("tp")
    tp_pos = lax.axis_index("tp")
    patches, patch_rows, part_cols = latents.shape
    rows_core = patch_rows // 2
    rows = patches * rows_core
    share = seq_size // patches
    w_own = jnp.transpose(w_qkv[0], (1, 0, 2))
    heads_cols, width = w_out.shape[1:]
    head_dim = qk_gain.shape[-1]

    place = jnp.stack([core, lax.rem(chip, patches), chip // share]).astype(jnp.int32)
    x_rounds = to_work(deal_latents(place, latents))
    w_other = shifted(w_own, "segment", 1)
    small_own = jnp.concatenate([modulation[0].reshape(-1), qk_gain[0].reshape(-1)])
    small_other = shifted(small_own, "segment", 1)
    hidden = jnp.concatenate(x_rounds, axis=0)
    blocks = gather_features(hidden)
    stale_own, stale_send = halve_stale(place, stale_cache[0])
    stale_other = shifted(stale_send, "segment", 1)
    stale_rounds = list(deal_stale(place, stale_own, stale_other))
    stale_rounds[:4], w_out = after((stale_rounds[:4], w_out), blocks[2], blocks[5])
    stale_rounds[4:] = after(stale_rounds[4:], blocks)
    stale_rounds = to_work(stale_rounds)

    rows_chip = heads_cols // seq_size
    slab = lax.dynamic_slice_in_dim(w_out[0], chip * rows_chip, rows_chip, 0)
    pieces = [
        lax.dynamic_slice_in_dim(slab, lax.rem(tp_pos + j, tp_size) * part_cols, part_cols, 1)
        for j in range(tp_size)
    ]
    pieces[1:] = [shifted(pieces[j], "tp", j) for j in range(1, tp_size)]
    wo_own = lax.all_gather(jnp.stack(pieces), "seq", axis=1, tiled=True)

    turns = jnp.arange(patches, dtype=jnp.int32)
    asked = jnp.stack([chip, chip - 1, chip + 1, chip - seq_size // 2 - 1]) % seq_size // share
    ranks = jnp.sum(jnp.where(patch_order[None] == asked[:, None], turns[None], 0), axis=-1)
    fresh = (ranks[0] <= ranks[1:]).astype(jnp.int32)

    for section in range(2):
        is_own = core == section
        start = chip // share if section == 0 else jnp.zeros_like(chip)
        meta = jnp.concatenate(
            [jnp.stack([tp_pos, is_own.astype(tp_pos.dtype), start]).astype(jnp.int32), fresh]
        )
        small = jnp.where(is_own, small_own, small_other)
        modul = small[: 3 * width].reshape(3, tp_size, 1, part_cols)
        gain = small[3 * width :].reshape(2, head_dim)
        gate = lax.dynamic_index_in_dim(modul[2], tp_pos, 0, keepdims=False)
        if section > 0:
            blocks = gather_features(hidden)
            early[:4] = after(early[:4], blocks[2], blocks[5])
            early[4:] = after(early[4:], blocks)
            early = to_home(early)
            blocks, early[:4] = lax.optimization_barrier((blocks, early[:4]))
        hidden, q_own, kv, *going = project(
            meta,
            blocks,
            modul[0],
            modul[1],
            gain,
            w_own,
            w_other,
            stale if section > 0 else None,
            stale_own.shape,
        )
        if section == 0:
            going = choose_alone(meta, kv, stale_rounds)
            stale = sort_stale(place, after(stale_rounds, going))
        to_below, to_above, to_far = going
        above = shifted(to_below, "seq", -1)
        below = shifted(to_above, "seq", 1)
        q_other = shifted(q_own, "segment", 1)
        far = shifted(to_far, "seq", -(seq_size // 2) - 1)
        if section == 0:
            kv_tiles, tile_counts = after((kv_tiles, tile_counts), q_own)
            multiple_own = count_tiles(kv_tiles[0], tile_counts[0], chip, patches, rows_core)
            multiple_other = shifted(multiple_own, "segment", 1)
        else:
            above, early = lax.optimization_barrier((above, early))
        multiple = jnp.where(is_own, multiple_own, multiple_other)
        cut = multiple.shape[-1] - rows_core
        before = attend_near(q_own, q_other, below, kv, above, multiple[..., :cut])
        part_own, part_other = attend_far(q_own, q_other, far, multiple[..., cut:], before)
        if section == 0:
            wo_other = shifted(after(wo_own, part_other), "segment", 1)
        part_back = shifted(part_other, "segment", 1)
        att = merge(part_own, part_back)
        atts = [att] + [shifted(att, "tp", j) for j in (1, 2, 3)]
        hidden = output(meta, atts, wo_own, wo_other, hidden, gate)

        features = hidden.reshape(patches, rows_core, part_cols)
        pair = (kv, features) if section == 0 else (features, kv)
        got = shifted(jnp.where(core == 0, pair[1], pair[0]), "segment", 1)
        dealt = list(deal_results(place, *pair, got))
        if section == 0:
            early = dealt
        else:
            late = to_home(dealt)

    handed, new_cache = collect(place, early, late)
    return (handed[None], new_cache[None])


def solution(mesh):
    in_specs = (
        P(None, "seq", "tp"),
        P("segment", None, None, "tp"),
        P("segment", "tp", None),
        P("segment", None, None),
        P("segment", None, None),
        P("segment", None, None, "seq", "tp"),
        P("segment", None, None),
        P("segment", None),
        P(),
    )
    out_specs = (P("segment", None, "seq", "tp"), P("segment", None, None, "seq", "tp"))
    return jax.shard_map(local, mesh=mesh, in_specs=in_specs, out_specs=out_specs, check_vma=False)
```

time: 1610 us -> 329 us (0.20)
  the two profiles are of different devices: /device:TPU:1 before, /device:TPU:6 now
where the time goes in v2:
time: 329 us; the launch traced here: 323 us
  starting transfers between devices  155 us (47%)
  waiting for transfers between devices  90.9 us (28%)
  Pallas kernels  48.3 us (15%)
  between operations  15.4 us (5%)
  local copies, waits for them, and re-layouts  11.5 us (3%)
    ppermute x38, waiting for transfers between devices, shifted(): return lax.ppermute(block, axis, route)  62.1 us
    ppermute x16, starting transfers between devices, to_home(): out.append(lax.ppermute(block, 'seq', route))  60.4 us
    ppermute x16, starting transfers between devices, to_work(): out.append(lax.ppermute(block, 'seq', route))  54.1 us
    ppermute x38, starting transfers between devices, shifted(): return lax.ppermute(block, axis, route)  40.5 us
    ppermute x16, waiting for transfers between devices, to_home(): out.append(lax.ppermute(block, 'seq', route))  21.4 us
    pallas_call x2, Pallas kernels, project(): pl.pallas_call(kernel, in_specs=[SCALARS] + [ON_CHIP] * (len(blocks) + 3)...  14.6 us
    pallas_call x2, Pallas kernels, attend_near(): pl.pallas_call(attend_near_kernel, in_specs=[ON_CHIP] * 6, out_specs=ON_C...  13.1 us
    pallas_call x2, Pallas kernels, attend_far(): pl.pallas_call(attend_far_kernel, in_specs=[ON_CHIP] * 5, out_specs=[ON_C...  9.6 us
  transfers between devices with their start and end apart: 71, of which 28 were waited for; matrix products, arithmetic and copies ran while one was open for 2% of the time, Pallas kernels for 9%

profile of v2, /device:TPU:6, one launch (start us, length us, event | category | flops | bytes accessed | tf_op | source)
XLA Modules:
  0.0 323.4 jit_solution(16721579318347840183)
XLA Ops:
  18.0 8.3 %collective-permute-start.3 = (bf16[32,768]{1,0:T(8,128)(2,1)S(1)}, bf16[32,768]{1,0:T(8,128)(2,1)S(1)}, u32[]{:S(2)}, u32[]{:S(2)}) collective-permute-start(bf16[32,768]{1,0:T(8,128)(2,1)S(1)} %get-tuple-element.109), channel_id=1, source_target_pairs={{0,40},{4,48},{8,56},{12,0},{16,8},{20,16},{24,24},{28,32},{32,44}... | collective-permute-start | bytes 147464 | tf_op jit(solution)/shard_map/ppermute | solution.py:42
  28.5 5.2 %collective-permute-start.5 = (bf16[32,768]{1,0:T(8,128)(2,1)S(1)}, bf16[32,768]{1,0:T(8,128)(2,1)S(1)}, u32[]{:S(2)}, u32[]{:S(2)}) collective-permute-start(bf16[32,768]{1,0:T(8,128)(2,1)S(1)} %get-tuple-element.111), channel_id=1, source_target_pairs={{0,24},{4,32},{8,40},{12,48},{16,56},{20,0},{24,8},{28,16},{32,28}... | collective-permute-start | bytes 147464 | tf_op jit(solution)/shard_map/ppermute | solution.py:42
  40.9 5.3 %collective-permute-done.7 = bf16[32,768]{1,0:T(8,128)(2,1)S(1)} collective-permute-done((bf16[32,768]{1,0:T(8,128)(2,1)S(1)}, bf16[32,768]{1,0:T(8,128)(2,1)S(1)}, u32[]{:S(2)}, u32[]{:S(2)}) %collective-permute-start.7) | collective-permute-done | bytes 49184 | tf_op jit(solution)/shard_map/ppermute | solution.py:42
  83.5 7.4 %collective-permute-start.21 = (bf16[64,768]{1,0:T(8,128)(2,1)S(1)}, bf16[64,768]{1,0:T(8,128)(2,1)S(1)}, u32[]{:S(2)}, u32[]{:S(2)}) collective-permute-start(bf16[64,768]{1,0:T(8,128)(2,1)S(1)} %get-tuple-element.127), channel_id=1, source_target_pairs={{0,40},{4,48},{8,56},{12,0},{16,8},{20,16},{24,24},{28,32},{32,44}... | collective-permute-start | bytes 294920 | tf_op jit(solution)/shard_map/ppermute | solution.py:42
  92.9 4.5 %collective-permute-start.23 = (bf16[64,768]{1,0:T(8,128)(2,1)S(1)}, bf16[64,768]{1,0:T(8,128)(2,1)S(1)}, u32[]{:S(2)}, u32[]{:S(2)}) collective-permute-start(bf16[64,768]{1,0:T(8,128)(2,1)S(1)} %get-tuple-element.133), channel_id=1, source_target_pairs={{0,24},{4,32},{8,40},{12,48},{16,56},{20,0},{24,8},{28,16},{32,28}... | collective-permute-start | bytes 294920 | tf_op jit(solution)/shard_map/ppermute | solution.py:42
  103.7 7.8 %project.2 = (bf16[256,768]{1,0:T(8,128)(2,1)S(1)}, bf16[8,32,384]{2,1,0:T(8,128)(2,1)S(1)}, bf16[8,32,768]{2,1,0:T(8,128)(2,1)S(1)}) custom-call(s32[6]{0:T(128)S(1)} %get-tuple-element.242.refs_0_.meta, bf16[256,768]{1,0:T(8,128)(2,1)S(1)} %get-tuple-element.219.refs_1_, bf16[128,768]{1,0:T(8,128)(2,1)S(1)} %collective-permute-done.8.refs_2_, ...), custom_call_target="tpu_custom_call" | custom-call | tf_op jit(solution)/shard_map/project/pallas_call | solution.py:351
  122.6 8.4 %collective-permute-done.29.above = bf16[3,32,768]{2,1,0:T(8,128)(2,1)S(1)} collective-permute-done((bf16[3,32,768]{2,1,0:T(8,128)(2,1)S(1)}, bf16[3,32,768]{2,1,0:T(8,128)(2,1)S(1)}, u32[]{:S(2)}, u32[]{:S(2)}) %collective-permute-start.29) | collective-permute-done | bytes 147488 | tf_op jit(solution)/shard_map/ppermute | solution.py:19
  131.0 6.5 %attend_near.2.before = f32[8,64,512]{2,1,0:T(8,128)S(1)} custom-call(bf16[8,32,384]{2,1,0:T(8,128)(2,1)S(1)} %get-tuple-element.116.q_own, bf16[8,32,384]{2,1,0:T(8,128)(2,1)S(1)} %collective-permute-done.16.q_other, bf16[3,32,768]{2,1,0:T(8,128)(2,1)S(1)} %collective-permute-done.28.below, bf16[8,32,768]{2,1,0:T(8,128)(2,1)S(1)} %get-tuple-element.117.kv.own.for_first, ...), custom_call_target="tpu_custom_call" | custom-call | tf_op jit(solution)/shard_map/attend_near/pallas_call | solution.py:413
  137.6 4.8 %attend_far.2 = (f32[8,32,512]{2,1,0:T(8,128)S(1)}, f32[8,32,512]{2,1,0:T(8,128)S(1)}) custom-call(bf16[8,32,384]{2,1,0:T(8,128)(2,1)S(1)} %get-tuple-element.116.q_own, bf16[8,32,384]{2,1,0:T(8,128)(2,1)S(1)} %collective-permute-done.16.q_other, bf16[8,32,768]{2,1,0:T(8,128)(2,1)S(1)} %collective-permute-done.26.far, f32[8,1,32]{2,1,0:T(1,128)S(1)} %slice.137.multiple, ...), custom_call_target="tpu_custom_call" | custom-call | tf_op jit(solution)/shard_map/attend_far/pallas_call | solution.py:455
  143.7 5.0 %collective-permute-done.30.part_b = f32[8,32,512]{2,1,0:T(8,128)S(1)} collective-permute-done((f32[8,32,512]{2,1,0:T(8,128)}, f32[8,32,512]{2,1,0:T(8,128)S(1)}, u32[]{:S(2)}, u32[]{:S(2)}) %collective-permute-start.30) | collective-permute-done | bytes 524320 | tf_op jit(solution)/shard_map/ppermute | solution.py:19
  152.9 4.6 %collective-permute-done.33.att3 = bf16[256,384]{1,0:T(8,128)(2,1)S(1)} collective-permute-done((bf16[256,384]{1,0:T(8,128)(2,1)S(1)}, bf16[256,384]{1,0:T(8,128)(2,1)S(1)}, u32[]{:S(2)}, u32[]{:S(2)}) %collective-permute-start.33) | collective-permute-done | bytes 196640 | tf_op jit(solution)/shard_map/ppermute | solution.py:19
  178.5 8.5 %collective-permute-start.42 = (bf16[128,768]{1,0:T(8,128)(2,1)S(1)}, bf16[128,768]{1,0:T(8,128)(2,1)S(1)}, u32[]{:S(2)}, u32[]{:S(2)}) collective-permute-start(bf16[128,768]{1,0:T(8,128)(2,1)S(1)} %collective-permute-done.40.refs_3_), channel_id=1, source_target_pairs={{1,0},{2,1},{3,2},{0,3},{5,4},{6,5},{7,6},{4,7},{9,8},{10,9},{11,1... | collective-permute-start | bytes 589832 | tf_op jit(solution)/shard_map/ppermute | solution.py:19
  189.7 5.7 %collective-permute-start.45 = (bf16[64,768]{1,0:T(8,128)(2,1)S(1)}, bf16[64,768]{1,0:T(8,128)(2,1)S(1)}, u32[]{:S(2)}, u32[]{:S(2)}) collective-permute-start(bf16[64,768]{1,0:T(8,128)(2,1)S(1)} %get-tuple-element.152), channel_id=1, source_target_pairs={{0,0},{4,32},{8,4},{12,36},{16,8},{20,40},{24,12},{28,44},{32,16},... | collective-permute-start | bytes 294920 | tf_op jit(solution)/shard_map/ppermute | solution.py:54
  197.3 5.1 %collective-permute-start.47 = (bf16[64,768]{1,0:T(8,128)(2,1)S(1)}, bf16[64,768]{1,0:T(8,128)(2,1)S(1)}, u32[]{:S(2)}, u32[]{:S(2)}) collective-permute-start(bf16[64,768]{1,0:T(8,128)(2,1)S(1)} %get-tuple-element.154), channel_id=1, source_target_pairs={{0,8},{4,40},{8,12},{12,44},{16,16},{20,48},{24,20},{28,52},{32,24... | collective-permute-start | bytes 294920 | tf_op jit(solution)/shard_map/ppermute | solution.py:54
  210.9 6.8 %project.3 = (bf16[256,768]{1,0:T(8,128)(2,1)S(1)}, bf16[8,32,384]{2,1,0:T(8,128)(2,1)S(1)}, bf16[8,32,768]{2,1,0:T(8,128)(2,1)S(1)}, bf16[3,32,768]{2,1,0:T(8,1...) custom-call(s32[6]{0:T(128)S(1)} %copy-done.27, bf16[256,768]{1,0:T(8,128)(2,1)S(1)} %output.2.refs_1_, ...), custom_call_target="tpu_custom_call" | custom-call | tf_op jit(solution)/shard_map/project/pallas_call | solution.py:351
  228.4 7.6 %collective-permute-done.51.refs_5_ = bf16[64,768]{1,0:T(8,128)(2,1)S(1)} collective-permute-done((bf16[64,768]{1,0:T(8,128)(2,1)S(1)}, bf16[64,768]{1,0:T(8,128)(2,1)S(1)}, u32[]{:S(2)}, u32[]{:S(2)}) %collective-permute-start.51) | collective-permute-done | bytes 98336 | tf_op jit(solution)/shard_map/ppermute | solution.py:54
  235.9 4.7 %collective-permute-start.53 = (bf16[64,768]{1,0:T(8,128)(2,1)S(1)}, bf16[64,768]{1,0:T(8,128)(2,1)S(1)}, u32[]{:S(2)}, u32[]{:S(2)}) collective-permute-start(bf16[64,768]{1,0:T(8,128)(2,1)S(1)} %get-tuple-element.183), channel_id=1, source_target_pairs={{0,28},{4,60},{8,0},{12,32},{16,4},{20,36},{24,8},{28,40},{32,12},... | collective-permute-start | bytes 294920 | tf_op jit(solution)/shard_map/ppermute | solution.py:54
  240.8 5.3 %collective-permute-done.53.refs_7_ = bf16[64,768]{1,0:T(8,128)(2,1)S(1)} collective-permute-done((bf16[64,768]{1,0:T(8,128)(2,1)S(1)}, bf16[64,768]{1,0:T(8,128)(2,1)S(1)}, u32[]{:S(2)}, u32[]{:S(2)}) %collective-permute-start.53) | collective-permute-done | bytes 98336 | tf_op jit(solution)/shard_map/ppermute | solution.py:54
  246.1 6.5 %attend_near.3.before = f32[8,64,512]{2,1,0:T(8,128)S(1)} custom-call(bf16[8,32,384]{2,1,0:T(8,128)(2,1)S(1)} %get-tuple-element.192.q_own, bf16[8,32,384]{2,1,0:T(8,128)(2,1)S(1)} %collective-permute-done.54.q_other, bf16[3,32,768]{2,1,0:T(8,128)(2,1)S(1)} %collective-permute-done.56.below, bf16[8,32,768]{2,1,0:T(8,128)(2,1)S(1)} %get-tuple-element.195.own.for_second, ...), custom_call_target="tpu_custom_call" | custom-call | tf_op jit(solution)/shard_map/attend_near/pallas_call | solution.py:413
  252.6 4.8 %attend_far.3 = (f32[8,32,512]{2,1,0:T(8,128)S(1)}, f32[8,32,512]{2,1,0:T(8,128)S(1)}) custom-call(bf16[8,32,384]{2,1,0:T(8,128)(2,1)S(1)} %get-tuple-element.192.q_own, bf16[8,32,384]{2,1,0:T(8,128)(2,1)S(1)} %collective-permute-done.54.q_other, bf16[8,32,768]{2,1,0:T(8,128)(2,1)S(1)} %collective-permute-done.55.far, f32[8,1,32]{2,1,0:T(1,128)S(1)} %slice.145.multiple, ...), custom_call_target="tpu_custom_call" | custom-call | tf_op jit(solution)/shard_map/attend_far/pallas_call | solution.py:455
  264.2 7.1 %collective-permute-done.60.att3 = bf16[256,384]{1,0:T(8,128)(2,1)S(1)} collective-permute-done((bf16[256,384]{1,0:T(8,128)(2,1)S(1)}, bf16[256,384]{1,0:T(8,128)(2,1)S(1)}, u32[]{:S(2)}, u32[]{:S(2)}) %collective-permute-start.60) | collective-permute-done | bytes 196640 | tf_op jit(solution)/shard_map/ppermute | solution.py:19
  288.4 7.9 %collective-permute-start.65 = (bf16[64,768]{1,0:T(8,128)(2,1)S(1)}, bf16[64,768]{1,0:T(8,128)(2,1)S(1)}, u32[]{:S(2)}, u32[]{:S(2)}) collective-permute-start(bf16[64,768]{1,0:T(8,128)(2,1)S(1)} %get-tuple-element.203), channel_id=1, source_target_pairs={{0,12},{4,44},{8,16},{12,48},{16,20},{20,52},{24,24},{28,56},{32,2... | collective-permute-start | bytes 294920 | tf_op jit(solution)/shard_map/ppermute | solution.py:54
  296.4 6.0 %collective-permute-start.67 = (bf16[64,768]{1,0:T(8,128)(2,1)S(1)}, bf16[64,768]{1,0:T(8,128)(2,1)S(1)}, u32[]{:S(2)}, u32[]{:S(2)}) collective-permute-start(bf16[64,768]{1,0:T(8,128)(2,1)S(1)} %get-tuple-element.205), channel_id=1, source_target_pairs={{0,20},{4,52},{8,24},{12,56},{16,28},{20,60},{24,0},{28,32},{32,4}... | collective-permute-start | bytes 294920 | tf_op jit(solution)/shard_map/ppermute | solution.py:54
  304.4 4.6 %collective-permute-start.69 = (bf16[64,768]{1,0:T(8,128)(2,1)S(1)}, bf16[64,768]{1,0:T(8,128)(2,1)S(1)}, u32[]{:S(2)}, u32[]{:S(2)}) collective-permute-start(bf16[64,768]{1,0:T(8,128)(2,1)S(1)} %get-tuple-element.207), channel_id=1, source_target_pairs={{0,28},{4,60},{8,0},{12,32},{16,4},{20,36},{24,8},{28,40},{32,12},... | collective-permute-start | bytes 294920 | tf_op jit(solution)/shard_map/ppermute | solution.py:54
  (244 shorter events, 159.5 us)
Async XLA Ops:
  7.2 135.2 %all-gather.2.cloned.1.call-start = ((), (), s32[]{:S(2)}) async-start(), calls=%async_computation | async-start | bytes 2506752 | tf_op jit(solution)/shard_map/all_gather | solution.py:585
  7.3 92.5 %collective-permute-start.15 = (bf16[3,3072,384]{2,1,0:T(8,128)(2,1)}, bf16[3,3072,384]{2,1,0:T(8,128)(2,1)}, u32[]{:S(2)}, u32[]{:S(2)}) collective-permute-start(bf16[3,3072,384]{2,1,0:T(8,128)(2,1)} %bitcast.66), channel_id=1, source_target_pairs={{64,0},{0,64},{65,1},{1,65},{66,2},{2,66},{67,3},{3,67},{68,4},{4,... | collective-permute-start | bytes 21233672 | tf_op jit(solution)/shard_map/ppermute | solution.py:19
  9.2 18.9 %collective-permute-start = (bf16[32,768]{1,0:T(8,128)(2,1)S(1)}, bf16[32,768]{1,0:T(8,128)(2,1)S(1)}, u32[]{:S(2)}, u32[]{:S(2)}) collective-permute-start(bf16[32,768]{1,0:T(8,128)(2,1)S(1)} %get-tuple-element.106), channel_id=1, source_target_pairs={{0,0},{4,8},{8,16},{12,24},{16,32},{20,40},{24,48},{28,56},{32,4},... | collective-permute-start | bytes 147464 | tf_op jit(solution)/shard_map/ppermute | solution.py:42
  16.1 17.6 %collective-permute-start.2 = (bf16[32,768]{1,0:T(8,128)(2,1)S(1)}, bf16[32,768]{1,0:T(8,128)(2,1)S(1)}, u32[]{:S(2)}, u32[]{:S(2)}) collective-permute-start(bf16[32,768]{1,0:T(8,128)(2,1)S(1)} %get-tuple-element.108), channel_id=1, source_target_pairs={{0,48},{4,56},{8,0},{12,8},{16,16},{20,24},{24,32},{28,40},{32,52}... | collective-permute-start | bytes 147464 | tf_op jit(solution)/shard_map/ppermute | solution.py:42
  18.0 18.6 %collective-permute-start.3 = (bf16[32,768]{1,0:T(8,128)(2,1)S(1)}, bf16[32,768]{1,0:T(8,128)(2,1)S(1)}, u32[]{:S(2)}, u32[]{:S(2)}) collective-permute-start(bf16[32,768]{1,0:T(8,128)(2,1)S(1)} %get-tuple-element.109), channel_id=1, source_target_pairs={{0,40},{4,48},{8,56},{12,0},{16,8},{20,16},{24,24},{28,32},{32,44}... | collective-permute-start | bytes 147464 | tf_op jit(solution)/shard_map/ppermute | solution.py:42
  39.2 18.1 %collective-permute-start.17 = (bf16[8,32,768]{2,1,0:T(8,128)(2,1)S(1)}, bf16[8,32,768]{2,1,0:T(8,128)(2,1)S(1)}, u32[]{:S(2)}, u32[]{:S(2)}) collective-permute-start(bf16[8,32,768]{2,1,0:T(8,128)(2,1)S(1)} %get-tuple-element.119), channel_id=1, source_target_pairs={{64,0},{0,64},{65,1},{1,65},{66,2},{2,66},{67,3},{3,67},{68,4},{4,... | collective-permute-start | bytes 1179656 | tf_op jit(solution)/shard_map/ppermute | solution.py:19
  83.5 28.8 %collective-permute-start.21 = (bf16[64,768]{1,0:T(8,128)(2,1)S(1)}, bf16[64,768]{1,0:T(8,128)(2,1)S(1)}, u32[]{:S(2)}, u32[]{:S(2)}) collective-permute-start(bf16[64,768]{1,0:T(8,128)(2,1)S(1)} %get-tuple-element.127), channel_id=1, source_target_pairs={{0,40},{4,48},{8,56},{12,0},{16,8},{20,16},{24,24},{28,32},{32,44}... | collective-permute-start | bytes 294920 | tf_op jit(solution)/shard_map/ppermute | solution.py:42
  91.0 21.4 %collective-permute-start.22 = (bf16[64,768]{1,0:T(8,128)(2,1)S(1)}, bf16[64,768]{1,0:T(8,128)(2,1)S(1)}, u32[]{:S(2)}, u32[]{:S(2)}) collective-permute-start(bf16[64,768]{1,0:T(8,128)(2,1)S(1)} %get-tuple-element.132), channel_id=1, source_target_pairs={{0,32},{4,40},{8,48},{12,56},{16,0},{20,8},{24,16},{28,24},{32,36}... | collective-permute-start | bytes 294920 | tf_op jit(solution)/shard_map/ppermute | solution.py:42
  92.9 19.4 %collective-permute-start.23 = (bf16[64,768]{1,0:T(8,128)(2,1)S(1)}, bf16[64,768]{1,0:T(8,128)(2,1)S(1)}, u32[]{:S(2)}, u32[]{:S(2)}) collective-permute-start(bf16[64,768]{1,0:T(8,128)(2,1)S(1)} %get-tuple-element.133), channel_id=1, source_target_pairs={{0,24},{4,32},{8,40},{12,48},{16,56},{20,0},{24,8},{28,16},{32,28}... | collective-permute-start | bytes 294920 | tf_op jit(solution)/shard_map/ppermute | solution.py:42
  113.1 24.4 %collective-permute-start.26 = (bf16[8,32,768]{2,1,0:T(8,128)(2,1)S(1)}, bf16[8,32,768]{2,1,0:T(8,128)(2,1)S(1)}, u32[]{:S(2)}, u32[]{:S(2)}) collective-permute-start(bf16[8,32,768]{2,1,0:T(8,128)(2,1)S(1)} %get-tuple-element.136), channel_id=1, source_target_pairs={{36,0},{40,4},{44,8},{48,12},{52,16},{56,20},{60,24},{0,28},{4,32}... | collective-permute-start | bytes 1179656 | tf_op jit(solution)/shard_map/ppermute | solution.py:19
  143.2 20.5 %collective-permute-start.37 = (bf16[4,384,768]{2,1,0:T(8,128)(2,1)}, bf16[4,384,768]{2,1,0:T(8,128)(2,1)S(1)}, u32[]{:S(2)}, u32[]{:S(2)}) collective-permute-start(bf16[4,384,768]{2,1,0:T(8,128)(2,1)} %all-gather.2.cloned.1.call-done.wo_own), channel_id=1, source_target_pairs={{64,0},{0,64},{65,1},{1,65},{66,2},{2,66},{67,3},{3,67},{68,4},{4,... | collective-permute-start | bytes 7077896 | tf_op jit(solution)/shard_map/ppermute | solution.py:19
  168.7 20.3 %collective-permute-start.44 = (bf16[8,32,768]{2,1,0:T(8,128)(2,1)S(1)}, bf16[8,32,768]{2,1,0:T(8,128)(2,1)S(1)}, u32[]{:S(2)}, u32[]{:S(2)}) collective-permute-start(bf16[8,32,768]{2,1,0:T(8,128)(2,1)S(1)} %broadcast_select_fusion.1), channel_id=1, source_target_pairs={{64,0},{0,64},{65,1},{1,65},{66,2},{2,66},{67,3},{3,67},{68,4},{4,... | collective-permute-start | bytes 1179656 | tf_op jit(solution)/shard_map/ppermute | solution.py:19
  170.9 24.4 %collective-permute-start.43 = (bf16[128,768]{1,0:T(8,128)(2,1)S(1)}, bf16[128,768]{1,0:T(8,128)(2,1)S(1)}, u32[]{:S(2)}, u32[]{:S(2)}) collective-permute-start(bf16[128,768]{1,0:T(8,128)(2,1)S(1)} %get-tuple-element.214), channel_id=1, source_target_pairs={{3,0},{0,1},{1,2},{2,3},{7,4},{4,5},{5,6},{6,7},{11,8},{8,9},{9,10... | collective-permute-start | bytes 589832 | tf_op jit(solution)/shard_map/ppermute | solution.py:19
  171.0 26.3 %collective-permute-start.38 = (bf16[128,768]{1,0:T(8,128)(2,1)S(1)}, bf16[128,768]{1,0:T(8,128)(2,1)S(1)}, u32[]{:S(2)}, u32[]{:S(2)}) collective-permute-start(bf16[128,768]{1,0:T(8,128)(2,1)S(1)} %get-tuple-element.215), channel_id=1, source_target_pairs={{1,0},{2,1},{3,2},{0,3},{5,4},{6,5},{7,6},{4,7},{9,8},{10,9},{11,1... | collective-permute-start | bytes 589832 | tf_op jit(solution)/shard_map/ppermute | solution.py:19
  178.5 23.9 %collective-permute-start.42 = (bf16[128,768]{1,0:T(8,128)(2,1)S(1)}, bf16[128,768]{1,0:T(8,128)(2,1)S(1)}, u32[]{:S(2)}, u32[]{:S(2)}) collective-permute-start(bf16[128,768]{1,0:T(8,128)(2,1)S(1)} %collective-permute-done.40.refs_3_), channel_id=1, source_target_pairs={{1,0},{2,1},{3,2},{0,3},{5,4},{6,5},{7,6},{4,7},{9,8},{10,9},{11,1... | collective-permute-start | bytes 589832 | tf_op jit(solution)/shard_map/ppermute | solution.py:19
  187.0 21.2 %collective-permute-start.41 = (bf16[128,768]{1,0:T(8,128)(2,1)S(1)}, bf16[128,768]{1,0:T(8,128)(2,1)S(1)}, u32[]{:S(2)}, u32[]{:S(2)}) collective-permute-start(bf16[128,768]{1,0:T(8,128)(2,1)S(1)} %collective-permute-done.39.refs_6_), channel_id=1, source_target_pairs={{3,0},{0,1},{1,2},{2,3},{7,4},{4,5},{5,6},{6,7},{11,8},{8,9},{9,10... | collective-permute-start | bytes 589832 | tf_op jit(solution)/shard_map/ppermute | solution.py:19
  189.7 18.6 %collective-permute-start.45 = (bf16[64,768]{1,0:T(8,128)(2,1)S(1)}, bf16[64,768]{1,0:T(8,128)(2,1)S(1)}, u32[]{:S(2)}, u32[]{:S(2)}) collective-permute-start(bf16[64,768]{1,0:T(8,128)(2,1)S(1)} %get-tuple-element.152), channel_id=1, source_target_pairs={{0,0},{4,32},{8,4},{12,36},{16,8},{20,40},{24,12},{28,44},{32,16},... | collective-permute-start | bytes 294920 | tf_op jit(solution)/shard_map/ppermute | solution.py:54
  217.7 34.9 %collective-permute-start.55 = (bf16[8,32,768]{2,1,0:T(8,128)(2,1)S(1)}, bf16[8,32,768]{2,1,0:T(8,128)(2,1)S(1)}, u32[]{:S(2)}, u32[]{:S(2)}) collective-permute-start(bf16[8,32,768]{2,1,0:T(8,128)(2,1)S(1)} %get-tuple-element.193), channel_id=1, source_target_pairs={{36,0},{40,4},{44,8},{48,12},{52,16},{56,20},{60,24},{0,28},{4,32}... | collective-permute-start | bytes 1179656 | tf_op jit(solution)/shard_map/ppermute | solution.py:19
  227.5 18.5 %collective-permute-start.54 = (bf16[8,32,384]{2,1,0:T(8,128)(2,1)S(1)}, bf16[8,32,384]{2,1,0:T(8,128)(2,1)S(1)}, u32[]{:S(2)}, u32[]{:S(2)}) collective-permute-start(bf16[8,32,384]{2,1,0:T(8,128)(2,1)S(1)} %get-tuple-element.192.q_own), channel_id=1, source_target_pairs={{64,0},{0,64},{65,1},{1,65},{66,2},{2,66},{67,3},{3,67},{68,4},{4,... | collective-permute-start | bytes 589832 | tf_op jit(solution)/shard_map/ppermute | solution.py:19
  228.0 18.1 %collective-permute-start.49 = (bf16[3,32,768]{2,1,0:T(8,128)(2,1)S(1)}, bf16[3,32,768]{2,1,0:T(8,128)(2,1)S(1)}, u32[]{:S(2)}, u32[]{:S(2)}) collective-permute-start(bf16[3,32,768]{2,1,0:T(8,128)(2,1)S(1)} %get-tuple-element.171), channel_id=1, source_target_pairs={{4,0},{8,4},{12,8},{16,12},{20,16},{24,20},{28,24},{32,28},{36,32}... | collective-permute-start | bytes 442376 | tf_op jit(solution)/shard_map/ppermute | solution.py:19
  278.8 17.6 %collective-permute-start.62 = (bf16[64,768]{1,0:T(8,128)(2,1)S(1)}, bf16[64,768]{1,0:T(8,128)(2,1)S(1)}, u32[]{:S(2)}, u32[]{:S(2)}) collective-permute-start(bf16[64,768]{1,0:T(8,128)(2,1)S(1)} %get-tuple-element.200), channel_id=1, source_target_pairs={{0,0},{4,32},{8,4},{12,36},{16,8},{20,40},{24,12},{28,44},{32,16},... | collective-permute-start | bytes 294920 | tf_op jit(solution)/shard_map/ppermute | solution.py:54
  280.7 21.7 %collective-permute-start.63 = (bf16[64,768]{1,0:T(8,128)(2,1)S(1)}, bf16[64,768]{1,0:T(8,128)(2,1)S(1)}, u32[]{:S(2)}, u32[]{:S(2)}) collective-permute-start(bf16[64,768]{1,0:T(8,128)(2,1)S(1)} %get-tuple-element.201), channel_id=1, source_target_pairs={{0,4},{4,36},{8,8},{12,40},{16,12},{20,44},{24,16},{28,48},{32,20}... | collective-permute-start | bytes 294920 | tf_op jit(solution)/shard_map/ppermute | solution.py:54
  284.5 19.9 %collective-permute-start.64 = (bf16[64,768]{1,0:T(8,128)(2,1)S(1)}, bf16[64,768]{1,0:T(8,128)(2,1)S(1)}, u32[]{:S(2)}, u32[]{:S(2)}) collective-permute-start(bf16[64,768]{1,0:T(8,128)(2,1)S(1)} %get-tuple-element.202), channel_id=1, source_target_pairs={{0,8},{4,40},{8,12},{12,44},{16,16},{20,48},{24,20},{28,52},{32,24... | collective-permute-start | bytes 294920 | tf_op jit(solution)/shard_map/ppermute | solution.py:54
  288.4 20.6 %collective-permute-start.65 = (bf16[64,768]{1,0:T(8,128)(2,1)S(1)}, bf16[64,768]{1,0:T(8,128)(2,1)S(1)}, u32[]{:S(2)}, u32[]{:S(2)}) collective-permute-start(bf16[64,768]{1,0:T(8,128)(2,1)S(1)} %get-tuple-element.203), channel_id=1, source_target_pairs={{0,12},{4,44},{8,16},{12,48},{16,20},{20,52},{24,24},{28,56},{32,2... | collective-permute-start | bytes 294920 | tf_op jit(solution)/shard_map/ppermute | solution.py:54
  (82 other events, 1478.8 us)
Sparse Core Ops, SparseCore 0:
  66.5 57.6 all-gather.1

commit v3 on v2

--- a/solution.py
+++ b/solution.py
@@ -31,174 +31,47 @@
     return jax.ShapeDtypeStruct(shape, dtype)
 
 
-def to_work(blocks):
-    rounds, size = len(blocks), lax.axis_size("seq")
-    share = size // rounds
-    out = []
-    for r, block in enumerate(blocks):
-        route = [
-            (s, share * ((s % rounds - r) % rounds) + s // rounds) for s in range(size)
-        ]
-        out.append(lax.ppermute(block, "seq", route))
-    return out
-
-
-def to_home(blocks):
-    rounds, size = len(blocks), lax.axis_size("seq")
-    share = size // rounds
-    out = []
-    for r, block in enumerate(blocks):
-        route = [
-            (i, rounds * (i % share) + (i // share + r) % rounds) for i in range(size)
-        ]
-        out.append(lax.ppermute(block, "seq", route))
-    return out
-
-
-def deal_latents_kernel(meta, latents, *outs):
-    rounds, rows = len(outs), outs[0].shape[0]
-    first = pl.multiple_of(meta[0] * rows, rows)
-    for r, out in enumerate(outs):
-        patch = lax.rem(meta[1] + rounds - r, rounds)
-        out[...] = latents[patch, pl.ds(first, rows)]
-
-
-def deal_latents(meta, latents):
-    patches, rows, cols = latents.shape
-    return pl.pallas_call(
-        deal_latents_kernel,
-        in_specs=[SCALARS, ON_CHIP],
-        out_specs=[ON_CHIP] * patches,
-        out_shape=[struct((rows // 2, cols))] * patches,
-        compiler_params=params(8),
-        name="deal_latents",
-    )(meta, latents)
-
-
-def halve_stale_kernel(meta, stale, mine, theirs):
-    rows, cols = mine.shape[1], stale.shape[-1]
-    for which, out in enumerate((mine, theirs)):
-        first = meta[0] if which == 0 else 1 - meta[0]
-        first = pl.multiple_of(first * rows, rows)
-        for half in range(2):
-            out[:, :, half * cols : (half + 1) * cols] = stale[half, :, pl.ds(first, rows)]
-
-
-def halve_stale(meta, stale):
-    _, patches, rows, cols = stale.shape
-    out = struct((patches, rows // 2, 2 * cols))
-    return pl.pallas_call(
-        halve_stale_kernel,
-        in_specs=[SCALARS, ON_CHIP],
+def exchanged(tiles):
+    group = tiles.shape[0]
+    groups = [list(range(i, i + group)) for i in range(0, lax.axis_size("seq"), group)]
+    return lax.all_to_all(tiles, "seq", 0, 0, axis_index_groups=groups)
+
+
+def along_ring(block, distance, per_chip):
+    size = lax.axis_size("seq")
+    share = size // per_chip
+    place = [per_chip * (i % share) + i // share for i in range(size)]
+    route = [(place[(i + distance) % size], place[i]) for i in range(size)]
+    return lax.ppermute(block, "seq", route)
+
+
+def collect_kernel(core, early, late, handed, cache):
+    cols = cache.shape[-1]
+
+    def collect(features, keys):
+        handed[...] = features[...]
+        cache[0] = keys[:, :, :cols]
+        cache[1] = keys[:, :, cols:]
+
+    @pl.when(core[0] == 0)
+    def _():
+        collect(late, early)
+
+    @pl.when(core[0] == 1)
+    def _():
+        collect(early, late)
+
+
+def collect(core, early, late):
+    patches, rows, cols = early.shape
+    return pl.pallas_call(
+        collect_kernel,
+        in_specs=[SCALARS] + [ON_CHIP] * 2,
         out_specs=[ON_CHIP] * 2,
-        out_shape=[out] * 2,
-        compiler_params=params(8),
-        name="halve_stale",
-    )(meta, stale)
-
-
-def deal_stale_kernel(meta, own, other, *outs):
-    rounds, rows = len(outs), own.shape[1]
-    for r, out in enumerate(outs):
-        patch = lax.rem(meta[1] + rounds - r, rounds)
-        out[:rows] = own[patch]
-        out[rows:] = other[patch]
-
-
-def deal_stale(meta, own, other):
-    patches, rows, cols = own.shape
-    return pl.pallas_call(
-        deal_stale_kernel,
-        in_specs=[SCALARS] + [ON_CHIP] * 2,
-        out_specs=[ON_CHIP] * patches,
-        out_shape=[struct((2 * rows, cols))] * patches,
-        compiler_params=params(8),
-        name="deal_stale",
-    )(meta, own, other)
-
-
-def sort_stale_kernel(meta, *refs):
-    *blocks, out = refs
-    rounds, rows = len(blocks), out.shape[1]
-    first = pl.multiple_of((1 - meta[0]) * rows, rows)
-    for r, block in enumerate(blocks):
-        out[lax.rem(meta[2] + r, rounds)] = block[pl.ds(first, rows)]
-
-
-def sort_stale(meta, blocks):
-    rows, cols = blocks[0].shape
-    return pl.pallas_call(
-        sort_stale_kernel,
-        in_specs=[SCALARS] + [ON_CHIP] * len(blocks),
-        out_specs=ON_CHIP,
-        out_shape=struct((len(blocks), rows // 2, cols)),
-        compiler_params=params(8),
-        name="sort_stale",
-    )(meta, *blocks)
-
-
-def deal_results_kernel(meta, for_first, for_second, got, *outs):
-    rounds, rows = len(outs), got.shape[1]
-
-    def deal(upper, lower):
-        for r, out in enumerate(outs):
-            tile = lax.rem(meta[2] + r, rounds)
-            out[:rows] = upper[tile]
-            out[rows:] = lower[tile]
-
-    @pl.when(meta[0] == 0)
-    def _():
-        deal(for_first, got)
-
-    @pl.when(meta[0] == 1)
-    def _():
-        deal(got, for_second)
-
-
-def deal_results(meta, for_first, for_second, got):
-    tiles, rows, cols = got.shape
-    return pl.pallas_call(
-        deal_results_kernel,
-        in_specs=[SCALARS] + [ON_CHIP] * 3,
-        out_specs=[ON_CHIP] * tiles,
-        out_shape=[struct((2 * rows, cols))] * tiles,
-        compiler_params=params(8),
-        name="deal_results",
-    )(meta, for_first, for_second, got)
-
-
-def collect_kernel(meta, *refs):
-    *blocks, handed, cache = refs
-    rounds = len(blocks) // 2
-    cols = cache.shape[-1]
-
-    def collect(features, keys):
-        for r in range(rounds):
-            patch = lax.rem(meta[1] + rounds - r, rounds)
-            handed[patch] = features[r][...]
-            cache[0, patch] = keys[r][:, :cols]
-            cache[1, patch] = keys[r][:, cols:]
-
-    @pl.when(meta[0] == 0)
-    def _():
-        collect(blocks[rounds:], blocks[:rounds])
-
-    @pl.when(meta[0] == 1)
-    def _():
-        collect(blocks[:rounds], blocks[rounds:])
-
-
-def collect(meta, early, late):
-    rows, cols = early[0].shape
-    rounds = len(early)
-    return pl.pallas_call(
-        collect_kernel,
-        in_specs=[SCALARS] + [ON_CHIP] * (2 * rounds),
-        out_specs=[ON_CHIP] * 2,
-        out_shape=[struct((rounds, rows, cols)), struct((2, rounds, rows, cols // 2))],
+        out_shape=[struct(early.shape), struct((2, patches, rows, cols // 2))],
         compiler_params=params(8),
         name="collect",
-    )(meta, *early, *late)
+    )(core, early, late)
 
 
 def choose(meta, kv, stale, outs):
@@ -207,34 +80,17 @@
         first = tiles - REACH if place == 1 else 0
         cut = slice(first, first + out.shape[0])
 
-        @pl.when(meta[3 + place] == 1)
+        @pl.when(meta[2 + place] == 1)
         def _():
             out[...] = kv[cut]
 
-        @pl.when(meta[3 + place] == 0)
+        @pl.when(meta[2 + place] == 0)
         def _():
             out[...] = stale[cut]
 
 
-def choose_kernel(meta, kv, *refs):
-    *blocks, lo_out, hi_out, far_out = refs
-    rounds, rows, _ = kv.shape
-    first = pl.multiple_of((1 - meta[1]) * rows, rows)
-    for place, out in enumerate((lo_out, hi_out, far_out)):
-        start = rounds - REACH if place == 1 else 0
-
-        @pl.when(meta[3 + place] == 1)
-        def _():
-            out[...] = kv[start : start + out.shape[0]]
-
-        @pl.when(meta[3 + place] == 0)
-        def _():
-            for r, block in enumerate(blocks):
-                tile = lax.rem(meta[2] + r, rounds) - start
-
-                @pl.when((tile >= 0) & (tile < out.shape[0]))
-                def _():
-                    out[tile] = block[pl.ds(first, rows)]
+def choose_kernel(meta, kv, stale, lo_out, hi_out, far_out):
+    choose(meta, kv, stale, (lo_out, hi_out, far_out))
 
 
 def payloads(kv_shape):
@@ -242,27 +98,27 @@
     return [edge, edge, struct(kv_shape)]
 
 
-def choose_alone(meta, kv, blocks):
+def choose_alone(meta, kv, stale):
     return pl.pallas_call(
         choose_kernel,
-        in_specs=[SCALARS] + [ON_CHIP] * (1 + len(blocks)),
+        in_specs=[SCALARS] + [ON_CHIP] * 2,
         out_specs=[ON_CHIP] * 3,
         out_shape=payloads(kv.shape),
         compiler_params=params(8),
         name="choose",
-    )(meta, kv, *blocks)
+    )(meta, kv, stale)
 
 
 def project_kernel(meta, *refs, with_stale):
-    blocks = refs[:7]
-    shift, scale, gain, w_own, w_other = refs[7:12]
-    refs = refs[12:]
+    blocks = refs[:4]
+    shift, scale, gain, w_own, w_other = refs[4:9]
+    refs = refs[9:]
     if with_stale:
-        stale, x_out, q_out, kv_out, *outs = refs[:-4]
+        stale, q_out, kv_out, *outs = refs[:-3]
     else:
-        x_out, q_out, kv_out = refs[:-4]
-    xs, modded, weights, sems = refs[-4:]
-    rows, cols = x_out.shape
+        q_out, kv_out = refs[:-3]
+    modded, weights, sems = refs[-3:]
+    rows, cols = blocks[0].shape
     tiles, rows_tile, kv_cols = kv_out.shape
     heads_cols = kv_cols // 2
     parts = shift.shape[0]
@@ -284,29 +140,17 @@
             for j in range(parts):
                 fetch(j, source).start()
 
-    own, next_a, next_b, far_a, far_b, prev_a, prev_b = blocks
-    for r in range(tiles):
-        tile = lax.rem(meta[2] + r, tiles)
-        place = pl.ds(pl.multiple_of(tile * rows_tile, rows_tile), rows_tile)
-        here = slice(r * rows_tile, (r + 1) * rows_tile)
-        late = r >= tiles // 2
-        there = slice((r % (tiles // 2)) * rows_tile, (r % (tiles // 2) + 1) * rows_tile)
-        xs[0, place] = own[here]
-        xs[1, place] = (next_b if late else next_a)[there]
-        xs[2, place] = (far_b if late else far_a)[there]
-        xs[3, place] = (prev_b if late else prev_a)[there]
-    x_out[...] = xs[0]
     total = jnp.zeros((rows, 1), jnp.float32)
     for j in range(parts):
-        total += jnp.sum(xs[j].astype(jnp.float32), axis=-1, keepdims=True)
+        total += jnp.sum(blocks[j][...].astype(jnp.float32), axis=-1, keepdims=True)
     mean = total / width
     square = jnp.zeros((rows, 1), jnp.float32)
     for j in range(parts):
-        centred = xs[j].astype(jnp.float32) - mean
+        centred = blocks[j][...].astype(jnp.float32) - mean
         square += jnp.sum(centred * centred, axis=-1, keepdims=True)
     spread = lax.rsqrt(square / width + EPS)
     for j in range(parts):
-        normed = (xs[j].astype(jnp.float32) - mean) * spread
+        normed = (blocks[j][...].astype(jnp.float32) - mean) * spread
         modded[:, j * cols : (j + 1) * cols] = (
             normed * (1.0 + scale[features[j]]) + shift[features[j]]
         ).astype(jnp.bfloat16)
@@ -339,7 +183,7 @@
     tiles, rows_tile, kv_cols = kv_shape
     heads_cols = kv_cols // 2
     parts = shift.shape[0]
-    shapes = [struct((rows, cols)), struct((tiles, rows_tile, heads_cols)), struct(kv_shape)]
+    shapes = [struct((tiles, rows_tile, heads_cols)), struct(kv_shape)]
     extra = []
     if stale is not None:
         shapes += payloads(kv_shape)
@@ -357,7 +201,6 @@
         out_specs=[ON_CHIP] * len(shapes),
         out_shape=shapes,
         scratch_shapes=[
-            pltpu.VMEM((parts, rows, cols), jnp.bfloat16),
             pltpu.VMEM((rows, parts * cols), jnp.bfloat16),
             pltpu.VMEM((3, parts * cols, heads_cols), jnp.bfloat16),
             pltpu.SemaphoreType.DMA((parts,)),
@@ -533,16 +376,8 @@
 
 
 def gather_features(hidden):
-    half = hidden.shape[0] // 2
-    halves = (hidden[:half], hidden[half:])
-    prev_a = shifted(halves[0], "tp", 1)
-    next_b = shifted(halves[1], "tp", -1)
-    prev_b = shifted(halves[1], "tp", 1)
-    next_a = shifted(halves[0], "tp", -1)
-    prev_a, next_b = lax.optimization_barrier((prev_a, next_b))
-    far_a = shifted(prev_a, "tp", 1)
-    far_b = shifted(next_b, "tp", -1)
-    return hidden, next_a, next_b, far_a, far_b, prev_a, prev_b
+    across = shifted(hidden, "tp", 2)
+    return hidden, shifted(hidden, "tp", -1), across, shifted(hidden, "tp", 1)
 
 
 def local(
@@ -550,33 +385,32 @@
 ):
     core = lax.axis_index("segment")
     seq_size = lax.axis_size("seq")
-    chip = lax.axis_index("seq")
+    seq_pos = lax.axis_index("seq")
     tp_size = lax.axis_size("tp")
     tp_pos = lax.axis_index("tp")
     patches, patch_rows, part_cols = latents.shape
     rows_core = patch_rows // 2
     rows = patches * rows_core
     share = seq_size // patches
+    chip = share * lax.rem(seq_pos, patches) + seq_pos // patches
     w_own = jnp.transpose(w_qkv[0], (1, 0, 2))
     heads_cols, width = w_out.shape[1:]
     head_dim = qk_gain.shape[-1]
 
-    place = jnp.stack([core, lax.rem(chip, patches), chip // share]).astype(jnp.int32)
-    x_rounds = to_work(deal_latents(place, latents))
+    mine = lax.dynamic_slice_in_dim(latents, core * rows_core, rows_core, 1)
+    hidden = exchanged(mine).reshape(rows, part_cols)
     w_other = shifted(w_own, "segment", 1)
     small_own = jnp.concatenate([modulation[0].reshape(-1), qk_gain[0].reshape(-1)])
     small_other = shifted(small_own, "segment", 1)
-    hidden = jnp.concatenate(x_rounds, axis=0)
-    blocks = gather_features(hidden)
-    stale_own, stale_send = halve_stale(place, stale_cache[0])
-    stale_other = shifted(stale_send, "segment", 1)
-    stale_rounds = list(deal_stale(place, stale_own, stale_other))
-    stale_rounds[:4], w_out = after((stale_rounds[:4], w_out), blocks[2], blocks[5])
-    stale_rounds[4:] = after(stale_rounds[4:], blocks)
-    stale_rounds = to_work(stale_rounds)
+    stale, w_out = after((stale_cache[0], w_out), hidden)
+    stale = exchanged(jnp.concatenate([stale[0], stale[1]], axis=-1))
+    stale_own = lax.dynamic_slice_in_dim(stale, core * rows_core, rows_core, 1)
+    stale_other = shifted(
+        lax.dynamic_slice_in_dim(stale, (1 - core) * rows_core, rows_core, 1), "segment", 1
+    )
 
     rows_chip = heads_cols // seq_size
-    slab = lax.dynamic_slice_in_dim(w_out[0], chip * rows_chip, rows_chip, 0)
+    slab = lax.dynamic_slice_in_dim(w_out[0], seq_pos * rows_chip, rows_chip, 0)
     pieces = [
         lax.dynamic_slice_in_dim(slab, lax.rem(tp_pos + j, tp_size) * part_cols, part_cols, 1)
         for j in range(tp_size)
@@ -591,21 +425,20 @@
 
     for section in range(2):
         is_own = core == section
-        start = chip // share if section == 0 else jnp.zeros_like(chip)
         meta = jnp.concatenate(
-            [jnp.stack([tp_pos, is_own.astype(tp_pos.dtype), start]).astype(jnp.int32), fresh]
+            [jnp.stack([tp_pos, is_own.astype(tp_pos.dtype)]).astype(jnp.int32), fresh]
         )
         small = jnp.where(is_own, small_own, small_other)
         modul = small[: 3 * width].reshape(3, tp_size, 1, part_cols)
         gain = small[3 * width :].reshape(2, head_dim)
         gate = lax.dynamic_index_in_dim(modul[2], tp_pos, 0, keepdims=False)
+        stale = jnp.where(is_own, stale_own, stale_other)
+
+        blocks = gather_features(hidden)
         if section > 0:
-            blocks = gather_features(hidden)
-            early[:4] = after(early[:4], blocks[2], blocks[5])
-            early[4:] = after(early[4:], blocks)
-            early = to_home(early)
-            blocks, early[:4] = lax.optimization_barrier((blocks, early[:4]))
-        hidden, q_own, kv, *going = project(
+            early = exchanged(early)
+            blocks, early = lax.optimization_barrier((blocks, early))
+        q_own, kv, *going = project(
             meta,
             blocks,
             modul[0],
@@ -614,22 +447,19 @@
             w_own,
             w_other,
             stale if section > 0 else None,
-            stale_own.shape,
+            stale.shape,
         )
         if section == 0:
-            going = choose_alone(meta, kv, stale_rounds)
-            stale = sort_stale(place, after(stale_rounds, going))
+            going = choose_alone(meta, kv, stale)
         to_below, to_above, to_far = going
-        above = shifted(to_below, "seq", -1)
-        below = shifted(to_above, "seq", 1)
+        far = along_ring(to_far, seq_size // 2 + 1, patches)
+        above = along_ring(to_below, 1, patches)
+        below = along_ring(to_above, -1, patches)
         q_other = shifted(q_own, "segment", 1)
-        far = shifted(to_far, "seq", -(seq_size // 2) - 1)
         if section == 0:
             kv_tiles, tile_counts = after((kv_tiles, tile_counts), q_own)
             multiple_own = count_tiles(kv_tiles[0], tile_counts[0], chip, patches, rows_core)
             multiple_other = shifted(multiple_own, "segment", 1)
-        else:
-            above, early = lax.optimization_barrier((above, early))
         multiple = jnp.where(is_own, multiple_own, multiple_other)
         cut = multiple.shape[-1] - rows_core
         before = attend_near(q_own, q_other, below, kv, above, multiple[..., :cut])
@@ -644,13 +474,14 @@
         features = hidden.reshape(patches, rows_core, part_cols)
         pair = (kv, features) if section == 0 else (features, kv)
         got = shifted(jnp.where(core == 0, pair[1], pair[0]), "segment", 1)
-        dealt = list(deal_results(place, *pair, got))
+        own = jnp.where(core == 0, pair[0], pair[1])
+        halves = [jnp.where(core == place, own, got) for place in range(2)]
         if section == 0:
-            early = dealt
+            early = jnp.concatenate(halves, axis=1)
         else:
-            late = to_home(dealt)
-
-    handed, new_cache = collect(place, early, late)
+            late = exchanged(jnp.concatenate(halves, axis=1))
+
+    handed, new_cache = collect(core.astype(jnp.int32)[None], early, late)
     return (handed[None], new_cache[None])
 
 

time: 329 us -> 269 us (0.82)
  the two profiles are of different devices: /device:TPU:6 before, /device:TPU:1 now
where the time goes in v3:
time: 269 us; the launch traced here: 266 us
  waiting for transfers between devices  98.2 us (37%)
  starting transfers between devices  65.1 us (24%)
  Pallas kernels  45.9 us (17%)
  local copies, waits for them, and re-layouts  21.4 us (8%)
  blocking collectives  16 us (6%)
  between operations  14.4 us (5%)
  other arithmetic  4.54 us (2%)
    ppermute x26, waiting for transfers between devices, shifted(): return lax.ppermute(block, axis, route)  65 us
    ppermute x26, starting transfers between devices, shifted(): return lax.ppermute(block, axis, route)  31.7 us
    all_to_all x3, waiting for transfers between devices, exchanged(): return lax.all_to_all(tiles, 'seq', 0, 0, axis_index_groups=groups)  23.2 us
    ppermute x6, starting transfers between devices, along_ring(): return lax.ppermute(block, 'seq', route)  18.5 us
    unnamed x62, local copies, waits for them, and re-layouts  16.2 us
    all_to_all x1, blocking collectives, exchanged(): return lax.all_to_all(tiles, 'seq', 0, 0, axis_index_groups=groups)  16 us
    all_to_all x3, starting transfers between devices, exchanged(): return lax.all_to_all(tiles, 'seq', 0, 0, axis_index_groups=groups)  14.8 us
    pallas_call x2, Pallas kernels, project(): pl.pallas_call(kernel, in_specs=[SCALARS] + [ON_CHIP] * (len(blocks) + 3)...  14.7 us
  transfers between devices with their start and end apart: 36, of which 20 were waited for; matrix products, arithmetic and copies ran while one was open for 3% of the time, Pallas kernels for 10%

profile of v3, /device:TPU:1, one launch (start us, length us, event | category | flops | bytes accessed | tf_op | source)
XLA Modules:
  0.0 265.7 jit_solution(6318907728042119044)
XLA Ops:
  9.5 5.5 %all-to-all-start = ((bf16[8,32,768]{2,1,0:T(8,128)(2,1)}), bf16[8,32,768]{2,1,0:T(8,128)(2,1)S(1)}, u32[]{:S(2)}, u32[]{:S(2)}) async-start(bf16[8,32,768]{2,1,0:T(8,128)(2,1)} %constant_dynamic-slice_fusion.3), calls=%async_computation | async-start | bytes 786432 | tf_op jit(solution)/shard_map/all_to_all | solution.py:37
  15.1 8.7 %all-to-all-done = bf16[8,32,768]{2,1,0:T(8,128)(2,1)S(1)} async-done(((bf16[8,32,768]{2,1,0:T(8,128)(2,1)}), bf16[8,32,768]{2,1,0:T(8,128)(2,1)S(1)}, u32[]{:S(2)}, u32[]{:S(2)}) %all-to-all-start) | async-done | bytes 393248 | tf_op jit(solution)/shard_map/all_to_all | solution.py:37
  25.0 3.8 %collective-permute-start.17 = (bf16[24,768]{1,0:T(8,128)(2,1)S(1)}, bf16[24,768]{1,0:T(8,128)(2,1)S(1)}, u32[]{:S(2)}, u32[]{:S(2)}) collective-permute-start(bf16[24,768]{1,0:T(8,128)(2,1)S(1)} %get-tuple-element.55), channel_id=1, source_target_pairs={{1,0},{2,1},{3,2},{0,3},{5,4},{6,5},{7,6},{4,7},{9,8},{10,9},{11,1... | collective-permute-start | bytes 110600 | tf_op jit(solution)/shard_map/ppermute | solution.py:19
  41.6 14.5 %all-to-all-done.1 = bf16[8,64,768]{2,1,0:T(8,128)(2,1)S(1)} async-done(((bf16[8,64,768]{2,1,0:T(8,128)(2,1)}), bf16[8,64,768]{2,1,0:T(8,128)(2,1)S(1)}, u32[]{:S(2)}, u32[]{:S(2)}) %all-to-all-start.1) | async-done | bytes 786464 | tf_op jit(solution)/shard_map/all_to_all | solution.py:37
  62.1 15.9 %collective-permute-done.2.refs_4_ = bf16[256,768]{1,0:T(8,128)(2,1)S(1)} collective-permute-done((bf16[256,768]{1,0:T(8,128)(2,1)S(1)}, bf16[256,768]{1,0:T(8,128)(2,1)S(1)}, u32[]{:S(2)}, u32[]{:S(2)}) %collective-permute-start.2) | collective-permute-done | bytes 393248 | tf_op jit(solution)/shard_map/ppermute | solution.py:19
  78.4 6.8 %project.2 = (bf16[8,32,384]{2,1,0:T(8,128)(2,1)S(1)}, bf16[8,32,768]{2,1,0:T(8,128)(2,1)S(1)}) custom-call(s32[5]{0:T(128)S(1)} %get-tuple-element.77.refs_0_.meta, bf16[256,768]{1,0:T(8,128)(2,1)S(1)} %bitcast.65, bf16[256,768]{1,0:T(8,128)(2,1)S(1)} %collective-permute-done.refs_2_, bf16[256,768]{1,0:T(8,128)(2,1)S(1)} %collective-permute-done.1.refs_3_, ...), custom_call_target="tpu_custom_call" | custom-call | tf_op jit(solution)/shard_map/project/pallas_call | solution.py:195
  91.3 4.7 %collective-permute-start.10 = (bf16[3,32,768]{2,1,0:T(8,128)(2,1)S(1)}, bf16[3,32,768]{2,1,0:T(8,128)(2,1)S(1)}, u32[]{:S(2)}, u32[]{:S(2)}) collective-permute-start(bf16[3,32,768]{2,1,0:T(8,128)(2,1)S(1)} %get-tuple-element.35), channel_id=1, source_target_pairs={{32,0},{4,32},{36,4},{8,36},{40,8},{12,40},{44,12},{16,44},{48,16}... | collective-permute-start | bytes 442376 | tf_op jit(solution)/shard_map/ppermute | solution.py:45
  96.1 4.9 %collective-permute-done.9.below = bf16[3,32,768]{2,1,0:T(8,128)(2,1)S(1)} collective-permute-done((bf16[3,32,768]{2,1,0:T(8,128)(2,1)S(1)}, bf16[3,32,768]{2,1,0:T(8,128)(2,1)S(1)}, u32[]{:S(2)}, u32[]{:S(2)}) %collective-permute-start.9) | collective-permute-done | bytes 147488 | tf_op jit(solution)/shard_map/ppermute | solution.py:45
  101.0 6.5 %attend_near.2.before = f32[8,64,512]{2,1,0:T(8,128)S(1)} custom-call(bf16[8,32,384]{2,1,0:T(8,128)(2,1)S(1)} %get-tuple-element.28.q_own, bf16[8,32,384]{2,1,0:T(8,128)(2,1)S(1)} %collective-permute-done.5.q_other, bf16[3,32,768]{2,1,0:T(8,128)(2,1)S(1)} %collective-permute-done.9.below, bf16[8,32,768]{2,1,0:T(8,128)(2,1)S(1)} %get-tuple-element.29.kv.own, ...), custom_call_target="tpu_custom_call" | custom-call | tf_op jit(solution)/shard_map/attend_near/pallas_call | solution.py:256
  107.5 4.8 %attend_far.2 = (f32[8,32,512]{2,1,0:T(8,128)S(1)}, f32[8,32,512]{2,1,0:T(8,128)S(1)}) custom-call(bf16[8,32,384]{2,1,0:T(8,128)(2,1)S(1)} %get-tuple-element.28.q_own, bf16[8,32,384]{2,1,0:T(8,128)(2,1)S(1)} %collective-permute-done.5.q_other, bf16[8,32,768]{2,1,0:T(8,128)(2,1)S(1)} %collective-permute-done.7.far, f32[8,1,32]{2,1,0:T(1,128)S(1)} %slice.133.multiple, ...), custom_call_target="tpu_custom_call" | custom-call | tf_op jit(solution)/shard_map/attend_far/pallas_call | solution.py:298
  115.5 5.1 %collective-permute-done.11.part_b = f32[8,32,512]{2,1,0:T(8,128)S(1)} collective-permute-done((f32[8,32,512]{2,1,0:T(8,128)}, f32[8,32,512]{2,1,0:T(8,128)S(1)}, u32[]{:S(2)}, u32[]{:S(2)}) %collective-permute-start.11) | collective-permute-done | bytes 524320 | tf_op jit(solution)/shard_map/ppermute | solution.py:19
  132.6 5.1 %collective-permute-done.12.att1 = bf16[256,384]{1,0:T(8,128)(2,1)} collective-permute-done((bf16[256,384]{1,0:T(8,128)(2,1)S(1)}, bf16[256,384]{1,0:T(8,128)(2,1)}, u32[]{:S(2)}, u32[]{:S(2)}) %collective-permute-start.12) | collective-permute-done | bytes 196640 | tf_op jit(solution)/shard_map/ppermute | solution.py:19
  147.3 5.8 %all-to-all-start.2 = ((bf16[8,64,768]{2,1,0:T(8,128)(2,1)}), bf16[8,64,768]{2,1,0:T(8,128)(2,1)}, u32[]{:S(2)}, u32[]{:S(2)}) async-start(bf16[8,64,768]{2,1,0:T(8,128)(2,1)} %pad_maximum_fusion.1), calls=%async_computation.2 | async-start | bytes 1572864 | tf_op jit(solution)/shard_map/all_to_all | solution.py:37
  156.5 8.8 %collective-permute-done.21.refs_4_ = bf16[256,768]{1,0:T(8,128)(2,1)S(1)} collective-permute-done((bf16[256,768]{1,0:T(8,128)(2,1)S(1)}, bf16[256,768]{1,0:T(8,128)(2,1)S(1)}, u32[]{:S(2)}, u32[]{:S(2)}) %collective-permute-start.21) | collective-permute-done | bytes 393248 | tf_op jit(solution)/shard_map/ppermute | solution.py:19
  166.0 5.9 %collective-permute-done.20.refs_3_ = bf16[256,768]{1,0:T(8,128)(2,1)S(1)} collective-permute-done((bf16[256,768]{1,0:T(8,128)(2,1)S(1)}, bf16[256,768]{1,0:T(8,128)(2,1)S(1)}, u32[]{:S(2)}, u32[]{:S(2)}) %collective-permute-start.20) | collective-permute-done | bytes 393248 | tf_op jit(solution)/shard_map/ppermute | solution.py:19
  179.2 7.9 %project.3 = (bf16[8,32,384]{2,1,0:T(8,128)(2,1)S(1)}, bf16[8,32,768]{2,1,0:T(8,128)(2,1)S(1)}, bf16[3,32,768]{2,1,0:T(8,128)(2,1)S(1)}, bf16[3,32,768]{2,1,0:T(8,128)(2,1)S(1)}, bf16[8,32,768]{2,1,0:T(8,128)(2,1)S(1)}) custom-call(s32[5]{0:T(128)S(1)} %get-tuple-element.76.refs_0_.meta, bf16[256,768]{1,0:T(8,128)(2,1)S(1)} %output.2.refs_1_.hidden, ...), custom_call_target="tpu_custom_call" | custom-call | tf_op jit(solution)/shard_map/project/pallas_call | solution.py:195
  187.1 6.5 %collective-permute-start.24 = (bf16[8,32,768]{2,1,0:T(8,128)(2,1)S(1)}, bf16[8,32,768]{2,1,0:T(8,128)(2,1)S(1)}, u32[]{:S(2)}, u32[]{:S(2)}) collective-permute-start(bf16[8,32,768]{2,1,0:T(8,128)(2,1)S(1)} %get-tuple-element.46), channel_id=1, source_target_pairs={{48,0},{20,32},{52,4},{24,36},{56,8},{28,40},{60,12},{0,44},{32,16... | collective-permute-start | bytes 1179656 | tf_op jit(solution)/shard_map/ppermute | solution.py:45
  196.3 4.8 %collective-permute-start.26 = (bf16[3,32,768]{2,1,0:T(8,128)(2,1)S(1)}, bf16[3,32,768]{2,1,0:T(8,128)(2,1)S(1)}, u32[]{:S(2)}, u32[]{:S(2)}) collective-permute-start(bf16[3,32,768]{2,1,0:T(8,128)(2,1)S(1)} %get-tuple-element.49), channel_id=1, source_target_pairs={{32,0},{4,32},{36,4},{8,36},{40,8},{12,40},{44,12},{16,44},{48,16}... | collective-permute-start | bytes 442376 | tf_op jit(solution)/shard_map/ppermute | solution.py:45
  201.2 5.1 %collective-permute-done.25.below = bf16[3,32,768]{2,1,0:T(8,128)(2,1)S(1)} collective-permute-done((bf16[3,32,768]{2,1,0:T(8,128)(2,1)S(1)}, bf16[3,32,768]{2,1,0:T(8,128)(2,1)S(1)}, u32[]{:S(2)}, u32[]{:S(2)}) %collective-permute-start.25) | collective-permute-done | bytes 147488 | tf_op jit(solution)/shard_map/ppermute | solution.py:45
  206.3 6.5 %attend_near.3.before = f32[8,64,512]{2,1,0:T(8,128)S(1)} custom-call(bf16[8,32,384]{2,1,0:T(8,128)(2,1)S(1)} %get-tuple-element.45.q_own, bf16[8,32,384]{2,1,0:T(8,128)(2,1)S(1)} %collective-permute-done.23.q_other, bf16[3,32,768]{2,1,0:T(8,128)(2,1)S(1)} %collective-permute-done.25.below, bf16[8,32,768]{2,1,0:T(8,128)(2,1)S(1)} %get-tuple-element.48.own, ...), custom_call_target="tpu_custom_call" | custom-call | tf_op jit(solution)/shard_map/attend_near/pallas_call | solution.py:256
  212.8 4.8 %attend_far.3 = (f32[8,32,512]{2,1,0:T(8,128)S(1)}, f32[8,32,512]{2,1,0:T(8,128)S(1)}) custom-call(bf16[8,32,384]{2,1,0:T(8,128)(2,1)S(1)} %get-tuple-element.45.q_own, bf16[8,32,384]{2,1,0:T(8,128)(2,1)S(1)} %collective-permute-done.23.q_other, bf16[8,32,768]{2,1,0:T(8,128)(2,1)S(1)} %collective-permute-done.24.far, f32[8,1,32]{2,1,0:T(1,128)S(1)} %slice.139.multiple, ...), custom_call_target="tpu_custom_call" | custom-call | tf_op jit(solution)/shard_map/attend_far/pallas_call | solution.py:298
  225.9 6.4 %collective-permute-done.30.att3 = bf16[256,384]{1,0:T(8,128)(2,1)S(1)} collective-permute-done((bf16[256,384]{1,0:T(8,128)(2,1)S(1)}, bf16[256,384]{1,0:T(8,128)(2,1)S(1)}, u32[]{:S(2)}, u32[]{:S(2)}) %collective-permute-start.30) | collective-permute-done | bytes 196640 | tf_op jit(solution)/shard_map/ppermute | solution.py:19
  232.3 4.4 %collective-permute-done.28.att1 = bf16[256,384]{1,0:T(8,128)(2,1)S(1)} collective-permute-done((bf16[256,384]{1,0:T(8,128)(2,1)S(1)}, bf16[256,384]{1,0:T(8,128)(2,1)S(1)}, u32[]{:S(2)}, u32[]{:S(2)}) %collective-permute-start.28) | collective-permute-done | bytes 196640 | tf_op jit(solution)/shard_map/ppermute | solution.py:19
  240.4 16.0 %all_to_all.20.late = bf16[8,64,768]{2,1,0:T(8,128)(2,1)S(1)} all-to-all(bf16[8,64,768]{2,1,0:T(8,128)(2,1)S(1)} %pad_maximum_fusion.2), channel_id=1, replica_groups={{0,4,8,12,16,20,24,28},{32,36,40,44,48,52,56,60},{1,5,9,13,17,21,25,29}..., dimensions={0} | all-to-all | bytes 1572864 | tf_op jit(solution)/shard_map/all_to_all | solution.py:37
  (160 shorter events, 82.1 us)
Async XLA Ops:
  7.2 71.1 %collective-permute-start.4 = (bf16[3,3072,384]{2,1,0:T(8,128)(2,1)}, bf16[3,3072,384]{2,1,0:T(8,128)(2,1)}, u32[]{:S(2)}, u32[]{:S(2)}) collective-permute-start(bf16[3,3072,384]{2,1,0:T(8,128)(2,1)} %bitcast.73), channel_id=1, source_target_pairs={{64,0},{0,64},{65,1},{1,65},{66,2},{2,66},{67,3},{3,67},{68,4},{4,... | collective-permute-start | bytes 21233672 | tf_op jit(solution)/shard_map/ppermute | solution.py:19
  9.5 14.3 %all-to-all-start = ((bf16[8,32,768]{2,1,0:T(8,128)(2,1)}), bf16[8,32,768]{2,1,0:T(8,128)(2,1)S(1)}, u32[]{:S(2)}, u32[]{:S(2)}) async-start(bf16[8,32,768]{2,1,0:T(8,128)(2,1)} %constant_dynamic-slice_fusion.3), calls=%async_computation | async-start | bytes 786432 | tf_op jit(solution)/shard_map/all_to_all | solution.py:37
  15.0 98.9 %all-gather.2.cloned.1.call-start = ((), (), s32[]{:S(2)}) async-start(), calls=%async_computation.4 | async-start | bytes 2506752 | tf_op jit(solution)/shard_map/all_gather | solution.py:419
  37.6 18.4 %all-to-all-start.1 = ((bf16[8,64,768]{2,1,0:T(8,128)(2,1)}), bf16[8,64,768]{2,1,0:T(8,128)(2,1)S(1)}, u32[]{:S(2)}, u32[]{:S(2)}) async-start(bf16[8,64,768]{2,1,0:T(8,128)(2,1)} %pad_maximum_fusion), calls=%async_computation.1 | async-start | bytes 1572864 | tf_op jit(solution)/shard_map/all_to_all | solution.py:37
  57.6 20.5 %collective-permute-start.2 = (bf16[256,768]{1,0:T(8,128)(2,1)S(1)}, bf16[256,768]{1,0:T(8,128)(2,1)S(1)}, u32[]{:S(2)}, u32[]{:S(2)}) collective-permute-start(bf16[256,768]{1,0:T(8,128)(2,1)S(1)} %bitcast.62), channel_id=1, source_target_pairs={{3,0},{0,1},{1,2},{2,3},{7,4},{4,5},{5,6},{6,7},{11,8},{8,9},{9,10... | collective-permute-start | bytes 1179656 | tf_op jit(solution)/shard_map/ppermute | solution.py:19
  57.6 20.5 %collective-permute-start.1 = (bf16[256,768]{1,0:T(8,128)(2,1)S(1)}, bf16[256,768]{1,0:T(8,128)(2,1)S(1)}, u32[]{:S(2)}, u32[]{:S(2)}) collective-permute-start(bf16[256,768]{1,0:T(8,128)(2,1)S(1)} %bitcast.63), channel_id=1, source_target_pairs={{2,0},{3,1},{0,2},{1,3},{6,4},{7,5},{4,6},{5,7},{10,8},{11,9},{8,1... | collective-permute-start | bytes 1179656 | tf_op jit(solution)/shard_map/ppermute | solution.py:19
  59.1 19.2 %collective-permute-start = (bf16[256,768]{1,0:T(8,128)(2,1)S(1)}, bf16[256,768]{1,0:T(8,128)(2,1)S(1)}, u32[]{:S(2)}, u32[]{:S(2)}) collective-permute-start(bf16[256,768]{1,0:T(8,128)(2,1)S(1)} %bitcast.64), channel_id=1, source_target_pairs={{1,0},{2,1},{3,2},{0,3},{5,4},{6,5},{7,6},{4,7},{9,8},{10,9},{11,1... | collective-permute-start | bytes 1179656 | tf_op jit(solution)/shard_map/ppermute | solution.py:19
  85.9 21.6 %collective-permute-start.7 = (bf16[8,32,768]{2,1,0:T(8,128)(2,1)S(1)}, bf16[8,32,768]{2,1,0:T(8,128)(2,1)S(1)}, u32[]{:S(2)}, u32[]{:S(2)}) collective-permute-start(bf16[8,32,768]{2,1,0:T(8,128)(2,1)S(1)} %get-tuple-element.31), channel_id=1, source_target_pairs={{48,0},{20,32},{52,4},{24,36},{56,8},{28,40},{60,12},{0,44},{32,16... | collective-permute-start | bytes 1179656 | tf_op jit(solution)/shard_map/ppermute | solution.py:45
  91.1 9.9 %collective-permute-start.5 = (bf16[8,32,384]{2,1,0:T(8,128)(2,1)S(1)}, bf16[8,32,384]{2,1,0:T(8,128)(2,1)S(1)}, u32[]{:S(2)}, u32[]{:S(2)}) collective-permute-start(bf16[8,32,384]{2,1,0:T(8,128)(2,1)S(1)} %get-tuple-element.28.q_own), channel_id=1, source_target_pairs={{64,0},{0,64},{65,1},{1,65},{66,2},{2,66},{67,3},{3,67},{68,4},{4,... | collective-permute-start | bytes 589832 | tf_op jit(solution)/shard_map/ppermute | solution.py:19
  91.2 9.8 %collective-permute-start.9 = (bf16[3,32,768]{2,1,0:T(8,128)(2,1)S(1)}, bf16[3,32,768]{2,1,0:T(8,128)(2,1)S(1)}, u32[]{:S(2)}, u32[]{:S(2)}) collective-permute-start(bf16[3,32,768]{2,1,0:T(8,128)(2,1)S(1)} %get-tuple-element.34), channel_id=1, source_target_pairs={{60,0},{0,32},{32,4},{4,36},{36,8},{8,40},{40,12},{12,44},{44,16},... | collective-permute-start | bytes 442376 | tf_op jit(solution)/shard_map/ppermute | solution.py:45
  91.3 9.7 %collective-permute-start.10 = (bf16[3,32,768]{2,1,0:T(8,128)(2,1)S(1)}, bf16[3,32,768]{2,1,0:T(8,128)(2,1)S(1)}, u32[]{:S(2)}, u32[]{:S(2)}) collective-permute-start(bf16[3,32,768]{2,1,0:T(8,128)(2,1)S(1)} %get-tuple-element.35), channel_id=1, source_target_pairs={{32,0},{4,32},{36,4},{8,36},{40,8},{12,40},{44,12},{16,44},{48,16}... | collective-permute-start | bytes 442376 | tf_op jit(solution)/shard_map/ppermute | solution.py:45
  113.9 23.7 %collective-permute-start.18 = (bf16[4,384,768]{2,1,0:T(8,128)(2,1)}, bf16[4,384,768]{2,1,0:T(8,128)(2,1)S(1)}, u32[]{:S(2)}, u32[]{:S(2)}) collective-permute-start(bf16[4,384,768]{2,1,0:T(8,128)(2,1)} %all-gather.2.cloned.1.call-done.wo_own), channel_id=1, source_target_pairs={{64,0},{0,64},{65,1},{1,65},{66,2},{2,66},{67,3},{3,67},{68,4},{4,... | collective-permute-start | bytes 7077896 | tf_op jit(solution)/shard_map/ppermute | solution.py:19
  125.3 12.3 %collective-permute-start.12 = (bf16[256,384]{1,0:T(8,128)(2,1)S(1)}, bf16[256,384]{1,0:T(8,128)(2,1)}, u32[]{:S(2)}, u32[]{:S(2)}) collective-permute-start(bf16[256,384]{1,0:T(8,128)(2,1)S(1)} %merge.2.att0), channel_id=1, source_target_pairs={{3,0},{0,1},{1,2},{2,3},{7,4},{4,5},{5,6},{6,7},{11,8},{8,9},{9,10... | collective-permute-start | bytes 589832 | tf_op jit(solution)/shard_map/ppermute | solution.py:19
  147.3 26.5 %all-to-all-start.2 = ((bf16[8,64,768]{2,1,0:T(8,128)(2,1)}), bf16[8,64,768]{2,1,0:T(8,128)(2,1)}, u32[]{:S(2)}, u32[]{:S(2)}) async-start(bf16[8,64,768]{2,1,0:T(8,128)(2,1)} %pad_maximum_fusion.1), calls=%async_computation.2 | async-start | bytes 1572864 | tf_op jit(solution)/shard_map/all_to_all | solution.py:37
  153.1 12.2 %collective-permute-start.21 = (bf16[256,768]{1,0:T(8,128)(2,1)S(1)}, bf16[256,768]{1,0:T(8,128)(2,1)S(1)}, u32[]{:S(2)}, u32[]{:S(2)}) collective-permute-start(bf16[256,768]{1,0:T(8,128)(2,1)S(1)} %output.2.refs_1_.hidden), channel_id=1, source_target_pairs={{3,0},{0,1},{1,2},{2,3},{7,4},{4,5},{5,6},{6,7},{11,8},{8,9},{9,10... | collective-permute-start | bytes 1179656 | tf_op jit(solution)/shard_map/ppermute | solution.py:19
  153.1 18.8 %collective-permute-start.20 = (bf16[256,768]{1,0:T(8,128)(2,1)S(1)}, bf16[256,768]{1,0:T(8,128)(2,1)S(1)}, u32[]{:S(2)}, u32[]{:S(2)}) collective-permute-start(bf16[256,768]{1,0:T(8,128)(2,1)S(1)} %output.2.refs_1_.hidden), channel_id=1, source_target_pairs={{2,0},{3,1},{0,2},{1,3},{6,4},{7,5},{4,6},{5,7},{10,8},{11,9},{8,1... | collective-permute-start | bytes 1179656 | tf_op jit(solution)/shard_map/ppermute | solution.py:19
  154.9 18.2 %collective-permute-start.19 = (bf16[256,768]{1,0:T(8,128)(2,1)S(1)}, bf16[256,768]{1,0:T(8,128)(2,1)S(1)}, u32[]{:S(2)}, u32[]{:S(2)}) collective-permute-start(bf16[256,768]{1,0:T(8,128)(2,1)S(1)} %output.2.refs_1_.hidden), channel_id=1, source_target_pairs={{1,0},{2,1},{3,2},{0,3},{5,4},{6,5},{7,6},{4,7},{9,8},{10,9},{11,1... | collective-permute-start | bytes 1179656 | tf_op jit(solution)/shard_map/ppermute | solution.py:19
  187.1 25.7 %collective-permute-start.24 = (bf16[8,32,768]{2,1,0:T(8,128)(2,1)S(1)}, bf16[8,32,768]{2,1,0:T(8,128)(2,1)S(1)}, u32[]{:S(2)}, u32[]{:S(2)}) collective-permute-start(bf16[8,32,768]{2,1,0:T(8,128)(2,1)S(1)} %get-tuple-element.46), channel_id=1, source_target_pairs={{48,0},{20,32},{52,4},{24,36},{56,8},{28,40},{60,12},{0,44},{32,16... | collective-permute-start | bytes 1179656 | tf_op jit(solution)/shard_map/ppermute | solution.py:45
  193.6 12.6 %collective-permute-start.23 = (bf16[8,32,384]{2,1,0:T(8,128)(2,1)S(1)}, bf16[8,32,384]{2,1,0:T(8,128)(2,1)S(1)}, u32[]{:S(2)}, u32[]{:S(2)}) collective-permute-start(bf16[8,32,384]{2,1,0:T(8,128)(2,1)S(1)} %get-tuple-element.45.q_own), channel_id=1, source_target_pairs={{64,0},{0,64},{65,1},{1,65},{66,2},{2,66},{67,3},{3,67},{68,4},{4,... | collective-permute-start | bytes 589832 | tf_op jit(solution)/shard_map/ppermute | solution.py:19
  196.3 10.0 %collective-permute-start.25 = (bf16[3,32,768]{2,1,0:T(8,128)(2,1)S(1)}, bf16[3,32,768]{2,1,0:T(8,128)(2,1)S(1)}, u32[]{:S(2)}, u32[]{:S(2)}) collective-permute-start(bf16[3,32,768]{2,1,0:T(8,128)(2,1)S(1)} %get-tuple-element.47), channel_id=1, source_target_pairs={{60,0},{0,32},{32,4},{4,36},{36,8},{8,40},{40,12},{12,44},{44,16},... | collective-permute-start | bytes 442376 | tf_op jit(solution)/shard_map/ppermute | solution.py:45
  196.3 10.0 %collective-permute-start.26 = (bf16[3,32,768]{2,1,0:T(8,128)(2,1)S(1)}, bf16[3,32,768]{2,1,0:T(8,128)(2,1)S(1)}, u32[]{:S(2)}, u32[]{:S(2)}) collective-permute-start(bf16[3,32,768]{2,1,0:T(8,128)(2,1)S(1)} %get-tuple-element.49), channel_id=1, source_target_pairs={{32,0},{4,32},{36,4},{8,36},{40,8},{12,40},{44,12},{16,44},{48,16}... | collective-permute-start | bytes 442376 | tf_op jit(solution)/shard_map/ppermute | solution.py:45
  221.3 10.9 %collective-permute-start.30 = (bf16[256,384]{1,0:T(8,128)(2,1)S(1)}, bf16[256,384]{1,0:T(8,128)(2,1)S(1)}, u32[]{:S(2)}, u32[]{:S(2)}) collective-permute-start(bf16[256,384]{1,0:T(8,128)(2,1)S(1)} %merge.3.att0), channel_id=1, source_target_pairs={{1,0},{2,1},{3,2},{0,3},{5,4},{6,5},{7,6},{4,7},{9,8},{10,9},{11,1... | collective-permute-start | bytes 589832 | tf_op jit(solution)/shard_map/ppermute | solution.py:19
  224.3 8.0 %collective-permute-start.29 = (bf16[256,384]{1,0:T(8,128)(2,1)S(1)}, bf16[256,384]{1,0:T(8,128)(2,1)S(1)}, u32[]{:S(2)}, u32[]{:S(2)}) collective-permute-start(bf16[256,384]{1,0:T(8,128)(2,1)S(1)} %merge.3.att0), channel_id=1, source_target_pairs={{2,0},{3,1},{0,2},{1,3},{6,4},{7,5},{4,6},{5,7},{10,8},{11,9},{8,1... | collective-permute-start | bytes 589832 | tf_op jit(solution)/shard_map/ppermute | solution.py:19
  224.5 12.2 %collective-permute-start.28 = (bf16[256,384]{1,0:T(8,128)(2,1)S(1)}, bf16[256,384]{1,0:T(8,128)(2,1)S(1)}, u32[]{:S(2)}, u32[]{:S(2)}) collective-permute-start(bf16[256,384]{1,0:T(8,128)(2,1)S(1)} %merge.3.att0), channel_id=1, source_target_pairs={{3,0},{0,1},{1,2},{2,3},{7,4},{4,5},{5,6},{6,7},{11,8},{8,9},{9,10... | collective-permute-start | bytes 589832 | tf_op jit(solution)/shard_map/ppermute | solution.py:19
  (43 other events, 338.5 us)
Sparse Core Ops, SparseCore 0:
  34.0 47.6 all-gather.1

commit v4 on v3

--- a/solution.py
+++ b/solution.py
@@ -11,6 +11,7 @@
 MIB = 1024 * 1024
 ON_CHIP = pl.BlockSpec(memory_space=pltpu.VMEM)
 SCALARS = pl.BlockSpec(memory_space=pltpu.SMEM)
+ANYWHERE = pl.BlockSpec(memory_space=pl.ANY)
 
 
 def shifted(block, axis, distance):
@@ -75,7 +76,8 @@
 
 
 def choose(meta, kv, stale, outs):
-    tiles = kv.shape[0]
+    tiles, rows, _ = kv.shape
+    old = pl.ds(pl.multiple_of((1 - meta[1]) * rows, rows), rows)
     for place, out in enumerate(outs):
         first = tiles - REACH if place == 1 else 0
         cut = slice(first, first + out.shape[0])
@@ -86,7 +88,7 @@
 
         @pl.when(meta[2 + place] == 0)
         def _():
-            out[...] = stale[cut]
+            out[...] = stale[cut, old]
 
 
 def choose_kernel(meta, kv, stale, lo_out, hi_out, far_out):
@@ -114,11 +116,11 @@
     shift, scale, gain, w_own, w_other = refs[4:9]
     refs = refs[9:]
     if with_stale:
-        stale, q_out, kv_out, *outs = refs[:-3]
+        stale, q_out, kv_out, *outs = refs[:-4]
     else:
-        q_out, kv_out = refs[:-3]
-    modded, weights, sems = refs[-3:]
-    rows, cols = blocks[0].shape
+        q_out, kv_out = refs[:-4]
+    xs, modded, weights, sems = refs[-4:]
+    _, rows, cols = xs.shape
     tiles, rows_tile, kv_cols = kv_out.shape
     heads_cols = kv_cols // 2
     parts = shift.shape[0]
@@ -133,6 +135,11 @@
             sems.at[j],
         )
 
+    arriving = [
+        pltpu.make_async_copy(blocks[j], xs.at[j], sems.at[parts + j]) for j in range(parts)
+    ]
+    for copy in arriving:
+        copy.start()
     for chosen, source in enumerate((w_other, w_own)):
 
         @pl.when(meta[1] == chosen)
@@ -140,17 +147,19 @@
             for j in range(parts):
                 fetch(j, source).start()
 
+    for copy in arriving:
+        copy.wait()
     total = jnp.zeros((rows, 1), jnp.float32)
     for j in range(parts):
-        total += jnp.sum(blocks[j][...].astype(jnp.float32), axis=-1, keepdims=True)
+        total += jnp.sum(xs[j].astype(jnp.float32), axis=-1, keepdims=True)
     mean = total / width
     square = jnp.zeros((rows, 1), jnp.float32)
     for j in range(parts):
-        centred = blocks[j][...].astype(jnp.float32) - mean
+        centred = xs[j].astype(jnp.float32) - mean
         square += jnp.sum(centred * centred, axis=-1, keepdims=True)
     spread = lax.rsqrt(square / width + EPS)
     for j in range(parts):
-        normed = (blocks[j][...].astype(jnp.float32) - mean) * spread
+        normed = (xs[j].astype(jnp.float32) - mean) * spread
         modded[:, j * cols : (j + 1) * cols] = (
             normed * (1.0 + scale[features[j]]) + shift[features[j]]
         ).astype(jnp.bfloat16)
@@ -195,17 +204,19 @@
     return pl.pallas_call(
         kernel,
         in_specs=[SCALARS]
-        + [ON_CHIP] * (len(blocks) + 3)
-        + [pl.BlockSpec(memory_space=pltpu.HBM)] * 2
+        + [ANYWHERE] * len(blocks)
+        + [ON_CHIP] * 3
+        + [ANYWHERE] * 2
         + [ON_CHIP] * len(extra),
         out_specs=[ON_CHIP] * len(shapes),
         out_shape=shapes,
         scratch_shapes=[
+            pltpu.VMEM((parts, rows, cols), jnp.bfloat16),
             pltpu.VMEM((rows, parts * cols), jnp.bfloat16),
             pltpu.VMEM((3, parts * cols, heads_cols), jnp.bfloat16),
-            pltpu.SemaphoreType.DMA((parts,)),
+            pltpu.SemaphoreType.DMA((2 * parts,)),
         ],
-        compiler_params=params(46),
+        compiler_params=params(16),
         name="project",
     )(meta, *blocks, shift, scale, gain, w_own, w_other, *extra)
 
@@ -224,25 +235,23 @@
     return peak, total, summed
 
 
-def attend_near_kernel(q_own, q_other, below, own, above, multiple, out, window):
+def attend_own_kernel(q_own, q_other, own, multiple, out):
     tiles, rows, heads_cols = q_own.shape
-    window[: REACH * rows] = below[...].reshape(REACH * rows, 2 * heads_cols)
-    window[REACH * rows : (REACH + tiles) * rows] = own[...].reshape(tiles * rows, 2 * heads_cols)
-    window[(REACH + tiles) * rows :] = above[...].reshape(REACH * rows, 2 * heads_cols)
     lane = lax.broadcasted_iota(jnp.int32, (2 * rows, HEAD_DIM), 1)
     for tile in range(tiles):
-        times = multiple[tile]
-        span = slice(tile * rows, tile * rows + times.shape[-1])
+        first, last = max(0, tile - REACH), min(tiles, tile + REACH + 1)
+        count = (last - first) * rows
         extra = jnp.zeros((2 * rows, HEAD_DIM), jnp.float32)
         for head in range(heads_cols // HEAD_DIM):
-            first = head * HEAD_DIM
-            cut = slice(first, first + HEAD_DIM)
+            start = head * HEAD_DIM
+            cut = slice(start, start + HEAD_DIM)
+            second = slice(heads_cols + start, heads_cols + start + HEAD_DIM)
             queries = jnp.concatenate([q_own[tile, :, cut], q_other[tile, :, cut]], axis=0)
             peak, total, summed = soften(
                 queries,
-                window[span, cut],
-                window[span, heads_cols + first : heads_cols + first + HEAD_DIM],
-                times,
+                own[first:last, :, cut].reshape(count, HEAD_DIM),
+                own[first:last, :, second].reshape(count, HEAD_DIM),
+                multiple[tile, :, :count],
                 None,
             )
             out[tile, :, cut] = summed
@@ -251,35 +260,39 @@
         out[tile, :, heads_cols:] = extra
 
 
-def attend_near(q_own, q_other, below, own, above, multiple):
+def attend_own(q_own, q_other, own, multiple):
     tiles, rows, heads_cols = q_own.shape
     return pl.pallas_call(
-        attend_near_kernel,
-        in_specs=[ON_CHIP] * 6,
+        attend_own_kernel,
+        in_specs=[ON_CHIP] * 4,
         out_specs=ON_CHIP,
         out_shape=struct((tiles, 2 * rows, heads_cols + HEAD_DIM), jnp.float32),
-        scratch_shapes=[pltpu.VMEM(((tiles + 2 * REACH) * rows, 2 * heads_cols), jnp.bfloat16)],
         compiler_params=params(8),
-        name="attend_near",
-    )(q_own, q_other, below, own, above, multiple)
-
-
-def attend_far_kernel(q_own, q_other, far, multiple, before, out_own, out_other):
+        name="attend_own",
+    )(q_own, q_other, own, multiple)
+
+
+def attend_rest_kernel(q_own, q_other, below, above, far, multiple, before, out_own, out_other):
     tiles, rows, heads_cols = q_own.shape
     lane = lax.broadcasted_iota(jnp.int32, (2 * rows, HEAD_DIM), 1)
     for tile in range(tiles):
+        pieces = [below[place] for place in range(tile, REACH)]
+        pieces += [above[place] for place in range(tile + REACH + 1 - tiles)]
+        pieces += [far[tile]]
+        keys_values = jnp.concatenate(pieces, axis=0)
         extra = jnp.zeros((2 * rows, HEAD_DIM), jnp.float32)
         for head in range(heads_cols // HEAD_DIM):
-            first = head * HEAD_DIM
-            cut = slice(first, first + HEAD_DIM)
+            start = head * HEAD_DIM
+            cut = slice(start, start + HEAD_DIM)
+            second = slice(heads_cols + start, heads_cols + start + HEAD_DIM)
             queries = jnp.concatenate([q_own[tile, :, cut], q_other[tile, :, cut]], axis=0)
             peak_before = before[tile, :, heads_cols + head : heads_cols + head + 1]
             total_before = before[tile, :, heads_cols + 64 + head : heads_cols + 65 + head]
             peak, total, summed = soften(
                 queries,
-                far[tile, :, cut],
-                far[tile, :, heads_cols + first : heads_cols + first + HEAD_DIM],
-                multiple[tile],
+                keys_values[:, cut],
+                keys_values[:, second],
+                multiple[tile, :, : keys_values.shape[0]],
                 peak_before,
             )
             shrink = jnp.exp(peak_before - peak)
@@ -293,21 +306,37 @@
         out_other[tile, :, heads_cols:] = extra[rows:]
 
 
-def attend_far(q_own, q_other, far, multiple, before):
+def attend_rest(q_own, q_other, below, above, far, multiple, before):
     tiles, rows, heads_cols = q_own.shape
     return pl.pallas_call(
-        attend_far_kernel,
-        in_specs=[ON_CHIP] * 5,
+        attend_rest_kernel,
+        in_specs=[ON_CHIP] * 7,
         out_specs=[ON_CHIP] * 2,
         out_shape=[struct((tiles, rows, heads_cols + HEAD_DIM), jnp.float32)] * 2,
         compiler_params=params(8),
-        name="attend_far",
-    )(q_own, q_other, far, multiple, before)
-
-
-def merge_kernel(part_a, part_b, att):
+        name="attend_rest",
+    )(q_own, q_other, below, above, far, multiple, before)
+
+
+def spread_kernel(
+    meta, part_a, part_b, wo_own, wo_other, keep, to_next, to_across, to_prev, att, weights, sems
+):
     tiles, rows, _ = part_a.shape
-    heads_cols = att.shape[-1]
+    parts, heads_cols, cols = weights.shape
+
+    def fetch(j, source):
+        first = pl.multiple_of(lax.rem(meta[0] + j, parts) * cols, cols)
+        return pltpu.make_async_copy(
+            source.at[:, pl.ds(first, cols)], weights.at[j], sems.at[j]
+        )
+
+    for chosen, source in enumerate((wo_other, wo_own)):
+
+        @pl.when(meta[1] == chosen)
+        def _():
+            for j in range(parts):
+                fetch(j, source).start()
+
     for tile in range(tiles):
         extra_a = part_a[tile, :, heads_cols:]
         extra_b = part_b[tile, :, heads_cols:]
@@ -320,45 +349,48 @@
             total = total_a * grow_a + total_b * grow_b
             summed = part_a[tile, :, cut] * grow_a + part_b[tile, :, cut] * grow_b
             att[tile * rows : (tile + 1) * rows, cut] = (summed / total).astype(jnp.bfloat16)
-
-
-def merge(part_a, part_b):
-    tiles, rows, cols = part_a.shape
-    return pl.pallas_call(
-        merge_kernel,
-        in_specs=[ON_CHIP] * 2,
-        out_specs=ON_CHIP,
-        out_shape=struct((tiles * rows, cols - HEAD_DIM)),
-        compiler_params=params(8),
-        name="merge",
-    )(part_a, part_b)
-
-
-def output_kernel(meta, att0, att1, att2, att3, wo_own, wo_other, hidden, gate, out):
-    def finish(weight):
-        product = jnp.zeros(out.shape, jnp.float32)
-        for place, att in enumerate((att0, att1, att2, att3)):
-            product += jnp.dot(att[...], weight[place], preferred_element_type=jnp.float32)
-        out[...] = (hidden[...].astype(jnp.float32) + gate[...] * product).astype(out.dtype)
-
-    @pl.when(meta[1] == 1)
-    def _():
-        finish(wo_own)
-
-    @pl.when(meta[1] == 0)
-    def _():
-        finish(wo_other)
-
-
-def output(meta, atts, wo_own, wo_other, hidden, gate):
-    return pl.pallas_call(
-        output_kernel,
-        in_specs=[SCALARS] + [ON_CHIP] * 8,
+    for j in range(parts):
+        fetch(j, wo_own).wait()
+    for j, out in enumerate((keep, to_next, to_across, to_prev)):
+        product = jnp.dot(att[...], weights[j], preferred_element_type=jnp.float32)
+        out[...] = product.astype(out.dtype)
+
+
+def spread(meta, part_a, part_b, wo_own, wo_other, parts):
+    tiles, rows, _ = part_a.shape
+    heads_cols, width = wo_own.shape
+    shape = (tiles * rows, width // parts)
+    return pl.pallas_call(
+        spread_kernel,
+        in_specs=[SCALARS] + [ON_CHIP] * 2 + [ANYWHERE] * 2,
+        out_specs=[ON_CHIP] * 4,
+        out_shape=[struct(shape, jnp.float32)] + [struct(shape)] * 3,
+        scratch_shapes=[
+            pltpu.VMEM((tiles * rows, heads_cols), jnp.bfloat16),
+            pltpu.VMEM((parts, heads_cols, width // parts), jnp.bfloat16),
+            pltpu.SemaphoreType.DMA((parts,)),
+        ],
+        compiler_params=params(12),
+        name="spread",
+    )(meta, part_a, part_b, wo_own, wo_other)
+
+
+def finish_kernel(hidden, gate, keep, from_prev, from_across, from_next, out):
+    total = keep[...]
+    for part in (from_prev, from_across, from_next):
+        total += part[...].astype(jnp.float32)
+    out[...] = (hidden[...].astype(jnp.float32) + gate[...] * total).astype(out.dtype)
+
+
+def finish(hidden, gate, *parts):
+    return pl.pallas_call(
+        finish_kernel,
+        in_specs=[ON_CHIP] * (2 + len(parts)),
         out_specs=ON_CHIP,
         out_shape=struct(hidden.shape),
         compiler_params=params(8),
-        name="output",
-    )(meta, *atts, wo_own, wo_other, hidden, gate)
+        name="finish",
+    )(hidden, gate, *parts)
 
 
 def count_tiles(table, counts, chip, per_chip, repeat):
@@ -367,11 +399,20 @@
     counts = lax.dynamic_slice_in_dim(counts, chip * per_chip, per_chip, 0)
     query_tiles = jnp.arange(per_chip, dtype=jnp.int32) + chip * per_chip
     across = tiles // 2 + (tiles // per_chip) // 2
-    distances = list(range(-REACH, REACH + 1)) + [across]
-    reach = jnp.repeat(jnp.array([d % tiles for d in distances], jnp.int32), repeat)
+    rows = []
+    for tile in range(per_chip):
+        first, last = max(0, tile - REACH), min(per_chip, tile + REACH + 1)
+        own = [place - tile for place in range(first, last)]
+        rest = [place - REACH - tile for place in range(tile, REACH)]
+        rest += [per_chip + place - tile for place in range(tile + REACH + 1 - per_chip)]
+        rest += [across]
+        own = [d % tiles for d in own] + [-1] * (256 // repeat - len(own))
+        rest = [d % tiles for d in rest] + [-1] * (128 // repeat - len(rest))
+        rows.append([d for d in own + rest for _ in range(repeat)])
+    reach = jnp.array(rows, jnp.int32)
     relative = (table - query_tiles[:, None]) % tiles
     live = jnp.arange(slots, dtype=jnp.int32)[None] < counts[:, None]
-    hits = (relative[:, :, None] == reach[None, None]) & live[:, :, None]
+    hits = (relative[:, :, None] == reach[:, None]) & live[:, :, None]
     return jnp.sum(hits.astype(jnp.float32), axis=1)[:, None]
 
 
@@ -402,21 +443,15 @@
     w_other = shifted(w_own, "segment", 1)
     small_own = jnp.concatenate([modulation[0].reshape(-1), qk_gain[0].reshape(-1)])
     small_other = shifted(small_own, "segment", 1)
-    stale, w_out = after((stale_cache[0], w_out), hidden)
-    stale = exchanged(jnp.concatenate([stale[0], stale[1]], axis=-1))
+    stale = after(stale_cache[0], mine)
+    stale = jnp.concatenate([stale[0], stale[1]], axis=-1)
     stale_own = lax.dynamic_slice_in_dim(stale, core * rows_core, rows_core, 1)
     stale_other = shifted(
         lax.dynamic_slice_in_dim(stale, (1 - core) * rows_core, rows_core, 1), "segment", 1
     )
-
-    rows_chip = heads_cols // seq_size
-    slab = lax.dynamic_slice_in_dim(w_out[0], seq_pos * rows_chip, rows_chip, 0)
-    pieces = [
-        lax.dynamic_slice_in_dim(slab, lax.rem(tp_pos + j, tp_size) * part_cols, part_cols, 1)
-        for j in range(tp_size)
-    ]
-    pieces[1:] = [shifted(pieces[j], "tp", j) for j in range(1, tp_size)]
-    wo_own = lax.all_gather(jnp.stack(pieces), "seq", axis=1, tiled=True)
+    stale = jnp.concatenate([stale_own, stale_other], axis=1)
+    wo_own = after(w_out[0], hidden)
+    wo_other = shifted(wo_own, "segment", 1)
 
     turns = jnp.arange(patches, dtype=jnp.int32)
     asked = jnp.stack([chip, chip - 1, chip + 1, chip - seq_size // 2 - 1]) % seq_size // share
@@ -432,12 +467,12 @@
         modul = small[: 3 * width].reshape(3, tp_size, 1, part_cols)
         gain = small[3 * width :].reshape(2, head_dim)
         gate = lax.dynamic_index_in_dim(modul[2], tp_pos, 0, keepdims=False)
-        stale = jnp.where(is_own, stale_own, stale_other)
 
         blocks = gather_features(hidden)
-        if section > 0:
-            early = exchanged(early)
-            blocks, early = lax.optimization_barrier((blocks, early))
+        if section == 0:
+            stale = exchanged(after(stale, blocks[1], blocks[3]))
+        else:
+            early = exchanged(after(early, blocks[1], blocks[3]))
         q_own, kv, *going = project(
             meta,
             blocks,
@@ -447,7 +482,7 @@
             w_own,
             w_other,
             stale if section > 0 else None,
-            stale.shape,
+            stale_own.shape,
         )
         if section == 0:
             going = choose_alone(meta, kv, stale)
@@ -460,16 +495,21 @@
             kv_tiles, tile_counts = after((kv_tiles, tile_counts), q_own)
             multiple_own = count_tiles(kv_tiles[0], tile_counts[0], chip, patches, rows_core)
             multiple_other = shifted(multiple_own, "segment", 1)
+        else:
+            above, early = lax.optimization_barrier((above, early))
         multiple = jnp.where(is_own, multiple_own, multiple_other)
-        cut = multiple.shape[-1] - rows_core
-        before = attend_near(q_own, q_other, below, kv, above, multiple[..., :cut])
-        part_own, part_other = attend_far(q_own, q_other, far, multiple[..., cut:], before)
-        if section == 0:
-            wo_other = shifted(after(wo_own, part_other), "segment", 1)
+        before = attend_own(q_own, q_other, kv, multiple[..., :256])
+        part_own, part_other = attend_rest(
+            q_own, q_other, below, above, far, multiple[..., 256:], before
+        )
         part_back = shifted(part_other, "segment", 1)
-        att = merge(part_own, part_back)
-        atts = [att] + [shifted(att, "tp", j) for j in (1, 2, 3)]
-        hidden = output(meta, atts, wo_own, wo_other, hidden, gate)
+        keep, to_next, to_across, to_prev = spread(
+            meta, part_own, part_back, wo_own, wo_other, tp_size
+        )
+        from_across = shifted(to_across, "tp", 2)
+        from_prev = shifted(to_next, "tp", 1)
+        from_next = shifted(to_prev, "tp", -1)
+        hidden = finish(hidden, gate, keep, from_prev, from_across, from_next)
 
         features = hidden.reshape(patches, rows_core, part_cols)
         pair = (kv, features) if section == 0 else (features, kv)

time: 269 us -> 248 us (0.922)
  waiting for transfers between devices: 98.2 us -> 78 us
  between operations: 14.4 us -> 1.08 us
  starting transfers between devices: 65.1 us -> 54.8 us
  local copies, waits for them, and re-layouts: 21.4 us -> 31.5 us
  Pallas kernels: 45.9 us -> 53.9 us
  other arithmetic: 4.54 us -> 10.4 us
    all_to_all x3, waiting for transfers between devices: 23.2 us -> 4.55 us  [exchanged(): return lax.all_to_all(tiles, 'seq', 0, 0, axis_index_groups=groups)]
    ppermute x6, waiting for transfers between devices: 10 us -> 0.44 us  [along_ring(): return lax.ppermute(block, 'seq', route)]
    unnamed x62 -> x78, local copies, waits for them, and re-layouts: 16.2 us -> 24.6 us
    ppermute x26 -> x23, waiting for transfers between devices: 65 us -> 73 us  [shifted(): return lax.ppermute(block, axis, route)]
    pallas_call x10, Pallas kernels: 42.9 us -> 49.4 us  [the longest x2 14.4 us: project(): pl.pallas_call(kernel, in_specs=[SCALARS] + [ANYWHERE] * len(blocks) + [O...]
    ppermute x26 -> x23, starting transfers between devices: 31.7 us -> 27 us  [shifted(): return lax.ppermute(block, axis, route)]
    ppermute x6, starting transfers between devices: 18.5 us -> 14 us  [along_ring(): return lax.ppermute(block, 'seq', route)]
  transfers between devices with their start and end apart: 36 -> 32, of which waited for: 20 -> 14; matrix products, arithmetic and copies ran while one was open for 3% -> 7% of each run, Pallas kernels for 10% -> 15%
where the time goes in v4:
time: 248 us; the launch traced here: 246 us
  waiting for transfers between devices  78 us (31%)
  starting transfers between devices  54.8 us (22%)
  Pallas kernels  53.9 us (22%)
  local copies, waits for them, and re-layouts  31.5 us (13%)
  blocking collectives  16.2 us (7%)
  other arithmetic  10.4 us (4%)
    ppermute x23, waiting for transfers between devices, shifted(): return lax.ppermute(block, axis, route)  73 us
    ppermute x23, starting transfers between devices, shifted(): return lax.ppermute(block, axis, route)  27 us
    unnamed x78, local copies, waits for them, and re-layouts  24.6 us
    all_to_all x1, blocking collectives, exchanged(): return lax.all_to_all(tiles, 'seq', 0, 0, axis_index_groups=groups)  16.2 us
    pallas_call x2, Pallas kernels, project(): pl.pallas_call(kernel, in_specs=[SCALARS] + [ANYWHERE] * len(blocks) + [O...  14.4 us
    ppermute x6, starting transfers between devices, along_ring(): return lax.ppermute(block, 'seq', route)  14 us
    all_to_all x3, starting transfers between devices, exchanged(): return lax.all_to_all(tiles, 'seq', 0, 0, axis_index_groups=groups)  13.9 us
    pallas_call x2, Pallas kernels, attend_rest(): pl.pallas_call(attend_rest_kernel, in_specs=[ON_CHIP] * 7, out_specs=[ON_...  13.9 us
  transfers between devices with their start and end apart: 32, of which 14 were waited for; matrix products, arithmetic and copies ran while one was open for 7% of the time, Pallas kernels for 15%

profile of v4, /device:TPU:1, one launch (start us, length us, event | category | flops | bytes accessed | tf_op | source)
XLA Modules:
  0.0 246.0 jit_solution(13157872932045808113)
XLA Ops:
  2.9 5.5 %all-to-all-start = ((bf16[8,32,768]{2,1,0:T(8,128)(2,1)}), bf16[8,32,768]{2,1,0:T(8,128)(2,1)S(1)}, u32[]{:S(2)}, u32[]{:S(2)}) async-start(bf16[8,32,768]{2,1,0:T(8,128)(2,1)} %constant_dynamic-slice_fusion.1), calls=%async_computation | async-start | bytes 786432 | tf_op jit(solution)/shard_map/all_to_all | solution.py:38
  12.7 4.5 %all-to-all-done = bf16[8,32,768]{2,1,0:T(8,128)(2,1)S(1)} async-done(((bf16[8,32,768]{2,1,0:T(8,128)(2,1)}), bf16[8,32,768]{2,1,0:T(8,128)(2,1)S(1)}, u32[]{:S(2)}, u32[]{:S(2)}) %all-to-all-start) | async-done | bytes 393248 | tf_op jit(solution)/shard_map/all_to_all | solution.py:38
  17.2 3.8 %collective-permute-start.1 = (bf16[256,768]{1,0:T(8,128)(2,1)S(1)}, bf16[256,768]{1,0:T(8,128)(2,1)}, u32[]{:S(2)}, u32[]{:S(2)}) collective-permute-start(bf16[256,768]{1,0:T(8,128)(2,1)S(1)} %bitcast.58), channel_id=1, source_target_pairs={{1,0},{2,1},{3,2},{0,3},{5,4},{6,5},{7,6},{4,7},{9,8},{10,9},{11,1... | collective-permute-start | bytes 1179656 | tf_op jit(solution)/shard_map/ppermute | solution.py:20
  25.4 3.2 %collective-permute-done.1.refs_2_ = bf16[256,768]{1,0:T(8,128)(2,1)} collective-permute-done((bf16[256,768]{1,0:T(8,128)(2,1)S(1)}, bf16[256,768]{1,0:T(8,128)(2,1)}, u32[]{:S(2)}, u32[]{:S(2)}) %collective-permute-start.1) | collective-permute-done | bytes 393248 | tf_op jit(solution)/shard_map/ppermute | solution.py:20
  28.5 3.2 %collective-permute-done.3.refs_4_ = bf16[256,768]{1,0:T(8,128)(2,1)} collective-permute-done((bf16[256,768]{1,0:T(8,128)(2,1)S(1)}, bf16[256,768]{1,0:T(8,128)(2,1)}, u32[]{:S(2)}, u32[]{:S(2)}) %collective-permute-start.3) | collective-permute-done | bytes 393248 | tf_op jit(solution)/shard_map/ppermute | solution.py:20
  31.8 4.2 %all-to-all-start.1 = ((bf16[8,64,768]{2,1,0:T(8,128)(2,1)}), bf16[8,64,768]{2,1,0:T(8,128)(2,1)}, u32[]{:S(2)}, u32[]{:S(2)}) async-start(bf16[8,64,768]{2,1,0:T(8,128)(2,1)} %pad_maximum_fusion), calls=%async_computation.1 | async-start | bytes 1572864 | tf_op jit(solution)/shard_map/all_to_all | solution.py:38
  37.5 9.5 %collective-permute-done.2.refs_3_ = bf16[256,768]{1,0:T(8,128)(2,1)S(1)} collective-permute-done((bf16[256,768]{1,0:T(8,128)(2,1)S(1)}, bf16[256,768]{1,0:T(8,128)(2,1)S(1)}, u32[]{:S(2)}, u32[]{:S(2)}) %collective-permute-start.2) | collective-permute-done | bytes 393248 | tf_op jit(solution)/shard_map/ppermute | solution.py:20
  51.1 6.9 %project.2 = (bf16[8,32,384]{2,1,0:T(8,128)(2,1)S(1)}, bf16[8,32,768]{2,1,0:T(8,128)(2,1)S(1)}) custom-call(s32[5]{0:T(128)S(1)} %get-tuple-element.84.refs_0_.meta, bf16[256,768]{1,0:T(8,128)(2,1)S(1)} %bitcast.61, bf16[256,768]{1,0:T(8,128)(2,1)} %collective-permute-done.1.refs_2_, bf16[256,768]{1,0:T(8,128)(2,1)S(1)} %collective-permute-done.2.refs_3_, ...), custom_call_target="tpu_custom_call" | custom-call | tf_op jit(solution)/shard_map/project/pallas_call | solution.py:204
  62.2 4.6 %collective-permute-start.9 = (bf16[8,32,768]{2,1,0:T(8,128)(2,1)}, bf16[8,32,768]{2,1,0:T(8,128)(2,1)}, u32[]{:S(2)}, u32[]{:S(2)}) collective-permute-start(bf16[8,32,768]{2,1,0:T(8,128)(2,1)} %get-tuple-element.40), channel_id=1, source_target_pairs={{48,0},{20,32},{52,4},{24,36},{56,8},{28,40},{60,12},{0,44},{32,16... | collective-permute-start | bytes 1179656 | tf_op jit(solution)/shard_map/ppermute | solution.py:46
  74.0 4.0 %collective-permute-start.8 = (bf16[3,32,768]{2,1,0:T(8,128)(2,1)}, bf16[3,32,768]{2,1,0:T(8,128)(2,1)S(1)}, u32[]{:S(2)}, u32[]{:S(2)}) collective-permute-start(bf16[3,32,768]{2,1,0:T(8,128)(2,1)} %copy-done.32), channel_id=1, source_target_pairs={{32,0},{4,32},{36,4},{8,36},{40,8},{12,40},{44,12},{16,44},{48,16}... | collective-permute-start | bytes 442376 | tf_op jit(solution)/shard_map/ppermute | solution.py:46
  79.6 6.2 %attend_own.2.before = f32[8,64,512]{2,1,0:T(8,128)S(1)} custom-call(bf16[8,32,384]{2,1,0:T(8,128)(2,1)S(1)} %copy-done.14, bf16[8,32,384]{2,1,0:T(8,128)(2,1)S(1)} %collective-permute-done.5.q_other, bf16[8,32,768]{2,1,0:T(8,128)(2,1)S(1)} %get-tuple-element.35.kv.own, f32[8,1,256]{2,1,0:T(1,128)S(1)} %slice.135.multiple), custom_call_target="tpu_custom_call" | custom-call | tf_op jit(solution)/shard_map/attend_own/pallas_call | solution.py:265
  85.8 6.9 %attend_rest.2 = (f32[8,32,512]{2,1,0:T(8,128)S(1)}, f32[8,32,512]{2,1,0:T(8,128)S(1)}) custom-call(bf16[8,32,384]{2,1,0:T(8,128)(2,1)S(1)} %copy-done.15, bf16[8,32,384]{2,1,0:T(8,128)(2,1)S(1)} %collective-permute-done.5.q_other, bf16[3,32,768]{2,1,0:T(8,128)(2,1)S(1)} %collective-permute-done.7.below, ...), custom_call_target="tpu_custom_call" | custom-call | tf_op jit(solution)/shard_map/attend_rest/pallas_call | solution.py:311
  95.3 4.0 %spread.2 = (f32[256,768]{1,0:T(8,128)S(1)}, bf16[256,768]{1,0:T(8,128)(2,1)}, bf16[256,768]{1,0:T(8,128)(2,1)}, bf16[256,768]{1,0:T(8,128)(2,1)}) custom-call(s32[5]{0:T(128)S(1)} %get-tuple-element.84.refs_0_.meta, f32[8,32,512]{2,1,0:T(8,128)S(1)} %get-tuple-element.43.part_a, f32[8,32,512]{2,1,0:T(8,128)S(1)} %collective-permute-done.11.part_b, ...), custom_call_target="tpu_custom_call" | custom-call | tf_op jit(solution)/shard_map/spread/pallas_call | solution.py:363
  103.5 17.2 %collective-permute-done.13.from_prev = bf16[256,768]{1,0:T(8,128)(2,1)S(1)} collective-permute-done((bf16[256,768]{1,0:T(8,128)(2,1)}, bf16[256,768]{1,0:T(8,128)(2,1)S(1)}, u32[]{:S(2)}, u32[]{:S(2)}) %collective-permute-start.13) | collective-permute-done | bytes 393248 | tf_op jit(solution)/shard_map/ppermute | solution.py:20
  131.0 6.8 %collective-permute-done.16.refs_2_ = bf16[256,768]{1,0:T(8,128)(2,1)S(1)} collective-permute-done((bf16[256,768]{1,0:T(8,128)(2,1)S(1)}, bf16[256,768]{1,0:T(8,128)(2,1)S(1)}, u32[]{:S(2)}, u32[]{:S(2)}) %collective-permute-start.16) | collective-permute-done | bytes 393248 | tf_op jit(solution)/shard_map/ppermute | solution.py:20
  138.6 11.1 %collective-permute-done.18.refs_4_ = bf16[256,768]{1,0:T(8,128)(2,1)S(1)} collective-permute-done((bf16[256,768]{1,0:T(8,128)(2,1)S(1)}, bf16[256,768]{1,0:T(8,128)(2,1)S(1)}, u32[]{:S(2)}, u32[]{:S(2)}) %collective-permute-start.18) | collective-permute-done | bytes 393248 | tf_op jit(solution)/shard_map/ppermute | solution.py:20
  150.4 4.2 %all-to-all-start.2 = ((bf16[8,64,768]{2,1,0:T(8,128)(2,1)}), bf16[8,64,768]{2,1,0:T(8,128)(2,1)}, u32[]{:S(2)}, u32[]{:S(2)}) async-start(bf16[8,64,768]{2,1,0:T(8,128)(2,1)} %pad_maximum_fusion.1), calls=%async_computation.2 | async-start | bytes 1572864 | tf_op jit(solution)/shard_map/all_to_all | solution.py:38
  161.0 7.5 %project.3 = (bf16[8,32,384]{2,1,0:T(8,128)(2,1)S(1)}, bf16[8,32,768]{2,1,0:T(8,128)(2,1)S(1)}, bf16[3,32,768]{2,1,0:T(8,128)(2,1)S(1)}, bf16[3,32,768]{2,1,0:T(8,128)(2,1)}, bf16[8,32,768]{2,1,0:T(8,128)(2,1)}) custom-call(s32[5]{0:T(128)S(1)} %copy-done.31, bf16[256,768]{1,0:T(8,128)(2,1)S(1)} %finish.2.refs_1_.hidden, bf16[256,768]{1,0:T(8,128)(2,1)S(1)} %copy-done.25, ...), custom_call_target="tpu_custom_call" | custom-call | tf_op jit(solution)/shard_map/project/pallas_call | solution.py:204
  176.6 6.2 %attend_own.3.before = f32[8,64,512]{2,1,0:T(8,128)S(1)} custom-call(bf16[8,32,384]{2,1,0:T(8,128)(2,1)S(1)} %get-tuple-element.53.q_own, bf16[8,32,384]{2,1,0:T(8,128)(2,1)S(1)} %collective-permute-done.21.q_other, bf16[8,32,768]{2,1,0:T(8,128)(2,1)S(1)} %get-tuple-element.57.own, f32[8,1,256]{2,1,0:T(1,128)S(1)} %slice.141.multiple), custom_call_target="tpu_custom_call" | custom-call | tf_op jit(solution)/shard_map/attend_own/pallas_call | solution.py:265
  188.9 7.0 %attend_rest.3 = (f32[8,32,512]{2,1,0:T(8,128)S(1)}, f32[8,32,512]{2,1,0:T(8,128)S(1)}) custom-call(bf16[8,32,384]{2,1,0:T(8,128)(2,1)S(1)} %copy-done.17, bf16[8,32,384]{2,1,0:T(8,128)(2,1)S(1)} %copy-done.19, bf16[3,32,768]{2,1,0:T(8,128)(2,1)} %collective-permute-done.22.below, bf16[3,32,768]{2,1,0:T(8,128)(2,1)S(1)} %copy-done.29, ...), custom_call_target="tpu_custom_call" | custom-call | tf_op jit(solution)/shard_map/attend_rest/pallas_call | solution.py:311
  195.8 3.2 %collective-permute-start.24 = (f32[8,32,512]{2,1,0:T(8,128)S(1)}, f32[8,32,512]{2,1,0:T(8,128)S(1)}, u32[]{:S(2)}, u32[]{:S(2)}) collective-permute-start(f32[8,32,512]{2,1,0:T(8,128)S(1)} %get-tuple-element.59), channel_id=1, source_target_pairs={{64,0},{0,64},{65,1},{1,65},{66,2},{2,66},{67,3},{3,67},{68,4},{4,... | collective-permute-start | bytes 1572872 | tf_op jit(solution)/shard_map/ppermute | solution.py:20
  200.5 3.1 %spread.3 = (f32[256,768]{1,0:T(8,128)S(1)}, bf16[256,768]{1,0:T(8,128)(2,1)S(1)}, bf16[256,768]{1,0:T(8,128)(2,1)S(1)}, bf16[256,768]{1,0:T(8,128)(2,1)S(1)}) custom-call(s32[5]{0:T(128)S(1)} %copy-done.31, f32[8,32,512]{2,1,0:T(8,128)S(1)} %get-tuple-element.58.part_a, f32[8,32,512]{2,1,0:T(8,128)S(1)} %collective-permute-done.24.part_b, ...), custom_call_target="tpu_custom_call" | custom-call | tf_op jit(solution)/shard_map/spread/pallas_call | solution.py:363
  207.1 16.5 %collective-permute-done.25.from_prev = bf16[256,768]{1,0:T(8,128)(2,1)S(1)} collective-permute-done((bf16[256,768]{1,0:T(8,128)(2,1)S(1)}, bf16[256,768]{1,0:T(8,128)(2,1)S(1)}, u32[]{:S(2)}, u32[]{:S(2)}) %collective-permute-start.25) | collective-permute-done | bytes 393248 | tf_op jit(solution)/shard_map/ppermute | solution.py:20
  227.4 16.2 %all_to_all.20.late = bf16[8,64,768]{2,1,0:T(8,128)(2,1)S(1)} all-to-all(bf16[8,64,768]{2,1,0:T(8,128)(2,1)S(1)} %pad_maximum_fusion.2), channel_id=1, replica_groups={{0,4,8,12,16,20,24,28},{32,36,40,44,48,52,56,60},{1,5,9,13,17,21,25,29}..., dimensions={0} | all-to-all | bytes 1572864 | tf_op jit(solution)/shard_map/all_to_all | solution.py:38
  (164 shorter events, 79.5 us)
Async XLA Ops:
  0.7 46.4 %collective-permute-start.4 = (bf16[3,3072,384]{2,1,0:T(8,128)(2,1)}, bf16[3,3072,384]{2,1,0:T(8,128)(2,1)}, u32[]{:S(2)}, u32[]{:S(2)}) collective-permute-start(bf16[3,3072,384]{2,1,0:T(8,128)(2,1)} %bitcast.48), channel_id=1, source_target_pairs={{64,0},{0,64},{65,1},{1,65},{66,2},{2,66},{67,3},{3,67},{68,4},{4,... | collective-permute-start | bytes 21233672 | tf_op jit(solution)/shard_map/ppermute | solution.py:20
  2.9 14.2 %all-to-all-start = ((bf16[8,32,768]{2,1,0:T(8,128)(2,1)}), bf16[8,32,768]{2,1,0:T(8,128)(2,1)S(1)}, u32[]{:S(2)}, u32[]{:S(2)}) async-start(bf16[8,32,768]{2,1,0:T(8,128)(2,1)} %constant_dynamic-slice_fusion.1), calls=%async_computation | async-start | bytes 786432 | tf_op jit(solution)/shard_map/all_to_all | solution.py:38
  9.0 27.0 %collective-permute-start = (f32[9472]{0:T(1024)}, f32[9472]{0:T(1024)}, u32[]{:S(2)}, u32[]{:S(2)}) collective-permute-start(f32[9472]{0:T(1024)} %pad_maximum_fusion.3), channel_id=1, source_target_pairs={{64,0},{0,64},{65,1},{1,65},{66,2},{2,66},{67,3},{3,67},{68,4},{4,... | collective-permute-start | bytes 113672 | tf_op jit(solution)/shard_map/ppermute | solution.py:20
  12.4 9.8 %collective-permute-start.6 = (bf16[8,32,768]{2,1,0:T(8,128)(2,1)}, bf16[8,32,768]{2,1,0:T(8,128)(2,1)}, u32[]{:S(2)}, u32[]{:S(2)}) collective-permute-start(bf16[8,32,768]{2,1,0:T(8,128)(2,1)} %get-tuple-element.71), channel_id=1, source_target_pairs={{64,0},{0,64},{65,1},{1,65},{66,2},{2,66},{67,3},{3,67},{68,4},{4,... | collective-permute-start | bytes 1179656 | tf_op jit(solution)/shard_map/ppermute | solution.py:20
  17.2 11.3 %collective-permute-start.1 = (bf16[256,768]{1,0:T(8,128)(2,1)S(1)}, bf16[256,768]{1,0:T(8,128)(2,1)}, u32[]{:S(2)}, u32[]{:S(2)}) collective-permute-start(bf16[256,768]{1,0:T(8,128)(2,1)S(1)} %bitcast.58), channel_id=1, source_target_pairs={{1,0},{2,1},{3,2},{0,3},{5,4},{6,5},{7,6},{4,7},{9,8},{10,9},{11,1... | collective-permute-start | bytes 1179656 | tf_op jit(solution)/shard_map/ppermute | solution.py:20
  21.0 10.8 %collective-permute-start.3 = (bf16[256,768]{1,0:T(8,128)(2,1)S(1)}, bf16[256,768]{1,0:T(8,128)(2,1)}, u32[]{:S(2)}, u32[]{:S(2)}) collective-permute-start(bf16[256,768]{1,0:T(8,128)(2,1)S(1)} %bitcast.59), channel_id=1, source_target_pairs={{3,0},{0,1},{1,2},{2,3},{7,4},{4,5},{5,6},{6,7},{11,8},{8,9},{9,10... | collective-permute-start | bytes 1179656 | tf_op jit(solution)/shard_map/ppermute | solution.py:20
  22.2 71.6 %collective-permute-start.12 = (bf16[384,3072]{1,0:T(8,128)(2,1)S(1)}, bf16[384,3072]{1,0:T(8,128)(2,1)}, u32[]{:S(2)}, u32[]{:S(2)}) collective-permute-start(bf16[384,3072]{1,0:T(8,128)(2,1)S(1)} %bitcast.53), channel_id=1, source_target_pairs={{64,0},{0,64},{65,1},{1,65},{66,2},{2,66},{67,3},{3,67},{68,4},{4,... | collective-permute-start | bytes 7077896 | tf_op jit(solution)/shard_map/ppermute | solution.py:20
  31.8 27.0 %all-to-all-start.1 = ((bf16[8,64,768]{2,1,0:T(8,128)(2,1)}), bf16[8,64,768]{2,1,0:T(8,128)(2,1)}, u32[]{:S(2)}, u32[]{:S(2)}) async-start(bf16[8,64,768]{2,1,0:T(8,128)(2,1)} %pad_maximum_fusion), calls=%async_computation.1 | async-start | bytes 1572864 | tf_op jit(solution)/shard_map/all_to_all | solution.py:38
  36.8 10.3 %collective-permute-start.2 = (bf16[256,768]{1,0:T(8,128)(2,1)S(1)}, bf16[256,768]{1,0:T(8,128)(2,1)S(1)}, u32[]{:S(2)}, u32[]{:S(2)}) collective-permute-start(bf16[256,768]{1,0:T(8,128)(2,1)S(1)} %bitcast.60), channel_id=1, source_target_pairs={{2,0},{3,1},{0,2},{1,3},{6,4},{7,5},{4,6},{5,7},{10,8},{11,9},{8,1... | collective-permute-start | bytes 1179656 | tf_op jit(solution)/shard_map/ppermute | solution.py:20
  62.2 23.6 %collective-permute-start.9 = (bf16[8,32,768]{2,1,0:T(8,128)(2,1)}, bf16[8,32,768]{2,1,0:T(8,128)(2,1)}, u32[]{:S(2)}, u32[]{:S(2)}) collective-permute-start(bf16[8,32,768]{2,1,0:T(8,128)(2,1)} %get-tuple-element.40), channel_id=1, source_target_pairs={{48,0},{20,32},{52,4},{24,36},{56,8},{28,40},{60,12},{0,44},{32,16... | collective-permute-start | bytes 1179656 | tf_op jit(solution)/shard_map/ppermute | solution.py:46
  73.2 12.5 %collective-permute-start.7 = (bf16[3,32,768]{2,1,0:T(8,128)(2,1)}, bf16[3,32,768]{2,1,0:T(8,128)(2,1)S(1)}, u32[]{:S(2)}, u32[]{:S(2)}) collective-permute-start(bf16[3,32,768]{2,1,0:T(8,128)(2,1)} %copy-done.33), channel_id=1, source_target_pairs={{60,0},{0,32},{32,4},{4,36},{36,8},{8,40},{40,12},{12,44},{44,16},... | collective-permute-start | bytes 442376 | tf_op jit(solution)/shard_map/ppermute | solution.py:46
  74.0 11.8 %collective-permute-start.8 = (bf16[3,32,768]{2,1,0:T(8,128)(2,1)}, bf16[3,32,768]{2,1,0:T(8,128)(2,1)S(1)}, u32[]{:S(2)}, u32[]{:S(2)}) collective-permute-start(bf16[3,32,768]{2,1,0:T(8,128)(2,1)} %copy-done.32), channel_id=1, source_target_pairs={{32,0},{4,32},{36,4},{8,36},{40,8},{12,40},{44,12},{16,44},{48,16}... | collective-permute-start | bytes 442376 | tf_op jit(solution)/shard_map/ppermute | solution.py:46
  100.2 20.5 %collective-permute-start.13 = (bf16[256,768]{1,0:T(8,128)(2,1)}, bf16[256,768]{1,0:T(8,128)(2,1)S(1)}, u32[]{:S(2)}, u32[]{:S(2)}) collective-permute-start(bf16[256,768]{1,0:T(8,128)(2,1)} %get-tuple-element.47), channel_id=1, source_target_pairs={{3,0},{0,1},{1,2},{2,3},{7,4},{4,5},{5,6},{6,7},{11,8},{8,9},{9,10... | collective-permute-start | bytes 1179656 | tf_op jit(solution)/shard_map/ppermute | solution.py:20
  100.2 21.3 %collective-permute-start.14 = (bf16[256,768]{1,0:T(8,128)(2,1)}, bf16[256,768]{1,0:T(8,128)(2,1)}, u32[]{:S(2)}, u32[]{:S(2)}) collective-permute-start(bf16[256,768]{1,0:T(8,128)(2,1)} %get-tuple-element.48), channel_id=1, source_target_pairs={{2,0},{3,1},{0,2},{1,3},{6,4},{7,5},{4,6},{5,7},{10,8},{11,9},{8,1... | collective-permute-start | bytes 1179656 | tf_op jit(solution)/shard_map/ppermute | solution.py:20
  101.6 19.8 %collective-permute-start.15 = (bf16[256,768]{1,0:T(8,128)(2,1)}, bf16[256,768]{1,0:T(8,128)(2,1)}, u32[]{:S(2)}, u32[]{:S(2)}) collective-permute-start(bf16[256,768]{1,0:T(8,128)(2,1)} %get-tuple-element.49), channel_id=1, source_target_pairs={{1,0},{2,1},{3,2},{0,3},{5,4},{6,5},{7,6},{4,7},{9,8},{10,9},{11,1... | collective-permute-start | bytes 1179656 | tf_op jit(solution)/shard_map/ppermute | solution.py:20
  127.1 10.7 %collective-permute-start.16 = (bf16[256,768]{1,0:T(8,128)(2,1)S(1)}, bf16[256,768]{1,0:T(8,128)(2,1)S(1)}, u32[]{:S(2)}, u32[]{:S(2)}) collective-permute-start(bf16[256,768]{1,0:T(8,128)(2,1)S(1)} %finish.2.refs_1_.hidden), channel_id=1, source_target_pairs={{1,0},{2,1},{3,2},{0,3},{5,4},{6,5},{7,6},{4,7},{9,8},{10,9},{11,1... | collective-permute-start | bytes 1179656 | tf_op jit(solution)/shard_map/ppermute | solution.py:20
  129.3 26.0 %collective-permute-start.17 = (bf16[256,768]{1,0:T(8,128)(2,1)S(1)}, bf16[256,768]{1,0:T(8,128)(2,1)}, u32[]{:S(2)}, u32[]{:S(2)}) collective-permute-start(bf16[256,768]{1,0:T(8,128)(2,1)S(1)} %finish.2.refs_1_.hidden), channel_id=1, source_target_pairs={{2,0},{3,1},{0,2},{1,3},{6,4},{7,5},{4,6},{5,7},{10,8},{11,9},{8,1... | collective-permute-start | bytes 1179656 | tf_op jit(solution)/shard_map/ppermute | solution.py:20
  129.3 20.3 %collective-permute-start.18 = (bf16[256,768]{1,0:T(8,128)(2,1)S(1)}, bf16[256,768]{1,0:T(8,128)(2,1)S(1)}, u32[]{:S(2)}, u32[]{:S(2)}) collective-permute-start(bf16[256,768]{1,0:T(8,128)(2,1)S(1)} %finish.2.refs_1_.hidden), channel_id=1, source_target_pairs={{3,0},{0,1},{1,2},{2,3},{7,4},{4,5},{5,6},{6,7},{11,8},{8,9},{9,10... | collective-permute-start | bytes 1179656 | tf_op jit(solution)/shard_map/ppermute | solution.py:20
  150.4 34.0 %all-to-all-start.2 = ((bf16[8,64,768]{2,1,0:T(8,128)(2,1)}), bf16[8,64,768]{2,1,0:T(8,128)(2,1)}, u32[]{:S(2)}, u32[]{:S(2)}) async-start(bf16[8,64,768]{2,1,0:T(8,128)(2,1)} %pad_maximum_fusion.1), calls=%async_computation.2 | async-start | bytes 1572864 | tf_op jit(solution)/shard_map/all_to_all | solution.py:38
  168.6 16.3 %collective-permute-start.23 = (bf16[8,32,768]{2,1,0:T(8,128)(2,1)}, bf16[8,32,768]{2,1,0:T(8,128)(2,1)}, u32[]{:S(2)}, u32[]{:S(2)}) collective-permute-start(bf16[8,32,768]{2,1,0:T(8,128)(2,1)} %get-tuple-element.56), channel_id=1, source_target_pairs={{48,0},{20,32},{52,4},{24,36},{56,8},{28,40},{60,12},{0,44},{32,16... | collective-permute-start | bytes 1179656 | tf_op jit(solution)/shard_map/ppermute | solution.py:46
  173.6 10.2 %collective-permute-start.19 = (bf16[3,32,768]{2,1,0:T(8,128)(2,1)S(1)}, bf16[3,32,768]{2,1,0:T(8,128)(2,1)S(1)}, u32[]{:S(2)}, u32[]{:S(2)}) collective-permute-start(bf16[3,32,768]{2,1,0:T(8,128)(2,1)S(1)} %get-tuple-element.50), channel_id=1, source_target_pairs={{32,0},{4,32},{36,4},{8,36},{40,8},{12,40},{44,12},{16,44},{48,16}... | collective-permute-start | bytes 442376 | tf_op jit(solution)/shard_map/ppermute | solution.py:46
  203.7 20.0 %collective-permute-start.25 = (bf16[256,768]{1,0:T(8,128)(2,1)S(1)}, bf16[256,768]{1,0:T(8,128)(2,1)S(1)}, u32[]{:S(2)}, u32[]{:S(2)}) collective-permute-start(bf16[256,768]{1,0:T(8,128)(2,1)S(1)} %get-tuple-element.61), channel_id=1, source_target_pairs={{3,0},{0,1},{1,2},{2,3},{7,4},{4,5},{5,6},{6,7},{11,8},{8,9},{9,10... | collective-permute-start | bytes 1179656 | tf_op jit(solution)/shard_map/ppermute | solution.py:20
  203.7 19.9 %collective-permute-start.26 = (bf16[256,768]{1,0:T(8,128)(2,1)S(1)}, bf16[256,768]{1,0:T(8,128)(2,1)S(1)}, u32[]{:S(2)}, u32[]{:S(2)}) collective-permute-start(bf16[256,768]{1,0:T(8,128)(2,1)S(1)} %get-tuple-element.62), channel_id=1, source_target_pairs={{2,0},{3,1},{0,2},{1,3},{6,4},{7,5},{4,6},{5,7},{10,8},{11,9},{8,1... | collective-permute-start | bytes 1179656 | tf_op jit(solution)/shard_map/ppermute | solution.py:20
  204.8 19.1 %collective-permute-start.27 = (bf16[256,768]{1,0:T(8,128)(2,1)S(1)}, bf16[256,768]{1,0:T(8,128)(2,1)S(1)}, u32[]{:S(2)}, u32[]{:S(2)}) collective-permute-start(bf16[256,768]{1,0:T(8,128)(2,1)S(1)} %get-tuple-element.63), channel_id=1, source_target_pairs={{1,0},{2,1},{3,2},{0,3},{5,4},{6,5},{7,6},{4,7},{9,8},{10,9},{11,1... | collective-permute-start | bytes 1179656 | tf_op jit(solution)/shard_map/ppermute | solution.py:20
  (47 other events, 257.6 us)

commit v5 on v4

--- a/solution.py
+++ b/solution.py
@@ -125,7 +125,7 @@
     heads_cols = kv_cols // 2
     parts = shift.shape[0]
     width = cols * parts
-    features = [lax.rem(meta[0] + j, parts) for j in range(parts)]
+    features = [lax.rem(meta[0] + j, parts) for j in (2, 1, 3, 0)]
 
     def fetch(j, source):
         first = pl.multiple_of(features[j] * cols, cols)
@@ -216,48 +216,65 @@
             pltpu.VMEM((3, parts * cols, heads_cols), jnp.bfloat16),
             pltpu.SemaphoreType.DMA((2 * parts,)),
         ],
-        compiler_params=params(16),
+        compiler_params=params(56),
         name="project",
     )(meta, *blocks, shift, scale, gain, w_own, w_other, *extra)
 
 
-def soften(queries, keys, values, times, floor):
-    scores = lax.dot_general(
-        queries, keys, (((1,), (1,)), ((), ())), preferred_element_type=jnp.float32
-    )
-    scores = jnp.where(times > 0.0, scores * HEAD_DIM ** (-0.5), -1e30)
-    peak = jnp.max(scores, axis=-1, keepdims=True)
-    if floor is not None:
-        peak = jnp.maximum(peak, floor)
-    weights = jnp.exp(scores - peak) * times
-    total = jnp.sum(weights, axis=-1, keepdims=True)
-    summed = jnp.dot(weights.astype(jnp.bfloat16), values, preferred_element_type=jnp.float32)
-    return peak, total, summed
+def soften(queries, keys, values, times, floors):
+    scores = [
+        lax.dot_general(q, k, (((1,), (1,)), ((), ())), preferred_element_type=jnp.float32)
+        for q, k in zip(queries, keys)
+    ]
+    scores = [
+        jnp.where(count > 0.0, each * HEAD_DIM ** (-0.5), -1e30)
+        for each, count in zip(scores, times)
+    ]
+    peaks = [jnp.max(each, axis=-1, keepdims=True) for each in scores]
+    if floors is not None:
+        peaks = [jnp.maximum(peak, floor) for peak, floor in zip(peaks, floors)]
+    weights = [
+        jnp.exp(each - peak) * count for each, peak, count in zip(scores, peaks, times)
+    ]
+    totals = [jnp.sum(each, axis=-1, keepdims=True) for each in weights]
+    summed = [
+        jnp.dot(each.astype(jnp.bfloat16), v, preferred_element_type=jnp.float32)
+        for each, v in zip(weights, values)
+    ]
+    return peaks, totals, summed
+
+
+def head_cuts(heads_cols):
+    return [slice(first, first + HEAD_DIM) for first in range(0, heads_cols, HEAD_DIM)]
+
+
+def packed(peaks, totals):
+    lane = lax.broadcasted_iota(jnp.int32, (peaks[0].shape[0], HEAD_DIM), 1)
+    out = jnp.zeros((peaks[0].shape[0], HEAD_DIM), jnp.float32)
+    for head, (peak, total) in enumerate(zip(peaks, totals)):
+        out = jnp.where(lane == head, peak, out)
+        out = jnp.where(lane == 64 + head, total, out)
+    return out
 
 
 def attend_own_kernel(q_own, q_other, own, multiple, out):
     tiles, rows, heads_cols = q_own.shape
-    lane = lax.broadcasted_iota(jnp.int32, (2 * rows, HEAD_DIM), 1)
+    cuts = head_cuts(heads_cols)
     for tile in range(tiles):
         first, last = max(0, tile - REACH), min(tiles, tile + REACH + 1)
         count = (last - first) * rows
-        extra = jnp.zeros((2 * rows, HEAD_DIM), jnp.float32)
-        for head in range(heads_cols // HEAD_DIM):
-            start = head * HEAD_DIM
-            cut = slice(start, start + HEAD_DIM)
-            second = slice(heads_cols + start, heads_cols + start + HEAD_DIM)
-            queries = jnp.concatenate([q_own[tile, :, cut], q_other[tile, :, cut]], axis=0)
-            peak, total, summed = soften(
-                queries,
-                own[first:last, :, cut].reshape(count, HEAD_DIM),
-                own[first:last, :, second].reshape(count, HEAD_DIM),
-                multiple[tile, :, :count],
-                None,
-            )
-            out[tile, :, cut] = summed
-            extra = jnp.where(lane == head, peak, extra)
-            extra = jnp.where(lane == 64 + head, total, extra)
-        out[tile, :, heads_cols:] = extra
+        both = own[first:last].reshape(count, 2 * heads_cols)
+        queries = jnp.concatenate([q_own[tile], q_other[tile]], axis=0)
+        peaks, totals, summed = soften(
+            [queries[:, cut] for cut in cuts],
+            [both[:, cut] for cut in cuts],
+            [both[:, heads_cols + cut.start : heads_cols + cut.stop] for cut in cuts],
+            [multiple[tile, :, :count]] * len(cuts),
+            None,
+        )
+        for cut, each in zip(cuts, summed):
+            out[tile, :, cut] = each
+        out[tile, :, heads_cols:] = packed(peaks, totals)
 
 
 def attend_own(q_own, q_other, own, multiple):
@@ -274,36 +291,35 @@
 
 def attend_rest_kernel(q_own, q_other, below, above, far, multiple, before, out_own, out_other):
     tiles, rows, heads_cols = q_own.shape
-    lane = lax.broadcasted_iota(jnp.int32, (2 * rows, HEAD_DIM), 1)
-    for tile in range(tiles):
-        pieces = [below[place] for place in range(tile, REACH)]
-        pieces += [above[place] for place in range(tile + REACH + 1 - tiles)]
-        pieces += [far[tile]]
-        keys_values = jnp.concatenate(pieces, axis=0)
-        extra = jnp.zeros((2 * rows, HEAD_DIM), jnp.float32)
-        for head in range(heads_cols // HEAD_DIM):
-            start = head * HEAD_DIM
-            cut = slice(start, start + HEAD_DIM)
-            second = slice(heads_cols + start, heads_cols + start + HEAD_DIM)
-            queries = jnp.concatenate([q_own[tile, :, cut], q_other[tile, :, cut]], axis=0)
-            peak_before = before[tile, :, heads_cols + head : heads_cols + head + 1]
-            total_before = before[tile, :, heads_cols + 64 + head : heads_cols + 65 + head]
-            peak, total, summed = soften(
-                queries,
-                keys_values[:, cut],
-                keys_values[:, second],
-                multiple[tile, :, : keys_values.shape[0]],
-                peak_before,
-            )
-            shrink = jnp.exp(peak_before - peak)
-            total += total_before * shrink
-            summed += before[tile, :, cut] * shrink
-            out_own[tile, :, cut] = summed[:rows]
-            out_other[tile, :, cut] = summed[rows:]
-            extra = jnp.where(lane == head, peak, extra)
-            extra = jnp.where(lane == 64 + head, total, extra)
-        out_own[tile, :, heads_cols:] = extra[:rows]
-        out_other[tile, :, heads_cols:] = extra[rows:]
+    cuts = head_cuts(heads_cols)
+    heads = len(cuts)
+    for pair in range(0, tiles, 2):
+        queries, keys, values, times, floors, earlier = [], [], [], [], [], []
+        for tile in (pair, pair + 1):
+            pieces = [below[place] for place in range(tile, REACH)]
+            pieces += [above[place] for place in range(tile + REACH + 1 - tiles)]
+            pieces += [far[tile]]
+            both = jnp.concatenate(pieces, axis=0)
+            asked = jnp.concatenate([q_own[tile], q_other[tile]], axis=0)
+            extra = before[tile, :, heads_cols:]
+            queries += [asked[:, cut] for cut in cuts]
+            keys += [both[:, cut] for cut in cuts]
+            values += [both[:, heads_cols + cut.start : heads_cols + cut.stop] for cut in cuts]
+            times += [multiple[tile, :, : both.shape[0]]] * heads
+            floors += [extra[:, head : head + 1] for head in range(heads)]
+            earlier += [extra[:, 64 + head : 65 + head] for head in range(heads)]
+        peaks, totals, summed = soften(queries, keys, values, times, floors)
+        shrink = [jnp.exp(floor - peak) for floor, peak in zip(floors, peaks)]
+        totals = [total + old * less for total, old, less in zip(totals, earlier, shrink)]
+        for place, tile in enumerate((pair, pair + 1)):
+            here = slice(place * heads, (place + 1) * heads)
+            for cut, each, less in zip(cuts, summed[here], shrink[here]):
+                result = each + before[tile, :, cut] * less
+                out_own[tile, :, cut] = result[:rows]
+                out_other[tile, :, cut] = result[rows:]
+            extra = packed(peaks[here], totals[here])
+            out_own[tile, :, heads_cols:] = extra[:rows]
+            out_other[tile, :, heads_cols:] = extra[rows:]
 
 
 def attend_rest(q_own, q_other, below, above, far, multiple, before):
@@ -337,18 +353,19 @@
             for j in range(parts):
                 fetch(j, source).start()
 
-    for tile in range(tiles):
-        extra_a = part_a[tile, :, heads_cols:]
-        extra_b = part_b[tile, :, heads_cols:]
-        for head in range(heads_cols // HEAD_DIM):
-            cut = slice(head * HEAD_DIM, (head + 1) * HEAD_DIM)
-            peak_a, total_a = extra_a[:, head : head + 1], extra_a[:, 64 + head : 65 + head]
-            peak_b, total_b = extra_b[:, head : head + 1], extra_b[:, 64 + head : 65 + head]
-            peak = jnp.maximum(peak_a, peak_b)
-            grow_a, grow_b = jnp.exp(peak_a - peak), jnp.exp(peak_b - peak)
-            total = total_a * grow_a + total_b * grow_b
-            summed = part_a[tile, :, cut] * grow_a + part_b[tile, :, cut] * grow_b
-            att[tile * rows : (tile + 1) * rows, cut] = (summed / total).astype(jnp.bfloat16)
+    extra_a = part_a[:, :, heads_cols:].reshape(tiles * rows, HEAD_DIM)
+    extra_b = part_b[:, :, heads_cols:].reshape(tiles * rows, HEAD_DIM)
+    for head, cut in enumerate(head_cuts(heads_cols)):
+        peak_a, total_a = extra_a[:, head : head + 1], extra_a[:, 64 + head : 65 + head]
+        peak_b, total_b = extra_b[:, head : head + 1], extra_b[:, 64 + head : 65 + head]
+        peak = jnp.maximum(peak_a, peak_b)
+        grow_a, grow_b = jnp.exp(peak_a - peak), jnp.exp(peak_b - peak)
+        total = total_a * grow_a + total_b * grow_b
+        summed_a = part_a[:, :, cut].reshape(tiles * rows, HEAD_DIM)
+        summed_b = part_b[:, :, cut].reshape(tiles * rows, HEAD_DIM)
+        att[:, cut] = (summed_a * (grow_a / total) + summed_b * (grow_b / total)).astype(
+            jnp.bfloat16
+        )
     for j in range(parts):
         fetch(j, wo_own).wait()
     for j, out in enumerate((keep, to_next, to_across, to_prev)):
@@ -375,22 +392,23 @@
     )(meta, part_a, part_b, wo_own, wo_other)
 
 
-def finish_kernel(hidden, gate, keep, from_prev, from_across, from_next, out):
+def finish_kernel(meta, from_across, from_prev, from_next, keep, hidden, gates, out):
     total = keep[...]
     for part in (from_prev, from_across, from_next):
         total += part[...].astype(jnp.float32)
-    out[...] = (hidden[...].astype(jnp.float32) + gate[...] * total).astype(out.dtype)
-
-
-def finish(hidden, gate, *parts):
+    gate = gates[meta[0]]
+    out[...] = (hidden[...].astype(jnp.float32) + gate * total).astype(out.dtype)
+
+
+def finish(meta, from_across, from_prev, from_next, keep, hidden, gates):
     return pl.pallas_call(
         finish_kernel,
-        in_specs=[ON_CHIP] * (2 + len(parts)),
+        in_specs=[SCALARS] + [ON_CHIP] * 6,
         out_specs=ON_CHIP,
         out_shape=struct(hidden.shape),
         compiler_params=params(8),
         name="finish",
-    )(hidden, gate, *parts)
+    )(meta, from_across, from_prev, from_next, keep, hidden, gates)
 
 
 def count_tiles(table, counts, chip, per_chip, repeat):
@@ -418,7 +436,7 @@
 
 def gather_features(hidden):
     across = shifted(hidden, "tp", 2)
-    return hidden, shifted(hidden, "tp", -1), across, shifted(hidden, "tp", 1)
+    return across, shifted(hidden, "tp", -1), shifted(hidden, "tp", 1), hidden
 
 
 def local(
@@ -450,14 +468,13 @@
         lax.dynamic_slice_in_dim(stale, (1 - core) * rows_core, rows_core, 1), "segment", 1
     )
     stale = jnp.concatenate([stale_own, stale_other], axis=1)
-    wo_own = after(w_out[0], hidden)
-    wo_other = shifted(wo_own, "segment", 1)
-
     turns = jnp.arange(patches, dtype=jnp.int32)
     asked = jnp.stack([chip, chip - 1, chip + 1, chip - seq_size // 2 - 1]) % seq_size // share
     ranks = jnp.sum(jnp.where(patch_order[None] == asked[:, None], turns[None], 0), axis=-1)
     fresh = (ranks[0] <= ranks[1:]).astype(jnp.int32)
-
+    multiple_own = count_tiles(kv_tiles[0], tile_counts[0], chip, patches, rows_core)
+    multiple_other = shifted(multiple_own, "segment", 1)
+    given = []
     for section in range(2):
         is_own = core == section
         meta = jnp.concatenate(
@@ -466,18 +483,26 @@
         small = jnp.where(is_own, small_own, small_other)
         modul = small[: 3 * width].reshape(3, tp_size, 1, part_cols)
         gain = small[3 * width :].reshape(2, head_dim)
-        gate = lax.dynamic_index_in_dim(modul[2], tp_pos, 0, keepdims=False)
-
+        multiple = jnp.where(is_own, multiple_own, multiple_other)
+        given.append(
+            (meta, modul[0], modul[1], modul[2], gain, multiple[..., :256], multiple[..., 256:])
+        )
+    hidden, given, stale, w_out = lax.optimization_barrier((hidden, given, stale, w_out))
+    wo_own = w_out[0]
+    wo_other = shifted(wo_own, "segment", 1)
+
+    for section in range(2):
+        meta, shift, scale, gates, gain, times_own, times_rest = given[section]
         blocks = gather_features(hidden)
         if section == 0:
-            stale = exchanged(after(stale, blocks[1], blocks[3]))
+            stale = exchanged(after(stale, blocks[1], blocks[2]))
         else:
-            early = exchanged(after(early, blocks[1], blocks[3]))
+            early = exchanged(after(early, blocks[1], blocks[2]))
         q_own, kv, *going = project(
             meta,
             blocks,
-            modul[0],
-            modul[1],
+            shift,
+            scale,
             gain,
             w_own,
             w_other,
@@ -491,16 +516,11 @@
         above = along_ring(to_below, 1, patches)
         below = along_ring(to_above, -1, patches)
         q_other = shifted(q_own, "segment", 1)
-        if section == 0:
-            kv_tiles, tile_counts = after((kv_tiles, tile_counts), q_own)
-            multiple_own = count_tiles(kv_tiles[0], tile_counts[0], chip, patches, rows_core)
-            multiple_other = shifted(multiple_own, "segment", 1)
-        else:
+        if section > 0:
             above, early = lax.optimization_barrier((above, early))
-        multiple = jnp.where(is_own, multiple_own, multiple_other)
-        before = attend_own(q_own, q_other, kv, multiple[..., :256])
+        before = attend_own(q_own, q_other, kv, times_own)
         part_own, part_other = attend_rest(
-            q_own, q_other, below, above, far, multiple[..., 256:], before
+            q_own, q_other, below, above, far, times_rest, before
         )
         part_back = shifted(part_other, "segment", 1)
         keep, to_next, to_across, to_prev = spread(
@@ -509,7 +529,7 @@
         from_across = shifted(to_across, "tp", 2)
         from_prev = shifted(to_next, "tp", 1)
         from_next = shifted(to_prev, "tp", -1)
-        hidden = finish(hidden, gate, keep, from_prev, from_across, from_next)
+        hidden = finish(meta, from_across, from_prev, from_next, keep, hidden, gates)
 
         features = hidden.reshape(patches, rows_core, part_cols)
         pair = (kv, features) if section == 0 else (features, kv)

time: 248 us -> 227 us (0.915)
  Pallas kernels: 53.9 us -> 37.7 us
  local copies, waits for them, and re-layouts: 31.5 us -> 18.3 us
  waiting for transfers between devices: 78 us -> 82.1 us
  starting transfers between devices: 54.8 us -> 58.6 us
    unnamed x78 -> x65, local copies, waits for them, and re-layouts: 24.6 us -> 12.3 us
    pallas_call x2, Pallas kernels: 13.9 us -> 5.53 us  [attend_rest(): pl.pallas_call(attend_rest_kernel, in_specs=[ON_CHIP] * 7, out_specs=[ON_...]
    pallas_call x2, Pallas kernels: 12.3 us -> 4.84 us  [attend_own(): pl.pallas_call(attend_own_kernel, in_specs=[ON_CHIP] * 4, out_specs=ON_CH...]
    ppermute x23, waiting for transfers between devices: 73 us -> 79.3 us  [shifted(): return lax.ppermute(block, axis, route)]
    ppermute x6, starting transfers between devices: 14 us -> 19.4 us  [along_ring(): return lax.ppermute(block, 'seq', route)]
    all_to_all x3, waiting for transfers between devices: 4.55 us -> 0.01 us  [exchanged(): return lax.all_to_all(tiles, 'seq', 0, 0, axis_index_groups=groups)]
    ppermute x23, starting transfers between devices: 27 us -> 23.4 us  [shifted(): return lax.ppermute(block, axis, route)]
  transfers between devices with their start and end apart: 32 -> 32, of which waited for: 14 -> 16; matrix products, arithmetic and copies ran while one was open for 7% -> 7% of each run, Pallas kernels for 15% -> 11%
where the time goes in v5:
time: 227 us; the launch traced here: 224 us
  waiting for transfers between devices  82.1 us (36%)
  starting transfers between devices  58.6 us (26%)
  Pallas kernels  37.7 us (17%)
  local copies, waits for them, and re-layouts  18.3 us (8%)
  blocking collectives  17.4 us (8%)
  other arithmetic  9.07 us (4%)
    ppermute x23, waiting for transfers between devices, shifted(): return lax.ppermute(block, axis, route)  79.3 us
    ppermute x23, starting transfers between devices, shifted(): return lax.ppermute(block, axis, route)  23.4 us
    ppermute x6, starting transfers between devices, along_ring(): return lax.ppermute(block, 'seq', route)  19.4 us
    all_to_all x1, blocking collectives, exchanged(): return lax.all_to_all(tiles, 'seq', 0, 0, axis_index_groups=groups)  17.4 us
    pallas_call x2, Pallas kernels, project(): pl.pallas_call(kernel, in_specs=[SCALARS] + [ANYWHERE] * len(blocks) + [O...  16.5 us
    all_to_all x3, starting transfers between devices, exchanged(): return lax.all_to_all(tiles, 'seq', 0, 0, axis_index_groups=groups)  15.8 us
    unnamed x65, local copies, waits for them, and re-layouts  12.3 us
    pallas_call x2, Pallas kernels, attend_rest(): pl.pallas_call(attend_rest_kernel, in_specs=[ON_CHIP] * 7, out_specs=[ON_...  5.53 us
  transfers between devices with their start and end apart: 32, of which 16 were waited for; matrix products, arithmetic and copies ran while one was open for 7% of the time, Pallas kernels for 11%

profile of v5, /device:TPU:1, one launch (start us, length us, event | category | flops | bytes accessed | tf_op | source)
XLA Modules:
  0.0 224.0 jit_solution(62189406405368760)
XLA Ops:
  6.2 5.1 %all-to-all-start = ((bf16[8,32,768]{2,1,0:T(8,128)(2,1)}), bf16[8,32,768]{2,1,0:T(8,128)(2,1)S(1)}, u32[]{:S(2)}, u32[]{:S(2)}) async-start(bf16[8,32,768]{2,1,0:T(8,128)(2,1)} %constant_dynamic-slice_fusion.2), calls=%async_computation | async-start | bytes 786432 | tf_op jit(solution)/shard_map/all_to_all | solution.py:38
  22.6 3.8 %collective-permute-start.4 = (bf16[256,768]{1,0:T(8,128)(2,1)S(1)}, bf16[256,768]{1,0:T(8,128)(2,1)S(1)}, u32[]{:S(2)}, u32[]{:S(2)}) collective-permute-start(bf16[256,768]{1,0:T(8,128)(2,1)S(1)} %bitcast.51), channel_id=1, source_target_pairs={{1,0},{2,1},{3,2},{0,3},{5,4},{6,5},{7,6},{4,7},{9,8},{10,9},{11,1... | collective-permute-start | bytes 1179656 | tf_op jit(solution)/shard_map/ppermute | solution.py:20
  26.4 8.5 %collective-permute-done.4.refs_2_ = bf16[256,768]{1,0:T(8,128)(2,1)S(1)} collective-permute-done((bf16[256,768]{1,0:T(8,128)(2,1)S(1)}, bf16[256,768]{1,0:T(8,128)(2,1)S(1)}, u32[]{:S(2)}, u32[]{:S(2)}) %collective-permute-start.4) | collective-permute-done | bytes 393248 | tf_op jit(solution)/shard_map/ppermute | solution.py:20
  35.7 2.4 %collective-permute-done.5.refs_3_ = bf16[256,768]{1,0:T(8,128)(2,1)} collective-permute-done((bf16[256,768]{1,0:T(8,128)(2,1)S(1)}, bf16[256,768]{1,0:T(8,128)(2,1)}, u32[]{:S(2)}, u32[]{:S(2)}) %collective-permute-start.5) | collective-permute-done | bytes 393248 | tf_op jit(solution)/shard_map/ppermute | solution.py:20
  38.1 5.4 %all-to-all-start.1 = ((bf16[8,64,768]{2,1,0:T(8,128)(2,1)}), bf16[8,64,768]{2,1,0:T(8,128)(2,1)}, u32[]{:S(2)}, u32[]{:S(2)}) async-start(bf16[8,64,768]{2,1,0:T(8,128)(2,1)} %pad_maximum_fusion), calls=%async_computation.1 | async-start | bytes 1572864 | tf_op jit(solution)/shard_map/all_to_all | solution.py:38
  43.5 10.8 %collective-permute-done.3.refs_1_ = bf16[256,768]{1,0:T(8,128)(2,1)S(1)} collective-permute-done((bf16[256,768]{1,0:T(8,128)(2,1)S(1)}, bf16[256,768]{1,0:T(8,128)(2,1)S(1)}, u32[]{:S(2)}, u32[]{:S(2)}) %collective-permute-start.3) | collective-permute-done | bytes 393248 | tf_op jit(solution)/shard_map/ppermute | solution.py:20
  55.0 7.8 %project.2 = (bf16[8,32,384]{2,1,0:T(8,128)(2,1)}, bf16[8,32,768]{2,1,0:T(8,128)(2,1)}) custom-call(s32[5]{0:T(128)} %get-tuple-element.50.refs_0_.meta, bf16[256,768]{1,0:T(8,128)(2,1)} %copy-done.29, bf16[256,768]{1,0:T(8,128)(2,1)} %copy-done.28, bf16[256,768]{1,0:T(8,128)(2,1)} %collective-permute-done.5.refs_3_, bf16[256,768]{1,0:T(8,128)(2,1)} %bitcast.54, ...), custom_call_target="tpu_custom_call" | custom-call | tf_op jit(solution)/shard_map/project/pallas_call | solution.py:204
  65.7 4.8 %collective-permute-start.10 = (bf16[8,32,768]{2,1,0:T(8,128)(2,1)S(1)}, bf16[8,32,768]{2,1,0:T(8,128)(2,1)S(1)}, u32[]{:S(2)}, u32[]{:S(2)}) collective-permute-start(bf16[8,32,768]{2,1,0:T(8,128)(2,1)S(1)} %get-tuple-element.61), channel_id=1, source_target_pairs={{48,0},{20,32},{52,4},{24,36},{56,8},{28,40},{60,12},{0,44},{32,16... | collective-permute-start | bytes 1179656 | tf_op jit(solution)/shard_map/ppermute | solution.py:46
  70.5 2.8 %collective-permute-start.7 = (bf16[8,32,384]{2,1,0:T(8,128)(2,1)}, bf16[8,32,384]{2,1,0:T(8,128)(2,1)S(1)}, u32[]{:S(2)}, u32[]{:S(2)}) collective-permute-start(bf16[8,32,384]{2,1,0:T(8,128)(2,1)} %get-tuple-element.55.q_own), channel_id=1, source_target_pairs={{64,0},{0,64},{65,1},{1,65},{66,2},{2,66},{67,3},{3,67},{68,4},{4,... | collective-permute-start | bytes 589832 | tf_op jit(solution)/shard_map/ppermute | solution.py:20
  73.3 4.8 %collective-permute-start.9 = (bf16[3,32,768]{2,1,0:T(8,128)(2,1)S(1)}, bf16[3,32,768]{2,1,0:T(8,128)(2,1)S(1)}, u32[]{:S(2)}, u32[]{:S(2)}) collective-permute-start(bf16[3,32,768]{2,1,0:T(8,128)(2,1)S(1)} %get-tuple-element.60), channel_id=1, source_target_pairs={{32,0},{4,32},{36,4},{8,36},{40,8},{12,40},{44,12},{16,44},{48,16}... | collective-permute-start | bytes 442376 | tf_op jit(solution)/shard_map/ppermute | solution.py:46
  80.7 2.4 %attend_own.2.before = f32[8,64,512]{2,1,0:T(8,128)S(1)} custom-call(bf16[8,32,384]{2,1,0:T(8,128)(2,1)S(1)} %copy-done.13, bf16[8,32,384]{2,1,0:T(8,128)(2,1)S(1)} %collective-permute-done.7.q_other, bf16[8,32,768]{2,1,0:T(8,128)(2,1)S(1)} %copy-done.5, f32[8,1,256]{2,1,0:T(1,128)S(1)} %copy-done.21), custom_call_target="tpu_custom_call" | custom-call | tf_op jit(solution)/shard_map/attend_own/pallas_call | solution.py:282
  88.7 3.2 %spread.2 = (f32[256,768]{1,0:T(8,128)S(1)}, bf16[256,768]{1,0:T(8,128)(2,1)S(1)}, bf16[256,768]{1,0:T(8,128)(2,1)S(1)}, bf16[256,768]{1,0:T(8,128)(2,1)S(1)}) custom-call(s32[5]{0:T(128)S(1)} %copy-done.24, f32[8,32,512]{2,1,0:T(8,128)S(1)} %get-tuple-element.64.part_a, f32[8,32,512]{2,1,0:T(8,128)S(1)} %collective-permute-done.11.part_b, ...), custom_call_target="tpu_custom_call" | custom-call | tf_op jit(solution)/shard_map/spread/pallas_call | solution.py:380
  94.9 9.7 %collective-permute-done.13.from_across = bf16[256,768]{1,0:T(8,128)(2,1)S(1)} collective-permute-done((bf16[256,768]{1,0:T(8,128)(2,1)S(1)}, bf16[256,768]{1,0:T(8,128)(2,1)S(1)}, u32[]{:S(2)}, u32[]{:S(2)}) %collective-permute-start.13) | collective-permute-done | bytes 393248 | tf_op jit(solution)/shard_map/ppermute | solution.py:20
  104.6 8.3 %collective-permute-done.14.from_prev = bf16[256,768]{1,0:T(8,128)(2,1)S(1)} collective-permute-done((bf16[256,768]{1,0:T(8,128)(2,1)S(1)}, bf16[256,768]{1,0:T(8,128)(2,1)S(1)}, u32[]{:S(2)}, u32[]{:S(2)}) %collective-permute-start.14) | collective-permute-done | bytes 393248 | tf_op jit(solution)/shard_map/ppermute | solution.py:20
  117.3 16.7 %collective-permute-done.17.refs_2_ = bf16[256,768]{1,0:T(8,128)(2,1)S(1)} collective-permute-done((bf16[256,768]{1,0:T(8,128)(2,1)S(1)}, bf16[256,768]{1,0:T(8,128)(2,1)S(1)}, u32[]{:S(2)}, u32[]{:S(2)}) %collective-permute-start.17) | collective-permute-done | bytes 393248 | tf_op jit(solution)/shard_map/ppermute | solution.py:20
  135.5 5.3 %all-to-all-start.2 = ((bf16[8,64,768]{2,1,0:T(8,128)(2,1)}), bf16[8,64,768]{2,1,0:T(8,128)(2,1)}, u32[]{:S(2)}, u32[]{:S(2)}) async-start(bf16[8,64,768]{2,1,0:T(8,128)(2,1)} %pad_maximum_fusion.1), calls=%async_computation.2 | async-start | bytes 1572864 | tf_op jit(solution)/shard_map/all_to_all | solution.py:38
  140.8 8.7 %project.3 = (bf16[8,32,384]{2,1,0:T(8,128)(2,1)}, bf16[8,32,768]{2,1,0:T(8,128)(2,1)}, bf16[3,32,768]{2,1,0:T(8,128)(2,1)}, bf16[3,32,768]{2,1,0:T(8,128)(2,1)}, bf16[8,32,768]{2,1,0:T(8,128)(2,1)}) custom-call(s32[5]{0:T(128)} %get-tuple-element.49.refs_0_.meta, bf16[256,768]{1,0:T(8,128)(2,1)} %collective-permute-done.16.refs_1_, ...), custom_call_target="tpu_custom_call" | custom-call | tf_op jit(solution)/shard_map/project/pallas_call | solution.py:204
  149.5 6.8 %collective-permute-start.23 = (bf16[8,32,768]{2,1,0:T(8,128)(2,1)}, bf16[8,32,768]{2,1,0:T(8,128)(2,1)}, u32[]{:S(2)}, u32[]{:S(2)}) collective-permute-start(bf16[8,32,768]{2,1,0:T(8,128)(2,1)} %get-tuple-element.81), channel_id=1, source_target_pairs={{48,0},{20,32},{52,4},{24,36},{56,8},{28,40},{60,12},{0,44},{32,16... | collective-permute-start | bytes 1179656 | tf_op jit(solution)/shard_map/ppermute | solution.py:46
  157.6 3.0 %collective-permute-start.22 = (bf16[3,32,768]{2,1,0:T(8,128)(2,1)}, bf16[3,32,768]{2,1,0:T(8,128)(2,1)}, u32[]{:S(2)}, u32[]{:S(2)}) collective-permute-start(bf16[3,32,768]{2,1,0:T(8,128)(2,1)} %get-tuple-element.79), channel_id=1, source_target_pairs={{60,0},{0,32},{32,4},{4,36},{36,8},{8,40},{40,12},{12,44},{44,16},... | collective-permute-start | bytes 442376 | tf_op jit(solution)/shard_map/ppermute | solution.py:46
  162.5 2.4 %attend_own.3.before = f32[8,64,512]{2,1,0:T(8,128)S(1)} custom-call(bf16[8,32,384]{2,1,0:T(8,128)(2,1)S(1)} %copy-done.15, bf16[8,32,384]{2,1,0:T(8,128)(2,1)S(1)} %collective-permute-done.21.q_other, bf16[8,32,768]{2,1,0:T(8,128)(2,1)S(1)} %copy-done.9, f32[8,1,256]{2,1,0:T(1,128)S(1)} %copy-done.20), custom_call_target="tpu_custom_call" | custom-call | tf_op jit(solution)/shard_map/attend_own/pallas_call | solution.py:282
  171.4 3.3 %attend_rest.3 = (f32[8,32,512]{2,1,0:T(8,128)S(1)}, f32[8,32,512]{2,1,0:T(8,128)S(1)}) custom-call(bf16[8,32,384]{2,1,0:T(8,128)(2,1)S(1)} %copy-done.16, bf16[8,32,384]{2,1,0:T(8,128)(2,1)S(1)} %collective-permute-done.21.q_other, bf16[3,32,768]{2,1,0:T(8,128)(2,1)} %collective-permute-done.22.below, bf16[3,32,768]{2,1,0:T(8,128)(2,1)S(1)} %copy-done.18, ...), custom_call_target="tpu_custom_call" | custom-call | tf_op jit(solution)/shard_map/attend_rest/pallas_call | solution.py:327
  183.4 7.8 %collective-permute-done.25.from_across = bf16[256,768]{1,0:T(8,128)(2,1)S(1)} collective-permute-done((bf16[256,768]{1,0:T(8,128)(2,1)S(1)}, bf16[256,768]{1,0:T(8,128)(2,1)S(1)}, u32[]{:S(2)}, u32[]{:S(2)}) %collective-permute-start.25) | collective-permute-done | bytes 393248 | tf_op jit(solution)/shard_map/ppermute | solution.py:20
  191.2 10.1 %collective-permute-done.26.from_prev = bf16[256,768]{1,0:T(8,128)(2,1)S(1)} collective-permute-done((bf16[256,768]{1,0:T(8,128)(2,1)S(1)}, bf16[256,768]{1,0:T(8,128)(2,1)S(1)}, u32[]{:S(2)}, u32[]{:S(2)}) %collective-permute-start.26) | collective-permute-done | bytes 393248 | tf_op jit(solution)/shard_map/ppermute | solution.py:20
  204.2 17.4 %all_to_all.20.late = bf16[8,64,768]{2,1,0:T(8,128)(2,1)S(1)} all-to-all(bf16[8,64,768]{2,1,0:T(8,128)(2,1)S(1)} %pad_maximum_fusion.2), channel_id=1, replica_groups={{0,4,8,12,16,20,24,28},{32,36,40,44,48,52,56,60},{1,5,9,13,17,21,25,29}..., dimensions={0} | all-to-all | bytes 1572864 | tf_op jit(solution)/shard_map/all_to_all | solution.py:38
  (148 shorter events, 61.9 us)
Async XLA Ops:
  0.7 53.6 %collective-permute-start.6 = (bf16[3,3072,384]{2,1,0:T(8,128)(2,1)}, bf16[3,3072,384]{2,1,0:T(8,128)(2,1)}, u32[]{:S(2)}, u32[]{:S(2)}) collective-permute-start(bf16[3,3072,384]{2,1,0:T(8,128)(2,1)} %bitcast.58), channel_id=1, source_target_pairs={{64,0},{0,64},{65,1},{1,65},{66,2},{2,66},{67,3},{3,67},{68,4},{4,... | collective-permute-start | bytes 21233672 | tf_op jit(solution)/shard_map/ppermute | solution.py:20
  5.3 10.1 %collective-permute-start.1 = (f32[8,1,384]{2,1,0:T(1,128)}, f32[8,1,384]{2,1,0:T(1,128)}, u32[]{:S(2)}, u32[]{:S(2)}) collective-permute-start(f32[8,1,384]{2,1,0:T(1,128)} %broadcast_in_dim.36), channel_id=1, source_target_pairs={{64,0},{0,64},{65,1},{1,65},{66,2},{2,66},{67,3},{3,67},{68,4},{4,... | collective-permute-start | bytes 36872 | tf_op jit(solution)/shard_map/ppermute | solution.py:20
  6.2 15.8 %all-to-all-start = ((bf16[8,32,768]{2,1,0:T(8,128)(2,1)}), bf16[8,32,768]{2,1,0:T(8,128)(2,1)S(1)}, u32[]{:S(2)}, u32[]{:S(2)}) async-start(bf16[8,32,768]{2,1,0:T(8,128)(2,1)} %constant_dynamic-slice_fusion.2), calls=%async_computation | async-start | bytes 786432 | tf_op jit(solution)/shard_map/all_to_all | solution.py:38
  22.1 65.1 %collective-permute-start.12 = (bf16[384,3072]{1,0:T(8,128)(2,1)S(1)}, bf16[384,3072]{1,0:T(8,128)(2,1)}, u32[]{:S(2)}, u32[]{:S(2)}) collective-permute-start(bf16[384,3072]{1,0:T(8,128)(2,1)S(1)} %bitcast.46), channel_id=1, source_target_pairs={{64,0},{0,64},{65,1},{1,65},{66,2},{2,66},{67,3},{3,67},{68,4},{4,... | collective-permute-start | bytes 7077896 | tf_op jit(solution)/shard_map/ppermute | solution.py:20
  22.6 12.2 %collective-permute-start.4 = (bf16[256,768]{1,0:T(8,128)(2,1)S(1)}, bf16[256,768]{1,0:T(8,128)(2,1)S(1)}, u32[]{:S(2)}, u32[]{:S(2)}) collective-permute-start(bf16[256,768]{1,0:T(8,128)(2,1)S(1)} %bitcast.51), channel_id=1, source_target_pairs={{1,0},{2,1},{3,2},{0,3},{5,4},{6,5},{7,6},{4,7},{9,8},{10,9},{11,1... | collective-permute-start | bytes 1179656 | tf_op jit(solution)/shard_map/ppermute | solution.py:20
  26.4 11.7 %collective-permute-start.5 = (bf16[256,768]{1,0:T(8,128)(2,1)S(1)}, bf16[256,768]{1,0:T(8,128)(2,1)}, u32[]{:S(2)}, u32[]{:S(2)}) collective-permute-start(bf16[256,768]{1,0:T(8,128)(2,1)S(1)} %bitcast.52), channel_id=1, source_target_pairs={{3,0},{0,1},{1,2},{2,3},{7,4},{4,5},{5,6},{6,7},{11,8},{8,9},{9,10... | collective-permute-start | bytes 1179656 | tf_op jit(solution)/shard_map/ppermute | solution.py:20
  38.1 24.7 %all-to-all-start.1 = ((bf16[8,64,768]{2,1,0:T(8,128)(2,1)}), bf16[8,64,768]{2,1,0:T(8,128)(2,1)}, u32[]{:S(2)}, u32[]{:S(2)}) async-start(bf16[8,64,768]{2,1,0:T(8,128)(2,1)} %pad_maximum_fusion), calls=%async_computation.1 | async-start | bytes 1572864 | tf_op jit(solution)/shard_map/all_to_all | solution.py:38
  43.5 10.8 %collective-permute-start.3 = (bf16[256,768]{1,0:T(8,128)(2,1)S(1)}, bf16[256,768]{1,0:T(8,128)(2,1)S(1)}, u32[]{:S(2)}, u32[]{:S(2)}) collective-permute-start(bf16[256,768]{1,0:T(8,128)(2,1)S(1)} %bitcast.53), channel_id=1, source_target_pairs={{2,0},{3,1},{0,2},{1,3},{6,4},{7,5},{4,6},{5,7},{10,8},{11,9},{8,1... | collective-permute-start | bytes 1179656 | tf_op jit(solution)/shard_map/ppermute | solution.py:20
  65.7 17.6 %collective-permute-start.10 = (bf16[8,32,768]{2,1,0:T(8,128)(2,1)S(1)}, bf16[8,32,768]{2,1,0:T(8,128)(2,1)S(1)}, u32[]{:S(2)}, u32[]{:S(2)}) collective-permute-start(bf16[8,32,768]{2,1,0:T(8,128)(2,1)S(1)} %get-tuple-element.61), channel_id=1, source_target_pairs={{48,0},{20,32},{52,4},{24,36},{56,8},{28,40},{60,12},{0,44},{32,16... | collective-permute-start | bytes 1179656 | tf_op jit(solution)/shard_map/ppermute | solution.py:46
  73.3 10.0 %collective-permute-start.8 = (bf16[3,32,768]{2,1,0:T(8,128)(2,1)S(1)}, bf16[3,32,768]{2,1,0:T(8,128)(2,1)S(1)}, u32[]{:S(2)}, u32[]{:S(2)}) collective-permute-start(bf16[3,32,768]{2,1,0:T(8,128)(2,1)S(1)} %get-tuple-element.59), channel_id=1, source_target_pairs={{60,0},{0,32},{32,4},{4,36},{36,8},{8,40},{40,12},{12,44},{44,16},... | collective-permute-start | bytes 442376 | tf_op jit(solution)/shard_map/ppermute | solution.py:46
  73.3 10.0 %collective-permute-start.9 = (bf16[3,32,768]{2,1,0:T(8,128)(2,1)S(1)}, bf16[3,32,768]{2,1,0:T(8,128)(2,1)S(1)}, u32[]{:S(2)}, u32[]{:S(2)}) collective-permute-start(bf16[3,32,768]{2,1,0:T(8,128)(2,1)S(1)} %get-tuple-element.60), channel_id=1, source_target_pairs={{32,0},{4,32},{36,4},{8,36},{40,8},{12,40},{44,12},{16,44},{48,16}... | collective-permute-start | bytes 442376 | tf_op jit(solution)/shard_map/ppermute | solution.py:46
  91.9 12.7 %collective-permute-start.13 = (bf16[256,768]{1,0:T(8,128)(2,1)S(1)}, bf16[256,768]{1,0:T(8,128)(2,1)S(1)}, u32[]{:S(2)}, u32[]{:S(2)}) collective-permute-start(bf16[256,768]{1,0:T(8,128)(2,1)S(1)} %get-tuple-element.67), channel_id=1, source_target_pairs={{2,0},{3,1},{0,2},{1,3},{6,4},{7,5},{4,6},{5,7},{10,8},{11,9},{8,1... | collective-permute-start | bytes 1179656 | tf_op jit(solution)/shard_map/ppermute | solution.py:20
  92.2 20.7 %collective-permute-start.14 = (bf16[256,768]{1,0:T(8,128)(2,1)S(1)}, bf16[256,768]{1,0:T(8,128)(2,1)S(1)}, u32[]{:S(2)}, u32[]{:S(2)}) collective-permute-start(bf16[256,768]{1,0:T(8,128)(2,1)S(1)} %get-tuple-element.68), channel_id=1, source_target_pairs={{3,0},{0,1},{1,2},{2,3},{7,4},{4,5},{5,6},{6,7},{11,8},{8,9},{9,10... | collective-permute-start | bytes 1179656 | tf_op jit(solution)/shard_map/ppermute | solution.py:20
  93.9 19.0 %collective-permute-start.15 = (bf16[256,768]{1,0:T(8,128)(2,1)S(1)}, bf16[256,768]{1,0:T(8,128)(2,1)S(1)}, u32[]{:S(2)}, u32[]{:S(2)}) collective-permute-start(bf16[256,768]{1,0:T(8,128)(2,1)S(1)} %get-tuple-element.69), channel_id=1, source_target_pairs={{1,0},{2,1},{3,2},{0,3},{5,4},{6,5},{7,6},{4,7},{9,8},{10,9},{11,1... | collective-permute-start | bytes 1179656 | tf_op jit(solution)/shard_map/ppermute | solution.py:20
  114.4 26.4 %collective-permute-start.16 = (bf16[256,768]{1,0:T(8,128)(2,1)S(1)}, bf16[256,768]{1,0:T(8,128)(2,1)}, u32[]{:S(2)}, u32[]{:S(2)}) collective-permute-start(bf16[256,768]{1,0:T(8,128)(2,1)S(1)} %finish.2.refs_4_.hidden), channel_id=1, source_target_pairs={{2,0},{3,1},{0,2},{1,3},{6,4},{7,5},{4,6},{5,7},{10,8},{11,9},{8,1... | collective-permute-start | bytes 1179656 | tf_op jit(solution)/shard_map/ppermute | solution.py:20
  114.6 19.4 %collective-permute-start.17 = (bf16[256,768]{1,0:T(8,128)(2,1)S(1)}, bf16[256,768]{1,0:T(8,128)(2,1)S(1)}, u32[]{:S(2)}, u32[]{:S(2)}) collective-permute-start(bf16[256,768]{1,0:T(8,128)(2,1)S(1)} %finish.2.refs_4_.hidden), channel_id=1, source_target_pairs={{1,0},{2,1},{3,2},{0,3},{5,4},{6,5},{7,6},{4,7},{9,8},{10,9},{11,1... | collective-permute-start | bytes 1179656 | tf_op jit(solution)/shard_map/ppermute | solution.py:20
  116.2 19.3 %collective-permute-start.18 = (bf16[256,768]{1,0:T(8,128)(2,1)S(1)}, bf16[256,768]{1,0:T(8,128)(2,1)}, u32[]{:S(2)}, u32[]{:S(2)}) collective-permute-start(bf16[256,768]{1,0:T(8,128)(2,1)S(1)} %finish.2.refs_4_.hidden), channel_id=1, source_target_pairs={{3,0},{0,1},{1,2},{2,3},{7,4},{4,5},{5,6},{6,7},{11,8},{8,9},{9,10... | collective-permute-start | bytes 1179656 | tf_op jit(solution)/shard_map/ppermute | solution.py:20
  135.5 32.3 %all-to-all-start.2 = ((bf16[8,64,768]{2,1,0:T(8,128)(2,1)}), bf16[8,64,768]{2,1,0:T(8,128)(2,1)}, u32[]{:S(2)}, u32[]{:S(2)}) async-start(bf16[8,64,768]{2,1,0:T(8,128)(2,1)} %pad_maximum_fusion.1), calls=%async_computation.2 | async-start | bytes 1572864 | tf_op jit(solution)/shard_map/all_to_all | solution.py:38
  149.5 19.7 %collective-permute-start.23 = (bf16[8,32,768]{2,1,0:T(8,128)(2,1)}, bf16[8,32,768]{2,1,0:T(8,128)(2,1)}, u32[]{:S(2)}, u32[]{:S(2)}) collective-permute-start(bf16[8,32,768]{2,1,0:T(8,128)(2,1)} %get-tuple-element.81), channel_id=1, source_target_pairs={{48,0},{20,32},{52,4},{24,36},{56,8},{28,40},{60,12},{0,44},{32,16... | collective-permute-start | bytes 1179656 | tf_op jit(solution)/shard_map/ppermute | solution.py:46
  157.6 9.5 %collective-permute-start.19 = (bf16[3,32,768]{2,1,0:T(8,128)(2,1)}, bf16[3,32,768]{2,1,0:T(8,128)(2,1)S(1)}, u32[]{:S(2)}, u32[]{:S(2)}) collective-permute-start(bf16[3,32,768]{2,1,0:T(8,128)(2,1)} %get-tuple-element.75), channel_id=1, source_target_pairs={{32,0},{4,32},{36,4},{8,36},{40,8},{12,40},{44,12},{16,44},{48,16}... | collective-permute-start | bytes 442376 | tf_op jit(solution)/shard_map/ppermute | solution.py:46
  157.6 10.4 %collective-permute-start.22 = (bf16[3,32,768]{2,1,0:T(8,128)(2,1)}, bf16[3,32,768]{2,1,0:T(8,128)(2,1)}, u32[]{:S(2)}, u32[]{:S(2)}) collective-permute-start(bf16[3,32,768]{2,1,0:T(8,128)(2,1)} %get-tuple-element.79), channel_id=1, source_target_pairs={{60,0},{0,32},{32,4},{4,36},{36,8},{8,40},{40,12},{12,44},{44,16},... | collective-permute-start | bytes 442376 | tf_op jit(solution)/shard_map/ppermute | solution.py:46
  180.2 11.0 %collective-permute-start.25 = (bf16[256,768]{1,0:T(8,128)(2,1)S(1)}, bf16[256,768]{1,0:T(8,128)(2,1)S(1)}, u32[]{:S(2)}, u32[]{:S(2)}) collective-permute-start(bf16[256,768]{1,0:T(8,128)(2,1)S(1)} %get-tuple-element.87), channel_id=1, source_target_pairs={{2,0},{3,1},{0,2},{1,3},{6,4},{7,5},{4,6},{5,7},{10,8},{11,9},{8,1... | collective-permute-start | bytes 1179656 | tf_op jit(solution)/shard_map/ppermute | solution.py:20
  180.8 20.5 %collective-permute-start.26 = (bf16[256,768]{1,0:T(8,128)(2,1)S(1)}, bf16[256,768]{1,0:T(8,128)(2,1)S(1)}, u32[]{:S(2)}, u32[]{:S(2)}) collective-permute-start(bf16[256,768]{1,0:T(8,128)(2,1)S(1)} %get-tuple-element.88), channel_id=1, source_target_pairs={{3,0},{0,1},{1,2},{2,3},{7,4},{4,5},{5,6},{6,7},{11,8},{8,9},{9,10... | collective-permute-start | bytes 1179656 | tf_op jit(solution)/shard_map/ppermute | solution.py:20
  182.9 18.4 %collective-permute-start.27 = (bf16[256,768]{1,0:T(8,128)(2,1)S(1)}, bf16[256,768]{1,0:T(8,128)(2,1)S(1)}, u32[]{:S(2)}, u32[]{:S(2)}) collective-permute-start(bf16[256,768]{1,0:T(8,128)(2,1)S(1)} %get-tuple-element.89), channel_id=1, source_target_pairs={{1,0},{2,1},{3,2},{0,3},{5,4},{6,5},{7,6},{4,7},{9,8},{10,9},{11,1... | collective-permute-start | bytes 1179656 | tf_op jit(solution)/shard_map/ppermute | solution.py:20
  (40 other events, 312.9 us)

commit v6 on v5

--- a/solution.py
+++ b/solution.py
@@ -46,38 +46,43 @@
     return lax.ppermute(block, "seq", route)
 
 
-def collect_kernel(core, early, late, handed, cache):
+def collect_kernel(core, early, own, got, handed, cache):
+    patches, rows, _ = own.shape
     cols = cache.shape[-1]
-
-    def collect(features, keys):
-        handed[...] = features[...]
-        cache[0] = keys[:, :, :cols]
-        cache[1] = keys[:, :, cols:]
 
     @pl.when(core[0] == 0)
     def _():
-        collect(late, early)
+        handed[:, :rows] = own[...]
+        handed[:, rows:] = got[...]
+        cache[0] = early[:, : 2 * rows, :cols]
+        cache[1] = early[:, : 2 * rows, cols:]
 
     @pl.when(core[0] == 1)
     def _():
-        collect(early, late)
-
-
-def collect(core, early, late):
-    patches, rows, cols = early.shape
+        handed[...] = early[:, : 2 * rows]
+        for half in range(2):
+            cut = slice(half * cols, (half + 1) * cols)
+            cache[half, :, :rows] = got[:, :, cut]
+            cache[half, :, rows:] = own[:, :, cut]
+
+
+def collect(core, early, own, got):
+    patches, rows, cols = own.shape
     return pl.pallas_call(
         collect_kernel,
-        in_specs=[SCALARS] + [ON_CHIP] * 2,
+        in_specs=[SCALARS] + [ON_CHIP] * 3,
         out_specs=[ON_CHIP] * 2,
-        out_shape=[struct(early.shape), struct((2, patches, rows, cols // 2))],
+        out_shape=[
+            struct((patches, 2 * rows, cols)),
+            struct((2, patches, 2 * rows, cols // 2)),
+        ],
         compiler_params=params(8),
         name="collect",
-    )(core, early, late)
+    )(core, early, own, got)
 
 
 def choose(meta, kv, stale, outs):
-    tiles, rows, _ = kv.shape
-    old = pl.ds(pl.multiple_of((1 - meta[1]) * rows, rows), rows)
+    tiles = kv.shape[0]
     for place, out in enumerate(outs):
         first = tiles - REACH if place == 1 else 0
         cut = slice(first, first + out.shape[0])
@@ -88,11 +93,7 @@
 
         @pl.when(meta[2 + place] == 0)
         def _():
-            out[...] = stale[cut, old]
-
-
-def choose_kernel(meta, kv, stale, lo_out, hi_out, far_out):
-    choose(meta, kv, stale, (lo_out, hi_out, far_out))
+            out[...] = stale[cut]
 
 
 def payloads(kv_shape):
@@ -100,25 +101,11 @@
     return [edge, edge, struct(kv_shape)]
 
 
-def choose_alone(meta, kv, stale):
-    return pl.pallas_call(
-        choose_kernel,
-        in_specs=[SCALARS] + [ON_CHIP] * 2,
-        out_specs=[ON_CHIP] * 3,
-        out_shape=payloads(kv.shape),
-        compiler_params=params(8),
-        name="choose",
-    )(meta, kv, stale)
-
-
-def project_kernel(meta, *refs, with_stale):
+def project_kernel(meta, *refs):
     blocks = refs[:4]
     shift, scale, gain, w_own, w_other = refs[4:9]
     refs = refs[9:]
-    if with_stale:
-        stale, q_out, kv_out, *outs = refs[:-4]
-    else:
-        q_out, kv_out = refs[:-4]
+    stale, q_out, kv_out, *outs = refs[:-4]
     xs, modded, weights, sems = refs[-4:]
     _, rows, cols = xs.shape
     tiles, rows_tile, kv_cols = kv_out.shape
@@ -183,31 +170,23 @@
                 q_out[:, :, cut] = vec
             else:
                 kv_out[:, :, cut] = vec
-    if with_stale:
-        choose(meta, kv_out, stale, outs)
-
-
-def project(meta, blocks, shift, scale, gain, w_own, w_other, stale, kv_shape):
+    choose(meta, kv_out, stale, outs)
+
+
+def project(meta, blocks, shift, scale, gain, w_own, w_other, stale):
     rows, cols = blocks[0].shape
-    tiles, rows_tile, kv_cols = kv_shape
+    tiles, rows_tile, kv_cols = stale.shape
     heads_cols = kv_cols // 2
     parts = shift.shape[0]
-    shapes = [struct((tiles, rows_tile, heads_cols)), struct(kv_shape)]
-    extra = []
-    if stale is not None:
-        shapes += payloads(kv_shape)
-        extra = [stale]
-
-    def kernel(*refs):
-        project_kernel(*refs, with_stale=stale is not None)
-
+    shapes = [struct((tiles, rows_tile, heads_cols)), struct(stale.shape)]
+    shapes += payloads(stale.shape)
     return pl.pallas_call(
-        kernel,
+        project_kernel,
         in_specs=[SCALARS]
         + [ANYWHERE] * len(blocks)
         + [ON_CHIP] * 3
         + [ANYWHERE] * 2
-        + [ON_CHIP] * len(extra),
+        + [ON_CHIP],
         out_specs=[ON_CHIP] * len(shapes),
         out_shape=shapes,
         scratch_shapes=[
@@ -216,9 +195,9 @@
             pltpu.VMEM((3, parts * cols, heads_cols), jnp.bfloat16),
             pltpu.SemaphoreType.DMA((2 * parts,)),
         ],
-        compiler_params=params(56),
+        compiler_params=params(52),
         name="project",
-    )(meta, *blocks, shift, scale, gain, w_own, w_other, *extra)
+    )(meta, *blocks, shift, scale, gain, w_own, w_other, stale)
 
 
 def soften(queries, keys, values, times, floors):
@@ -461,13 +440,9 @@
     w_other = shifted(w_own, "segment", 1)
     small_own = jnp.concatenate([modulation[0].reshape(-1), qk_gain[0].reshape(-1)])
     small_other = shifted(small_own, "segment", 1)
-    stale = after(stale_cache[0], mine)
-    stale = jnp.concatenate([stale[0], stale[1]], axis=-1)
-    stale_own = lax.dynamic_slice_in_dim(stale, core * rows_core, rows_core, 1)
-    stale_other = shifted(
-        lax.dynamic_slice_in_dim(stale, (1 - core) * rows_core, rows_core, 1), "segment", 1
-    )
-    stale = jnp.concatenate([stale_own, stale_other], axis=1)
+    stale_all, kv_tiles, tile_counts = after((stale_cache[0], kv_tiles, tile_counts), mine)
+    stale_all = exchanged(jnp.concatenate([stale_all[0], stale_all[1]], axis=-1))
+    kv_tiles, tile_counts = after((kv_tiles, tile_counts), small_other)
     turns = jnp.arange(patches, dtype=jnp.int32)
     asked = jnp.stack([chip, chip - 1, chip + 1, chip - seq_size // 2 - 1]) % seq_size // share
     ranks = jnp.sum(jnp.where(patch_order[None] == asked[:, None], turns[None], 0), axis=-1)
@@ -487,18 +462,21 @@
         given.append(
             (meta, modul[0], modul[1], modul[2], gain, multiple[..., :256], multiple[..., 256:])
         )
-    hidden, given, stale, w_out = lax.optimization_barrier((hidden, given, stale, w_out))
+    hidden, given, stale_all, w_out = lax.optimization_barrier(
+        (hidden, given, stale_all, w_out)
+    )
+    stale_own = lax.dynamic_slice_in_dim(stale_all, core * rows_core, rows_core, 1)
+    stale_other = shifted(
+        lax.dynamic_slice_in_dim(stale_all, (1 - core) * rows_core, rows_core, 1), "segment", 1
+    )
     wo_own = w_out[0]
     wo_other = shifted(wo_own, "segment", 1)
 
     for section in range(2):
         meta, shift, scale, gates, gain, times_own, times_rest = given[section]
         blocks = gather_features(hidden)
-        if section == 0:
-            stale = exchanged(after(stale, blocks[1], blocks[2]))
-        else:
-            early = exchanged(after(early, blocks[1], blocks[2]))
-        q_own, kv, *going = project(
+        stale = jnp.where(core == section, stale_own, stale_other)
+        q_own, kv, to_below, to_above, to_far = project(
             meta,
             blocks,
             shift,
@@ -506,18 +484,12 @@
             gain,
             w_own,
             w_other,
-            stale if section > 0 else None,
-            stale_own.shape,
-        )
-        if section == 0:
-            going = choose_alone(meta, kv, stale)
-        to_below, to_above, to_far = going
+            stale,
+        )
         far = along_ring(to_far, seq_size // 2 + 1, patches)
         above = along_ring(to_below, 1, patches)
         below = along_ring(to_above, -1, patches)
         q_other = shifted(q_own, "segment", 1)
-        if section > 0:
-            above, early = lax.optimization_barrier((above, early))
         before = attend_own(q_own, q_other, kv, times_own)
         part_own, part_other = attend_rest(
             q_own, q_other, below, above, far, times_rest, before
@@ -529,19 +501,23 @@
         from_across = shifted(to_across, "tp", 2)
         from_prev = shifted(to_next, "tp", 1)
         from_next = shifted(to_prev, "tp", -1)
+        if section > 0:
+            early = jnp.concatenate([early, kv], axis=1)
+            early = exchanged(after(early, from_prev))
         hidden = finish(meta, from_across, from_prev, from_next, keep, hidden, gates)
-
         features = hidden.reshape(patches, rows_core, part_cols)
-        pair = (kv, features) if section == 0 else (features, kv)
-        got = shifted(jnp.where(core == 0, pair[1], pair[0]), "segment", 1)
-        own = jnp.where(core == 0, pair[0], pair[1])
-        halves = [jnp.where(core == place, own, got) for place in range(2)]
         if section == 0:
+            got = shifted(jnp.where(core == 0, features, kv), "segment", 1)
+            own = jnp.where(core == 0, kv, features)
+            halves = [jnp.where(core == place, own, got) for place in range(2)]
             early = jnp.concatenate(halves, axis=1)
         else:
-            late = exchanged(jnp.concatenate(halves, axis=1))
-
-    handed, new_cache = collect(core.astype(jnp.int32)[None], early, late)
+            features = exchanged(features)
+
+    keys = early[:, patch_rows:]
+    got = shifted(jnp.where(core == 0, keys, features), "segment", 1)
+    own = jnp.where(core == 0, features, keys)
+    handed, new_cache = collect(core.astype(jnp.int32)[None], early, own, got)
     return (handed[None], new_cache[None])
 
 

time: 227 us -> 232 us (1.022)
  waiting for transfers between devices: 82.1 us -> 95.1 us
  local copies, waits for them, and re-layouts: 18.3 us -> 9.37 us
  starting transfers between devices: 58.6 us -> 63.5 us
  Pallas kernels: 37.7 us -> 33.4 us
    all_to_all x3, waiting for transfers between devices: 0.01 us -> 15.6 us  [exchanged(): return lax.all_to_all(tiles, 'seq', 0, 0, axis_index_groups=groups)]
    ppermute x23, waiting for transfers between devices: 79.3 us -> 68.2 us  [shifted(): return lax.ppermute(block, axis, route)]
    unnamed x65 -> x62, local copies, waits for them, and re-layouts: 12.3 us -> 1.73 us
    ppermute x23, starting transfers between devices: 23.4 us -> 33 us  [shifted(): return lax.ppermute(block, axis, route)]
    ppermute x6, waiting for transfers between devices: 2.73 us -> 11.3 us  [along_ring(): return lax.ppermute(block, 'seq', route)]
    pallas_call x4 -> x3, Pallas kernels: 20.2 us -> 16.3 us  [the longest x2 15 us: project(): pl.pallas_call(project_kernel, in_specs=[SCALARS] + [ANYWHERE] * len(bloc...]
    concatenate x4 -> x2, other arithmetic: 4 us -> 1.03 us  [the longest x1 0.95 us: local(): jnp.concatenate([stale_all[0], stale_all[1]], axis=-1)]
    ppermute x6, starting transfers between devices: 19.4 us -> 16.7 us  [along_ring(): return lax.ppermute(block, 'seq', route)]
  transfers between devices with their start and end apart: 32 -> 32, of which waited for: 16 -> 22; matrix products, arithmetic and copies ran while one was open for 7% -> 8% of each run, Pallas kernels for 11% -> 7%
where the time goes in v6:
time: 232 us; the launch traced here: 229 us
  waiting for transfers between devices  95.1 us (41%)
  starting transfers between devices  63.5 us (27%)
  Pallas kernels  33.4 us (14%)
  blocking collectives  16.5 us (7%)
  other arithmetic  10 us (4%)
  local copies, waits for them, and re-layouts  9.37 us (4%)
    ppermute x23, waiting for transfers between devices, shifted(): return lax.ppermute(block, axis, route)  68.2 us
    ppermute x23, starting transfers between devices, shifted(): return lax.ppermute(block, axis, route)  33 us
    ppermute x6, starting transfers between devices, along_ring(): return lax.ppermute(block, 'seq', route)  16.7 us
    all_to_all x1, blocking collectives, exchanged(): return lax.all_to_all(tiles, 'seq', 0, 0, axis_index_groups=groups)  16.5 us
    all_to_all x3, waiting for transfers between devices, exchanged(): return lax.all_to_all(tiles, 'seq', 0, 0, axis_index_groups=groups)  15.6 us
    pallas_call x2, Pallas kernels, project(): pl.pallas_call(project_kernel, in_specs=[SCALARS] + [ANYWHERE] * len(bloc...  15 us
    all_to_all x3, starting transfers between devices, exchanged(): return lax.all_to_all(tiles, 'seq', 0, 0, axis_index_groups=groups)  13.8 us
    ppermute x6, waiting for transfers between devices, along_ring(): return lax.ppermute(block, 'seq', route)  11.3 us
  transfers between devices with their start and end apart: 32, of which 22 were waited for; matrix products, arithmetic and copies ran while one was open for 8% of the time, Pallas kernels for 7%

profile of v6, /device:TPU:1, one launch (start us, length us, event | category | flops | bytes accessed | tf_op | source)
XLA Modules:
  0.0 228.9 jit_solution(9330005120191718587)
XLA Ops:
  4.5 5.1 %all-to-all-start = ((bf16[8,32,768]{2,1,0:T(8,128)(2,1)}), bf16[8,32,768]{2,1,0:T(8,128)(2,1)S(1)}, u32[]{:S(2)}, u32[]{:S(2)}) async-start(bf16[8,32,768]{2,1,0:T(8,128)(2,1)} %constant_dynamic-slice_fusion.2), calls=%async_computation | async-start | bytes 786432 | tf_op jit(solution)/shard_map/all_to_all | solution.py:38
  18.8 5.1 %all-to-all-start.1 = ((bf16[8,64,768]{2,1,0:T(8,128)(2,1)}), bf16[8,64,768]{2,1,0:T(8,128)(2,1)}, u32[]{:S(2)}, u32[]{:S(2)}) async-start(bf16[8,64,768]{2,1,0:T(8,128)(2,1)} %pad_maximum_fusion.1), calls=%async_computation.1 | async-start | bytes 1572864 | tf_op jit(solution)/shard_map/all_to_all | solution.py:38
  28.5 8.6 %all-to-all-done.1 = bf16[8,64,768]{2,1,0:T(8,128)(2,1)} async-done(((bf16[8,64,768]{2,1,0:T(8,128)(2,1)}), bf16[8,64,768]{2,1,0:T(8,128)(2,1)}, u32[]{:S(2)}, u32[]{:S(2)}) %all-to-all-start.1) | async-done | bytes 786464 | tf_op jit(solution)/shard_map/all_to_all | solution.py:38
  39.0 3.7 %collective-permute-start.2 = (bf16[256,768]{1,0:T(8,128)(2,1)S(1)}, bf16[256,768]{1,0:T(8,128)(2,1)S(1)}, u32[]{:S(2)}, u32[]{:S(2)}) collective-permute-start(bf16[256,768]{1,0:T(8,128)(2,1)S(1)} %bitcast.49), channel_id=1, source_target_pairs={{2,0},{3,1},{0,2},{1,3},{6,4},{7,5},{4,6},{5,7},{10,8},{11,9},{8,1... | collective-permute-start | bytes 1179656 | tf_op jit(solution)/shard_map/ppermute | solution.py:20
  46.3 5.6 %collective-permute-done.2.refs_0_ = bf16[256,768]{1,0:T(8,128)(2,1)S(1)} collective-permute-done((bf16[256,768]{1,0:T(8,128)(2,1)S(1)}, bf16[256,768]{1,0:T(8,128)(2,1)S(1)}, u32[]{:S(2)}, u32[]{:S(2)}) %collective-permute-start.2) | collective-permute-done | bytes 393248 | tf_op jit(solution)/shard_map/ppermute | solution.py:20
  51.9 8.8 %collective-permute-done.3.refs_1_ = bf16[256,768]{1,0:T(8,128)(2,1)S(1)} collective-permute-done((bf16[256,768]{1,0:T(8,128)(2,1)S(1)}, bf16[256,768]{1,0:T(8,128)(2,1)S(1)}, u32[]{:S(2)}, u32[]{:S(2)}) %collective-permute-start.3) | collective-permute-done | bytes 393248 | tf_op jit(solution)/shard_map/ppermute | solution.py:20
  61.6 7.5 %project.2 = (bf16[8,32,384]{2,1,0:T(8,128)(2,1)S(1)}, bf16[8,32,768]{2,1,0:T(8,128)(2,1)S(1)}, bf16[3,32,768]{2,1,0:T(8,128)(2,1)S(1)}, bf16[3,32,768]{2,1,0:T(8,128)(2,1)S(1)}, bf16[8,32,768]{2,1,0:T(8,128)(2,1)S(1)}) custom-call(s32[5]{0:T(128)S(1)} %copy-done.19, bf16[256,768]{1,0:T(8,128)(2,1)S(1)} %collective-permute-done.2.refs_0_, ...), custom_call_target="tpu_custom_call" | custom-call | tf_op jit(solution)/shard_map/project/pallas_call | solution.py:183
  73.4 4.8 %collective-permute-start.9 = (bf16[3,32,768]{2,1,0:T(8,128)(2,1)S(1)}, bf16[3,32,768]{2,1,0:T(8,128)(2,1)S(1)}, u32[]{:S(2)}, u32[]{:S(2)}) collective-permute-start(bf16[3,32,768]{2,1,0:T(8,128)(2,1)S(1)} %get-tuple-element.63), channel_id=1, source_target_pairs={{32,0},{4,32},{36,4},{8,36},{40,8},{12,40},{44,12},{16,44},{48,16}... | collective-permute-start | bytes 442376 | tf_op jit(solution)/shard_map/ppermute | solution.py:46
  92.2 3.2 %spread.2 = (f32[256,768]{1,0:T(8,128)S(1)}, bf16[256,768]{1,0:T(8,128)(2,1)S(1)}, bf16[256,768]{1,0:T(8,128)(2,1)S(1)}, bf16[256,768]{1,0:T(8,128)(2,1)S(1)}) custom-call(s32[5]{0:T(128)S(1)} %copy-done.19, f32[8,32,512]{2,1,0:T(8,128)S(1)} %get-tuple-element.67.part_a, f32[8,32,512]{2,1,0:T(8,128)S(1)} %collective-permute-done.11.part_b, ...), custom_call_target="tpu_custom_call" | custom-call | tf_op jit(solution)/shard_map/spread/pallas_call | solution.py:359
  95.4 2.9 %collective-permute-start.13 = (bf16[256,768]{1,0:T(8,128)(2,1)S(1)}, bf16[256,768]{1,0:T(8,128)(2,1)S(1)}, u32[]{:S(2)}, u32[]{:S(2)}) collective-permute-start(bf16[256,768]{1,0:T(8,128)(2,1)S(1)} %get-tuple-element.70), channel_id=1, source_target_pairs={{2,0},{3,1},{0,2},{1,3},{6,4},{7,5},{4,6},{5,7},{10,8},{11,9},{8,1... | collective-permute-start | bytes 1179656 | tf_op jit(solution)/shard_map/ppermute | solution.py:20
  101.0 7.1 %collective-permute-done.13.from_across = bf16[256,768]{1,0:T(8,128)(2,1)S(1)} collective-permute-done((bf16[256,768]{1,0:T(8,128)(2,1)S(1)}, bf16[256,768]{1,0:T(8,128)(2,1)S(1)}, u32[]{:S(2)}, u32[]{:S(2)}) %collective-permute-start.13) | collective-permute-done | bytes 393248 | tf_op jit(solution)/shard_map/ppermute | solution.py:20
  108.1 8.4 %collective-permute-done.14.from_prev = bf16[256,768]{1,0:T(8,128)(2,1)S(1)} collective-permute-done((bf16[256,768]{1,0:T(8,128)(2,1)S(1)}, bf16[256,768]{1,0:T(8,128)(2,1)S(1)}, u32[]{:S(2)}, u32[]{:S(2)}) %collective-permute-start.14) | collective-permute-done | bytes 393248 | tf_op jit(solution)/shard_map/ppermute | solution.py:20
  121.3 8.6 %collective-permute-done.17.refs_0_ = bf16[256,768]{1,0:T(8,128)(2,1)S(1)} collective-permute-done((bf16[256,768]{1,0:T(8,128)(2,1)S(1)}, bf16[256,768]{1,0:T(8,128)(2,1)S(1)}, u32[]{:S(2)}, u32[]{:S(2)}) %collective-permute-start.17) | collective-permute-done | bytes 393248 | tf_op jit(solution)/shard_map/ppermute | solution.py:20
  129.9 8.3 %collective-permute-done.18.refs_1_ = bf16[256,768]{1,0:T(8,128)(2,1)S(1)} collective-permute-done((bf16[256,768]{1,0:T(8,128)(2,1)S(1)}, bf16[256,768]{1,0:T(8,128)(2,1)S(1)}, u32[]{:S(2)}, u32[]{:S(2)}) %collective-permute-start.18) | collective-permute-done | bytes 393248 | tf_op jit(solution)/shard_map/ppermute | solution.py:20
  139.8 7.5 %project.3 = (bf16[8,32,384]{2,1,0:T(8,128)(2,1)S(1)}, bf16[8,32,768]{2,1,0:T(8,128)(2,1)S(1)}, bf16[3,32,768]{2,1,0:T(8,128)(2,1)S(1)}, bf16[3,32,768]{2,1,0:T(8,128)(2,1)S(1)}, bf16[8,32,768]{2,1,0:T(8,128)(2,1)S(1)}) custom-call(s32[5]{0:T(128)S(1)} %copy-done.18, bf16[256,768]{1,0:T(8,128)(2,1)S(1)} %collective-permute-done.17.refs_0_, ...), custom_call_target="tpu_custom_call" | custom-call | tf_op jit(solution)/shard_map/project/pallas_call | solution.py:183
  147.3 4.4 %collective-permute-start.23 = (bf16[8,32,768]{2,1,0:T(8,128)(2,1)S(1)}, bf16[8,32,768]{2,1,0:T(8,128)(2,1)S(1)}, u32[]{:S(2)}, u32[]{:S(2)}) collective-permute-start(bf16[8,32,768]{2,1,0:T(8,128)(2,1)S(1)} %get-tuple-element.83), channel_id=1, source_target_pairs={{48,0},{20,32},{52,4},{24,36},{56,8},{28,40},{60,12},{0,44},{32,16... | collective-permute-start | bytes 1179656 | tf_op jit(solution)/shard_map/ppermute | solution.py:46
  152.6 4.8 %collective-permute-start.22 = (bf16[3,32,768]{2,1,0:T(8,128)(2,1)S(1)}, bf16[3,32,768]{2,1,0:T(8,128)(2,1)S(1)}, u32[]{:S(2)}, u32[]{:S(2)}) collective-permute-start(bf16[3,32,768]{2,1,0:T(8,128)(2,1)S(1)} %get-tuple-element.82), channel_id=1, source_target_pairs={{32,0},{4,32},{36,4},{8,36},{40,8},{12,40},{44,12},{16,44},{48,16}... | collective-permute-start | bytes 442376 | tf_op jit(solution)/shard_map/ppermute | solution.py:46
  173.9 2.9 %collective-permute-start.26 = (bf16[256,768]{1,0:T(8,128)(2,1)S(1)}, bf16[256,768]{1,0:T(8,128)(2,1)S(1)}, u32[]{:S(2)}, u32[]{:S(2)}) collective-permute-start(bf16[256,768]{1,0:T(8,128)(2,1)S(1)} %get-tuple-element.90), channel_id=1, source_target_pairs={{2,0},{3,1},{0,2},{1,3},{6,4},{7,5},{4,6},{5,7},{10,8},{11,9},{8,1... | collective-permute-start | bytes 1179656 | tf_op jit(solution)/shard_map/ppermute | solution.py:20
  179.2 4.5 %collective-permute-done.25.from_prev = bf16[256,768]{1,0:T(8,128)(2,1)S(1)} collective-permute-done((bf16[256,768]{1,0:T(8,128)(2,1)S(1)}, bf16[256,768]{1,0:T(8,128)(2,1)S(1)}, u32[]{:S(2)}, u32[]{:S(2)}) %collective-permute-start.25) | collective-permute-done | bytes 393248 | tf_op jit(solution)/shard_map/ppermute | solution.py:20
  183.7 9.4 %collective-permute-done.26.from_across = bf16[256,768]{1,0:T(8,128)(2,1)S(1)} collective-permute-done((bf16[256,768]{1,0:T(8,128)(2,1)S(1)}, bf16[256,768]{1,0:T(8,128)(2,1)S(1)}, u32[]{:S(2)}, u32[]{:S(2)}) %collective-permute-start.26) | collective-permute-done | bytes 393248 | tf_op jit(solution)/shard_map/ppermute | solution.py:20
  194.9 3.6 %all-to-all-start.3 = ((bf16[8,32,768]{2,1,0:T(8,128)(2,1)}), bf16[8,32,768]{2,1,0:T(8,128)(2,1)S(1)}, u32[]{:S(2)}, u32[]{:S(2)}) async-start(bf16[8,32,768]{2,1,0:T(8,128)(2,1)} %bitcast.30), calls=%async_computation.3 | async-start | bytes 786432 | tf_op jit(solution)/shard_map/all_to_all | solution.py:38
  198.7 7.0 %all-to-all-done.3 = bf16[8,32,768]{2,1,0:T(8,128)(2,1)S(1)} async-done(((bf16[8,32,768]{2,1,0:T(8,128)(2,1)}), bf16[8,32,768]{2,1,0:T(8,128)(2,1)S(1)}, u32[]{:S(2)}, u32[]{:S(2)}) %all-to-all-start.3) | async-done | bytes 393248 | tf_op jit(solution)/shard_map/all_to_all | solution.py:38
  205.7 16.5 %all_to_all.20.early = bf16[8,96,768]{2,1,0:T(8,128)(2,1)S(1)} all-to-all(bf16[8,96,768]{2,1,0:T(8,128)(2,1)S(1)} %pad_maximum_fusion), channel_id=1, replica_groups={{0,4,8,12,16,20,24,28},{32,36,40,44,48,52,56,60},{1,5,9,13,17,21,25,29}..., dimensions={0} | all-to-all | bytes 2359296 | tf_op jit(solution)/shard_map/all_to_all | solution.py:38
  222.3 4.0 %collective-permute-start.28 = (bf16[8,32,768]{2,1,0:T(8,128)(2,1)S(1)}, bf16[8,32,768]{2,1,0:T(8,128)(2,1)S(1)}, u32[]{:S(2)}, u32[]{:S(2)}) collective-permute-start(bf16[8,32,768]{2,1,0:T(8,128)(2,1)S(1)} %get-tuple-element.96), channel_id=1, source_target_pairs={{64,0},{0,64},{65,1},{1,65},{66,2},{2,66},{67,3},{3,67},{68,4},{4,... | collective-permute-start | bytes 1179656 | tf_op jit(solution)/shard_map/ppermute | solution.py:20
  (143 shorter events, 75.5 us)
Async XLA Ops:
  0.7 60.1 %collective-permute-start.5 = (bf16[3,3072,384]{2,1,0:T(8,128)(2,1)}, bf16[3,3072,384]{2,1,0:T(8,128)(2,1)}, u32[]{:S(2)}, u32[]{:S(2)}) collective-permute-start(bf16[3,3072,384]{2,1,0:T(8,128)(2,1)} %bitcast.60), channel_id=1, source_target_pairs={{64,0},{0,64},{65,1},{1,65},{66,2},{2,66},{67,3},{3,67},{68,4},{4,... | collective-permute-start | bytes 21233672 | tf_op jit(solution)/shard_map/ppermute | solution.py:20
  4.5 14.3 %all-to-all-start = ((bf16[8,32,768]{2,1,0:T(8,128)(2,1)}), bf16[8,32,768]{2,1,0:T(8,128)(2,1)S(1)}, u32[]{:S(2)}, u32[]{:S(2)}) async-start(bf16[8,32,768]{2,1,0:T(8,128)(2,1)} %constant_dynamic-slice_fusion.2), calls=%async_computation | async-start | bytes 786432 | tf_op jit(solution)/shard_map/all_to_all | solution.py:38
  18.8 18.3 %all-to-all-start.1 = ((bf16[8,64,768]{2,1,0:T(8,128)(2,1)}), bf16[8,64,768]{2,1,0:T(8,128)(2,1)}, u32[]{:S(2)}, u32[]{:S(2)}) async-start(bf16[8,64,768]{2,1,0:T(8,128)(2,1)} %pad_maximum_fusion.1), calls=%async_computation.1 | async-start | bytes 1572864 | tf_op jit(solution)/shard_map/all_to_all | solution.py:38
  37.1 53.5 %collective-permute-start.12 = (bf16[384,3072]{1,0:T(8,128)(2,1)S(1)}, bf16[384,3072]{1,0:T(8,128)(2,1)}, u32[]{:S(2)}, u32[]{:S(2)}) collective-permute-start(bf16[384,3072]{1,0:T(8,128)(2,1)S(1)} %bitcast.46), channel_id=1, source_target_pairs={{64,0},{0,64},{65,1},{1,65},{66,2},{2,66},{67,3},{3,67},{68,4},{4,... | collective-permute-start | bytes 7077896 | tf_op jit(solution)/shard_map/ppermute | solution.py:20
  39.0 12.9 %collective-permute-start.2 = (bf16[256,768]{1,0:T(8,128)(2,1)S(1)}, bf16[256,768]{1,0:T(8,128)(2,1)S(1)}, u32[]{:S(2)}, u32[]{:S(2)}) collective-permute-start(bf16[256,768]{1,0:T(8,128)(2,1)S(1)} %bitcast.49), channel_id=1, source_target_pairs={{2,0},{3,1},{0,2},{1,3},{6,4},{7,5},{4,6},{5,7},{10,8},{11,9},{8,1... | collective-permute-start | bytes 1179656 | tf_op jit(solution)/shard_map/ppermute | solution.py:20
  42.7 18.0 %collective-permute-start.3 = (bf16[256,768]{1,0:T(8,128)(2,1)S(1)}, bf16[256,768]{1,0:T(8,128)(2,1)S(1)}, u32[]{:S(2)}, u32[]{:S(2)}) collective-permute-start(bf16[256,768]{1,0:T(8,128)(2,1)S(1)} %bitcast.50), channel_id=1, source_target_pairs={{1,0},{2,1},{3,2},{0,3},{5,4},{6,5},{7,6},{4,7},{9,8},{10,9},{11,1... | collective-permute-start | bytes 1179656 | tf_op jit(solution)/shard_map/ppermute | solution.py:20
  43.2 17.6 %collective-permute-start.4 = (bf16[256,768]{1,0:T(8,128)(2,1)S(1)}, bf16[256,768]{1,0:T(8,128)(2,1)S(1)}, u32[]{:S(2)}, u32[]{:S(2)}) collective-permute-start(bf16[256,768]{1,0:T(8,128)(2,1)S(1)} %bitcast.51), channel_id=1, source_target_pairs={{3,0},{0,1},{1,2},{2,3},{7,4},{4,5},{5,6},{6,7},{11,8},{8,9},{9,10... | collective-permute-start | bytes 1179656 | tf_op jit(solution)/shard_map/ppermute | solution.py:20
  69.2 17.0 %collective-permute-start.10 = (bf16[8,32,768]{2,1,0:T(8,128)(2,1)S(1)}, bf16[8,32,768]{2,1,0:T(8,128)(2,1)S(1)}, u32[]{:S(2)}, u32[]{:S(2)}) collective-permute-start(bf16[8,32,768]{2,1,0:T(8,128)(2,1)S(1)} %get-tuple-element.64), channel_id=1, source_target_pairs={{48,0},{20,32},{52,4},{24,36},{56,8},{28,40},{60,12},{0,44},{32,16... | collective-permute-start | bytes 1179656 | tf_op jit(solution)/shard_map/ppermute | solution.py:46
  73.4 10.0 %collective-permute-start.8 = (bf16[3,32,768]{2,1,0:T(8,128)(2,1)S(1)}, bf16[3,32,768]{2,1,0:T(8,128)(2,1)S(1)}, u32[]{:S(2)}, u32[]{:S(2)}) collective-permute-start(bf16[3,32,768]{2,1,0:T(8,128)(2,1)S(1)} %get-tuple-element.62), channel_id=1, source_target_pairs={{60,0},{0,32},{32,4},{4,36},{36,8},{8,40},{40,12},{12,44},{44,16},... | collective-permute-start | bytes 442376 | tf_op jit(solution)/shard_map/ppermute | solution.py:46
  73.4 10.0 %collective-permute-start.9 = (bf16[3,32,768]{2,1,0:T(8,128)(2,1)S(1)}, bf16[3,32,768]{2,1,0:T(8,128)(2,1)S(1)}, u32[]{:S(2)}, u32[]{:S(2)}) collective-permute-start(bf16[3,32,768]{2,1,0:T(8,128)(2,1)S(1)} %get-tuple-element.63), channel_id=1, source_target_pairs={{32,0},{4,32},{36,4},{8,36},{40,8},{12,40},{44,12},{16,44},{48,16}... | collective-permute-start | bytes 442376 | tf_op jit(solution)/shard_map/ppermute | solution.py:46
  95.4 12.7 %collective-permute-start.13 = (bf16[256,768]{1,0:T(8,128)(2,1)S(1)}, bf16[256,768]{1,0:T(8,128)(2,1)S(1)}, u32[]{:S(2)}, u32[]{:S(2)}) collective-permute-start(bf16[256,768]{1,0:T(8,128)(2,1)S(1)} %get-tuple-element.70), channel_id=1, source_target_pairs={{2,0},{3,1},{0,2},{1,3},{6,4},{7,5},{4,6},{5,7},{10,8},{11,9},{8,1... | collective-permute-start | bytes 1179656 | tf_op jit(solution)/shard_map/ppermute | solution.py:20
  98.3 18.2 %collective-permute-start.14 = (bf16[256,768]{1,0:T(8,128)(2,1)S(1)}, bf16[256,768]{1,0:T(8,128)(2,1)S(1)}, u32[]{:S(2)}, u32[]{:S(2)}) collective-permute-start(bf16[256,768]{1,0:T(8,128)(2,1)S(1)} %get-tuple-element.71), channel_id=1, source_target_pairs={{3,0},{0,1},{1,2},{2,3},{7,4},{4,5},{5,6},{6,7},{11,8},{8,9},{9,10... | collective-permute-start | bytes 1179656 | tf_op jit(solution)/shard_map/ppermute | solution.py:20
  99.1 18.1 %collective-permute-start.15 = (bf16[256,768]{1,0:T(8,128)(2,1)S(1)}, bf16[256,768]{1,0:T(8,128)(2,1)S(1)}, u32[]{:S(2)}, u32[]{:S(2)}) collective-permute-start(bf16[256,768]{1,0:T(8,128)(2,1)S(1)} %get-tuple-element.72), channel_id=1, source_target_pairs={{1,0},{2,1},{3,2},{0,3},{5,4},{6,5},{7,6},{4,7},{9,8},{10,9},{11,1... | collective-permute-start | bytes 1179656 | tf_op jit(solution)/shard_map/ppermute | solution.py:20
  118.0 11.9 %collective-permute-start.17 = (bf16[256,768]{1,0:T(8,128)(2,1)S(1)}, bf16[256,768]{1,0:T(8,128)(2,1)S(1)}, u32[]{:S(2)}, u32[]{:S(2)}) collective-permute-start(bf16[256,768]{1,0:T(8,128)(2,1)S(1)} %finish.2.refs_3_.hidden), channel_id=1, source_target_pairs={{2,0},{3,1},{0,2},{1,3},{6,4},{7,5},{4,6},{5,7},{10,8},{11,9},{8,1... | collective-permute-start | bytes 1179656 | tf_op jit(solution)/shard_map/ppermute | solution.py:20
  119.8 18.4 %collective-permute-start.18 = (bf16[256,768]{1,0:T(8,128)(2,1)S(1)}, bf16[256,768]{1,0:T(8,128)(2,1)S(1)}, u32[]{:S(2)}, u32[]{:S(2)}) collective-permute-start(bf16[256,768]{1,0:T(8,128)(2,1)S(1)} %finish.2.refs_3_.hidden), channel_id=1, source_target_pairs={{1,0},{2,1},{3,2},{0,3},{5,4},{6,5},{7,6},{4,7},{9,8},{10,9},{11,1... | collective-permute-start | bytes 1179656 | tf_op jit(solution)/shard_map/ppermute | solution.py:20
  121.1 17.9 %collective-permute-start.19 = (bf16[256,768]{1,0:T(8,128)(2,1)S(1)}, bf16[256,768]{1,0:T(8,128)(2,1)S(1)}, u32[]{:S(2)}, u32[]{:S(2)}) collective-permute-start(bf16[256,768]{1,0:T(8,128)(2,1)S(1)} %finish.2.refs_3_.hidden), channel_id=1, source_target_pairs={{3,0},{0,1},{1,2},{2,3},{7,4},{4,5},{5,6},{6,7},{11,8},{8,9},{9,10... | collective-permute-start | bytes 1179656 | tf_op jit(solution)/shard_map/ppermute | solution.py:20
  147.3 18.3 %collective-permute-start.23 = (bf16[8,32,768]{2,1,0:T(8,128)(2,1)S(1)}, bf16[8,32,768]{2,1,0:T(8,128)(2,1)S(1)}, u32[]{:S(2)}, u32[]{:S(2)}) collective-permute-start(bf16[8,32,768]{2,1,0:T(8,128)(2,1)S(1)} %get-tuple-element.83), channel_id=1, source_target_pairs={{48,0},{20,32},{52,4},{24,36},{56,8},{28,40},{60,12},{0,44},{32,16... | collective-permute-start | bytes 1179656 | tf_op jit(solution)/shard_map/ppermute | solution.py:46
  152.6 10.0 %collective-permute-start.21 = (bf16[3,32,768]{2,1,0:T(8,128)(2,1)S(1)}, bf16[3,32,768]{2,1,0:T(8,128)(2,1)S(1)}, u32[]{:S(2)}, u32[]{:S(2)}) collective-permute-start(bf16[3,32,768]{2,1,0:T(8,128)(2,1)S(1)} %get-tuple-element.81), channel_id=1, source_target_pairs={{60,0},{0,32},{32,4},{4,36},{36,8},{8,40},{40,12},{12,44},{44,16},... | collective-permute-start | bytes 442376 | tf_op jit(solution)/shard_map/ppermute | solution.py:46
  152.6 10.3 %collective-permute-start.22 = (bf16[3,32,768]{2,1,0:T(8,128)(2,1)S(1)}, bf16[3,32,768]{2,1,0:T(8,128)(2,1)S(1)}, u32[]{:S(2)}, u32[]{:S(2)}) collective-permute-start(bf16[3,32,768]{2,1,0:T(8,128)(2,1)S(1)} %get-tuple-element.82), channel_id=1, source_target_pairs={{32,0},{4,32},{36,4},{8,36},{40,8},{12,40},{44,12},{16,44},{48,16}... | collective-permute-start | bytes 442376 | tf_op jit(solution)/shard_map/ppermute | solution.py:46
  173.0 10.6 %collective-permute-start.25 = (bf16[256,768]{1,0:T(8,128)(2,1)S(1)}, bf16[256,768]{1,0:T(8,128)(2,1)S(1)}, u32[]{:S(2)}, u32[]{:S(2)}) collective-permute-start(bf16[256,768]{1,0:T(8,128)(2,1)S(1)} %get-tuple-element.88), channel_id=1, source_target_pairs={{3,0},{0,1},{1,2},{2,3},{7,4},{4,5},{5,6},{6,7},{11,8},{8,9},{9,10... | collective-permute-start | bytes 1179656 | tf_op jit(solution)/shard_map/ppermute | solution.py:20
  173.9 19.2 %collective-permute-start.26 = (bf16[256,768]{1,0:T(8,128)(2,1)S(1)}, bf16[256,768]{1,0:T(8,128)(2,1)S(1)}, u32[]{:S(2)}, u32[]{:S(2)}) collective-permute-start(bf16[256,768]{1,0:T(8,128)(2,1)S(1)} %get-tuple-element.90), channel_id=1, source_target_pairs={{2,0},{3,1},{0,2},{1,3},{6,4},{7,5},{4,6},{5,7},{10,8},{11,9},{8,1... | collective-permute-start | bytes 1179656 | tf_op jit(solution)/shard_map/ppermute | solution.py:20
  176.8 16.6 %collective-permute-start.27 = (bf16[256,768]{1,0:T(8,128)(2,1)S(1)}, bf16[256,768]{1,0:T(8,128)(2,1)S(1)}, u32[]{:S(2)}, u32[]{:S(2)}) collective-permute-start(bf16[256,768]{1,0:T(8,128)(2,1)S(1)} %get-tuple-element.91), channel_id=1, source_target_pairs={{1,0},{2,1},{3,2},{0,3},{5,4},{6,5},{7,6},{4,7},{9,8},{10,9},{11,1... | collective-permute-start | bytes 1179656 | tf_op jit(solution)/shard_map/ppermute | solution.py:20
  177.0 21.5 %collective-permute-start.16 = (bf16[8,32,768]{2,1,0:T(8,128)(2,1)S(1)}, bf16[8,32,768]{2,1,0:T(8,128)(2,1)S(1)}, u32[]{:S(2)}, u32[]{:S(2)}) collective-permute-start(bf16[8,32,768]{2,1,0:T(8,128)(2,1)S(1)} %broadcast_select_fusion.5), channel_id=1, source_target_pairs={{64,0},{0,64},{65,1},{1,65},{66,2},{2,66},{67,3},{3,67},{68,4},{4,... | collective-permute-start | bytes 1179656 | tf_op jit(solution)/shard_map/ppermute | solution.py:20
  194.9 10.8 %all-to-all-start.3 = ((bf16[8,32,768]{2,1,0:T(8,128)(2,1)}), bf16[8,32,768]{2,1,0:T(8,128)(2,1)S(1)}, u32[]{:S(2)}, u32[]{:S(2)}) async-start(bf16[8,32,768]{2,1,0:T(8,128)(2,1)} %bitcast.30), calls=%async_computation.3 | async-start | bytes 786432 | tf_op jit(solution)/shard_map/all_to_all | solution.py:38
  (39 other events, 683.0 us)

commit v7 on v6

--- a/solution.py
+++ b/solution.py
@@ -46,31 +46,58 @@
     return lax.ppermute(block, "seq", route)
 
 
-def collect_kernel(core, early, own, got, handed, cache):
-    patches, rows, _ = own.shape
-    cols = cache.shape[-1]
+def pack_kernel(core, latents, stale, out, sems):
+    rows, cols = latents.shape[1] // 2, stale.shape[-1]
+    first = pl.multiple_of(core[0] * rows, rows)
+    copies = [
+        pltpu.make_async_copy(latents.at[:, pl.ds(first, rows)], out.at[:, :rows], sems.at[0])
+    ]
+    for half in range(2):
+        there = out.at[:, rows:, half * cols : (half + 1) * cols]
+        copies.append(pltpu.make_async_copy(stale.at[half], there, sems.at[1 + half]))
+    for copy in copies:
+        copy.start()
+    for copy in copies:
+        copy.wait()
+
+
+def pack(core, latents, stale):
+    patches, rows, cols = latents.shape
+    return pl.pallas_call(
+        pack_kernel,
+        in_specs=[SCALARS] + [ANYWHERE] * 2,
+        out_specs=ON_CHIP,
+        out_shape=struct((patches, rows // 2 + rows, cols)),
+        scratch_shapes=[pltpu.SemaphoreType.DMA((3,))],
+        compiler_params=params(8),
+        name="pack",
+    )(core, latents, stale)
+
+
+def collect_kernel(core, keys0, features1, keys1, features2, got1, got2, handed, cache):
+    rows, cols = keys0.shape[1], cache.shape[-1]
+
+    def collect(features, keys):
+        for half in range(2):
+            here = slice(half * rows, (half + 1) * rows)
+            handed[:, here] = features[half][...]
+            for which in range(2):
+                cache[which, :, here] = keys[half][:, :, which * cols : (which + 1) * cols]
 
     @pl.when(core[0] == 0)
     def _():
-        handed[:, :rows] = own[...]
-        handed[:, rows:] = got[...]
-        cache[0] = early[:, : 2 * rows, :cols]
-        cache[1] = early[:, : 2 * rows, cols:]
+        collect((features2, got2), (keys0, got1))
 
     @pl.when(core[0] == 1)
     def _():
-        handed[...] = early[:, : 2 * rows]
-        for half in range(2):
-            cut = slice(half * cols, (half + 1) * cols)
-            cache[half, :, :rows] = got[:, :, cut]
-            cache[half, :, rows:] = own[:, :, cut]
-
-
-def collect(core, early, own, got):
-    patches, rows, cols = own.shape
+        collect((got1, features1), (got2, keys1))
+
+
+def collect(core, *halves):
+    patches, rows, cols = halves[0].shape
     return pl.pallas_call(
         collect_kernel,
-        in_specs=[SCALARS] + [ON_CHIP] * 3,
+        in_specs=[SCALARS] + [ON_CHIP] * 6,
         out_specs=[ON_CHIP] * 2,
         out_shape=[
             struct((patches, 2 * rows, cols)),
@@ -78,7 +105,7 @@
         ],
         compiler_params=params(8),
         name="collect",
-    )(core, early, own, got)
+    )(core, *halves)
 
 
 def choose(meta, kv, stale, outs):
@@ -435,13 +462,13 @@
     heads_cols, width = w_out.shape[1:]
     head_dim = qk_gain.shape[-1]
 
-    mine = lax.dynamic_slice_in_dim(latents, core * rows_core, rows_core, 1)
-    hidden = exchanged(mine).reshape(rows, part_cols)
+    core_scalar = core.astype(jnp.int32)[None]
+    arrived = exchanged(pack(core_scalar, latents, stale_cache[0]))
+    hidden = arrived[:, :rows_core].reshape(rows, part_cols)
+    stale_all = arrived[:, rows_core:]
     w_other = shifted(w_own, "segment", 1)
     small_own = jnp.concatenate([modulation[0].reshape(-1), qk_gain[0].reshape(-1)])
     small_other = shifted(small_own, "segment", 1)
-    stale_all, kv_tiles, tile_counts = after((stale_cache[0], kv_tiles, tile_counts), mine)
-    stale_all = exchanged(jnp.concatenate([stale_all[0], stale_all[1]], axis=-1))
     kv_tiles, tile_counts = after((kv_tiles, tile_counts), small_other)
     turns = jnp.arange(patches, dtype=jnp.int32)
     asked = jnp.stack([chip, chip - 1, chip + 1, chip - seq_size // 2 - 1]) % seq_size // share
@@ -472,6 +499,7 @@
     wo_own = w_out[0]
     wo_other = shifted(wo_own, "segment", 1)
 
+    home = []
     for section in range(2):
         meta, shift, scale, gates, gain, times_own, times_rest = given[section]
         blocks = gather_features(hidden)
@@ -501,23 +529,18 @@
         from_across = shifted(to_across, "tp", 2)
         from_prev = shifted(to_next, "tp", 1)
         from_next = shifted(to_prev, "tp", -1)
-        if section > 0:
-            early = jnp.concatenate([early, kv], axis=1)
-            early = exchanged(after(early, from_prev))
+        tiled = hidden.reshape(patches, rows_core, part_cols)
+        leaving = kv if section == 0 else jnp.concatenate([tiled, kv], axis=1)
+        leaving = exchanged(after(leaving, from_across))
+        from_prev, from_next, leaving = lax.optimization_barrier((from_prev, from_next, leaving))
+        home.append(leaving)
         hidden = finish(meta, from_across, from_prev, from_next, keep, hidden, gates)
-        features = hidden.reshape(patches, rows_core, part_cols)
-        if section == 0:
-            got = shifted(jnp.where(core == 0, features, kv), "segment", 1)
-            own = jnp.where(core == 0, kv, features)
-            halves = [jnp.where(core == place, own, got) for place in range(2)]
-            early = jnp.concatenate(halves, axis=1)
-        else:
-            features = exchanged(features)
-
-    keys = early[:, patch_rows:]
-    got = shifted(jnp.where(core == 0, keys, features), "segment", 1)
-    own = jnp.where(core == 0, features, keys)
-    handed, new_cache = collect(core.astype(jnp.int32)[None], early, own, got)
+
+    keys0, features1, keys1 = home[0], home[1][:, :rows_core], home[1][:, rows_core:]
+    features2 = exchanged(hidden.reshape(patches, rows_core, part_cols))
+    got1 = shifted(jnp.where(core == 0, features1, keys0), "segment", 1)
+    got2 = shifted(jnp.where(core == 0, keys1, features2), "segment", 1)
+    handed, new_cache = collect(core_scalar, keys0, features1, keys1, features2, got1, got2)
     return (handed[None], new_cache[None])
 
 

time: 232 us -> 227 us (0.978)
  blocking collectives: 16.5 us -> 9.34 us
  local copies, waits for them, and re-layouts: 9.37 us -> 15.4 us
  Pallas kernels: 33.4 us -> 37.6 us
  waiting for transfers between devices: 95.1 us -> 91.5 us
  other arithmetic: 10 us -> 6.43 us
    all_to_all x1, blocking collectives: 16.5 us -> 9.34 us  [exchanged(): return lax.all_to_all(tiles, 'seq', 0, 0, axis_index_groups=groups)]
    unnamed x62, local copies, waits for them, and re-layouts: 1.73 us -> 8.67 us
    ppermute x23, waiting for transfers between devices: 68.2 us -> 63.1 us  [shifted(): return lax.ppermute(block, axis, route)]
    ppermute x23, starting transfers between devices: 33 us -> 36.7 us  [shifted(): return lax.ppermute(block, axis, route)]
    slice x0 -> x2, local copies, waits for them, and re-layouts: none -> 3.09 us  [the longest x1 2.06 us: local(): stale_all = arrived[:, rows_core:]]
  transfers between devices with their start and end apart: 32 -> 32, of which waited for: 22 -> 22; matrix products, arithmetic and copies ran while one was open for 8% -> 5% of each run, Pallas kernels for 7% -> 8%
where the time goes in v7:
time: 227 us; the launch traced here: 226 us
  waiting for transfers between devices  91.5 us (40%)
  starting transfers between devices  64.6 us (28%)
  Pallas kernels  37.6 us (17%)
  local copies, waits for them, and re-layouts  15.4 us (7%)
  blocking collectives  9.34 us (4%)
  other arithmetic  6.43 us (3%)
    ppermute x23, waiting for transfers between devices, shifted(): return lax.ppermute(block, axis, route)  63.1 us
    ppermute x23, starting transfers between devices, shifted(): return lax.ppermute(block, axis, route)  36.7 us
    all_to_all x3, waiting for transfers between devices, exchanged(): return lax.all_to_all(tiles, 'seq', 0, 0, axis_index_groups=groups)  17.6 us
    pallas_call x2, Pallas kernels, project(): pl.pallas_call(project_kernel, in_specs=[SCALARS] + [ANYWHERE] * len(bloc...  15.8 us
    ppermute x6, starting transfers between devices, along_ring(): return lax.ppermute(block, 'seq', route)  14.8 us
    all_to_all x3, starting transfers between devices, exchanged(): return lax.all_to_all(tiles, 'seq', 0, 0, axis_index_groups=groups)  13.1 us
    ppermute x6, waiting for transfers between devices, along_ring(): return lax.ppermute(block, 'seq', route)  10.8 us
    all_to_all x1, blocking collectives, exchanged(): return lax.all_to_all(tiles, 'seq', 0, 0, axis_index_groups=groups)  9.34 us
  transfers between devices with their start and end apart: 32, of which 22 were waited for; matrix products, arithmetic and copies ran while one was open for 5% of the time, Pallas kernels for 8%

profile of v7, /device:TPU:1, one launch (start us, length us, event | category | flops | bytes accessed | tf_op | source)
XLA Modules:
  0.0 225.8 jit_solution(6901560886696005897)
XLA Ops:
  6.4 5.3 %all-to-all-start = ((bf16[8,96,768]{2,1,0:T(8,128)(2,1)}), bf16[8,96,768]{2,1,0:T(8,128)(2,1)}, u32[]{:S(2)}, u32[]{:S(2)}) async-start(bf16[8,96,768]{2,1,0:T(8,128)(2,1)} %pack.1), calls=%async_computation | async-start | bytes 2359296 | tf_op jit(solution)/shard_map/all_to_all | solution.py:38
  16.5 12.5 %all-to-all-done = bf16[8,96,768]{2,1,0:T(8,128)(2,1)} async-done(((bf16[8,96,768]{2,1,0:T(8,128)(2,1)}), bf16[8,96,768]{2,1,0:T(8,128)(2,1)}, u32[]{:S(2)}, u32[]{:S(2)}) %all-to-all-start) | async-done | bytes 1179680 | tf_op jit(solution)/shard_map/all_to_all | solution.py:38
  34.2 3.6 %collective-permute-start.2 = (bf16[256,768]{1,0:T(8,128)(2,1)S(1)}, bf16[256,768]{1,0:T(8,128)(2,1)S(1)}, u32[]{:S(2)}, u32[]{:S(2)}) collective-permute-start(bf16[256,768]{1,0:T(8,128)(2,1)S(1)} %bitcast.44), channel_id=1, source_target_pairs={{2,0},{3,1},{0,2},{1,3},{6,4},{7,5},{4,6},{5,7},{10,8},{11,9},{8,1... | collective-permute-start | bytes 1179656 | tf_op jit(solution)/shard_map/ppermute | solution.py:20
  41.8 5.3 %collective-permute-done.2.refs_0_ = bf16[256,768]{1,0:T(8,128)(2,1)S(1)} collective-permute-done((bf16[256,768]{1,0:T(8,128)(2,1)S(1)}, bf16[256,768]{1,0:T(8,128)(2,1)S(1)}, u32[]{:S(2)}, u32[]{:S(2)}) %collective-permute-start.2) | collective-permute-done | bytes 393248 | tf_op jit(solution)/shard_map/ppermute | solution.py:20
  47.0 8.9 %collective-permute-done.3.refs_1_ = bf16[256,768]{1,0:T(8,128)(2,1)} collective-permute-done((bf16[256,768]{1,0:T(8,128)(2,1)S(1)}, bf16[256,768]{1,0:T(8,128)(2,1)}, u32[]{:S(2)}, u32[]{:S(2)}) %collective-permute-start.3) | collective-permute-done | bytes 393248 | tf_op jit(solution)/shard_map/ppermute | solution.py:20
  56.0 8.3 %project.2 = (bf16[8,32,384]{2,1,0:T(8,128)(2,1)S(1)}, bf16[8,32,768]{2,1,0:T(8,128)(2,1)}, bf16[3,32,768]{2,1,0:T(8,128)(2,1)S(1)}, bf16[3,32,768]{2,1,0:T(8,128)(2,1)S(1)}, bf16[8,32,768]{2,1,0:T(8,128)(2,1)S(1)}) custom-call(s32[5]{0:T(128)S(1)} %get-tuple-element.55.meta, bf16[256,768]{1,0:T(8,128)(2,1)S(1)} %collective-permute-done.2.refs_0_, ...), custom_call_target="tpu_custom_call" | custom-call | tf_op jit(solution)/shard_map/project/pallas_call | solution.py:210
  68.5 4.8 %collective-permute-start.9 = (bf16[3,32,768]{2,1,0:T(8,128)(2,1)S(1)}, bf16[3,32,768]{2,1,0:T(8,128)(2,1)S(1)}, u32[]{:S(2)}, u32[]{:S(2)}) collective-permute-start(bf16[3,32,768]{2,1,0:T(8,128)(2,1)S(1)} %get-tuple-element.63), channel_id=1, source_target_pairs={{32,0},{4,32},{36,4},{8,36},{40,8},{12,40},{44,12},{16,44},{48,16}... | collective-permute-start | bytes 442376 | tf_op jit(solution)/shard_map/ppermute | solution.py:46
  73.3 3.4 %attend_own.2.before = f32[8,64,512]{2,1,0:T(8,128)S(1)} custom-call(bf16[8,32,384]{2,1,0:T(8,128)(2,1)S(1)} %get-tuple-element.61.q_own, bf16[8,32,384]{2,1,0:T(8,128)(2,1)S(1)} %collective-permute-done.7.q_other, bf16[8,32,768]{2,1,0:T(8,128)(2,1)} %get-tuple-element.74.own, f32[8,1,256]{2,1,0:T(1,128)S(1)} %slice.143.multiple), custom_call_target="tpu_custom_call" | custom-call | tf_op jit(solution)/shard_map/attend_own/pallas_call | solution.py:288
  87.3 3.9 %spread.2 = (f32[256,768]{1,0:T(8,128)S(1)}, bf16[256,768]{1,0:T(8,128)(2,1)}, bf16[256,768]{1,0:T(8,128)(2,1)S(1)}, bf16[256,768]{1,0:T(8,128)(2,1)}) custom-call(s32[5]{0:T(128)S(1)} %get-tuple-element.55.meta, f32[8,32,512]{2,1,0:T(8,128)S(1)} %get-tuple-element.68.part_a, f32[8,32,512]{2,1,0:T(8,128)S(1)} %collective-permute-done.11.part_b, ...), custom_call_target="tpu_custom_call" | custom-call | tf_op jit(solution)/shard_map/spread/pallas_call | solution.py:386
  97.7 7.0 %collective-permute-done.15.from_across = bf16[256,768]{1,0:T(8,128)(2,1)S(1)} collective-permute-done((bf16[256,768]{1,0:T(8,128)(2,1)S(1)}, bf16[256,768]{1,0:T(8,128)(2,1)S(1)}, u32[]{:S(2)}, u32[]{:S(2)}) %collective-permute-start.15) | collective-permute-done | bytes 393248 | tf_op jit(solution)/shard_map/ppermute | solution.py:20
  104.7 3.5 %all-to-all-start.1 = ((bf16[8,32,768]{2,1,0:T(8,128)(2,1)}), bf16[8,32,768]{2,1,0:T(8,128)(2,1)S(1)}, u32[]{:S(2)}, u32[]{:S(2)}) async-start(bf16[8,32,768]{2,1,0:T(8,128)(2,1)} %get-tuple-element.74.own), calls=%async_computation.1 | async-start | bytes 786432 | tf_op jit(solution)/shard_map/all_to_all | solution.py:38
  108.2 5.0 %collective-permute-done.13.from_prev = bf16[256,768]{1,0:T(8,128)(2,1)} collective-permute-done((bf16[256,768]{1,0:T(8,128)(2,1)}, bf16[256,768]{1,0:T(8,128)(2,1)}, u32[]{:S(2)}, u32[]{:S(2)}) %collective-permute-start.13) | collective-permute-done | bytes 393248 | tf_op jit(solution)/shard_map/ppermute | solution.py:20
  113.9 3.1 %all-to-all-done.1.keys0 = bf16[8,32,768]{2,1,0:T(8,128)(2,1)S(1)} async-done(((bf16[8,32,768]{2,1,0:T(8,128)(2,1)}), bf16[8,32,768]{2,1,0:T(8,128)(2,1)S(1)}, u32[]{:S(2)}, u32[]{:S(2)}) %all-to-all-start.1) | async-done | bytes 393248 | tf_op jit(solution)/shard_map/all_to_all | solution.py:38
  126.3 7.0 %collective-permute-done.16.refs_0_ = bf16[256,768]{1,0:T(8,128)(2,1)S(1)} collective-permute-done((bf16[256,768]{1,0:T(8,128)(2,1)S(1)}, bf16[256,768]{1,0:T(8,128)(2,1)S(1)}, u32[]{:S(2)}, u32[]{:S(2)}) %collective-permute-start.16) | collective-permute-done | bytes 393248 | tf_op jit(solution)/shard_map/ppermute | solution.py:20
  133.3 9.2 %collective-permute-done.17.refs_1_ = bf16[256,768]{1,0:T(8,128)(2,1)S(1)} collective-permute-done((bf16[256,768]{1,0:T(8,128)(2,1)S(1)}, bf16[256,768]{1,0:T(8,128)(2,1)S(1)}, u32[]{:S(2)}, u32[]{:S(2)}) %collective-permute-start.17) | collective-permute-done | bytes 393248 | tf_op jit(solution)/shard_map/ppermute | solution.py:20
  144.9 7.5 %project.3 = (bf16[8,32,384]{2,1,0:T(8,128)(2,1)S(1)}, bf16[8,32,768]{2,1,0:T(8,128)(2,1)S(1)}, bf16[3,32,768]{2,1,0:T(8,128)(2,1)S(1)}, bf16[3,32,768]{2,1,0:T(8,128)(2,1)S(1)}, bf16[8,32,768]{2,1,0:T(8,128)(2,1)S(1)}) custom-call(s32[5]{0:T(128)S(1)} %copy-done.19, bf16[256,768]{1,0:T(8,128)(2,1)S(1)} %collective-permute-done.16.refs_0_, ...), custom_call_target="tpu_custom_call" | custom-call | tf_op jit(solution)/shard_map/project/pallas_call | solution.py:210
  157.0 3.8 %collective-permute-start.21 = (bf16[3,32,768]{2,1,0:T(8,128)(2,1)S(1)}, bf16[3,32,768]{2,1,0:T(8,128)(2,1)S(1)}, u32[]{:S(2)}, u32[]{:S(2)}) collective-permute-start(bf16[3,32,768]{2,1,0:T(8,128)(2,1)S(1)} %get-tuple-element.86), channel_id=1, source_target_pairs={{32,0},{4,32},{36,4},{8,36},{40,8},{12,40},{44,12},{16,44},{48,16}... | collective-permute-start | bytes 442376 | tf_op jit(solution)/shard_map/ppermute | solution.py:46
  163.2 3.4 %collective-permute-done.20.below = bf16[3,32,768]{2,1,0:T(8,128)(2,1)S(1)} collective-permute-done((bf16[3,32,768]{2,1,0:T(8,128)(2,1)S(1)}, bf16[3,32,768]{2,1,0:T(8,128)(2,1)S(1)}, u32[]{:S(2)}, u32[]{:S(2)}) %collective-permute-start.20) | collective-permute-done | bytes 147488 | tf_op jit(solution)/shard_map/ppermute | solution.py:46
  178.6 3.0 %collective-permute-start.26 = (bf16[256,768]{1,0:T(8,128)(2,1)S(1)}, bf16[256,768]{1,0:T(8,128)(2,1)S(1)}, u32[]{:S(2)}, u32[]{:S(2)}) collective-permute-start(bf16[256,768]{1,0:T(8,128)(2,1)S(1)} %get-tuple-element.95), channel_id=1, source_target_pairs={{2,0},{3,1},{0,2},{1,3},{6,4},{7,5},{4,6},{5,7},{10,8},{11,9},{8,1... | collective-permute-start | bytes 1179656 | tf_op jit(solution)/shard_map/ppermute | solution.py:20
  182.6 7.0 %collective-permute-done.26.from_across = bf16[256,768]{1,0:T(8,128)(2,1)S(1)} collective-permute-done((bf16[256,768]{1,0:T(8,128)(2,1)S(1)}, bf16[256,768]{1,0:T(8,128)(2,1)S(1)}, u32[]{:S(2)}, u32[]{:S(2)}) %collective-permute-start.26) | collective-permute-done | bytes 393248 | tf_op jit(solution)/shard_map/ppermute | solution.py:20
  189.5 4.4 %all-to-all-start.2 = ((bf16[8,64,768]{2,1,0:T(8,128)(2,1)}), bf16[8,64,768]{2,1,0:T(8,128)(2,1)}, u32[]{:S(2)}, u32[]{:S(2)}) async-start(bf16[8,64,768]{2,1,0:T(8,128)(2,1)} %pad_maximum_fusion), calls=%async_computation.2 | async-start | bytes 1572864 | tf_op jit(solution)/shard_map/all_to_all | solution.py:38
  197.3 7.5 %collective-permute-done.24.from_prev = bf16[256,768]{1,0:T(8,128)(2,1)S(1)} collective-permute-done((bf16[256,768]{1,0:T(8,128)(2,1)}, bf16[256,768]{1,0:T(8,128)(2,1)S(1)}, u32[]{:S(2)}, u32[]{:S(2)}) %collective-permute-start.24) | collective-permute-done | bytes 393248 | tf_op jit(solution)/shard_map/ppermute | solution.py:20
  207.6 9.3 %all_to_all.20.features2 = bf16[8,32,768]{2,1,0:T(8,128)(2,1)S(1)} all-to-all(bf16[8,32,768]{2,1,0:T(8,128)(2,1)S(1)} %bitcast.49), channel_id=1, replica_groups={{0,4,8,12,16,20,24,28},{32,36,40,44,48,52,56,60},{1,5,9,13,17,21,25,29}..., dimensions={0} | all-to-all | bytes 786432 | tf_op jit(solution)/shard_map/all_to_all | solution.py:38
  218.2 4.5 %collective-permute-start.27 = (bf16[8,32,768]{2,1,0:T(8,128)(2,1)S(1)}, bf16[8,32,768]{2,1,0:T(8,128)(2,1)S(1)}, u32[]{:S(2)}, u32[]{:S(2)}) collective-permute-start(bf16[8,32,768]{2,1,0:T(8,128)(2,1)S(1)} %get-tuple-element.109), channel_id=1, source_target_pairs={{64,0},{0,64},{65,1},{1,65},{66,2},{2,66},{67,3},{3,67},{68,4},{4,... | collective-permute-start | bytes 1179656 | tf_op jit(solution)/shard_map/ppermute | solution.py:20
  (141 shorter events, 83.6 us)
Async XLA Ops:
  0.6 55.3 %collective-permute-start.5 = (bf16[3,3072,384]{2,1,0:T(8,128)(2,1)}, bf16[3,3072,384]{2,1,0:T(8,128)(2,1)}, u32[]{:S(2)}, u32[]{:S(2)}) collective-permute-start(bf16[3,3072,384]{2,1,0:T(8,128)(2,1)} %bitcast.57), channel_id=1, source_target_pairs={{64,0},{0,64},{65,1},{1,65},{66,2},{2,66},{67,3},{3,67},{68,4},{4,... | collective-permute-start | bytes 21233672 | tf_op jit(solution)/shard_map/ppermute | solution.py:20
  2.9 10.1 %collective-permute-start = (f32[9472]{0:T(1024)S(1)}, f32[9472]{0:T(1024)S(1)}, u32[]{:S(2)}, u32[]{:S(2)}) collective-permute-start(f32[9472]{0:T(1024)S(1)} %pad_maximum_fusion.1), channel_id=1, source_target_pairs={{64,0},{0,64},{65,1},{1,65},{66,2},{2,66},{67,3},{3,67},{68,4},{4,... | collective-permute-start | bytes 113672 | tf_op jit(solution)/shard_map/ppermute | solution.py:20
  6.4 22.6 %all-to-all-start = ((bf16[8,96,768]{2,1,0:T(8,128)(2,1)}), bf16[8,96,768]{2,1,0:T(8,128)(2,1)}, u32[]{:S(2)}, u32[]{:S(2)}) async-start(bf16[8,96,768]{2,1,0:T(8,128)(2,1)} %pack.1), calls=%async_computation | async-start | bytes 2359296 | tf_op jit(solution)/shard_map/all_to_all | solution.py:38
  32.2 53.6 %collective-permute-start.12 = (bf16[384,3072]{1,0:T(8,128)(2,1)S(1)}, bf16[384,3072]{1,0:T(8,128)(2,1)}, u32[]{:S(2)}, u32[]{:S(2)}) collective-permute-start(bf16[384,3072]{1,0:T(8,128)(2,1)S(1)} %bitcast.40), channel_id=1, source_target_pairs={{64,0},{0,64},{65,1},{1,65},{66,2},{2,66},{67,3},{3,67},{68,4},{4,... | collective-permute-start | bytes 7077896 | tf_op jit(solution)/shard_map/ppermute | solution.py:20
  34.2 12.8 %collective-permute-start.2 = (bf16[256,768]{1,0:T(8,128)(2,1)S(1)}, bf16[256,768]{1,0:T(8,128)(2,1)S(1)}, u32[]{:S(2)}, u32[]{:S(2)}) collective-permute-start(bf16[256,768]{1,0:T(8,128)(2,1)S(1)} %bitcast.44), channel_id=1, source_target_pairs={{2,0},{3,1},{0,2},{1,3},{6,4},{7,5},{4,6},{5,7},{10,8},{11,9},{8,1... | collective-permute-start | bytes 1179656 | tf_op jit(solution)/shard_map/ppermute | solution.py:20
  37.8 18.1 %collective-permute-start.3 = (bf16[256,768]{1,0:T(8,128)(2,1)S(1)}, bf16[256,768]{1,0:T(8,128)(2,1)}, u32[]{:S(2)}, u32[]{:S(2)}) collective-permute-start(bf16[256,768]{1,0:T(8,128)(2,1)S(1)} %bitcast.45), channel_id=1, source_target_pairs={{1,0},{2,1},{3,2},{0,3},{5,4},{6,5},{7,6},{4,7},{9,8},{10,9},{11,1... | collective-permute-start | bytes 1179656 | tf_op jit(solution)/shard_map/ppermute | solution.py:20
  38.3 17.7 %collective-permute-start.4 = (bf16[256,768]{1,0:T(8,128)(2,1)S(1)}, bf16[256,768]{1,0:T(8,128)(2,1)}, u32[]{:S(2)}, u32[]{:S(2)}) collective-permute-start(bf16[256,768]{1,0:T(8,128)(2,1)S(1)} %bitcast.46), channel_id=1, source_target_pairs={{3,0},{0,1},{1,2},{2,3},{7,4},{4,5},{5,6},{6,7},{11,8},{8,9},{9,10... | collective-permute-start | bytes 1179656 | tf_op jit(solution)/shard_map/ppermute | solution.py:20
  64.3 17.0 %collective-permute-start.10 = (bf16[8,32,768]{2,1,0:T(8,128)(2,1)S(1)}, bf16[8,32,768]{2,1,0:T(8,128)(2,1)S(1)}, u32[]{:S(2)}, u32[]{:S(2)}) collective-permute-start(bf16[8,32,768]{2,1,0:T(8,128)(2,1)S(1)} %get-tuple-element.64), channel_id=1, source_target_pairs={{48,0},{20,32},{52,4},{24,36},{56,8},{28,40},{60,12},{0,44},{32,16... | collective-permute-start | bytes 1179656 | tf_op jit(solution)/shard_map/ppermute | solution.py:46
  68.5 10.0 %collective-permute-start.8 = (bf16[3,32,768]{2,1,0:T(8,128)(2,1)S(1)}, bf16[3,32,768]{2,1,0:T(8,128)(2,1)S(1)}, u32[]{:S(2)}, u32[]{:S(2)}) collective-permute-start(bf16[3,32,768]{2,1,0:T(8,128)(2,1)S(1)} %get-tuple-element.62), channel_id=1, source_target_pairs={{60,0},{0,32},{32,4},{4,36},{36,8},{8,40},{40,12},{12,44},{44,16},... | collective-permute-start | bytes 442376 | tf_op jit(solution)/shard_map/ppermute | solution.py:46
  68.5 10.0 %collective-permute-start.9 = (bf16[3,32,768]{2,1,0:T(8,128)(2,1)S(1)}, bf16[3,32,768]{2,1,0:T(8,128)(2,1)S(1)}, u32[]{:S(2)}, u32[]{:S(2)}) collective-permute-start(bf16[3,32,768]{2,1,0:T(8,128)(2,1)S(1)} %get-tuple-element.63), channel_id=1, source_target_pairs={{32,0},{4,32},{36,4},{8,36},{40,8},{12,40},{44,12},{16,44},{48,16}... | collective-permute-start | bytes 442376 | tf_op jit(solution)/shard_map/ppermute | solution.py:46
  92.1 12.6 %collective-permute-start.15 = (bf16[256,768]{1,0:T(8,128)(2,1)S(1)}, bf16[256,768]{1,0:T(8,128)(2,1)S(1)}, u32[]{:S(2)}, u32[]{:S(2)}) collective-permute-start(bf16[256,768]{1,0:T(8,128)(2,1)S(1)} %get-tuple-element.73), channel_id=1, source_target_pairs={{2,0},{3,1},{0,2},{1,3},{6,4},{7,5},{4,6},{5,7},{10,8},{11,9},{8,1... | collective-permute-start | bytes 1179656 | tf_op jit(solution)/shard_map/ppermute | solution.py:20
  95.0 18.2 %collective-permute-start.13 = (bf16[256,768]{1,0:T(8,128)(2,1)}, bf16[256,768]{1,0:T(8,128)(2,1)}, u32[]{:S(2)}, u32[]{:S(2)}) collective-permute-start(bf16[256,768]{1,0:T(8,128)(2,1)} %get-tuple-element.71), channel_id=1, source_target_pairs={{3,0},{0,1},{1,2},{2,3},{7,4},{4,5},{5,6},{6,7},{11,8},{8,9},{9,10... | collective-permute-start | bytes 1179656 | tf_op jit(solution)/shard_map/ppermute | solution.py:20
  95.7 18.2 %collective-permute-start.14 = (bf16[256,768]{1,0:T(8,128)(2,1)}, bf16[256,768]{1,0:T(8,128)(2,1)}, u32[]{:S(2)}, u32[]{:S(2)}) collective-permute-start(bf16[256,768]{1,0:T(8,128)(2,1)} %get-tuple-element.72), channel_id=1, source_target_pairs={{1,0},{2,1},{3,2},{0,3},{5,4},{6,5},{7,6},{4,7},{9,8},{10,9},{11,1... | collective-permute-start | bytes 1179656 | tf_op jit(solution)/shard_map/ppermute | solution.py:20
  104.7 12.3 %all-to-all-start.1 = ((bf16[8,32,768]{2,1,0:T(8,128)(2,1)}), bf16[8,32,768]{2,1,0:T(8,128)(2,1)S(1)}, u32[]{:S(2)}, u32[]{:S(2)}) async-start(bf16[8,32,768]{2,1,0:T(8,128)(2,1)} %get-tuple-element.74.own), calls=%async_computation.1 | async-start | bytes 786432 | tf_op jit(solution)/shard_map/all_to_all | solution.py:38
  121.8 11.5 %collective-permute-start.16 = (bf16[256,768]{1,0:T(8,128)(2,1)S(1)}, bf16[256,768]{1,0:T(8,128)(2,1)S(1)}, u32[]{:S(2)}, u32[]{:S(2)}) collective-permute-start(bf16[256,768]{1,0:T(8,128)(2,1)S(1)} %finish.2.refs_3_.hidden), channel_id=1, source_target_pairs={{2,0},{3,1},{0,2},{1,3},{6,4},{7,5},{4,6},{5,7},{10,8},{11,9},{8,1... | collective-permute-start | bytes 1179656 | tf_op jit(solution)/shard_map/ppermute | solution.py:20
  124.8 17.7 %collective-permute-start.17 = (bf16[256,768]{1,0:T(8,128)(2,1)S(1)}, bf16[256,768]{1,0:T(8,128)(2,1)S(1)}, u32[]{:S(2)}, u32[]{:S(2)}) collective-permute-start(bf16[256,768]{1,0:T(8,128)(2,1)S(1)} %finish.2.refs_3_.hidden), channel_id=1, source_target_pairs={{1,0},{2,1},{3,2},{0,3},{5,4},{6,5},{7,6},{4,7},{9,8},{10,9},{11,1... | collective-permute-start | bytes 1179656 | tf_op jit(solution)/shard_map/ppermute | solution.py:20
  125.3 17.6 %collective-permute-start.18 = (bf16[256,768]{1,0:T(8,128)(2,1)S(1)}, bf16[256,768]{1,0:T(8,128)(2,1)S(1)}, u32[]{:S(2)}, u32[]{:S(2)}) collective-permute-start(bf16[256,768]{1,0:T(8,128)(2,1)S(1)} %finish.2.refs_3_.hidden), channel_id=1, source_target_pairs={{3,0},{0,1},{1,2},{2,3},{7,4},{4,5},{5,6},{6,7},{11,8},{8,9},{9,10... | collective-permute-start | bytes 1179656 | tf_op jit(solution)/shard_map/ppermute | solution.py:20
  152.4 17.1 %collective-permute-start.22 = (bf16[8,32,768]{2,1,0:T(8,128)(2,1)S(1)}, bf16[8,32,768]{2,1,0:T(8,128)(2,1)S(1)}, u32[]{:S(2)}, u32[]{:S(2)}) collective-permute-start(bf16[8,32,768]{2,1,0:T(8,128)(2,1)S(1)} %get-tuple-element.87), channel_id=1, source_target_pairs={{48,0},{20,32},{52,4},{24,36},{56,8},{28,40},{60,12},{0,44},{32,16... | collective-permute-start | bytes 1179656 | tf_op jit(solution)/shard_map/ppermute | solution.py:46
  156.0 10.7 %collective-permute-start.20 = (bf16[3,32,768]{2,1,0:T(8,128)(2,1)S(1)}, bf16[3,32,768]{2,1,0:T(8,128)(2,1)S(1)}, u32[]{:S(2)}, u32[]{:S(2)}) collective-permute-start(bf16[3,32,768]{2,1,0:T(8,128)(2,1)S(1)} %get-tuple-element.85), channel_id=1, source_target_pairs={{60,0},{0,32},{32,4},{4,36},{36,8},{8,40},{40,12},{12,44},{44,16},... | collective-permute-start | bytes 442376 | tf_op jit(solution)/shard_map/ppermute | solution.py:46
  157.0 9.7 %collective-permute-start.21 = (bf16[3,32,768]{2,1,0:T(8,128)(2,1)S(1)}, bf16[3,32,768]{2,1,0:T(8,128)(2,1)S(1)}, u32[]{:S(2)}, u32[]{:S(2)}) collective-permute-start(bf16[3,32,768]{2,1,0:T(8,128)(2,1)S(1)} %get-tuple-element.86), channel_id=1, source_target_pairs={{32,0},{4,32},{36,4},{8,36},{40,8},{12,40},{44,12},{16,44},{48,16}... | collective-permute-start | bytes 442376 | tf_op jit(solution)/shard_map/ppermute | solution.py:46
  178.6 10.9 %collective-permute-start.26 = (bf16[256,768]{1,0:T(8,128)(2,1)S(1)}, bf16[256,768]{1,0:T(8,128)(2,1)S(1)}, u32[]{:S(2)}, u32[]{:S(2)}) collective-permute-start(bf16[256,768]{1,0:T(8,128)(2,1)S(1)} %get-tuple-element.95), channel_id=1, source_target_pairs={{2,0},{3,1},{0,2},{1,3},{6,4},{7,5},{4,6},{5,7},{10,8},{11,9},{8,1... | collective-permute-start | bytes 1179656 | tf_op jit(solution)/shard_map/ppermute | solution.py:20
  189.5 17.2 %all-to-all-start.2 = ((bf16[8,64,768]{2,1,0:T(8,128)(2,1)}), bf16[8,64,768]{2,1,0:T(8,128)(2,1)}, u32[]{:S(2)}, u32[]{:S(2)}) async-start(bf16[8,64,768]{2,1,0:T(8,128)(2,1)} %pad_maximum_fusion), calls=%async_computation.2 | async-start | bytes 1572864 | tf_op jit(solution)/shard_map/all_to_all | solution.py:38
  193.9 10.8 %collective-permute-start.24 = (bf16[256,768]{1,0:T(8,128)(2,1)}, bf16[256,768]{1,0:T(8,128)(2,1)S(1)}, u32[]{:S(2)}, u32[]{:S(2)}) collective-permute-start(bf16[256,768]{1,0:T(8,128)(2,1)} %get-tuple-element.93), channel_id=1, source_target_pairs={{3,0},{0,1},{1,2},{2,3},{7,4},{4,5},{5,6},{6,7},{11,8},{8,9},{9,10... | collective-permute-start | bytes 1179656 | tf_op jit(solution)/shard_map/ppermute | solution.py:20
  195.1 9.6 %collective-permute-start.25 = (bf16[256,768]{1,0:T(8,128)(2,1)S(1)}, bf16[256,768]{1,0:T(8,128)(2,1)S(1)}, u32[]{:S(2)}, u32[]{:S(2)}) collective-permute-start(bf16[256,768]{1,0:T(8,128)(2,1)S(1)} %get-tuple-element.94), channel_id=1, source_target_pairs={{1,0},{2,1},{3,2},{0,3},{5,4},{6,5},{7,6},{4,7},{9,8},{10,9},{11,1... | collective-permute-start | bytes 1179656 | tf_op jit(solution)/shard_map/ppermute | solution.py:20
  (39 other events, 403.4 us)

commit v8 on v5

--- a/solution.py
+++ b/solution.py
@@ -46,33 +46,99 @@
     return lax.ppermute(block, "seq", route)
 
 
-def collect_kernel(core, early, late, handed, cache):
-    cols = cache.shape[-1]
+def halve_kernel(core, stale, mine, theirs, sems):
+    rows, cols = mine.shape[1], stale.shape[-1]
+    copies = []
+    for place, out in enumerate((mine, theirs)):
+        first = core[0] if place == 0 else 1 - core[0]
+        first = pl.multiple_of(first * rows, rows)
+        for half in range(2):
+            copies.append(
+                pltpu.make_async_copy(
+                    stale.at[half, :, pl.ds(first, rows)],
+                    out.at[:, :, half * cols : (half + 1) * cols],
+                    sems.at[2 * place + half],
+                )
+            )
+    for copy in copies:
+        copy.start()
+    for copy in copies:
+        copy.wait()
+
+
+def halve(core, stale):
+    _, patches, rows, cols = stale.shape
+    return pl.pallas_call(
+        halve_kernel,
+        in_specs=[SCALARS, ANYWHERE],
+        out_specs=[ON_CHIP] * 2,
+        out_shape=[struct((patches, rows // 2, 2 * cols))] * 2,
+        scratch_shapes=[pltpu.SemaphoreType.DMA((4,))],
+        compiler_params=params(8),
+        name="halve",
+    )(core, stale)
+
+
+def join_kernel(upper, lower, out, sems):
+    rows = upper.shape[1]
+    copies = [
+        pltpu.make_async_copy(upper, out.at[:, :rows], sems.at[0]),
+        pltpu.make_async_copy(lower, out.at[:, rows:], sems.at[1]),
+    ]
+    for copy in copies:
+        copy.start()
+    for copy in copies:
+        copy.wait()
+
+
+def join(upper, lower):
+    tiles, rows, cols = upper.shape
+    return pl.pallas_call(
+        join_kernel,
+        in_specs=[ANYWHERE] * 2,
+        out_specs=ON_CHIP,
+        out_shape=struct((tiles, 2 * rows, cols)),
+        scratch_shapes=[pltpu.SemaphoreType.DMA((2,))],
+        compiler_params=params(8),
+        name="join",
+    )(upper, lower)
+
+
+def collect_kernel(core, early, late, got1, got2, handed, cache):
+    rows, cols = got1.shape[1], cache.shape[-1]
+    upper, lower = slice(0, rows), slice(rows, 2 * rows)
 
     def collect(features, keys):
-        handed[...] = features[...]
-        cache[0] = keys[:, :, :cols]
-        cache[1] = keys[:, :, cols:]
+        for half in range(2):
+            here = slice(half * rows, (half + 1) * rows)
+            ref, there = features[half]
+            handed[:, here] = ref[:, there]
+            ref, there = keys[half]
+            for which in range(2):
+                cache[which, :, here] = ref[:, there, which * cols : (which + 1) * cols]
 
     @pl.when(core[0] == 0)
     def _():
-        collect(late, early)
+        collect(((late, lower), (got2, upper)), ((early, upper), (got1, upper)))
 
     @pl.when(core[0] == 1)
     def _():
-        collect(early, late)
-
-
-def collect(core, early, late):
-    patches, rows, cols = early.shape
+        collect(((got1, upper), (early, lower)), ((got2, upper), (late, upper)))
+
+
+def collect(core, early, late, got1, got2):
+    patches, rows, cols = got1.shape
     return pl.pallas_call(
         collect_kernel,
-        in_specs=[SCALARS] + [ON_CHIP] * 2,
+        in_specs=[SCALARS] + [ON_CHIP] * 4,
         out_specs=[ON_CHIP] * 2,
-        out_shape=[struct(early.shape), struct((2, patches, rows, cols // 2))],
+        out_shape=[
+            struct((patches, 2 * rows, cols)),
+            struct((2, patches, 2 * rows, cols // 2)),
+        ],
         compiler_params=params(8),
         name="collect",
-    )(core, early, late)
+    )(core, early, late, got1, got2)
 
 
 def choose(meta, kv, stale, outs):
@@ -216,7 +282,7 @@
             pltpu.VMEM((3, parts * cols, heads_cols), jnp.bfloat16),
             pltpu.SemaphoreType.DMA((2 * parts,)),
         ],
-        compiler_params=params(56),
+        compiler_params=params(52),
         name="project",
     )(meta, *blocks, shift, scale, gain, w_own, w_other, *extra)
 
@@ -334,25 +400,9 @@
     )(q_own, q_other, below, above, far, multiple, before)
 
 
-def spread_kernel(
-    meta, part_a, part_b, wo_own, wo_other, keep, to_next, to_across, to_prev, att, weights, sems
-):
+def merge_kernel(part_a, part_b, att):
     tiles, rows, _ = part_a.shape
-    parts, heads_cols, cols = weights.shape
-
-    def fetch(j, source):
-        first = pl.multiple_of(lax.rem(meta[0] + j, parts) * cols, cols)
-        return pltpu.make_async_copy(
-            source.at[:, pl.ds(first, cols)], weights.at[j], sems.at[j]
-        )
-
-    for chosen, source in enumerate((wo_other, wo_own)):
-
-        @pl.when(meta[1] == chosen)
-        def _():
-            for j in range(parts):
-                fetch(j, source).start()
-
+    heads_cols = att.shape[-1]
     extra_a = part_a[:, :, heads_cols:].reshape(tiles * rows, HEAD_DIM)
     extra_b = part_b[:, :, heads_cols:].reshape(tiles * rows, HEAD_DIM)
     for head, cut in enumerate(head_cuts(heads_cols)):
@@ -366,49 +416,57 @@
         att[:, cut] = (summed_a * (grow_a / total) + summed_b * (grow_b / total)).astype(
             jnp.bfloat16
         )
+
+
+def merge(part_a, part_b):
+    tiles, rows, cols = part_a.shape
+    return pl.pallas_call(
+        merge_kernel,
+        in_specs=[ON_CHIP] * 2,
+        out_specs=ON_CHIP,
+        out_shape=struct((tiles * rows, cols - HEAD_DIM)),
+        compiler_params=params(8),
+        name="merge",
+    )(part_a, part_b)
+
+
+def output_kernel(meta, *refs):
+    *refs, out, weights, sems = refs
+    parts = weights.shape[0]
+    atts, refs = refs[:parts], refs[parts:]
+    own, other, (hidden, gates) = refs[:parts], refs[parts : 2 * parts], refs[2 * parts :]
+
+    def fetch(j, sources):
+        return pltpu.make_async_copy(sources[j], weights.at[j], sems.at[j])
+
+    for chosen, sources in enumerate((other, own)):
+
+        @pl.when(meta[1] == chosen)
+        def _():
+            for j in range(parts):
+                fetch(j, sources).start()
+
+    product = jnp.zeros(out.shape, jnp.float32)
     for j in range(parts):
-        fetch(j, wo_own).wait()
-    for j, out in enumerate((keep, to_next, to_across, to_prev)):
-        product = jnp.dot(att[...], weights[j], preferred_element_type=jnp.float32)
-        out[...] = product.astype(out.dtype)
-
-
-def spread(meta, part_a, part_b, wo_own, wo_other, parts):
-    tiles, rows, _ = part_a.shape
-    heads_cols, width = wo_own.shape
-    shape = (tiles * rows, width // parts)
-    return pl.pallas_call(
-        spread_kernel,
-        in_specs=[SCALARS] + [ON_CHIP] * 2 + [ANYWHERE] * 2,
-        out_specs=[ON_CHIP] * 4,
-        out_shape=[struct(shape, jnp.float32)] + [struct(shape)] * 3,
+        fetch(j, own).wait()
+        product += jnp.dot(atts[j][...], weights[j], preferred_element_type=jnp.float32)
+    out[...] = (hidden[...].astype(jnp.float32) + gates[meta[0]] * product).astype(out.dtype)
+
+
+def output(meta, atts, own, other, hidden, gates):
+    parts = len(atts)
+    return pl.pallas_call(
+        output_kernel,
+        in_specs=[SCALARS] + [ON_CHIP] * parts + [ANYWHERE] * (2 * parts) + [ON_CHIP] * 2,
+        out_specs=ON_CHIP,
+        out_shape=struct(hidden.shape),
         scratch_shapes=[
-            pltpu.VMEM((tiles * rows, heads_cols), jnp.bfloat16),
-            pltpu.VMEM((parts, heads_cols, width // parts), jnp.bfloat16),
+            pltpu.VMEM((parts,) + own[0].shape, jnp.bfloat16),
             pltpu.SemaphoreType.DMA((parts,)),
         ],
         compiler_params=params(12),
-        name="spread",
-    )(meta, part_a, part_b, wo_own, wo_other)
-
-
-def finish_kernel(meta, from_across, from_prev, from_next, keep, hidden, gates, out):
-    total = keep[...]
-    for part in (from_prev, from_across, from_next):
-        total += part[...].astype(jnp.float32)
-    gate = gates[meta[0]]
-    out[...] = (hidden[...].astype(jnp.float32) + gate * total).astype(out.dtype)
-
-
-def finish(meta, from_across, from_prev, from_next, keep, hidden, gates):
-    return pl.pallas_call(
-        finish_kernel,
-        in_specs=[SCALARS] + [ON_CHIP] * 6,
-        out_specs=ON_CHIP,
-        out_shape=struct(hidden.shape),
-        compiler_params=params(8),
-        name="finish",
-    )(meta, from_across, from_prev, from_next, keep, hidden, gates)
+        name="output",
+    )(meta, *atts, *own, *other, hidden, gates)
 
 
 def count_tiles(table, counts, chip, per_chip, repeat):
@@ -456,18 +514,16 @@
     heads_cols, width = w_out.shape[1:]
     head_dim = qk_gain.shape[-1]
 
+    core_scalar = core.astype(jnp.int32)[None]
     mine = lax.dynamic_slice_in_dim(latents, core * rows_core, rows_core, 1)
     hidden = exchanged(mine).reshape(rows, part_cols)
+    stale, stale_send = halve(core_scalar, after(stale_cache[0], mine))
+    stale = join(stale, shifted(stale_send, "segment", 1))
+    hidden, stale = lax.optimization_barrier((hidden, stale))
     w_other = shifted(w_own, "segment", 1)
     small_own = jnp.concatenate([modulation[0].reshape(-1), qk_gain[0].reshape(-1)])
     small_other = shifted(small_own, "segment", 1)
-    stale = after(stale_cache[0], mine)
-    stale = jnp.concatenate([stale[0], stale[1]], axis=-1)
-    stale_own = lax.dynamic_slice_in_dim(stale, core * rows_core, rows_core, 1)
-    stale_other = shifted(
-        lax.dynamic_slice_in_dim(stale, (1 - core) * rows_core, rows_core, 1), "segment", 1
-    )
-    stale = jnp.concatenate([stale_own, stale_other], axis=1)
+    kv_tiles, tile_counts = after((kv_tiles, tile_counts), small_other)
     turns = jnp.arange(patches, dtype=jnp.int32)
     asked = jnp.stack([chip, chip - 1, chip + 1, chip - seq_size // 2 - 1]) % seq_size // share
     ranks = jnp.sum(jnp.where(patch_order[None] == asked[:, None], turns[None], 0), axis=-1)
@@ -487,17 +543,23 @@
         given.append(
             (meta, modul[0], modul[1], modul[2], gain, multiple[..., :256], multiple[..., 256:])
         )
-    hidden, given, stale, w_out = lax.optimization_barrier((hidden, given, stale, w_out))
-    wo_own = w_out[0]
-    wo_other = shifted(wo_own, "segment", 1)
+    slices = [
+        lax.dynamic_slice_in_dim(
+            w_out[0], lax.rem(tp_pos + j, tp_size) * part_cols, part_cols, 1
+        )
+        for j in range(tp_size)
+    ]
 
     for section in range(2):
-        meta, shift, scale, gates, gain, times_own, times_rest = given[section]
         blocks = gather_features(hidden)
         if section == 0:
-            stale = exchanged(after(stale, blocks[1], blocks[2]))
+            stale = exchanged(after(stale, blocks[0]))
+            blocks, given, slices = lax.optimization_barrier((blocks, given, slices))
         else:
-            early = exchanged(after(early, blocks[1], blocks[2]))
+            early = join(kv, hidden.reshape(kv.shape))
+            early = exchanged(after(early, blocks[0]))
+            blocks, early = lax.optimization_barrier((blocks, early))
+        meta, shift, scale, gates, gain, times_own, times_rest = given[section]
         q_own, kv, *going = project(
             meta,
             blocks,
@@ -507,7 +569,7 @@
             w_own,
             w_other,
             stale if section > 0 else None,
-            stale_own.shape,
+            (patches, rows_core, 2 * heads_cols),
         )
         if section == 0:
             going = choose_alone(meta, kv, stale)
@@ -516,32 +578,26 @@
         above = along_ring(to_below, 1, patches)
         below = along_ring(to_above, -1, patches)
         q_other = shifted(q_own, "segment", 1)
-        if section > 0:
-            above, early = lax.optimization_barrier((above, early))
+        if section == 0:
+            slices = after(slices, q_other)
+            wo_own = slices[:1] + [shifted(slices[j], "tp", j) for j in range(1, tp_size)]
         before = attend_own(q_own, q_other, kv, times_own)
         part_own, part_other = attend_rest(
             q_own, q_other, below, above, far, times_rest, before
         )
         part_back = shifted(part_other, "segment", 1)
-        keep, to_next, to_across, to_prev = spread(
-            meta, part_own, part_back, wo_own, wo_other, tp_size
-        )
-        from_across = shifted(to_across, "tp", 2)
-        from_prev = shifted(to_next, "tp", 1)
-        from_next = shifted(to_prev, "tp", -1)
-        hidden = finish(meta, from_across, from_prev, from_next, keep, hidden, gates)
-
-        features = hidden.reshape(patches, rows_core, part_cols)
-        pair = (kv, features) if section == 0 else (features, kv)
-        got = shifted(jnp.where(core == 0, pair[1], pair[0]), "segment", 1)
-        own = jnp.where(core == 0, pair[0], pair[1])
-        halves = [jnp.where(core == place, own, got) for place in range(2)]
+        att = merge(part_own, part_back)
+        across = shifted(att, "tp", 2)
+        atts = [att, shifted(att, "tp", 1), across, shifted(att, "tp", 3)]
         if section == 0:
-            early = jnp.concatenate(halves, axis=1)
-        else:
-            late = exchanged(jnp.concatenate(halves, axis=1))
-
-    handed, new_cache = collect(core.astype(jnp.int32)[None], early, late)
+            wo_other = [shifted(piece, "segment", 1) for piece in after(wo_own, across)]
+        hidden = output(meta, atts, wo_own, wo_other, hidden, gates)
+
+    late = exchanged(join(kv, hidden.reshape(kv.shape)))
+    keys, features = slice(0, rows_core), slice(rows_core, 2 * rows_core)
+    got1 = shifted(jnp.where(core == 0, early[:, features], early[:, keys]), "segment", 1)
+    got2 = shifted(jnp.where(core == 0, late[:, keys], late[:, features]), "segment", 1)
+    handed, new_cache = collect(core_scalar, early, late, got1, got2)
     return (handed[None], new_cache[None])
 
 

time: 227 us -> 236 us (1.040)
  waiting for transfers between devices: 82.1 us -> 101 us
  blocking collectives: 17.4 us -> 0 us
  starting transfers between devices: 58.6 us -> 75.3 us
  other arithmetic: 9.07 us -> 2.79 us
  Pallas kernels: 37.7 us -> 33.8 us
    all_to_all x1 -> x0, blocking collectives: 17.4 us -> none  [exchanged(): return lax.all_to_all(tiles, 'seq', 0, 0, axis_index_groups=groups)]
    all_to_all x3 -> x4, waiting for transfers between devices: 0.01 us -> 15.6 us  [exchanged(): return lax.all_to_all(tiles, 'seq', 0, 0, axis_index_groups=groups)]
    ppermute x23 -> x29, starting transfers between devices: 23.4 us -> 37.7 us  [shifted(): return lax.ppermute(block, axis, route)]
    concatenate x4 -> x0, other arithmetic: 4 us -> none  [the longest x1 2.05 us: local(): stale = jnp.concatenate([stale_own, stale_other], axis=1)]
    all_to_all x3 -> x4, starting transfers between devices: 15.8 us -> 19.1 us  [exchanged(): return lax.all_to_all(tiles, 'seq', 0, 0, axis_index_groups=groups)]
    unnamed x65 -> x78, local copies, waits for them, and re-layouts: 12.3 us -> 13.4 us
    ppermute x23 -> x29, waiting for transfers between devices: 79.3 us -> 80.1 us  [shifted(): return lax.ppermute(block, axis, route)]
    pallas_call x5 -> x9, Pallas kernels: 9.52 us -> 9.03 us  [the longest x2 4.67 us: output(): pl.pallas_call(output_kernel, in_specs=[SCALARS] + [ON_CHIP] * parts + [A...]
  transfers between devices with their start and end apart: 32 -> 39, of which waited for: 16 -> 19; matrix products, arithmetic and copies ran while one was open for 7% -> 4% of each run, Pallas kernels for 11% -> 6%
where the time goes in v8:
time: 236 us; the launch traced here: 234 us
  waiting for transfers between devices  101 us (43%)
  starting transfers between devices  75.3 us (32%)
  Pallas kernels  33.8 us (14%)
  local copies, waits for them, and re-layouts  20.3 us (9%)
  other arithmetic  2.79 us (1%)
    ppermute x29, waiting for transfers between devices, shifted(): return lax.ppermute(block, axis, route)  80.1 us
    ppermute x29, starting transfers between devices, shifted(): return lax.ppermute(block, axis, route)  37.7 us
    all_to_all x4, starting transfers between devices, exchanged(): return lax.all_to_all(tiles, 'seq', 0, 0, axis_index_groups=groups)  19.1 us
    ppermute x6, starting transfers between devices, along_ring(): return lax.ppermute(block, 'seq', route)  18.5 us
    all_to_all x4, waiting for transfers between devices, exchanged(): return lax.all_to_all(tiles, 'seq', 0, 0, axis_index_groups=groups)  15.6 us
    pallas_call x2, Pallas kernels, project(): pl.pallas_call(kernel, in_specs=[SCALARS] + [ANYWHERE] * len(blocks) + [O...  14.9 us
    unnamed x78, local copies, waits for them, and re-layouts  13.4 us
    pallas_call x2, Pallas kernels, attend_own(): pl.pallas_call(attend_own_kernel, in_specs=[ON_CHIP] * 4, out_specs=ON_CH...  4.83 us
  transfers between devices with their start and end apart: 39, of which 19 were waited for; matrix products, arithmetic and copies ran while one was open for 4% of the time, Pallas kernels for 6%

profile of v8, /device:TPU:1, one launch (start us, length us, event | category | flops | bytes accessed | tf_op | source)
XLA Modules:
  0.0 233.9 jit_solution(17741756173359166120)
XLA Ops:
  3.9 5.1 %all-to-all-start = ((bf16[8,32,768]{2,1,0:T(8,128)(2,1)}), bf16[8,32,768]{2,1,0:T(8,128)(2,1)S(1)}, u32[]{:S(2)}, u32[]{:S(2)}) async-start(bf16[8,32,768]{2,1,0:T(8,128)(2,1)} %constant_dynamic-slice_fusion.1), calls=%async_computation | async-start | bytes 786432 | tf_op jit(solution)/shard_map/all_to_all | solution.py:38
  17.8 3.6 %collective-permute-start.1 = (bf16[256,768]{1,0:T(8,128)(2,1)S(1)}, bf16[256,768]{1,0:T(8,128)(2,1)S(1)}, u32[]{:S(2)}, u32[]{:S(2)}) collective-permute-start(bf16[256,768]{1,0:T(8,128)(2,1)S(1)} %bitcast.48), channel_id=1, source_target_pairs={{2,0},{3,1},{0,2},{1,3},{6,4},{7,5},{4,6},{5,7},{10,8},{11,9},{8,1... | collective-permute-start | bytes 1179656 | tf_op jit(solution)/shard_map/ppermute | solution.py:20
  23.0 7.1 %collective-permute-done.1.refs_1_ = bf16[256,768]{1,0:T(8,128)(2,1)S(1)} collective-permute-done((bf16[256,768]{1,0:T(8,128)(2,1)S(1)}, bf16[256,768]{1,0:T(8,128)(2,1)S(1)}, u32[]{:S(2)}, u32[]{:S(2)}) %collective-permute-start.1) | collective-permute-done | bytes 393248 | tf_op jit(solution)/shard_map/ppermute | solution.py:20
  30.1 5.1 %all-to-all-start.1 = ((bf16[8,64,768]{2,1,0:T(8,128)(2,1)}), bf16[8,64,768]{2,1,0:T(8,128)(2,1)S(1)}, u32[]{:S(2)}, u32[]{:S(2)}) async-start(bf16[8,64,768]{2,1,0:T(8,128)(2,1)} %join.3), calls=%async_computation.1 | async-start | bytes 1572864 | tf_op jit(solution)/shard_map/all_to_all | solution.py:38
  41.2 5.9 %collective-permute-done.3.refs_3_ = bf16[256,768]{1,0:T(8,128)(2,1)S(1)} collective-permute-done((bf16[256,768]{1,0:T(8,128)(2,1)S(1)}, bf16[256,768]{1,0:T(8,128)(2,1)S(1)}, u32[]{:S(2)}, u32[]{:S(2)}) %collective-permute-start.3) | collective-permute-done | bytes 393248 | tf_op jit(solution)/shard_map/ppermute | solution.py:20
  47.7 7.1 %project.2 = (bf16[8,32,384]{2,1,0:T(8,128)(2,1)S(1)}, bf16[8,32,768]{2,1,0:T(8,128)(2,1)S(1)}) custom-call(s32[5]{0:T(128)S(1)} %copy-done.28, bf16[256,768]{1,0:T(8,128)(2,1)S(1)} %collective-permute-done.1.refs_1_, bf16[256,768]{1,0:T(8,128)(2,1)S(1)} %collective-permute-done.2.refs_2_, bf16[256,768]{1,0:T(8,128)(2,1)S(1)} %collective-permute-done.3.refs_3_, ...), custom_call_target="tpu_custom_call" | custom-call | tf_op jit(solution)/shard_map/project/pallas_call | solution.py:270
  56.0 4.8 %collective-permute-start.10 = (bf16[8,32,768]{2,1,0:T(8,128)(2,1)S(1)}, bf16[8,32,768]{2,1,0:T(8,128)(2,1)S(1)}, u32[]{:S(2)}, u32[]{:S(2)}) collective-permute-start(bf16[8,32,768]{2,1,0:T(8,128)(2,1)S(1)} %get-tuple-element.82), channel_id=1, source_target_pairs={{48,0},{20,32},{52,4},{24,36},{56,8},{28,40},{60,12},{0,44},{32,16... | collective-permute-start | bytes 1179656 | tf_op jit(solution)/shard_map/ppermute | solution.py:46
  63.1 4.8 %collective-permute-start.9 = (bf16[3,32,768]{2,1,0:T(8,128)(2,1)S(1)}, bf16[3,32,768]{2,1,0:T(8,128)(2,1)S(1)}, u32[]{:S(2)}, u32[]{:S(2)}) collective-permute-start(bf16[3,32,768]{2,1,0:T(8,128)(2,1)S(1)} %get-tuple-element.81), channel_id=1, source_target_pairs={{32,0},{4,32},{36,4},{8,36},{40,8},{12,40},{44,12},{16,44},{48,16}... | collective-permute-start | bytes 442376 | tf_op jit(solution)/shard_map/ppermute | solution.py:46
  83.8 10.7 %collective-permute-done.15.refs_5_ = bf16[384,768]{1,0:T(8,128)(2,1)S(1)} collective-permute-done((bf16[384,768]{1,0:T(8,128)(2,1)}, bf16[384,768]{1,0:T(8,128)(2,1)S(1)}, u32[]{:S(2)}, u32[]{:S(2)}) %collective-permute-start.15) | collective-permute-done | bytes 589856 | tf_op jit(solution)/shard_map/ppermute | solution.py:20
  94.5 13.5 %collective-permute-done.16.refs_6_ = bf16[384,768]{1,0:T(8,128)(2,1)S(1)} collective-permute-done((bf16[384,768]{1,0:T(8,128)(2,1)}, bf16[384,768]{1,0:T(8,128)(2,1)S(1)}, u32[]{:S(2)}, u32[]{:S(2)}) %collective-permute-start.16) | collective-permute-done | bytes 589856 | tf_op jit(solution)/shard_map/ppermute | solution.py:20
  108.0 4.2 %collective-permute-done.13.refs_2_ = bf16[256,384]{1,0:T(8,128)(2,1)S(1)} collective-permute-done((bf16[256,384]{1,0:T(8,128)(2,1)S(1)}, bf16[256,384]{1,0:T(8,128)(2,1)S(1)}, u32[]{:S(2)}, u32[]{:S(2)}) %collective-permute-start.13) | collective-permute-done | bytes 196640 | tf_op jit(solution)/shard_map/ppermute | solution.py:20
  115.7 3.8 %collective-permute-done.14.refs_3_ = bf16[256,384]{1,0:T(8,128)(2,1)S(1)} collective-permute-done((bf16[256,384]{1,0:T(8,128)(2,1)S(1)}, bf16[256,384]{1,0:T(8,128)(2,1)S(1)}, u32[]{:S(2)}, u32[]{:S(2)}) %collective-permute-start.14) | collective-permute-done | bytes 196640 | tf_op jit(solution)/shard_map/ppermute | solution.py:20
  120.7 6.0 %collective-permute-done.12.refs_1_ = bf16[256,384]{1,0:T(8,128)(2,1)S(1)} collective-permute-done((bf16[256,384]{1,0:T(8,128)(2,1)S(1)}, bf16[256,384]{1,0:T(8,128)(2,1)S(1)}, u32[]{:S(2)}, u32[]{:S(2)}) %collective-permute-start.12) | collective-permute-done | bytes 196640 | tf_op jit(solution)/shard_map/ppermute | solution.py:20
  133.2 8.7 %collective-permute-done.22.refs_1_ = bf16[256,768]{1,0:T(8,128)(2,1)S(1)} collective-permute-done((bf16[256,768]{1,0:T(8,128)(2,1)S(1)}, bf16[256,768]{1,0:T(8,128)(2,1)S(1)}, u32[]{:S(2)}, u32[]{:S(2)}) %collective-permute-start.22) | collective-permute-done | bytes 393248 | tf_op jit(solution)/shard_map/ppermute | solution.py:20
  142.7 5.4 %all-to-all-start.2 = ((bf16[8,64,768]{2,1,0:T(8,128)(2,1)}), bf16[8,64,768]{2,1,0:T(8,128)(2,1)S(1)}, u32[]{:S(2)}, u32[]{:S(2)}) async-start(bf16[8,64,768]{2,1,0:T(8,128)(2,1)} %copy-done.6), calls=%async_computation.2 | async-start | bytes 1572864 | tf_op jit(solution)/shard_map/all_to_all | solution.py:38
  150.7 5.9 %collective-permute-done.24.refs_3_ = bf16[256,768]{1,0:T(8,128)(2,1)S(1)} collective-permute-done((bf16[256,768]{1,0:T(8,128)(2,1)S(1)}, bf16[256,768]{1,0:T(8,128)(2,1)S(1)}, u32[]{:S(2)}, u32[]{:S(2)}) %collective-permute-start.24) | collective-permute-done | bytes 393248 | tf_op jit(solution)/shard_map/ppermute | solution.py:20
  163.5 7.8 %project.3 = (bf16[8,32,384]{2,1,0:T(8,128)(2,1)S(1)}, bf16[8,32,768]{2,1,0:T(8,128)(2,1)S(1)}, bf16[3,32,768]{2,1,0:T(8,128)(2,1)S(1)}, bf16[3,32,768]{2,1,0:T(8,128)(2,1)S(1)}, bf16[8,32,768]{2,1,0:T(8,128)(2,1)S(1)}) custom-call(s32[5]{0:T(128)S(1)} %copy-done.31, bf16[256,768]{1,0:T(8,128)(2,1)S(1)} %copy-done.21, ...), custom_call_target="tpu_custom_call" | custom-call | tf_op jit(solution)/shard_map/project/pallas_call | solution.py:270
  171.3 4.2 %collective-permute-start.28 = (bf16[8,32,768]{2,1,0:T(8,128)(2,1)S(1)}, bf16[8,32,768]{2,1,0:T(8,128)(2,1)S(1)}, u32[]{:S(2)}, u32[]{:S(2)}) collective-permute-start(bf16[8,32,768]{2,1,0:T(8,128)(2,1)S(1)} %get-tuple-element.114), channel_id=1, source_target_pairs={{48,0},{20,32},{52,4},{24,36},{56,8},{28,40},{60,12},{0,44},{32,16... | collective-permute-start | bytes 1179656 | tf_op jit(solution)/shard_map/ppermute | solution.py:46
  175.4 4.7 %collective-permute-start.25 = (bf16[8,32,384]{2,1,0:T(8,128)(2,1)S(1)}, bf16[8,32,384]{2,1,0:T(8,128)(2,1)S(1)}, u32[]{:S(2)}, u32[]{:S(2)}) collective-permute-start(bf16[8,32,384]{2,1,0:T(8,128)(2,1)S(1)} %get-tuple-element.111.q_own), channel_id=1, source_target_pairs={{64,0},{0,64},{65,1},{1,65},{66,2},{2,66},{67,3},{3,67},{68,4},{4,... | collective-permute-start | bytes 589832 | tf_op jit(solution)/shard_map/ppermute | solution.py:20
  180.1 4.8 %collective-permute-start.27 = (bf16[3,32,768]{2,1,0:T(8,128)(2,1)S(1)}, bf16[3,32,768]{2,1,0:T(8,128)(2,1)S(1)}, u32[]{:S(2)}, u32[]{:S(2)}) collective-permute-start(bf16[3,32,768]{2,1,0:T(8,128)(2,1)S(1)} %get-tuple-element.113), channel_id=1, source_target_pairs={{32,0},{4,32},{36,4},{8,36},{40,8},{12,40},{44,12},{16,44},{48,16}... | collective-permute-start | bytes 442376 | tf_op jit(solution)/shard_map/ppermute | solution.py:46
  198.1 3.5 %collective-permute-done.32.refs_3_ = bf16[256,384]{1,0:T(8,128)(2,1)S(1)} collective-permute-done((bf16[256,384]{1,0:T(8,128)(2,1)S(1)}, bf16[256,384]{1,0:T(8,128)(2,1)S(1)}, u32[]{:S(2)}, u32[]{:S(2)}) %collective-permute-start.32) | collective-permute-done | bytes 196640 | tf_op jit(solution)/shard_map/ppermute | solution.py:20
  204.9 4.6 %collective-permute-done.30.refs_1_ = bf16[256,384]{1,0:T(8,128)(2,1)S(1)} collective-permute-done((bf16[256,384]{1,0:T(8,128)(2,1)S(1)}, bf16[256,384]{1,0:T(8,128)(2,1)S(1)}, u32[]{:S(2)}, u32[]{:S(2)}) %collective-permute-start.30) | collective-permute-done | bytes 196640 | tf_op jit(solution)/shard_map/ppermute | solution.py:20
  213.8 3.6 %all-to-all-start.3 = ((bf16[8,64,768]{2,1,0:T(8,128)(2,1)}), bf16[8,64,768]{2,1,0:T(8,128)(2,1)S(1)}, u32[]{:S(2)}, u32[]{:S(2)}) async-start(bf16[8,64,768]{2,1,0:T(8,128)(2,1)} %join.5), calls=%async_computation.3 | async-start | bytes 1572864 | tf_op jit(solution)/shard_map/all_to_all | solution.py:38
  218.3 12.0 %all-to-all-done.3.late = bf16[8,64,768]{2,1,0:T(8,128)(2,1)S(1)} async-done(((bf16[8,64,768]{2,1,0:T(8,128)(2,1)}), bf16[8,64,768]{2,1,0:T(8,128)(2,1)S(1)}, u32[]{:S(2)}, u32[]{:S(2)}) %all-to-all-start.3) | async-done | bytes 786464 | tf_op jit(solution)/shard_map/all_to_all | solution.py:38
  (172 shorter events, 85.9 us)
Async XLA Ops:
  0.7 46.4 %collective-permute-start.6 = (bf16[3,3072,384]{2,1,0:T(8,128)(2,1)}, bf16[3,3072,384]{2,1,0:T(8,128)(2,1)}, u32[]{:S(2)}, u32[]{:S(2)}) collective-permute-start(bf16[3,3072,384]{2,1,0:T(8,128)(2,1)} %bitcast.61), channel_id=1, source_target_pairs={{64,0},{0,64},{65,1},{1,65},{66,2},{2,66},{67,3},{3,67},{68,4},{4,... | collective-permute-start | bytes 21233672 | tf_op jit(solution)/shard_map/ppermute | solution.py:20
  3.0 12.6 %collective-permute-start.4 = (f32[9472]{0:T(1024)S(1)}, f32[9472]{0:T(1024)S(1)}, u32[]{:S(2)}, u32[]{:S(2)}) collective-permute-start(f32[9472]{0:T(1024)S(1)} %pad_maximum_fusion), channel_id=1, source_target_pairs={{64,0},{0,64},{65,1},{1,65},{66,2},{2,66},{67,3},{3,67},{68,4},{4,... | collective-permute-start | bytes 113672 | tf_op jit(solution)/shard_map/ppermute | solution.py:20
  3.9 13.9 %all-to-all-start = ((bf16[8,32,768]{2,1,0:T(8,128)(2,1)}), bf16[8,32,768]{2,1,0:T(8,128)(2,1)S(1)}, u32[]{:S(2)}, u32[]{:S(2)}) async-start(bf16[8,32,768]{2,1,0:T(8,128)(2,1)} %constant_dynamic-slice_fusion.1), calls=%async_computation | async-start | bytes 786432 | tf_op jit(solution)/shard_map/all_to_all | solution.py:38
  17.8 12.3 %collective-permute-start.1 = (bf16[256,768]{1,0:T(8,128)(2,1)S(1)}, bf16[256,768]{1,0:T(8,128)(2,1)S(1)}, u32[]{:S(2)}, u32[]{:S(2)}) collective-permute-start(bf16[256,768]{1,0:T(8,128)(2,1)S(1)} %bitcast.48), channel_id=1, source_target_pairs={{2,0},{3,1},{0,2},{1,3},{6,4},{7,5},{4,6},{5,7},{10,8},{11,9},{8,1... | collective-permute-start | bytes 1179656 | tf_op jit(solution)/shard_map/ppermute | solution.py:20
  21.8 17.5 %collective-permute-start.5 = (f32[8,1,384]{2,1,0:T(1,128)S(1)}, f32[8,1,384]{2,1,0:T(1,128)S(1)}, u32[]{:S(2)}, u32[]{:S(2)}) collective-permute-start(f32[8,1,384]{2,1,0:T(1,128)S(1)} %broadcast_in_dim.36), channel_id=1, source_target_pairs={{64,0},{0,64},{65,1},{1,65},{66,2},{2,66},{67,3},{3,67},{68,4},{4,... | collective-permute-start | bytes 36872 | tf_op jit(solution)/shard_map/ppermute | solution.py:20
  30.1 24.7 %all-to-all-start.1 = ((bf16[8,64,768]{2,1,0:T(8,128)(2,1)}), bf16[8,64,768]{2,1,0:T(8,128)(2,1)S(1)}, u32[]{:S(2)}, u32[]{:S(2)}) async-start(bf16[8,64,768]{2,1,0:T(8,128)(2,1)} %join.3), calls=%async_computation.1 | async-start | bytes 1572864 | tf_op jit(solution)/shard_map/all_to_all | solution.py:38
  35.8 11.2 %collective-permute-start.3 = (bf16[256,768]{1,0:T(8,128)(2,1)S(1)}, bf16[256,768]{1,0:T(8,128)(2,1)S(1)}, u32[]{:S(2)}, u32[]{:S(2)}) collective-permute-start(bf16[256,768]{1,0:T(8,128)(2,1)S(1)} %bitcast.49), channel_id=1, source_target_pairs={{3,0},{0,1},{1,2},{2,3},{7,4},{4,5},{5,6},{6,7},{11,8},{8,9},{9,10... | collective-permute-start | bytes 1179656 | tf_op jit(solution)/shard_map/ppermute | solution.py:20
  36.6 10.4 %collective-permute-start.2 = (bf16[256,768]{1,0:T(8,128)(2,1)S(1)}, bf16[256,768]{1,0:T(8,128)(2,1)S(1)}, u32[]{:S(2)}, u32[]{:S(2)}) collective-permute-start(bf16[256,768]{1,0:T(8,128)(2,1)S(1)} %bitcast.50), channel_id=1, source_target_pairs={{1,0},{2,1},{3,2},{0,3},{5,4},{6,5},{7,6},{4,7},{9,8},{10,9},{11,1... | collective-permute-start | bytes 1179656 | tf_op jit(solution)/shard_map/ppermute | solution.py:20
  56.0 17.1 %collective-permute-start.10 = (bf16[8,32,768]{2,1,0:T(8,128)(2,1)S(1)}, bf16[8,32,768]{2,1,0:T(8,128)(2,1)S(1)}, u32[]{:S(2)}, u32[]{:S(2)}) collective-permute-start(bf16[8,32,768]{2,1,0:T(8,128)(2,1)S(1)} %get-tuple-element.82), channel_id=1, source_target_pairs={{48,0},{20,32},{52,4},{24,36},{56,8},{28,40},{60,12},{0,44},{32,16... | collective-permute-start | bytes 1179656 | tf_op jit(solution)/shard_map/ppermute | solution.py:46
  63.1 10.0 %collective-permute-start.8 = (bf16[3,32,768]{2,1,0:T(8,128)(2,1)S(1)}, bf16[3,32,768]{2,1,0:T(8,128)(2,1)S(1)}, u32[]{:S(2)}, u32[]{:S(2)}) collective-permute-start(bf16[3,32,768]{2,1,0:T(8,128)(2,1)S(1)} %get-tuple-element.80), channel_id=1, source_target_pairs={{60,0},{0,32},{32,4},{4,36},{36,8},{8,40},{40,12},{12,44},{44,16},... | collective-permute-start | bytes 442376 | tf_op jit(solution)/shard_map/ppermute | solution.py:46
  78.2 16.3 %collective-permute-start.15 = (bf16[384,768]{1,0:T(8,128)(2,1)}, bf16[384,768]{1,0:T(8,128)(2,1)S(1)}, u32[]{:S(2)}, u32[]{:S(2)}) collective-permute-start(bf16[384,768]{1,0:T(8,128)(2,1)} %get-tuple-element.92), channel_id=1, source_target_pairs={{3,0},{0,1},{1,2},{2,3},{7,4},{4,5},{5,6},{6,7},{11,8},{8,9},{9,10... | collective-permute-start | bytes 1769480 | tf_op jit(solution)/shard_map/ppermute | solution.py:20
  78.6 29.4 %collective-permute-start.16 = (bf16[384,768]{1,0:T(8,128)(2,1)}, bf16[384,768]{1,0:T(8,128)(2,1)S(1)}, u32[]{:S(2)}, u32[]{:S(2)}) collective-permute-start(bf16[384,768]{1,0:T(8,128)(2,1)} %get-tuple-element.93), channel_id=1, source_target_pairs={{2,0},{3,1},{0,2},{1,3},{6,4},{7,5},{4,6},{5,7},{10,8},{11,9},{8,1... | collective-permute-start | bytes 1769480 | tf_op jit(solution)/shard_map/ppermute | solution.py:20
  81.7 26.3 %collective-permute-start.17 = (bf16[384,768]{1,0:T(8,128)(2,1)}, bf16[384,768]{1,0:T(8,128)(2,1)S(1)}, u32[]{:S(2)}, u32[]{:S(2)}) collective-permute-start(bf16[384,768]{1,0:T(8,128)(2,1)} %get-tuple-element.94), channel_id=1, source_target_pairs={{1,0},{2,1},{3,2},{0,3},{5,4},{6,5},{7,6},{4,7},{9,8},{10,9},{11,1... | collective-permute-start | bytes 1769480 | tf_op jit(solution)/shard_map/ppermute | solution.py:20
  82.8 29.4 %collective-permute-start.13 = (bf16[256,384]{1,0:T(8,128)(2,1)S(1)}, bf16[256,384]{1,0:T(8,128)(2,1)S(1)}, u32[]{:S(2)}, u32[]{:S(2)}) collective-permute-start(bf16[256,384]{1,0:T(8,128)(2,1)S(1)} %merge.2.refs_0_), channel_id=1, source_target_pairs={{2,0},{3,1},{0,2},{1,3},{6,4},{7,5},{4,6},{5,7},{10,8},{11,9},{8,1... | collective-permute-start | bytes 589832 | tf_op jit(solution)/shard_map/ppermute | solution.py:20
  112.2 14.5 %collective-permute-start.18 = (bf16[384,768]{1,0:T(8,128)(2,1)S(1)}, bf16[384,768]{1,0:T(8,128)(2,1)S(1)}, u32[]{:S(2)}, u32[]{:S(2)}) collective-permute-start(bf16[384,768]{1,0:T(8,128)(2,1)S(1)} %get-tuple-element.95.refs_4_), channel_id=1, source_target_pairs={{64,0},{0,64},{65,1},{1,65},{66,2},{2,66},{67,3},{3,67},{68,4},{4,... | collective-permute-start | bytes 1769480 | tf_op jit(solution)/shard_map/ppermute | solution.py:20
  113.1 13.7 %collective-permute-start.19 = (bf16[384,768]{1,0:T(8,128)(2,1)S(1)}, bf16[384,768]{1,0:T(8,128)(2,1)S(1)}, u32[]{:S(2)}, u32[]{:S(2)}) collective-permute-start(bf16[384,768]{1,0:T(8,128)(2,1)S(1)} %collective-permute-done.15.refs_5_), channel_id=1, source_target_pairs={{64,0},{0,64},{65,1},{1,65},{66,2},{2,66},{67,3},{3,67},{68,4},{4,... | collective-permute-start | bytes 1769480 | tf_op jit(solution)/shard_map/ppermute | solution.py:20
  113.1 13.7 %collective-permute-start.20 = (bf16[384,768]{1,0:T(8,128)(2,1)S(1)}, bf16[384,768]{1,0:T(8,128)(2,1)S(1)}, u32[]{:S(2)}, u32[]{:S(2)}) collective-permute-start(bf16[384,768]{1,0:T(8,128)(2,1)S(1)} %collective-permute-done.16.refs_6_), channel_id=1, source_target_pairs={{64,0},{0,64},{65,1},{1,65},{66,2},{2,66},{67,3},{3,67},{68,4},{4,... | collective-permute-start | bytes 1769480 | tf_op jit(solution)/shard_map/ppermute | solution.py:20
  113.6 13.2 %collective-permute-start.21 = (bf16[384,768]{1,0:T(8,128)(2,1)S(1)}, bf16[384,768]{1,0:T(8,128)(2,1)S(1)}, u32[]{:S(2)}, u32[]{:S(2)}) collective-permute-start(bf16[384,768]{1,0:T(8,128)(2,1)S(1)} %collective-permute-done.17.refs_7_), channel_id=1, source_target_pairs={{64,0},{0,64},{65,1},{1,65},{66,2},{2,66},{67,3},{3,67},{68,4},{4,... | collective-permute-start | bytes 1769480 | tf_op jit(solution)/shard_map/ppermute | solution.py:20
  131.7 10.2 %collective-permute-start.22 = (bf16[256,768]{1,0:T(8,128)(2,1)S(1)}, bf16[256,768]{1,0:T(8,128)(2,1)S(1)}, u32[]{:S(2)}, u32[]{:S(2)}) collective-permute-start(bf16[256,768]{1,0:T(8,128)(2,1)S(1)} %output.2.refs_4_.refs_12_), channel_id=1, source_target_pairs={{2,0},{3,1},{0,2},{1,3},{6,4},{7,5},{4,6},{5,7},{10,8},{11,9},{8,1... | collective-permute-start | bytes 1179656 | tf_op jit(solution)/shard_map/ppermute | solution.py:20
  142.7 17.1 %all-to-all-start.2 = ((bf16[8,64,768]{2,1,0:T(8,128)(2,1)}), bf16[8,64,768]{2,1,0:T(8,128)(2,1)S(1)}, u32[]{:S(2)}, u32[]{:S(2)}) async-start(bf16[8,64,768]{2,1,0:T(8,128)(2,1)} %copy-done.6), calls=%async_computation.2 | async-start | bytes 1572864 | tf_op jit(solution)/shard_map/all_to_all | solution.py:38
  171.3 18.8 %collective-permute-start.28 = (bf16[8,32,768]{2,1,0:T(8,128)(2,1)S(1)}, bf16[8,32,768]{2,1,0:T(8,128)(2,1)S(1)}, u32[]{:S(2)}, u32[]{:S(2)}) collective-permute-start(bf16[8,32,768]{2,1,0:T(8,128)(2,1)S(1)} %get-tuple-element.114), channel_id=1, source_target_pairs={{48,0},{20,32},{52,4},{24,36},{56,8},{28,40},{60,12},{0,44},{32,16... | collective-permute-start | bytes 1179656 | tf_op jit(solution)/shard_map/ppermute | solution.py:46
  197.5 11.9 %collective-permute-start.30 = (bf16[256,384]{1,0:T(8,128)(2,1)S(1)}, bf16[256,384]{1,0:T(8,128)(2,1)S(1)}, u32[]{:S(2)}, u32[]{:S(2)}) collective-permute-start(bf16[256,384]{1,0:T(8,128)(2,1)S(1)} %merge.3.refs_0_), channel_id=1, source_target_pairs={{3,0},{0,1},{1,2},{2,3},{7,4},{4,5},{5,6},{6,7},{11,8},{8,9},{9,10... | collective-permute-start | bytes 589832 | tf_op jit(solution)/shard_map/ppermute | solution.py:20
  213.8 16.5 %all-to-all-start.3 = ((bf16[8,64,768]{2,1,0:T(8,128)(2,1)}), bf16[8,64,768]{2,1,0:T(8,128)(2,1)S(1)}, u32[]{:S(2)}, u32[]{:S(2)}) async-start(bf16[8,64,768]{2,1,0:T(8,128)(2,1)} %join.5), calls=%async_computation.3 | async-start | bytes 1572864 | tf_op jit(solution)/shard_map/all_to_all | solution.py:38
  217.4 13.9 %collective-permute-start.33 = (bf16[8,32,768]{2,1,0:T(8,128)(2,1)S(1)}, bf16[8,32,768]{2,1,0:T(8,128)(2,1)S(1)}, u32[]{:S(2)}, u32[]{:S(2)}) collective-permute-start(bf16[8,32,768]{2,1,0:T(8,128)(2,1)S(1)} %slice_select_fusion.1), channel_id=1, source_target_pairs={{64,0},{0,64},{65,1},{1,65},{66,2},{2,66},{67,3},{3,67},{68,4},{4,... | collective-permute-start | bytes 1179656 | tf_op jit(solution)/shard_map/ppermute | solution.py:20
  (54 other events, 770.6 us)

commit v9 on v8

--- a/solution.py
+++ b/solution.py
@@ -79,11 +79,12 @@
     )(core, stale)
 
 
-def join_kernel(upper, lower, out, sems):
-    rows = upper.shape[1]
+def join_kernel(*refs):
+    *parts, out, sems = refs
+    rows = parts[0].shape[1]
     copies = [
-        pltpu.make_async_copy(upper, out.at[:, :rows], sems.at[0]),
-        pltpu.make_async_copy(lower, out.at[:, rows:], sems.at[1]),
+        pltpu.make_async_copy(part, out.at[:, i * rows : (i + 1) * rows], sems.at[i])
+        for i, part in enumerate(parts)
     ]
     for copy in copies:
         copy.start()
@@ -91,22 +92,23 @@
         copy.wait()
 
 
-def join(upper, lower):
-    tiles, rows, cols = upper.shape
+def join(*parts):
+    tiles, rows, cols = parts[0].shape
     return pl.pallas_call(
         join_kernel,
-        in_specs=[ANYWHERE] * 2,
+        in_specs=[ANYWHERE] * len(parts),
         out_specs=ON_CHIP,
-        out_shape=struct((tiles, 2 * rows, cols)),
-        scratch_shapes=[pltpu.SemaphoreType.DMA((2,))],
+        out_shape=struct((tiles, len(parts) * rows, cols)),
+        scratch_shapes=[pltpu.SemaphoreType.DMA((len(parts),))],
         compiler_params=params(8),
         name="join",
-    )(upper, lower)
-
-
-def collect_kernel(core, early, late, got1, got2, handed, cache):
-    rows, cols = got1.shape[1], cache.shape[-1]
-    upper, lower = slice(0, rows), slice(rows, 2 * rows)
+    )(*parts)
+
+
+def collect_kernel(core, early, got_early, late, got_late, handed, cache):
+    rows, cols = early.shape[1], cache.shape[-1]
+    features1, keys1, features2 = (slice(i * rows, (i + 1) * rows) for i in range(3))
+    whole = slice(0, rows)
 
     def collect(features, keys):
         for half in range(2):
@@ -119,15 +121,15 @@
 
     @pl.when(core[0] == 0)
     def _():
-        collect(((late, lower), (got2, upper)), ((early, upper), (got1, upper)))
+        collect(((late, features2), (got_late, features2)), ((early, whole), (got_early, whole)))
 
     @pl.when(core[0] == 1)
     def _():
-        collect(((got1, upper), (early, lower)), ((got2, upper), (late, upper)))
-
-
-def collect(core, early, late, got1, got2):
-    patches, rows, cols = got1.shape
+        collect(((got_late, features1), (late, features1)), ((got_late, keys1), (late, keys1)))
+
+
+def collect(core, early, got_early, late, got_late):
+    patches, rows, cols = early.shape
     return pl.pallas_call(
         collect_kernel,
         in_specs=[SCALARS] + [ON_CHIP] * 4,
@@ -138,27 +140,29 @@
         ],
         compiler_params=params(8),
         name="collect",
-    )(core, early, late, got1, got2)
-
-
-def choose(meta, kv, stale, outs):
-    tiles, rows, _ = kv.shape
-    old = pl.ds(pl.multiple_of((1 - meta[1]) * rows, rows), rows)
+    )(core, early, got_early, late, got_late)
+
+
+def choose(meta, kv, stale_own, stale_other, outs):
+    tiles = kv.shape[0]
     for place, out in enumerate(outs):
         first = tiles - REACH if place == 1 else 0
         cut = slice(first, first + out.shape[0])
-
-        @pl.when(meta[2 + place] == 1)
+        fresh = meta[2 + place] == 1
+
+        @pl.when(fresh)
         def _():
             out[...] = kv[cut]
 
-        @pl.when(meta[2 + place] == 0)
-        def _():
-            out[...] = stale[cut, old]
-
-
-def choose_kernel(meta, kv, stale, lo_out, hi_out, far_out):
-    choose(meta, kv, stale, (lo_out, hi_out, far_out))
+        for chosen, stale in enumerate((stale_other, stale_own)):
+
+            @pl.when(jnp.logical_not(fresh) & (meta[1] == chosen))
+            def _():
+                out[...] = stale[cut]
+
+
+def choose_kernel(meta, kv, stale_own, stale_other, lo_out, hi_out, far_out):
+    choose(meta, kv, stale_own, stale_other, (lo_out, hi_out, far_out))
 
 
 def payloads(kv_shape):
@@ -169,12 +173,12 @@
 def choose_alone(meta, kv, stale):
     return pl.pallas_call(
         choose_kernel,
-        in_specs=[SCALARS] + [ON_CHIP] * 2,
+        in_specs=[SCALARS] + [ON_CHIP] * 3,
         out_specs=[ON_CHIP] * 3,
         out_shape=payloads(kv.shape),
         compiler_params=params(8),
         name="choose",
-    )(meta, kv, stale)
+    )(meta, kv, *stale)
 
 
 def project_kernel(meta, *refs, with_stale):
@@ -182,7 +186,7 @@
     shift, scale, gain, w_own, w_other = refs[4:9]
     refs = refs[9:]
     if with_stale:
-        stale, q_out, kv_out, *outs = refs[:-4]
+        stale_own, stale_other, q_out, kv_out, *outs = refs[:-4]
     else:
         q_out, kv_out = refs[:-4]
     xs, modded, weights, sems = refs[-4:]
@@ -250,7 +254,7 @@
             else:
                 kv_out[:, :, cut] = vec
     if with_stale:
-        choose(meta, kv_out, stale, outs)
+        choose(meta, kv_out, stale_own, stale_other, outs)
 
 
 def project(meta, blocks, shift, scale, gain, w_own, w_other, stale, kv_shape):
@@ -262,7 +266,7 @@
     extra = []
     if stale is not None:
         shapes += payloads(kv_shape)
-        extra = [stale]
+        extra = list(stale)
 
     def kernel(*refs):
         project_kernel(*refs, with_stale=stale is not None)
@@ -431,42 +435,47 @@
 
 
 def output_kernel(meta, *refs):
-    *refs, out, weights, sems = refs
-    parts = weights.shape[0]
-    atts, refs = refs[:parts], refs[parts:]
-    own, other, (hidden, gates) = refs[:parts], refs[parts : 2 * parts], refs[2 * parts :]
-
-    def fetch(j, sources):
-        return pltpu.make_async_copy(sources[j], weights.at[j], sems.at[j])
+    atts, own, other = refs[:4], refs[4:6], refs[6:8]
+    hidden, gates, out, weights, sems = refs[8:]
+    rows = atts[0].shape[1]
+
+    def fetch(pair, sources):
+        return pltpu.make_async_copy(sources[pair], weights.at[pair], sems.at[pair])
 
     for chosen, sources in enumerate((other, own)):
 
         @pl.when(meta[1] == chosen)
         def _():
-            for j in range(parts):
-                fetch(j, sources).start()
+            for pair in range(2):
+                fetch(pair, sources).start()
 
     product = jnp.zeros(out.shape, jnp.float32)
-    for j in range(parts):
-        fetch(j, own).wait()
-        product += jnp.dot(atts[j][...], weights[j], preferred_element_type=jnp.float32)
+    for j, att in enumerate(atts):
+        if j % 2 == 0:
+            fetch(j // 2, own).wait()
+        weight = weights[j // 2, (j % 2) * rows : (j % 2 + 1) * rows]
+        product += jnp.dot(att[...], weight, preferred_element_type=jnp.float32)
     out[...] = (hidden[...].astype(jnp.float32) + gates[meta[0]] * product).astype(out.dtype)
 
 
 def output(meta, atts, own, other, hidden, gates):
-    parts = len(atts)
     return pl.pallas_call(
         output_kernel,
-        in_specs=[SCALARS] + [ON_CHIP] * parts + [ANYWHERE] * (2 * parts) + [ON_CHIP] * 2,
+        in_specs=[SCALARS] + [ON_CHIP] * 4 + [ANYWHERE] * 4 + [ON_CHIP] * 2,
         out_specs=ON_CHIP,
         out_shape=struct(hidden.shape),
         scratch_shapes=[
-            pltpu.VMEM((parts,) + own[0].shape, jnp.bfloat16),
-            pltpu.SemaphoreType.DMA((parts,)),
+            pltpu.VMEM((2,) + own[0].shape, jnp.bfloat16),
+            pltpu.SemaphoreType.DMA((2,)),
         ],
         compiler_params=params(12),
         name="output",
     )(meta, *atts, *own, *other, hidden, gates)
+
+
+def paired(first, second):
+    rows, cols = first.shape
+    return join(first[None], second[None]).reshape(2 * rows, cols)
 
 
 def count_tiles(table, counts, chip, per_chip, repeat):
@@ -517,9 +526,17 @@
     core_scalar = core.astype(jnp.int32)[None]
     mine = lax.dynamic_slice_in_dim(latents, core * rows_core, rows_core, 1)
     hidden = exchanged(mine).reshape(rows, part_cols)
-    stale, stale_send = halve(core_scalar, after(stale_cache[0], mine))
-    stale = join(stale, shifted(stale_send, "segment", 1))
-    hidden, stale = lax.optimization_barrier((hidden, stale))
+    stale_own, stale_send = halve(core_scalar, after(stale_cache[0], mine))
+    stale_other = shifted(stale_send, "segment", 1)
+
+    def columns(j):
+        first = lax.rem(tp_pos + j, tp_size) * part_cols
+        return lax.dynamic_slice_in_dim(w_out[0], first, part_cols, 1)
+
+    wo_across = shifted(columns(2), "tp", 2)
+    hidden, stale_own, stale_other, wo_across = lax.optimization_barrier(
+        (hidden, stale_own, stale_other, wo_across)
+    )
     w_other = shifted(w_own, "segment", 1)
     small_own = jnp.concatenate([modulation[0].reshape(-1), qk_gain[0].reshape(-1)])
     small_other = shifted(small_own, "segment", 1)
@@ -543,22 +560,21 @@
         given.append(
             (meta, modul[0], modul[1], modul[2], gain, multiple[..., :256], multiple[..., 256:])
         )
-    slices = [
-        lax.dynamic_slice_in_dim(
-            w_out[0], lax.rem(tp_pos + j, tp_size) * part_cols, part_cols, 1
-        )
-        for j in range(tp_size)
-    ]
+    slices = [columns(j) for j in (1, 3)]
+    wo_own = [paired(columns(0), wo_across)]
+    wo_other = [shifted(wo_own[0], "segment", 1)]
 
     for section in range(2):
         blocks = gather_features(hidden)
         if section == 0:
-            stale = exchanged(after(stale, blocks[0]))
-            blocks, given, slices = lax.optimization_barrier((blocks, given, slices))
+            stale = [exchanged(each) for each in after([stale_own, stale_other], blocks[0])]
+            blocks, given, slices, wo_other = lax.optimization_barrier(
+                (blocks, given, slices, wo_other)
+            )
         else:
-            early = join(kv, hidden.reshape(kv.shape))
-            early = exchanged(after(early, blocks[0]))
+            early = exchanged(after(kv, blocks[0]))
             blocks, early = lax.optimization_barrier((blocks, early))
+            hidden1 = hidden.reshape(kv.shape)
         meta, shift, scale, gates, gain, times_own, times_rest = given[section]
         q_own, kv, *going = project(
             meta,
@@ -579,25 +595,25 @@
         below = along_ring(to_above, -1, patches)
         q_other = shifted(q_own, "segment", 1)
         if section == 0:
-            slices = after(slices, q_other)
-            wo_own = slices[:1] + [shifted(slices[j], "tp", j) for j in range(1, tp_size)]
+            wo_prev, wo_next = after(slices, q_other)
+            wo_prev, wo_next = shifted(wo_prev, "tp", 1), shifted(wo_next, "tp", 3)
+            far, wo_prev, wo_next = lax.optimization_barrier((far, wo_prev, wo_next))
+            wo_own.append(paired(wo_prev, wo_next))
         before = attend_own(q_own, q_other, kv, times_own)
         part_own, part_other = attend_rest(
             q_own, q_other, below, above, far, times_rest, before
         )
         part_back = shifted(part_other, "segment", 1)
+        if section == 0:
+            wo_other.append(shifted(after(wo_own[1], part_back), "segment", 1))
         att = merge(part_own, part_back)
         across = shifted(att, "tp", 2)
-        atts = [att, shifted(att, "tp", 1), across, shifted(att, "tp", 3)]
-        if section == 0:
-            wo_other = [shifted(piece, "segment", 1) for piece in after(wo_own, across)]
+        atts = [att, across, shifted(att, "tp", 1), shifted(att, "tp", 3)]
         hidden = output(meta, atts, wo_own, wo_other, hidden, gates)
 
-    late = exchanged(join(kv, hidden.reshape(kv.shape)))
-    keys, features = slice(0, rows_core), slice(rows_core, 2 * rows_core)
-    got1 = shifted(jnp.where(core == 0, early[:, features], early[:, keys]), "segment", 1)
-    got2 = shifted(jnp.where(core == 0, late[:, keys], late[:, features]), "segment", 1)
-    handed, new_cache = collect(core_scalar, early, late, got1, got2)
+    late = exchanged(join(hidden1, kv, hidden.reshape(kv.shape)))
+    got_early, got_late = shifted(early, "segment", 1), shifted(late, "segment", 1)
+    handed, new_cache = collect(core_scalar, early, got_early, late, got_late)
     return (handed[None], new_cache[None])
 
 

time: 236 us -> 226 us (0.958)
  waiting for transfers between devices: 101 us -> 72.6 us
  blocking collectives: 0 us -> 17.1 us
  Pallas kernels: 33.8 us -> 37.1 us
  local copies, waits for them, and re-layouts: 20.3 us -> 17.9 us
    ppermute x29 -> x27, waiting for transfers between devices: 80.1 us -> 55.3 us  [shifted(): return lax.ppermute(block, axis, route)]
    all_to_all x0 -> x1, blocking collectives: none -> 17.1 us  [exchanged(): return lax.all_to_all(tiles, 'seq', 0, 0, axis_index_groups=groups)]
    all_to_all x4, waiting for transfers between devices: 15.6 us -> 7.29 us  [exchanged(): return lax.all_to_all(tiles, 'seq', 0, 0, axis_index_groups=groups)]
    ppermute x6, waiting for transfers between devices: 4.79 us -> 10 us  [along_ring(): return lax.ppermute(block, 'seq', route)]
    ppermute x6, starting transfers between devices: 18.5 us -> 14.9 us  [along_ring(): return lax.ppermute(block, 'seq', route)]
    unnamed x78 -> x84, local copies, waits for them, and re-layouts: 13.4 us -> 9.8 us
    ppermute x29 -> x27, starting transfers between devices: 37.7 us -> 40 us  [shifted(): return lax.ppermute(block, axis, route)]
  transfers between devices with their start and end apart: 39 -> 37, of which waited for: 19 -> 15; matrix products, arithmetic and copies ran while one was open for 4% -> 5% of each run, Pallas kernels for 6% -> 7%
where the time goes in v9:
time: 226 us; the launch traced here: 225 us
  starting transfers between devices  74.9 us (33%)
  waiting for transfers between devices  72.6 us (32%)
  Pallas kernels  37.1 us (16%)
  local copies, waits for them, and re-layouts  17.9 us (8%)
  blocking collectives  17.1 us (8%)
  other arithmetic  4.24 us (2%)
    ppermute x27, waiting for transfers between devices, shifted(): return lax.ppermute(block, axis, route)  55.3 us
    ppermute x27, starting transfers between devices, shifted(): return lax.ppermute(block, axis, route)  40 us
    all_to_all x4, starting transfers between devices, exchanged(): return lax.all_to_all(tiles, 'seq', 0, 0, axis_index_groups=groups)  20 us
    all_to_all x1, blocking collectives, exchanged(): return lax.all_to_all(tiles, 'seq', 0, 0, axis_index_groups=groups)  17.1 us
    pallas_call x2, Pallas kernels, project(): pl.pallas_call(kernel, in_specs=[SCALARS] + [ANYWHERE] * len(blocks) + [O...  15.3 us
    ppermute x6, starting transfers between devices, along_ring(): return lax.ppermute(block, 'seq', route)  14.9 us
    ppermute x6, waiting for transfers between devices, along_ring(): return lax.ppermute(block, 'seq', route)  10 us
    unnamed x84, local copies, waits for them, and re-layouts  9.8 us
  transfers between devices with their start and end apart: 37, of which 15 were waited for; matrix products, arithmetic and copies ran while one was open for 5% of the time, Pallas kernels for 7%

profile of v9, /device:TPU:1, one launch (start us, length us, event | category | flops | bytes accessed | tf_op | source)
XLA Modules:
  0.0 225.1 jit_solution(12462585380333231997)
XLA Ops:
  4.5 5.1 %all-to-all-start = ((bf16[8,32,768]{2,1,0:T(8,128)(2,1)}), bf16[8,32,768]{2,1,0:T(8,128)(2,1)S(1)}, u32[]{:S(2)}, u32[]{:S(2)}) async-start(bf16[8,32,768]{2,1,0:T(8,128)(2,1)} %constant_dynamic-slice_fusion.2), calls=%async_computation | async-start | bytes 786432 | tf_op jit(solution)/shard_map/all_to_all | solution.py:38
  14.0 3.6 %collective-permute-start.1 = (bf16[384,768]{1,0:T(8,128)(2,1)S(1)}, bf16[384,768]{1,0:T(8,128)(2,1)S(1)}, u32[]{:S(2)}, u32[]{:S(2)}) collective-permute-start(bf16[384,768]{1,0:T(8,128)(2,1)S(1)} %get-tuple-element.124), channel_id=1, source_target_pairs={{2,0},{3,1},{0,2},{1,3},{6,4},{7,5},{4,6},{5,7},{10,8},{11,9},{8,1... | collective-permute-start | bytes 1769480 | tf_op jit(solution)/shard_map/ppermute | solution.py:20
  19.0 12.3 %collective-permute-done.1 = bf16[384,768]{1,0:T(8,128)(2,1)S(1)} collective-permute-done((bf16[384,768]{1,0:T(8,128)(2,1)S(1)}, bf16[384,768]{1,0:T(8,128)(2,1)S(1)}, u32[]{:S(2)}, u32[]{:S(2)}) %collective-permute-start.1) | collective-permute-done | bytes 589856 | tf_op jit(solution)/shard_map/ppermute | solution.py:20
  38.5 7.0 %collective-permute-done.2.refs_1_ = bf16[256,768]{1,0:T(8,128)(2,1)S(1)} collective-permute-done((bf16[256,768]{1,0:T(8,128)(2,1)S(1)}, bf16[256,768]{1,0:T(8,128)(2,1)S(1)}, u32[]{:S(2)}, u32[]{:S(2)}) %collective-permute-start.2) | collective-permute-done | bytes 393248 | tf_op jit(solution)/shard_map/ppermute | solution.py:20
  49.3 5.4 %all-to-all-start.1 = ((bf16[8,32,768]{2,1,0:T(8,128)(2,1)}), bf16[8,32,768]{2,1,0:T(8,128)(2,1)}, u32[]{:S(2)}, u32[]{:S(2)}) async-start(bf16[8,32,768]{2,1,0:T(8,128)(2,1)} %copy-done.15), calls=%async_computation.1 | async-start | bytes 786432 | tf_op jit(solution)/shard_map/all_to_all | solution.py:38
  61.3 7.6 %project.2 = (bf16[8,32,384]{2,1,0:T(8,128)(2,1)}, bf16[8,32,768]{2,1,0:T(8,128)(2,1)S(1)}) custom-call(s32[5]{0:T(128)S(1)} %copy-done.28, bf16[256,768]{1,0:T(8,128)(2,1)S(1)} %copy-done.17, bf16[256,768]{1,0:T(8,128)(2,1)} %collective-permute-done.3.refs_2_, bf16[256,768]{1,0:T(8,128)(2,1)} %collective-permute-done.4.refs_3_, bf16[256,768]{1,0:T(8,128)(2,1)} %bitcast.60, ...), custom_call_target="tpu_custom_call" | custom-call | tf_op jit(solution)/shard_map/project/pallas_call | solution.py:274
  70.5 5.4 %all-to-all-start.2 = ((bf16[8,32,768]{2,1,0:T(8,128)(2,1)}), bf16[8,32,768]{2,1,0:T(8,128)(2,1)S(1)}, u32[]{:S(2)}, u32[]{:S(2)}) async-start(bf16[8,32,768]{2,1,0:T(8,128)(2,1)} %collective-permute-done), calls=%async_computation.2 | async-start | bytes 786432 | tf_op jit(solution)/shard_map/all_to_all | solution.py:38
  78.7 6.1 %all-to-all-done.2.stale_other.refs_11_ = bf16[8,32,768]{2,1,0:T(8,128)(2,1)S(1)} async-done(((bf16[8,32,768]{2,1,0:T(8,128)(2,1)}), bf16[8,32,768]{2,1,0:T(8,128)(2,1)S(1)}, u32[]{:S(2)}, u32[]{:S(2)}) %all-to-all-start.2) | async-done | bytes 393248 | tf_op jit(solution)/shard_map/all_to_all | solution.py:38
  89.4 4.0 %collective-permute-start.11 = (bf16[3,32,768]{2,1,0:T(8,128)(2,1)S(1)}, bf16[3,32,768]{2,1,0:T(8,128)(2,1)S(1)}, u32[]{:S(2)}, u32[]{:S(2)}) collective-permute-start(bf16[3,32,768]{2,1,0:T(8,128)(2,1)S(1)} %get-tuple-element.84), channel_id=1, source_target_pairs={{32,0},{4,32},{36,4},{8,36},{40,8},{12,40},{44,12},{16,44},{48,16}... | collective-permute-start | bytes 442376 | tf_op jit(solution)/shard_map/ppermute | solution.py:46
  93.4 3.3 %attend_own.2.before = f32[8,64,512]{2,1,0:T(8,128)S(1)} custom-call(bf16[8,32,384]{2,1,0:T(8,128)(2,1)} %get-tuple-element.77.q_own, bf16[8,32,384]{2,1,0:T(8,128)(2,1)S(1)} %collective-permute-done.9.q_other, bf16[8,32,768]{2,1,0:T(8,128)(2,1)S(1)} %get-tuple-element.100.kv.own, f32[8,1,256]{2,1,0:T(1,128)S(1)} %copy-done.26), custom_call_target="tpu_custom_call" | custom-call | tf_op jit(solution)/shard_map/attend_own/pallas_call | solution.py:352
  96.8 7.3 %collective-permute-done.12.far = bf16[8,32,768]{2,1,0:T(8,128)(2,1)S(1)} collective-permute-done((bf16[8,32,768]{2,1,0:T(8,128)(2,1)S(1)}, bf16[8,32,768]{2,1,0:T(8,128)(2,1)S(1)}, u32[]{:S(2)}, u32[]{:S(2)}) %collective-permute-start.12) | collective-permute-done | bytes 393248 | tf_op jit(solution)/shard_map/ppermute | solution.py:46
  104.2 3.3 %attend_rest.2 = (f32[8,32,512]{2,1,0:T(8,128)S(1)}, f32[8,32,512]{2,1,0:T(8,128)S(1)}) custom-call(bf16[8,32,384]{2,1,0:T(8,128)(2,1)} %get-tuple-element.77.q_own, bf16[8,32,384]{2,1,0:T(8,128)(2,1)S(1)} %collective-permute-done.9.q_other, bf16[3,32,768]{2,1,0:T(8,128)(2,1)S(1)} %collective-permute-done.10.below, ...), custom_call_target="tpu_custom_call" | custom-call | tf_op jit(solution)/shard_map/attend_rest/pallas_call | solution.py:397
  118.2 7.1 %collective-permute-done.17.refs_2_ = bf16[256,384]{1,0:T(8,128)(2,1)S(1)} collective-permute-done((bf16[256,384]{1,0:T(8,128)(2,1)S(1)}, bf16[256,384]{1,0:T(8,128)(2,1)S(1)}, u32[]{:S(2)}, u32[]{:S(2)}) %collective-permute-start.17) | collective-permute-done | bytes 196640 | tf_op jit(solution)/shard_map/ppermute | solution.py:20
  131.0 7.2 %collective-permute-done.20.refs_1_ = bf16[256,768]{1,0:T(8,128)(2,1)S(1)} collective-permute-done((bf16[256,768]{1,0:T(8,128)(2,1)S(1)}, bf16[256,768]{1,0:T(8,128)(2,1)S(1)}, u32[]{:S(2)}, u32[]{:S(2)}) %collective-permute-start.20) | collective-permute-done | bytes 393248 | tf_op jit(solution)/shard_map/ppermute | solution.py:20
  139.0 4.1 %all-to-all-start.3 = ((bf16[8,32,768]{2,1,0:T(8,128)(2,1)}), bf16[8,32,768]{2,1,0:T(8,128)(2,1)}, u32[]{:S(2)}, u32[]{:S(2)}) async-start(bf16[8,32,768]{2,1,0:T(8,128)(2,1)} %copy-done.8), calls=%async_computation.3 | async-start | bytes 786432 | tf_op jit(solution)/shard_map/all_to_all | solution.py:38
  143.1 5.7 %collective-permute-done.22.refs_3_ = bf16[256,768]{1,0:T(8,128)(2,1)} collective-permute-done((bf16[256,768]{1,0:T(8,128)(2,1)S(1)}, bf16[256,768]{1,0:T(8,128)(2,1)}, u32[]{:S(2)}, u32[]{:S(2)}) %collective-permute-start.22) | collective-permute-done | bytes 393248 | tf_op jit(solution)/shard_map/ppermute | solution.py:20
  152.9 7.7 %project.3 = (bf16[8,32,384]{2,1,0:T(8,128)(2,1)S(1)}, bf16[8,32,768]{2,1,0:T(8,128)(2,1)S(1)}, bf16[3,32,768]{2,1,0:T(8,128)(2,1)S(1)}, bf16[3,32,768]{2,1,0:T(8,128)(2,1)S(1)}, bf16[8,32,768]{2,1,0:T(8,128)(2,1)S(1)}) custom-call(s32[5]{0:T(128)S(1)} %copy-done.31, bf16[256,768]{1,0:T(8,128)(2,1)S(1)} %copy-done.19, ...), custom_call_target="tpu_custom_call" | custom-call | tf_op jit(solution)/shard_map/project/pallas_call | solution.py:274
  160.6 3.3 %collective-permute-start.27 = (bf16[8,32,768]{2,1,0:T(8,128)(2,1)S(1)}, bf16[8,32,768]{2,1,0:T(8,128)(2,1)S(1)}, u32[]{:S(2)}, u32[]{:S(2)}) collective-permute-start(bf16[8,32,768]{2,1,0:T(8,128)(2,1)S(1)} %get-tuple-element.114), channel_id=1, source_target_pairs={{48,0},{20,32},{52,4},{24,36},{56,8},{28,40},{60,12},{0,44},{32,16... | collective-permute-start | bytes 1179656 | tf_op jit(solution)/shard_map/ppermute | solution.py:46
  163.9 6.1 %collective-permute-start.24 = (bf16[8,32,384]{2,1,0:T(8,128)(2,1)S(1)}, bf16[8,32,384]{2,1,0:T(8,128)(2,1)S(1)}, u32[]{:S(2)}, u32[]{:S(2)}) collective-permute-start(bf16[8,32,384]{2,1,0:T(8,128)(2,1)S(1)} %get-tuple-element.111.q_own), channel_id=1, source_target_pairs={{64,0},{0,64},{65,1},{1,65},{66,2},{2,66},{67,3},{3,67},{68,4},{4,... | collective-permute-start | bytes 589832 | tf_op jit(solution)/shard_map/ppermute | solution.py:20
  170.0 4.8 %collective-permute-start.26 = (bf16[3,32,768]{2,1,0:T(8,128)(2,1)S(1)}, bf16[3,32,768]{2,1,0:T(8,128)(2,1)S(1)}, u32[]{:S(2)}, u32[]{:S(2)}) collective-permute-start(bf16[3,32,768]{2,1,0:T(8,128)(2,1)S(1)} %get-tuple-element.113), channel_id=1, source_target_pairs={{32,0},{4,32},{36,4},{8,36},{40,8},{12,40},{44,12},{16,44},{48,16}... | collective-permute-start | bytes 442376 | tf_op jit(solution)/shard_map/ppermute | solution.py:46
  188.2 4.3 %collective-permute-done.31.refs_3_ = bf16[256,384]{1,0:T(8,128)(2,1)S(1)} collective-permute-done((bf16[256,384]{1,0:T(8,128)(2,1)S(1)}, bf16[256,384]{1,0:T(8,128)(2,1)S(1)}, u32[]{:S(2)}, u32[]{:S(2)}) %collective-permute-start.31) | collective-permute-done | bytes 196640 | tf_op jit(solution)/shard_map/ppermute | solution.py:20
  199.2 17.1 %all_to_all.25.late = bf16[8,96,768]{2,1,0:T(8,128)(2,1)S(1)} all-to-all(bf16[8,96,768]{2,1,0:T(8,128)(2,1)S(1)} %join.5), channel_id=1, replica_groups={{0,4,8,12,16,20,24,28},{32,36,40,44,48,52,56,60},{1,5,9,13,17,21,25,29}..., dimensions={0} | all-to-all | bytes 2359296 | tf_op jit(solution)/shard_map/all_to_all | solution.py:38
  216.3 3.4 %collective-permute-start.32 = (bf16[8,96,768]{2,1,0:T(8,128)(2,1)S(1)}, bf16[8,96,768]{2,1,0:T(8,128)(2,1)S(1)}, u32[]{:S(2)}, u32[]{:S(2)}) collective-permute-start(bf16[8,96,768]{2,1,0:T(8,128)(2,1)S(1)} %all_to_all.25.late), channel_id=1, source_target_pairs={{64,0},{0,64},{65,1},{1,65},{66,2},{2,66},{67,3},{3,67},{68,4},{4,... | collective-permute-start | bytes 3538952 | tf_op jit(solution)/shard_map/ppermute | solution.py:20
  219.7 3.1 %collective-permute-done.23.got_early = bf16[8,32,768]{2,1,0:T(8,128)(2,1)S(1)} collective-permute-done((bf16[8,32,768]{2,1,0:T(8,128)(2,1)}, bf16[8,32,768]{2,1,0:T(8,128)(2,1)S(1)}, u32[]{:S(2)}, u32[]{:S(2)}) %collective-permute-start.23) | collective-permute-done | bytes 393248 | tf_op jit(solution)/shard_map/ppermute | solution.py:20
  (173 shorter events, 79.5 us)
Async XLA Ops:
  0.7 57.9 %collective-permute-start.8 = (bf16[3,3072,384]{2,1,0:T(8,128)(2,1)}, bf16[3,3072,384]{2,1,0:T(8,128)(2,1)}, u32[]{:S(2)}, u32[]{:S(2)}) collective-permute-start(bf16[3,3072,384]{2,1,0:T(8,128)(2,1)} %bitcast.72), channel_id=1, source_target_pairs={{64,0},{0,64},{65,1},{1,65},{66,2},{2,66},{67,3},{3,67},{68,4},{4,... | collective-permute-start | bytes 21233672 | tf_op jit(solution)/shard_map/ppermute | solution.py:20
  3.6 15.1 %collective-permute-start.5 = (f32[9472]{0:T(1024)}, f32[9472]{0:T(1024)}, u32[]{:S(2)}, u32[]{:S(2)}) collective-permute-start(f32[9472]{0:T(1024)} %pad_maximum_fusion), channel_id=1, source_target_pairs={{64,0},{0,64},{65,1},{1,65},{66,2},{2,66},{67,3},{3,67},{68,4},{4,... | collective-permute-start | bytes 113672 | tf_op jit(solution)/shard_map/ppermute | solution.py:20
  4.5 14.5 %all-to-all-start = ((bf16[8,32,768]{2,1,0:T(8,128)(2,1)}), bf16[8,32,768]{2,1,0:T(8,128)(2,1)S(1)}, u32[]{:S(2)}, u32[]{:S(2)}) async-start(bf16[8,32,768]{2,1,0:T(8,128)(2,1)} %constant_dynamic-slice_fusion.2), calls=%async_computation | async-start | bytes 786432 | tf_op jit(solution)/shard_map/all_to_all | solution.py:38
  14.0 17.3 %collective-permute-start.1 = (bf16[384,768]{1,0:T(8,128)(2,1)S(1)}, bf16[384,768]{1,0:T(8,128)(2,1)S(1)}, u32[]{:S(2)}, u32[]{:S(2)}) collective-permute-start(bf16[384,768]{1,0:T(8,128)(2,1)S(1)} %get-tuple-element.124), channel_id=1, source_target_pairs={{2,0},{3,1},{0,2},{1,3},{6,4},{7,5},{4,6},{5,7},{10,8},{11,9},{8,1... | collective-permute-start | bytes 1769480 | tf_op jit(solution)/shard_map/ppermute | solution.py:20
  31.6 27.0 %collective-permute-start.7 = (bf16[768,768]{1,0:T(8,128)(2,1)S(1)}, bf16[768,768]{1,0:T(8,128)(2,1)S(1)}, u32[]{:S(2)}, u32[]{:S(2)}) collective-permute-start(bf16[768,768]{1,0:T(8,128)(2,1)S(1)} %bitcast.50), channel_id=1, source_target_pairs={{64,0},{0,64},{65,1},{1,65},{66,2},{2,66},{67,3},{3,67},{68,4},{4,... | collective-permute-start | bytes 3538952 | tf_op jit(solution)/shard_map/ppermute | solution.py:20
  33.0 23.0 %collective-permute-start.6 = (f32[8,1,384]{2,1,0:T(1,128)}, f32[8,1,384]{2,1,0:T(1,128)}, u32[]{:S(2)}, u32[]{:S(2)}) collective-permute-start(f32[8,1,384]{2,1,0:T(1,128)} %broadcast_in_dim.46), channel_id=1, source_target_pairs={{64,0},{0,64},{65,1},{1,65},{66,2},{2,66},{67,3},{3,67},{68,4},{4,... | collective-permute-start | bytes 36872 | tf_op jit(solution)/shard_map/ppermute | solution.py:20
  33.3 12.1 %collective-permute-start.2 = (bf16[256,768]{1,0:T(8,128)(2,1)S(1)}, bf16[256,768]{1,0:T(8,128)(2,1)S(1)}, u32[]{:S(2)}, u32[]{:S(2)}) collective-permute-start(bf16[256,768]{1,0:T(8,128)(2,1)S(1)} %bitcast.57), channel_id=1, source_target_pairs={{2,0},{3,1},{0,2},{1,3},{6,4},{7,5},{4,6},{5,7},{10,8},{11,9},{8,1... | collective-permute-start | bytes 1179656 | tf_op jit(solution)/shard_map/ppermute | solution.py:20
  37.7 20.8 %collective-permute-start.4 = (bf16[256,768]{1,0:T(8,128)(2,1)S(1)}, bf16[256,768]{1,0:T(8,128)(2,1)}, u32[]{:S(2)}, u32[]{:S(2)}) collective-permute-start(bf16[256,768]{1,0:T(8,128)(2,1)S(1)} %bitcast.58), channel_id=1, source_target_pairs={{3,0},{0,1},{1,2},{2,3},{7,4},{4,5},{5,6},{6,7},{11,8},{8,9},{9,10... | collective-permute-start | bytes 1179656 | tf_op jit(solution)/shard_map/ppermute | solution.py:20
  46.2 12.3 %collective-permute-start.3 = (bf16[256,768]{1,0:T(8,128)(2,1)S(1)}, bf16[256,768]{1,0:T(8,128)(2,1)}, u32[]{:S(2)}, u32[]{:S(2)}) collective-permute-start(bf16[256,768]{1,0:T(8,128)(2,1)S(1)} %bitcast.59), channel_id=1, source_target_pairs={{1,0},{2,1},{3,2},{0,3},{5,4},{6,5},{7,6},{4,7},{9,8},{10,9},{11,1... | collective-permute-start | bytes 1179656 | tf_op jit(solution)/shard_map/ppermute | solution.py:20
  49.3 21.2 %all-to-all-start.1 = ((bf16[8,32,768]{2,1,0:T(8,128)(2,1)}), bf16[8,32,768]{2,1,0:T(8,128)(2,1)}, u32[]{:S(2)}, u32[]{:S(2)}) async-start(bf16[8,32,768]{2,1,0:T(8,128)(2,1)} %copy-done.15), calls=%async_computation.1 | async-start | bytes 786432 | tf_op jit(solution)/shard_map/all_to_all | solution.py:38
  70.5 14.3 %all-to-all-start.2 = ((bf16[8,32,768]{2,1,0:T(8,128)(2,1)}), bf16[8,32,768]{2,1,0:T(8,128)(2,1)S(1)}, u32[]{:S(2)}, u32[]{:S(2)}) async-start(bf16[8,32,768]{2,1,0:T(8,128)(2,1)} %collective-permute-done), calls=%async_computation.2 | async-start | bytes 786432 | tf_op jit(solution)/shard_map/all_to_all | solution.py:38
  76.0 28.2 %collective-permute-start.13 = (bf16[384,768]{1,0:T(8,128)(2,1)}, bf16[384,768]{1,0:T(8,128)(2,1)S(1)}, u32[]{:S(2)}, u32[]{:S(2)}) collective-permute-start(bf16[384,768]{1,0:T(8,128)(2,1)} %get-tuple-element.88), channel_id=1, source_target_pairs={{3,0},{0,1},{1,2},{2,3},{7,4},{4,5},{5,6},{6,7},{11,8},{8,9},{9,10... | collective-permute-start | bytes 1769480 | tf_op jit(solution)/shard_map/ppermute | solution.py:20
  76.1 28.1 %collective-permute-start.14 = (bf16[384,768]{1,0:T(8,128)(2,1)}, bf16[384,768]{1,0:T(8,128)(2,1)}, u32[]{:S(2)}, u32[]{:S(2)}) collective-permute-start(bf16[384,768]{1,0:T(8,128)(2,1)} %get-tuple-element.89), channel_id=1, source_target_pairs={{1,0},{2,1},{3,2},{0,3},{5,4},{6,5},{7,6},{4,7},{9,8},{10,9},{11,1... | collective-permute-start | bytes 1769480 | tf_op jit(solution)/shard_map/ppermute | solution.py:20
  86.6 17.5 %collective-permute-start.12 = (bf16[8,32,768]{2,1,0:T(8,128)(2,1)S(1)}, bf16[8,32,768]{2,1,0:T(8,128)(2,1)S(1)}, u32[]{:S(2)}, u32[]{:S(2)}) collective-permute-start(bf16[8,32,768]{2,1,0:T(8,128)(2,1)S(1)} %get-tuple-element.85), channel_id=1, source_target_pairs={{48,0},{20,32},{52,4},{24,36},{56,8},{28,40},{60,12},{0,44},{32,16... | collective-permute-start | bytes 1179656 | tf_op jit(solution)/shard_map/ppermute | solution.py:46
  88.7 15.5 %collective-permute-start.10 = (bf16[3,32,768]{2,1,0:T(8,128)(2,1)S(1)}, bf16[3,32,768]{2,1,0:T(8,128)(2,1)S(1)}, u32[]{:S(2)}, u32[]{:S(2)}) collective-permute-start(bf16[3,32,768]{2,1,0:T(8,128)(2,1)S(1)} %get-tuple-element.83), channel_id=1, source_target_pairs={{60,0},{0,32},{32,4},{4,36},{36,8},{8,40},{40,12},{12,44},{44,16},... | collective-permute-start | bytes 442376 | tf_op jit(solution)/shard_map/ppermute | solution.py:46
  89.4 14.7 %collective-permute-start.11 = (bf16[3,32,768]{2,1,0:T(8,128)(2,1)S(1)}, bf16[3,32,768]{2,1,0:T(8,128)(2,1)S(1)}, u32[]{:S(2)}, u32[]{:S(2)}) collective-permute-start(bf16[3,32,768]{2,1,0:T(8,128)(2,1)S(1)} %get-tuple-element.84), channel_id=1, source_target_pairs={{32,0},{4,32},{36,4},{8,36},{40,8},{12,40},{44,12},{16,44},{48,16}... | collective-permute-start | bytes 442376 | tf_op jit(solution)/shard_map/ppermute | solution.py:46
  111.6 13.7 %collective-permute-start.19 = (bf16[768,768]{1,0:T(8,128)(2,1)S(1)}, bf16[768,768]{1,0:T(8,128)(2,1)S(1)}, u32[]{:S(2)}, u32[]{:S(2)}) collective-permute-start(bf16[768,768]{1,0:T(8,128)(2,1)S(1)} %bitcast.53), channel_id=1, source_target_pairs={{64,0},{0,64},{65,1},{1,65},{66,2},{2,66},{67,3},{3,67},{68,4},{4,... | collective-permute-start | bytes 3538952 | tf_op jit(solution)/shard_map/ppermute | solution.py:20
  114.2 11.1 %collective-permute-start.17 = (bf16[256,384]{1,0:T(8,128)(2,1)S(1)}, bf16[256,384]{1,0:T(8,128)(2,1)S(1)}, u32[]{:S(2)}, u32[]{:S(2)}) collective-permute-start(bf16[256,384]{1,0:T(8,128)(2,1)S(1)} %merge.2.refs_0_), channel_id=1, source_target_pairs={{3,0},{0,1},{1,2},{2,3},{7,4},{4,5},{5,6},{6,7},{11,8},{8,9},{9,10... | collective-permute-start | bytes 589832 | tf_op jit(solution)/shard_map/ppermute | solution.py:20
  114.2 11.1 %collective-permute-start.16 = (bf16[256,384]{1,0:T(8,128)(2,1)S(1)}, bf16[256,384]{1,0:T(8,128)(2,1)S(1)}, u32[]{:S(2)}, u32[]{:S(2)}) collective-permute-start(bf16[256,384]{1,0:T(8,128)(2,1)S(1)} %merge.2.refs_0_), channel_id=1, source_target_pairs={{2,0},{3,1},{0,2},{1,3},{6,4},{7,5},{4,6},{5,7},{10,8},{11,9},{8,1... | collective-permute-start | bytes 589832 | tf_op jit(solution)/shard_map/ppermute | solution.py:20
  128.3 20.5 %collective-permute-start.22 = (bf16[256,768]{1,0:T(8,128)(2,1)S(1)}, bf16[256,768]{1,0:T(8,128)(2,1)}, u32[]{:S(2)}, u32[]{:S(2)}) collective-permute-start(bf16[256,768]{1,0:T(8,128)(2,1)S(1)} %output.2.refs_4_.refs_8_), channel_id=1, source_target_pairs={{3,0},{0,1},{1,2},{2,3},{7,4},{4,5},{5,6},{6,7},{11,8},{8,9},{9,10... | collective-permute-start | bytes 1179656 | tf_op jit(solution)/shard_map/ppermute | solution.py:20
  128.3 20.5 %collective-permute-start.21 = (bf16[256,768]{1,0:T(8,128)(2,1)S(1)}, bf16[256,768]{1,0:T(8,128)(2,1)}, u32[]{:S(2)}, u32[]{:S(2)}) collective-permute-start(bf16[256,768]{1,0:T(8,128)(2,1)S(1)} %output.2.refs_4_.refs_8_), channel_id=1, source_target_pairs={{1,0},{2,1},{3,2},{0,3},{5,4},{6,5},{7,6},{4,7},{9,8},{10,9},{11,1... | collective-permute-start | bytes 1179656 | tf_op jit(solution)/shard_map/ppermute | solution.py:20
  139.0 11.0 %all-to-all-start.3 = ((bf16[8,32,768]{2,1,0:T(8,128)(2,1)}), bf16[8,32,768]{2,1,0:T(8,128)(2,1)}, u32[]{:S(2)}, u32[]{:S(2)}) async-start(bf16[8,32,768]{2,1,0:T(8,128)(2,1)} %copy-done.8), calls=%async_computation.3 | async-start | bytes 786432 | tf_op jit(solution)/shard_map/all_to_all | solution.py:38
  160.6 19.3 %collective-permute-start.27 = (bf16[8,32,768]{2,1,0:T(8,128)(2,1)S(1)}, bf16[8,32,768]{2,1,0:T(8,128)(2,1)S(1)}, u32[]{:S(2)}, u32[]{:S(2)}) collective-permute-start(bf16[8,32,768]{2,1,0:T(8,128)(2,1)S(1)} %get-tuple-element.114), channel_id=1, source_target_pairs={{48,0},{20,32},{52,4},{24,36},{56,8},{28,40},{60,12},{0,44},{32,16... | collective-permute-start | bytes 1179656 | tf_op jit(solution)/shard_map/ppermute | solution.py:46
  163.9 10.9 %collective-permute-start.24 = (bf16[8,32,384]{2,1,0:T(8,128)(2,1)S(1)}, bf16[8,32,384]{2,1,0:T(8,128)(2,1)S(1)}, u32[]{:S(2)}, u32[]{:S(2)}) collective-permute-start(bf16[8,32,384]{2,1,0:T(8,128)(2,1)S(1)} %get-tuple-element.111.q_own), channel_id=1, source_target_pairs={{64,0},{0,64},{65,1},{1,65},{66,2},{2,66},{67,3},{3,67},{68,4},{4,... | collective-permute-start | bytes 589832 | tf_op jit(solution)/shard_map/ppermute | solution.py:20
  (55 other events, 506.9 us)

commit v10 on v9

--- a/solution.py
+++ b/solution.py
@@ -105,64 +105,59 @@
     )(*parts)
 
 
-def collect_kernel(core, early, got_early, late, got_late, handed, cache):
-    rows, cols = early.shape[1], cache.shape[-1]
-    features1, keys1, features2 = (slice(i * rows, (i + 1) * rows) for i in range(3))
-    whole = slice(0, rows)
-
-    def collect(features, keys):
-        for half in range(2):
+def collect_kernel(core, home, got, handed, cache):
+    rows, cols = home.shape[1] // 4, cache.shape[-1]
+    features1, keys1, features2, keys0 = (slice(i * rows, (i + 1) * rows) for i in range(4))
+
+    def collect(features, keys, refs):
+        for half, ref in enumerate(refs):
             here = slice(half * rows, (half + 1) * rows)
-            ref, there = features[half]
-            handed[:, here] = ref[:, there]
-            ref, there = keys[half]
+            handed[:, here] = ref[:, features]
             for which in range(2):
-                cache[which, :, here] = ref[:, there, which * cols : (which + 1) * cols]
+                cache[which, :, here] = ref[:, keys, which * cols : (which + 1) * cols]
 
     @pl.when(core[0] == 0)
     def _():
-        collect(((late, features2), (got_late, features2)), ((early, whole), (got_early, whole)))
+        collect(features2, keys0, (home, got))
 
     @pl.when(core[0] == 1)
     def _():
-        collect(((got_late, features1), (late, features1)), ((got_late, keys1), (late, keys1)))
-
-
-def collect(core, early, got_early, late, got_late):
-    patches, rows, cols = early.shape
+        collect(features1, keys1, (got, home))
+
+
+def collect(core, home, got):
+    patches, rows, cols = home.shape
     return pl.pallas_call(
         collect_kernel,
-        in_specs=[SCALARS] + [ON_CHIP] * 4,
+        in_specs=[SCALARS] + [ON_CHIP] * 2,
         out_specs=[ON_CHIP] * 2,
         out_shape=[
-            struct((patches, 2 * rows, cols)),
-            struct((2, patches, 2 * rows, cols // 2)),
+            struct((patches, rows // 2, cols)),
+            struct((2, patches, rows // 2, cols // 2)),
         ],
         compiler_params=params(8),
         name="collect",
-    )(core, early, got_early, late, got_late)
-
-
-def choose(meta, kv, stale_own, stale_other, outs):
-    tiles = kv.shape[0]
+    )(core, home, got)
+
+
+def choose(meta, kv, stale, outs):
+    tiles, rows, _ = kv.shape
+    old = pl.ds(pl.multiple_of((1 - meta[1]) * rows, rows), rows)
     for place, out in enumerate(outs):
         first = tiles - REACH if place == 1 else 0
         cut = slice(first, first + out.shape[0])
-        fresh = meta[2 + place] == 1
-
-        @pl.when(fresh)
+
+        @pl.when(meta[2 + place] == 1)
         def _():
             out[...] = kv[cut]
 
-        for chosen, stale in enumerate((stale_other, stale_own)):
-
-            @pl.when(jnp.logical_not(fresh) & (meta[1] == chosen))
-            def _():
-                out[...] = stale[cut]
-
-
-def choose_kernel(meta, kv, stale_own, stale_other, lo_out, hi_out, far_out):
-    choose(meta, kv, stale_own, stale_other, (lo_out, hi_out, far_out))
+        @pl.when(meta[2 + place] == 0)
+        def _():
+            out[...] = stale[cut, old]
+
+
+def choose_kernel(meta, kv, stale, lo_out, hi_out, far_out):
+    choose(meta, kv, stale, (lo_out, hi_out, far_out))
 
 
 def payloads(kv_shape):
@@ -173,12 +168,12 @@
 def choose_alone(meta, kv, stale):
     return pl.pallas_call(
         choose_kernel,
-        in_specs=[SCALARS] + [ON_CHIP] * 3,
+        in_specs=[SCALARS] + [ON_CHIP] * 2,
         out_specs=[ON_CHIP] * 3,
         out_shape=payloads(kv.shape),
         compiler_params=params(8),
         name="choose",
-    )(meta, kv, *stale)
+    )(meta, kv, stale)
 
 
 def project_kernel(meta, *refs, with_stale):
@@ -186,7 +181,7 @@
     shift, scale, gain, w_own, w_other = refs[4:9]
     refs = refs[9:]
     if with_stale:
-        stale_own, stale_other, q_out, kv_out, *outs = refs[:-4]
+        stale, q_out, kv_out, *outs = refs[:-4]
     else:
         q_out, kv_out = refs[:-4]
     xs, modded, weights, sems = refs[-4:]
@@ -254,7 +249,7 @@
             else:
                 kv_out[:, :, cut] = vec
     if with_stale:
-        choose(meta, kv_out, stale_own, stale_other, outs)
+        choose(meta, kv_out, stale, outs)
 
 
 def project(meta, blocks, shift, scale, gain, w_own, w_other, stale, kv_shape):
@@ -266,7 +261,7 @@
     extra = []
     if stale is not None:
         shapes += payloads(kv_shape)
-        extra = list(stale)
+        extra = [stale]
 
     def kernel(*refs):
         project_kernel(*refs, with_stale=stale is not None)
@@ -524,23 +519,27 @@
     head_dim = qk_gain.shape[-1]
 
     core_scalar = core.astype(jnp.int32)[None]
-    mine = lax.dynamic_slice_in_dim(latents, core * rows_core, rows_core, 1)
+    def columns(weight, j):
+        first = lax.rem(tp_pos + j, tp_size) * part_cols
+        return lax.dynamic_slice_in_dim(weight, first, part_cols, 1)
+
+    wo_across = columns(w_out[0], 2)
+    mine = lax.dynamic_slice_in_dim(after(latents, wo_across), core * rows_core, rows_core, 1)
+    wo_across = shifted(wo_across, "tp", 2)
     hidden = exchanged(mine).reshape(rows, part_cols)
-    stale_own, stale_send = halve(core_scalar, after(stale_cache[0], mine))
-    stale_other = shifted(stale_send, "segment", 1)
-
-    def columns(j):
-        first = lax.rem(tp_pos + j, tp_size) * part_cols
-        return lax.dynamic_slice_in_dim(w_out[0], first, part_cols, 1)
-
-    wo_across = shifted(columns(2), "tp", 2)
-    hidden, stale_own, stale_other, wo_across = lax.optimization_barrier(
-        (hidden, stale_own, stale_other, wo_across)
+    stale, stale_send = halve(core_scalar, after(stale_cache[0], mine))
+    stale = join(stale, shifted(stale_send, "segment", 1))
+    hidden, stale, wo_across, weight = lax.optimization_barrier(
+        (hidden, stale, wo_across, w_out[0])
     )
     w_other = shifted(w_own, "segment", 1)
     small_own = jnp.concatenate([modulation[0].reshape(-1), qk_gain[0].reshape(-1)])
     small_other = shifted(small_own, "segment", 1)
-    kv_tiles, tile_counts = after((kv_tiles, tile_counts), small_other)
+    blocks = gather_features(hidden)
+    stale, weight, kv_tiles, tile_counts, patch_order, small_own, small_other = after(
+        (stale, weight, kv_tiles, tile_counts, patch_order, small_own, small_other), blocks[0]
+    )
+    stale = exchanged(stale)
     turns = jnp.arange(patches, dtype=jnp.int32)
     asked = jnp.stack([chip, chip - 1, chip + 1, chip - seq_size // 2 - 1]) % seq_size // share
     ranks = jnp.sum(jnp.where(patch_order[None] == asked[:, None], turns[None], 0), axis=-1)
@@ -560,21 +559,18 @@
         given.append(
             (meta, modul[0], modul[1], modul[2], gain, multiple[..., :256], multiple[..., 256:])
         )
-    slices = [columns(j) for j in (1, 3)]
-    wo_own = [paired(columns(0), wo_across)]
+    slices = [columns(weight, j) for j in (1, 3)]
+    wo_own = [paired(columns(weight, 0), wo_across)]
     wo_other = [shifted(wo_own[0], "segment", 1)]
 
     for section in range(2):
-        blocks = gather_features(hidden)
         if section == 0:
-            stale = [exchanged(each) for each in after([stale_own, stale_other], blocks[0])]
             blocks, given, slices, wo_other = lax.optimization_barrier(
                 (blocks, given, slices, wo_other)
             )
         else:
-            early = exchanged(after(kv, blocks[0]))
-            blocks, early = lax.optimization_barrier((blocks, early))
-            hidden1 = hidden.reshape(kv.shape)
+            blocks = gather_features(hidden)
+            hidden1, keys0 = hidden.reshape(kv.shape), kv
         meta, shift, scale, gates, gain, times_own, times_rest = given[section]
         q_own, kv, *going = project(
             meta,
@@ -611,9 +607,8 @@
         atts = [att, across, shifted(att, "tp", 1), shifted(att, "tp", 3)]
         hidden = output(meta, atts, wo_own, wo_other, hidden, gates)
 
-    late = exchanged(join(hidden1, kv, hidden.reshape(kv.shape)))
-    got_early, got_late = shifted(early, "segment", 1), shifted(late, "segment", 1)
-    handed, new_cache = collect(core_scalar, early, got_early, late, got_late)
+    home = exchanged(join(hidden1, kv, hidden.reshape(kv.shape), keys0))
+    handed, new_cache = collect(core_scalar, home, shifted(home, "segment", 1))
     return (handed[None], new_cache[None])
 
 

time: 226 us -> 212 us (0.938)
  starting transfers between devices: 74.9 us -> 63.3 us
  blocking collectives: 17.1 us -> 23.2 us
  waiting for transfers between devices: 72.6 us -> 66.7 us
    all_to_all x4 -> x2, starting transfers between devices: 20 us -> 8.59 us  [exchanged(): return lax.all_to_all(tiles, 'seq', 0, 0, axis_index_groups=groups)]
    all_to_all x1, blocking collectives: 17.1 us -> 23.2 us  [exchanged(): return lax.all_to_all(tiles, 'seq', 0, 0, axis_index_groups=groups)]
    ppermute x27 -> x26, starting transfers between devices: 40 us -> 34.4 us  [shifted(): return lax.ppermute(block, axis, route)]
    ppermute x6, starting transfers between devices: 14.9 us -> 20.3 us  [along_ring(): return lax.ppermute(block, 'seq', route)]
    ppermute x27 -> x26, waiting for transfers between devices: 55.3 us -> 50.1 us  [shifted(): return lax.ppermute(block, axis, route)]
    unnamed x84 -> x70, local copies, waits for them, and re-layouts: 9.8 us -> 5.93 us
    broadcast_in_dim x0 -> x1, local copies, waits for them, and re-layouts: none -> 2.62 us  [paired(): return join(first[None], second[None]).reshape(2 * rows, cols)]
    all_to_all x4 -> x2, waiting for transfers between devices: 7.29 us -> 7.88 us  [exchanged(): return lax.all_to_all(tiles, 'seq', 0, 0, axis_index_groups=groups)]
  transfers between devices with their start and end apart: 37 -> 34, of which waited for: 15 -> 14; matrix products, arithmetic and copies ran while one was open for 5% -> 7% of each run, Pallas kernels for 7% -> 8%
where the time goes in v10:
time: 212 us; the launch traced here: 210 us
  waiting for transfers between devices  66.7 us (31%)
  starting transfers between devices  63.3 us (30%)
  Pallas kernels  35.6 us (17%)
  blocking collectives  23.2 us (11%)
  local copies, waits for them, and re-layouts  15.7 us (7%)
  other arithmetic  4.42 us (2%)
    ppermute x26, waiting for transfers between devices, shifted(): return lax.ppermute(block, axis, route)  50.1 us
    ppermute x26, starting transfers between devices, shifted(): return lax.ppermute(block, axis, route)  34.4 us
    all_to_all x1, blocking collectives, exchanged(): return lax.all_to_all(tiles, 'seq', 0, 0, axis_index_groups=groups)  23.2 us
    ppermute x6, starting transfers between devices, along_ring(): return lax.ppermute(block, 'seq', route)  20.3 us
    pallas_call x2, Pallas kernels, project(): pl.pallas_call(kernel, in_specs=[SCALARS] + [ANYWHERE] * len(blocks) + [O...  14.6 us
    ppermute x6, waiting for transfers between devices, along_ring(): return lax.ppermute(block, 'seq', route)  8.66 us
    all_to_all x2, starting transfers between devices, exchanged(): return lax.all_to_all(tiles, 'seq', 0, 0, axis_index_groups=groups)  8.59 us
    all_to_all x2, waiting for transfers between devices, exchanged(): return lax.all_to_all(tiles, 'seq', 0, 0, axis_index_groups=groups)  7.88 us
  transfers between devices with their start and end apart: 34, of which 14 were waited for; matrix products, arithmetic and copies ran while one was open for 7% of the time, Pallas kernels for 8%

profile of v10, /device:TPU:1, one launch (start us, length us, event | category | flops | bytes accessed | tf_op | source)
XLA Modules:
  0.0 210.0 jit_solution(5799938873188241640)
XLA Ops:
  3.3 3.8 %collective-permute-start.1 = (bf16[384,768]{1,0:T(8,128)(2,1)S(1)}, bf16[384,768]{1,0:T(8,128)(2,1)S(1)}, u32[]{:S(2)}, u32[]{:S(2)}) collective-permute-start(bf16[384,768]{1,0:T(8,128)(2,1)S(1)} %dynamic-slice_bitcast_fusion.1), channel_id=1, source_target_pairs={{2,0},{3,1},{0,2},{1,3},{6,4},{7,5},{4,6},{5,7},{10,8},{11,9},{8,1... | collective-permute-start | bytes 1769480 | tf_op jit(solution)/shard_map/ppermute | solution.py:20
  9.2 5.0 %all-to-all-start = ((bf16[8,32,768]{2,1,0:T(8,128)(2,1)}), bf16[8,32,768]{2,1,0:T(8,128)(2,1)S(1)}, u32[]{:S(2)}, u32[]{:S(2)}) async-start(bf16[8,32,768]{2,1,0:T(8,128)(2,1)} %constant_dynamic-slice_fusion.3), calls=%async_computation | async-start | bytes 786432 | tf_op jit(solution)/shard_map/all_to_all | solution.py:38
  15.2 7.9 %all-to-all-done = bf16[8,32,768]{2,1,0:T(8,128)(2,1)S(1)} async-done(((bf16[8,32,768]{2,1,0:T(8,128)(2,1)}), bf16[8,32,768]{2,1,0:T(8,128)(2,1)S(1)}, u32[]{:S(2)}, u32[]{:S(2)}) %all-to-all-start) | async-done | bytes 393248 | tf_op jit(solution)/shard_map/all_to_all | solution.py:38
  28.6 6.9 %collective-permute-done.2.refs_1_ = bf16[256,768]{1,0:T(8,128)(2,1)S(1)} collective-permute-done((bf16[256,768]{1,0:T(8,128)(2,1)S(1)}, bf16[256,768]{1,0:T(8,128)(2,1)S(1)}, u32[]{:S(2)}, u32[]{:S(2)}) %collective-permute-start.2) | collective-permute-done | bytes 393248 | tf_op jit(solution)/shard_map/ppermute | solution.py:20
  35.5 3.5 %all-to-all-start.1 = ((bf16[8,64,768]{2,1,0:T(8,128)(2,1)}), bf16[8,64,768]{2,1,0:T(8,128)(2,1)S(1)}, u32[]{:S(2)}, u32[]{:S(2)}) async-start(bf16[8,64,768]{2,1,0:T(8,128)(2,1)} %join.4), calls=%async_computation.1 | async-start | bytes 1572864 | tf_op jit(solution)/shard_map/all_to_all | solution.py:38
  39.0 2.6 %dynamic-slice_bitcast_fusion = (bf16[1,384,768]{2,1,0:T(8,128)(2,1)S(1)}, bf16[384,768]{1,0:T(8,128)(2,1)}, bf16[384,768]{1,0:T(8,128)(2,1)}) fusion(bf16[384,3072]{1,0:T(8,128)(2,1)} %bitcast.73, s32[]{:T(128)S(6)} %select_n.103, s32[]{:T(128)S(6)} %select_n.102, s32[]{:T(128)S(6)} %select_n.101), kind=kLoop, calls=%fused_computation | loop fusion | bytes 3538956 | tf_op jit(solution)/shard_map/broadcast_in_dim | solution.py:473
  42.0 3.0 %collective-permute-start.7 = (bf16[768,768]{1,0:T(8,128)(2,1)S(1)}, bf16[768,768]{1,0:T(8,128)(2,1)}, u32[]{:S(2)}, u32[]{:S(2)}) collective-permute-start(bf16[768,768]{1,0:T(8,128)(2,1)S(1)} %bitcast.49), channel_id=1, source_target_pairs={{64,0},{0,64},{65,1},{1,65},{66,2},{2,66},{67,3},{3,67},{68,4},{4,... | collective-permute-start | bytes 3538952 | tf_op jit(solution)/shard_map/ppermute | solution.py:20
  57.7 6.9 %project.2 = (bf16[8,32,384]{2,1,0:T(8,128)(2,1)S(1)}, bf16[8,32,768]{2,1,0:T(8,128)(2,1)S(1)}) custom-call(s32[5]{0:T(128)S(1)} %get-tuple-element.74.refs_0_.meta, bf16[256,768]{1,0:T(8,128)(2,1)S(1)} %copy-done.10, bf16[256,768]{1,0:T(8,128)(2,1)} %collective-permute-done.3.refs_2_, bf16[256,768]{1,0:T(8,128)(2,1)S(1)} %copy-done.12, ...), custom_call_target="tpu_custom_call" | custom-call | tf_op jit(solution)/shard_map/project/pallas_call | solution.py:269
  70.1 5.3 %collective-permute-start.12 = (bf16[8,32,768]{2,1,0:T(8,128)(2,1)S(1)}, bf16[8,32,768]{2,1,0:T(8,128)(2,1)S(1)}, u32[]{:S(2)}, u32[]{:S(2)}) collective-permute-start(bf16[8,32,768]{2,1,0:T(8,128)(2,1)S(1)} %get-tuple-element.87), channel_id=1, source_target_pairs={{48,0},{20,32},{52,4},{24,36},{56,8},{28,40},{60,12},{0,44},{32,16... | collective-permute-start | bytes 1179656 | tf_op jit(solution)/shard_map/ppermute | solution.py:46
  75.4 4.8 %collective-permute-start.11 = (bf16[3,32,768]{2,1,0:T(8,128)(2,1)S(1)}, bf16[3,32,768]{2,1,0:T(8,128)(2,1)S(1)}, u32[]{:S(2)}, u32[]{:S(2)}) collective-permute-start(bf16[3,32,768]{2,1,0:T(8,128)(2,1)S(1)} %get-tuple-element.86), channel_id=1, source_target_pairs={{32,0},{4,32},{36,4},{8,36},{40,8},{12,40},{44,12},{16,44},{48,16}... | collective-permute-start | bytes 442376 | tf_op jit(solution)/shard_map/ppermute | solution.py:46
  83.3 5.0 %collective-permute-done.12.far = bf16[8,32,768]{2,1,0:T(8,128)(2,1)S(1)} collective-permute-done((bf16[8,32,768]{2,1,0:T(8,128)(2,1)S(1)}, bf16[8,32,768]{2,1,0:T(8,128)(2,1)S(1)}, u32[]{:S(2)}, u32[]{:S(2)}) %collective-permute-start.12) | collective-permute-done | bytes 393248 | tf_op jit(solution)/shard_map/ppermute | solution.py:46
  97.0 3.9 %collective-permute-done.18.refs_3_ = bf16[256,384]{1,0:T(8,128)(2,1)S(1)} collective-permute-done((bf16[256,384]{1,0:T(8,128)(2,1)S(1)}, bf16[256,384]{1,0:T(8,128)(2,1)S(1)}, u32[]{:S(2)}, u32[]{:S(2)}) %collective-permute-start.18) | collective-permute-done | bytes 196640 | tf_op jit(solution)/shard_map/ppermute | solution.py:20
  100.9 6.3 %collective-permute-done.17.refs_2_ = bf16[256,384]{1,0:T(8,128)(2,1)S(1)} collective-permute-done((bf16[256,384]{1,0:T(8,128)(2,1)S(1)}, bf16[256,384]{1,0:T(8,128)(2,1)S(1)}, u32[]{:S(2)}, u32[]{:S(2)}) %collective-permute-start.17) | collective-permute-done | bytes 196640 | tf_op jit(solution)/shard_map/ppermute | solution.py:20
  107.2 3.0 %output.2.refs_4_.refs_8_ = bf16[256,768]{1,0:T(8,128)(2,1)S(1)} custom-call(s32[5]{0:T(128)S(1)} %copy-done.21, bf16[256,384]{1,0:T(8,128)(2,1)S(1)} %merge.2.refs_0_, bf16[256,384]{1,0:T(8,128)(2,1)S(1)} %collective-permute-done.16.refs_1_, bf16[256,384]{1,0:T(8,128)(2,1)S(1)} %collective-permute-done.17.refs_2_, ...), custom_call_target="tpu_custom_call" | custom-call | tf_op jit(solution)/shard_map/output/pallas_call | solution.py:457
  110.3 2.7 %collective-permute-start.21 = (bf16[256,768]{1,0:T(8,128)(2,1)S(1)}, bf16[256,768]{1,0:T(8,128)(2,1)S(1)}, u32[]{:S(2)}, u32[]{:S(2)}) collective-permute-start(bf16[256,768]{1,0:T(8,128)(2,1)S(1)} %output.2.refs_4_.refs_8_), channel_id=1, source_target_pairs={{1,0},{2,1},{3,2},{0,3},{5,4},{6,5},{7,6},{4,7},{9,8},{10,9},{11,1... | collective-permute-start | bytes 1179656 | tf_op jit(solution)/shard_map/ppermute | solution.py:20
  113.0 17.1 %collective-permute-done.22.refs_3_ = bf16[256,768]{1,0:T(8,128)(2,1)S(1)} collective-permute-done((bf16[256,768]{1,0:T(8,128)(2,1)S(1)}, bf16[256,768]{1,0:T(8,128)(2,1)S(1)}, u32[]{:S(2)}, u32[]{:S(2)}) %collective-permute-start.22) | collective-permute-done | bytes 393248 | tf_op jit(solution)/shard_map/ppermute | solution.py:20
  131.0 7.6 %project.3 = (bf16[8,32,384]{2,1,0:T(8,128)(2,1)S(1)}, bf16[8,32,768]{2,1,0:T(8,128)(2,1)S(1)}, bf16[3,32,768]{2,1,0:T(8,128)(2,1)S(1)}, bf16[3,32,768]{2,1,0:T(8,128)(2,1)S(1)}, bf16[8,32,768]{2,1,0:T(8,128)(2,1)S(1)}) custom-call(s32[5]{0:T(128)S(1)} %copy-done.22, bf16[256,768]{1,0:T(8,128)(2,1)S(1)} %collective-permute-done.20.refs_1_, ...), custom_call_target="tpu_custom_call" | custom-call | tf_op jit(solution)/shard_map/project/pallas_call | solution.py:269
  138.7 5.5 %collective-permute-start.26 = (bf16[8,32,768]{2,1,0:T(8,128)(2,1)S(1)}, bf16[8,32,768]{2,1,0:T(8,128)(2,1)S(1)}, u32[]{:S(2)}, u32[]{:S(2)}) collective-permute-start(bf16[8,32,768]{2,1,0:T(8,128)(2,1)S(1)} %get-tuple-element.110), channel_id=1, source_target_pairs={{48,0},{20,32},{52,4},{24,36},{56,8},{28,40},{60,12},{0,44},{32,16... | collective-permute-start | bytes 1179656 | tf_op jit(solution)/shard_map/ppermute | solution.py:46
  145.8 4.8 %collective-permute-start.25 = (bf16[3,32,768]{2,1,0:T(8,128)(2,1)S(1)}, bf16[3,32,768]{2,1,0:T(8,128)(2,1)S(1)}, u32[]{:S(2)}, u32[]{:S(2)}) collective-permute-start(bf16[3,32,768]{2,1,0:T(8,128)(2,1)S(1)} %get-tuple-element.109), channel_id=1, source_target_pairs={{32,0},{4,32},{36,4},{8,36},{40,8},{12,40},{44,12},{16,44},{48,16}... | collective-permute-start | bytes 442376 | tf_op jit(solution)/shard_map/ppermute | solution.py:46
  153.0 2.7 %collective-permute-done.24.below = bf16[3,32,768]{2,1,0:T(8,128)(2,1)S(1)} collective-permute-done((bf16[3,32,768]{2,1,0:T(8,128)(2,1)S(1)}, bf16[3,32,768]{2,1,0:T(8,128)(2,1)S(1)}, u32[]{:S(2)}, u32[]{:S(2)}) %collective-permute-start.24) | collective-permute-done | bytes 147488 | tf_op jit(solution)/shard_map/ppermute | solution.py:46
  169.2 7.3 %collective-permute-done.29.refs_2_ = bf16[256,384]{1,0:T(8,128)(2,1)S(1)} collective-permute-done((bf16[256,384]{1,0:T(8,128)(2,1)S(1)}, bf16[256,384]{1,0:T(8,128)(2,1)S(1)}, u32[]{:S(2)}, u32[]{:S(2)}) %collective-permute-start.29) | collective-permute-done | bytes 196640 | tf_op jit(solution)/shard_map/ppermute | solution.py:20
  179.0 23.2 %all_to_all.15.home = bf16[8,128,768]{2,1,0:T(8,128)(2,1)S(1)} all-to-all(bf16[8,128,768]{2,1,0:T(8,128)(2,1)S(1)} %join.7), channel_id=1, replica_groups={{0,4,8,12,16,20,24,28},{32,36,40,44,48,52,56,60},{1,5,9,13,17,21,25,29}..., dimensions={0} | all-to-all | bytes 3145728 | tf_op jit(solution)/shard_map/all_to_all | solution.py:38
  202.2 3.5 %collective-permute-start.31 = (bf16[8,128,768]{2,1,0:T(8,128)(2,1)S(1)}, bf16[8,128,768]{2,1,0:T(8,128)(2,1)S(1)}, u32[]{:S(2)}, u32[]{:S(2)}) collective-permute-start(bf16[8,128,768]{2,1,0:T(8,128)(2,1)S(1)} %all_to_all.15.home), channel_id=1, source_target_pairs={{64,0},{0,64},{65,1},{1,65},{66,2},{2,66},{67,3},{3,67},{68,4},{4,... | collective-permute-start | bytes 4718600 | tf_op jit(solution)/shard_map/ppermute | solution.py:20
  205.7 3.0 %collective-permute-done.31.got = bf16[8,128,768]{2,1,0:T(8,128)(2,1)S(1)} collective-permute-done((bf16[8,128,768]{2,1,0:T(8,128)(2,1)S(1)}, bf16[8,128,768]{2,1,0:T(8,128)(2,1)S(1)}, u32[]{:S(2)}, u32[]{:S(2)}) %collective-permute-start.31) | collective-permute-done | bytes 1572896 | tf_op jit(solution)/shard_map/ppermute | solution.py:20
  (155 shorter events, 63.5 us)
Async XLA Ops:
  0.7 55.0 %collective-permute-start.8 = (bf16[3,3072,384]{2,1,0:T(8,128)(2,1)}, bf16[3,3072,384]{2,1,0:T(8,128)(2,1)}, u32[]{:S(2)}, u32[]{:S(2)}) collective-permute-start(bf16[3,3072,384]{2,1,0:T(8,128)(2,1)} %bitcast.70), channel_id=1, source_target_pairs={{64,0},{0,64},{65,1},{1,65},{66,2},{2,66},{67,3},{3,67},{68,4},{4,... | collective-permute-start | bytes 21233672 | tf_op jit(solution)/shard_map/ppermute | solution.py:20
  3.3 19.9 %collective-permute-start.1 = (bf16[384,768]{1,0:T(8,128)(2,1)S(1)}, bf16[384,768]{1,0:T(8,128)(2,1)S(1)}, u32[]{:S(2)}, u32[]{:S(2)}) collective-permute-start(bf16[384,768]{1,0:T(8,128)(2,1)S(1)} %dynamic-slice_bitcast_fusion.1), channel_id=1, source_target_pairs={{2,0},{3,1},{0,2},{1,3},{6,4},{7,5},{4,6},{5,7},{10,8},{11,9},{8,1... | collective-permute-start | bytes 1769480 | tf_op jit(solution)/shard_map/ppermute | solution.py:20
  9.2 13.9 %all-to-all-start = ((bf16[8,32,768]{2,1,0:T(8,128)(2,1)}), bf16[8,32,768]{2,1,0:T(8,128)(2,1)S(1)}, u32[]{:S(2)}, u32[]{:S(2)}) async-start(bf16[8,32,768]{2,1,0:T(8,128)(2,1)} %constant_dynamic-slice_fusion.3), calls=%async_computation | async-start | bytes 786432 | tf_op jit(solution)/shard_map/all_to_all | solution.py:38
  24.0 11.4 %collective-permute-start.2 = (bf16[256,768]{1,0:T(8,128)(2,1)S(1)}, bf16[256,768]{1,0:T(8,128)(2,1)S(1)}, u32[]{:S(2)}, u32[]{:S(2)}) collective-permute-start(bf16[256,768]{1,0:T(8,128)(2,1)S(1)} %bitcast.56), channel_id=1, source_target_pairs={{2,0},{3,1},{0,2},{1,3},{6,4},{7,5},{4,6},{5,7},{10,8},{11,9},{8,1... | collective-permute-start | bytes 1179656 | tf_op jit(solution)/shard_map/ppermute | solution.py:20
  25.7 29.3 %collective-permute-start.4 = (bf16[256,768]{1,0:T(8,128)(2,1)S(1)}, bf16[256,768]{1,0:T(8,128)(2,1)S(1)}, u32[]{:S(2)}, u32[]{:S(2)}) collective-permute-start(bf16[256,768]{1,0:T(8,128)(2,1)S(1)} %bitcast.57), channel_id=1, source_target_pairs={{3,0},{0,1},{1,2},{2,3},{7,4},{4,5},{5,6},{6,7},{11,8},{8,9},{9,10... | collective-permute-start | bytes 1179656 | tf_op jit(solution)/shard_map/ppermute | solution.py:20
  26.5 29.2 %collective-permute-start.3 = (bf16[256,768]{1,0:T(8,128)(2,1)S(1)}, bf16[256,768]{1,0:T(8,128)(2,1)}, u32[]{:S(2)}, u32[]{:S(2)}) collective-permute-start(bf16[256,768]{1,0:T(8,128)(2,1)S(1)} %bitcast.58), channel_id=1, source_target_pairs={{1,0},{2,1},{3,2},{0,3},{5,4},{6,5},{7,6},{4,7},{9,8},{10,9},{11,1... | collective-permute-start | bytes 1179656 | tf_op jit(solution)/shard_map/ppermute | solution.py:20
  35.5 33.4 %all-to-all-start.1 = ((bf16[8,64,768]{2,1,0:T(8,128)(2,1)}), bf16[8,64,768]{2,1,0:T(8,128)(2,1)S(1)}, u32[]{:S(2)}, u32[]{:S(2)}) async-start(bf16[8,64,768]{2,1,0:T(8,128)(2,1)} %join.4), calls=%async_computation.1 | async-start | bytes 1572864 | tf_op jit(solution)/shard_map/all_to_all | solution.py:38
  42.0 13.7 %collective-permute-start.7 = (bf16[768,768]{1,0:T(8,128)(2,1)S(1)}, bf16[768,768]{1,0:T(8,128)(2,1)}, u32[]{:S(2)}, u32[]{:S(2)}) collective-permute-start(bf16[768,768]{1,0:T(8,128)(2,1)S(1)} %bitcast.49), channel_id=1, source_target_pairs={{64,0},{0,64},{65,1},{1,65},{66,2},{2,66},{67,3},{3,67},{68,4},{4,... | collective-permute-start | bytes 3538952 | tf_op jit(solution)/shard_map/ppermute | solution.py:20
  66.2 22.1 %collective-permute-start.13 = (bf16[384,768]{1,0:T(8,128)(2,1)}, bf16[384,768]{1,0:T(8,128)(2,1)}, u32[]{:S(2)}, u32[]{:S(2)}) collective-permute-start(bf16[384,768]{1,0:T(8,128)(2,1)} %get-tuple-element.90), channel_id=1, source_target_pairs={{3,0},{0,1},{1,2},{2,3},{7,4},{4,5},{5,6},{6,7},{11,8},{8,9},{9,10... | collective-permute-start | bytes 1769480 | tf_op jit(solution)/shard_map/ppermute | solution.py:20
  66.9 21.3 %collective-permute-start.14 = (bf16[384,768]{1,0:T(8,128)(2,1)}, bf16[384,768]{1,0:T(8,128)(2,1)}, u32[]{:S(2)}, u32[]{:S(2)}) collective-permute-start(bf16[384,768]{1,0:T(8,128)(2,1)} %get-tuple-element.91), channel_id=1, source_target_pairs={{1,0},{2,1},{3,2},{0,3},{5,4},{6,5},{7,6},{4,7},{9,8},{10,9},{11,1... | collective-permute-start | bytes 1769480 | tf_op jit(solution)/shard_map/ppermute | solution.py:20
  70.1 18.1 %collective-permute-start.12 = (bf16[8,32,768]{2,1,0:T(8,128)(2,1)S(1)}, bf16[8,32,768]{2,1,0:T(8,128)(2,1)S(1)}, u32[]{:S(2)}, u32[]{:S(2)}) collective-permute-start(bf16[8,32,768]{2,1,0:T(8,128)(2,1)S(1)} %get-tuple-element.87), channel_id=1, source_target_pairs={{48,0},{20,32},{52,4},{24,36},{56,8},{28,40},{60,12},{0,44},{32,16... | collective-permute-start | bytes 1179656 | tf_op jit(solution)/shard_map/ppermute | solution.py:46
  75.4 12.9 %collective-permute-start.10 = (bf16[3,32,768]{2,1,0:T(8,128)(2,1)S(1)}, bf16[3,32,768]{2,1,0:T(8,128)(2,1)S(1)}, u32[]{:S(2)}, u32[]{:S(2)}) collective-permute-start(bf16[3,32,768]{2,1,0:T(8,128)(2,1)S(1)} %get-tuple-element.85), channel_id=1, source_target_pairs={{60,0},{0,32},{32,4},{4,36},{36,8},{8,40},{40,12},{12,44},{44,16},... | collective-permute-start | bytes 442376 | tf_op jit(solution)/shard_map/ppermute | solution.py:46
  75.4 12.9 %collective-permute-start.11 = (bf16[3,32,768]{2,1,0:T(8,128)(2,1)S(1)}, bf16[3,32,768]{2,1,0:T(8,128)(2,1)S(1)}, u32[]{:S(2)}, u32[]{:S(2)}) collective-permute-start(bf16[3,32,768]{2,1,0:T(8,128)(2,1)S(1)} %get-tuple-element.86), channel_id=1, source_target_pairs={{32,0},{4,32},{36,4},{8,36},{40,8},{12,40},{44,12},{16,44},{48,16}... | collective-permute-start | bytes 442376 | tf_op jit(solution)/shard_map/ppermute | solution.py:46
  93.6 13.6 %collective-permute-start.19 = (bf16[768,768]{1,0:T(8,128)(2,1)S(1)}, bf16[768,768]{1,0:T(8,128)(2,1)S(1)}, u32[]{:S(2)}, u32[]{:S(2)}) collective-permute-start(bf16[768,768]{1,0:T(8,128)(2,1)S(1)} %bitcast.52), channel_id=1, source_target_pairs={{64,0},{0,64},{65,1},{1,65},{66,2},{2,66},{67,3},{3,67},{68,4},{4,... | collective-permute-start | bytes 3538952 | tf_op jit(solution)/shard_map/ppermute | solution.py:20
  95.7 11.5 %collective-permute-start.17 = (bf16[256,384]{1,0:T(8,128)(2,1)S(1)}, bf16[256,384]{1,0:T(8,128)(2,1)S(1)}, u32[]{:S(2)}, u32[]{:S(2)}) collective-permute-start(bf16[256,384]{1,0:T(8,128)(2,1)S(1)} %merge.2.refs_0_), channel_id=1, source_target_pairs={{3,0},{0,1},{1,2},{2,3},{7,4},{4,5},{5,6},{6,7},{11,8},{8,9},{9,10... | collective-permute-start | bytes 589832 | tf_op jit(solution)/shard_map/ppermute | solution.py:20
  96.0 11.2 %collective-permute-start.16 = (bf16[256,384]{1,0:T(8,128)(2,1)S(1)}, bf16[256,384]{1,0:T(8,128)(2,1)S(1)}, u32[]{:S(2)}, u32[]{:S(2)}) collective-permute-start(bf16[256,384]{1,0:T(8,128)(2,1)S(1)} %merge.2.refs_0_), channel_id=1, source_target_pairs={{2,0},{3,1},{0,2},{1,3},{6,4},{7,5},{4,6},{5,7},{10,8},{11,9},{8,1... | collective-permute-start | bytes 589832 | tf_op jit(solution)/shard_map/ppermute | solution.py:20
  110.3 19.9 %collective-permute-start.22 = (bf16[256,768]{1,0:T(8,128)(2,1)S(1)}, bf16[256,768]{1,0:T(8,128)(2,1)S(1)}, u32[]{:S(2)}, u32[]{:S(2)}) collective-permute-start(bf16[256,768]{1,0:T(8,128)(2,1)S(1)} %output.2.refs_4_.refs_8_), channel_id=1, source_target_pairs={{3,0},{0,1},{1,2},{2,3},{7,4},{4,5},{5,6},{6,7},{11,8},{8,9},{9,10... | collective-permute-start | bytes 1179656 | tf_op jit(solution)/shard_map/ppermute | solution.py:20
  110.3 19.8 %collective-permute-start.21 = (bf16[256,768]{1,0:T(8,128)(2,1)S(1)}, bf16[256,768]{1,0:T(8,128)(2,1)S(1)}, u32[]{:S(2)}, u32[]{:S(2)}) collective-permute-start(bf16[256,768]{1,0:T(8,128)(2,1)S(1)} %output.2.refs_4_.refs_8_), channel_id=1, source_target_pairs={{1,0},{2,1},{3,2},{0,3},{5,4},{6,5},{7,6},{4,7},{9,8},{10,9},{11,1... | collective-permute-start | bytes 1179656 | tf_op jit(solution)/shard_map/ppermute | solution.py:20
  113.0 17.2 %collective-permute-start.20 = (bf16[256,768]{1,0:T(8,128)(2,1)S(1)}, bf16[256,768]{1,0:T(8,128)(2,1)S(1)}, u32[]{:S(2)}, u32[]{:S(2)}) collective-permute-start(bf16[256,768]{1,0:T(8,128)(2,1)S(1)} %output.2.refs_4_.refs_8_), channel_id=1, source_target_pairs={{2,0},{3,1},{0,2},{1,3},{6,4},{7,5},{4,6},{5,7},{10,8},{11,9},{8,1... | collective-permute-start | bytes 1179656 | tf_op jit(solution)/shard_map/ppermute | solution.py:20
  138.7 18.0 %collective-permute-start.26 = (bf16[8,32,768]{2,1,0:T(8,128)(2,1)S(1)}, bf16[8,32,768]{2,1,0:T(8,128)(2,1)S(1)}, u32[]{:S(2)}, u32[]{:S(2)}) collective-permute-start(bf16[8,32,768]{2,1,0:T(8,128)(2,1)S(1)} %get-tuple-element.110), channel_id=1, source_target_pairs={{48,0},{20,32},{52,4},{24,36},{56,8},{28,40},{60,12},{0,44},{32,16... | collective-permute-start | bytes 1179656 | tf_op jit(solution)/shard_map/ppermute | solution.py:46
  145.8 10.0 %collective-permute-start.24 = (bf16[3,32,768]{2,1,0:T(8,128)(2,1)S(1)}, bf16[3,32,768]{2,1,0:T(8,128)(2,1)S(1)}, u32[]{:S(2)}, u32[]{:S(2)}) collective-permute-start(bf16[3,32,768]{2,1,0:T(8,128)(2,1)S(1)} %get-tuple-element.108), channel_id=1, source_target_pairs={{60,0},{0,32},{32,4},{4,36},{36,8},{8,40},{40,12},{12,44},{44,16},... | collective-permute-start | bytes 442376 | tf_op jit(solution)/shard_map/ppermute | solution.py:46
  145.8 10.0 %collective-permute-start.25 = (bf16[3,32,768]{2,1,0:T(8,128)(2,1)S(1)}, bf16[3,32,768]{2,1,0:T(8,128)(2,1)S(1)}, u32[]{:S(2)}, u32[]{:S(2)}) collective-permute-start(bf16[3,32,768]{2,1,0:T(8,128)(2,1)S(1)} %get-tuple-element.109), channel_id=1, source_target_pairs={{32,0},{4,32},{36,4},{8,36},{40,8},{12,40},{44,12},{16,44},{48,16}... | collective-permute-start | bytes 442376 | tf_op jit(solution)/shard_map/ppermute | solution.py:46
  165.3 11.2 %collective-permute-start.29 = (bf16[256,384]{1,0:T(8,128)(2,1)S(1)}, bf16[256,384]{1,0:T(8,128)(2,1)S(1)}, u32[]{:S(2)}, u32[]{:S(2)}) collective-permute-start(bf16[256,384]{1,0:T(8,128)(2,1)S(1)} %merge.3.refs_0_), channel_id=1, source_target_pairs={{3,0},{0,1},{1,2},{2,3},{7,4},{4,5},{5,6},{6,7},{11,8},{8,9},{9,10... | collective-permute-start | bytes 589832 | tf_op jit(solution)/shard_map/ppermute | solution.py:20
  165.3 11.2 %collective-permute-start.28 = (bf16[256,384]{1,0:T(8,128)(2,1)S(1)}, bf16[256,384]{1,0:T(8,128)(2,1)S(1)}, u32[]{:S(2)}, u32[]{:S(2)}) collective-permute-start(bf16[256,384]{1,0:T(8,128)(2,1)S(1)} %merge.3.refs_0_), channel_id=1, source_target_pairs={{2,0},{3,1},{0,2},{1,3},{6,4},{7,5},{4,6},{5,7},{10,8},{11,9},{8,1... | collective-permute-start | bytes 589832 | tf_op jit(solution)/shard_map/ppermute | solution.py:20
  (45 other events, 502.3 us)

commit v11 on v10

--- a/solution.py
+++ b/solution.py
@@ -105,39 +105,40 @@
     )(*parts)
 
 
-def collect_kernel(core, home, got, handed, cache):
-    rows, cols = home.shape[1] // 4, cache.shape[-1]
-    features1, keys1, features2, keys0 = (slice(i * rows, (i + 1) * rows) for i in range(4))
-
-    def collect(features, keys, refs):
-        for half, ref in enumerate(refs):
+def collect_kernel(core, early, got_early, home, got, handed, cache):
+    rows, cols = early.shape[1], cache.shape[-1]
+    features1, keys1, features2 = (slice(i * rows, (i + 1) * rows) for i in range(3))
+
+    def collect(features, feature_refs, keys, key_refs):
+        for half in range(2):
             here = slice(half * rows, (half + 1) * rows)
-            handed[:, here] = ref[:, features]
+            handed[:, here] = feature_refs[half][:, features]
             for which in range(2):
-                cache[which, :, here] = ref[:, keys, which * cols : (which + 1) * cols]
+                cut = slice(which * cols, (which + 1) * cols)
+                cache[which, :, here] = key_refs[half][:, keys, cut]
 
     @pl.when(core[0] == 0)
     def _():
-        collect(features2, keys0, (home, got))
+        collect(features2, (home, got), slice(0, rows), (early, got_early))
 
     @pl.when(core[0] == 1)
     def _():
-        collect(features1, keys1, (got, home))
-
-
-def collect(core, home, got):
-    patches, rows, cols = home.shape
+        collect(features1, (got, home), keys1, (got, home))
+
+
+def collect(core, early, got_early, home, got):
+    patches, rows, cols = early.shape
     return pl.pallas_call(
         collect_kernel,
-        in_specs=[SCALARS] + [ON_CHIP] * 2,
+        in_specs=[SCALARS] + [ON_CHIP] * 4,
         out_specs=[ON_CHIP] * 2,
         out_shape=[
-            struct((patches, rows // 2, cols)),
-            struct((2, patches, rows // 2, cols // 2)),
+            struct((patches, 2 * rows, cols)),
+            struct((2, patches, 2 * rows, cols // 2)),
         ],
         compiler_params=params(8),
         name="collect",
-    )(core, home, got)
+    )(core, early, got_early, home, got)
 
 
 def choose(meta, kv, stale, outs):
@@ -156,34 +157,16 @@
             out[...] = stale[cut, old]
 
 
-def choose_kernel(meta, kv, stale, lo_out, hi_out, far_out):
-    choose(meta, kv, stale, (lo_out, hi_out, far_out))
-
-
 def payloads(kv_shape):
     edge = struct((REACH,) + kv_shape[1:])
     return [edge, edge, struct(kv_shape)]
 
 
-def choose_alone(meta, kv, stale):
-    return pl.pallas_call(
-        choose_kernel,
-        in_specs=[SCALARS] + [ON_CHIP] * 2,
-        out_specs=[ON_CHIP] * 3,
-        out_shape=payloads(kv.shape),
-        compiler_params=params(8),
-        name="choose",
-    )(meta, kv, stale)
-
-
-def project_kernel(meta, *refs, with_stale):
+def project_kernel(meta, *refs):
     blocks = refs[:4]
-    shift, scale, gain, w_own, w_other = refs[4:9]
-    refs = refs[9:]
-    if with_stale:
-        stale, q_out, kv_out, *outs = refs[:-4]
-    else:
-        q_out, kv_out = refs[:-4]
+    shift, scale, gain, w_own, w_other, _ = refs[4:10]
+    refs = refs[10:]
+    stale, q_out, kv_out, *outs = refs[:-4]
     xs, modded, weights, sems = refs[-4:]
     _, rows, cols = xs.shape
     tiles, rows_tile, kv_cols = kv_out.shape
@@ -248,31 +231,23 @@
                 q_out[:, :, cut] = vec
             else:
                 kv_out[:, :, cut] = vec
-    if with_stale:
-        choose(meta, kv_out, stale, outs)
-
-
-def project(meta, blocks, shift, scale, gain, w_own, w_other, stale, kv_shape):
+    choose(meta, kv_out, stale, outs)
+
+
+def project(meta, blocks, shift, scale, gain, w_own, w_other, begun, stale):
     rows, cols = blocks[0].shape
-    tiles, rows_tile, kv_cols = kv_shape
+    tiles, rows_tile, kv_cols = stale.shape[0], stale.shape[1] // 2, stale.shape[2]
+    kv_shape = (tiles, rows_tile, kv_cols)
+    parts = shift.shape[0]
     heads_cols = kv_cols // 2
-    parts = shift.shape[0]
-    shapes = [struct((tiles, rows_tile, heads_cols)), struct(kv_shape)]
-    extra = []
-    if stale is not None:
-        shapes += payloads(kv_shape)
-        extra = [stale]
-
-    def kernel(*refs):
-        project_kernel(*refs, with_stale=stale is not None)
-
-    return pl.pallas_call(
-        kernel,
+    shapes = [struct((tiles, rows_tile, heads_cols)), struct(kv_shape)] + payloads(kv_shape)
+    return pl.pallas_call(
+        project_kernel,
         in_specs=[SCALARS]
         + [ANYWHERE] * len(blocks)
         + [ON_CHIP] * 3
-        + [ANYWHERE] * 2
-        + [ON_CHIP] * len(extra),
+        + [ANYWHERE] * 3
+        + [ON_CHIP],
         out_specs=[ON_CHIP] * len(shapes),
         out_shape=shapes,
         scratch_shapes=[
@@ -283,7 +258,7 @@
         ],
         compiler_params=params(52),
         name="project",
-    )(meta, *blocks, shift, scale, gain, w_own, w_other, *extra)
+    )(meta, *blocks, shift, scale, gain, w_own, w_other, begun, stale)
 
 
 def soften(queries, keys, values, times, floors):
@@ -370,7 +345,7 @@
             queries += [asked[:, cut] for cut in cuts]
             keys += [both[:, cut] for cut in cuts]
             values += [both[:, heads_cols + cut.start : heads_cols + cut.stop] for cut in cuts]
-            times += [multiple[tile, :, : both.shape[0]]] * heads
+            times += [multiple[tile, :, 256 : 256 + both.shape[0]]] * heads
             floors += [extra[:, head : head + 1] for head in range(heads)]
             earlier += [extra[:, 64 + head : 65 + head] for head in range(heads)]
         peaks, totals, summed = soften(queries, keys, values, times, floors)
@@ -528,18 +503,18 @@
     wo_across = shifted(wo_across, "tp", 2)
     hidden = exchanged(mine).reshape(rows, part_cols)
     stale, stale_send = halve(core_scalar, after(stale_cache[0], mine))
-    stale = join(stale, shifted(stale_send, "segment", 1))
-    hidden, stale, wo_across, weight = lax.optimization_barrier(
-        (hidden, stale, wo_across, w_out[0])
+    stale_got = shifted(stale_send, "segment", 1)
+    w_other = shifted(w_own, "segment", 1)
+    modulation, qk_gain, kv_tiles, tile_counts, patch_order = after(
+        (modulation, qk_gain, kv_tiles, tile_counts, patch_order), stale_got
     )
-    w_other = shifted(w_own, "segment", 1)
+    stale = exchanged(join(stale, stale_got))
+    weight = after(w_out[0], stale_got)
+    slices = [columns(weight, j) for j in (1, 3)]
+    wo_own = [paired(columns(weight, 0), wo_across)]
+    wo_other = [shifted(wo_own[0], "segment", 1)]
     small_own = jnp.concatenate([modulation[0].reshape(-1), qk_gain[0].reshape(-1)])
     small_other = shifted(small_own, "segment", 1)
-    blocks = gather_features(hidden)
-    stale, weight, kv_tiles, tile_counts, patch_order, small_own, small_other = after(
-        (stale, weight, kv_tiles, tile_counts, patch_order, small_own, small_other), blocks[0]
-    )
-    stale = exchanged(stale)
     turns = jnp.arange(patches, dtype=jnp.int32)
     asked = jnp.stack([chip, chip - 1, chip + 1, chip - seq_size // 2 - 1]) % seq_size // share
     ranks = jnp.sum(jnp.where(patch_order[None] == asked[:, None], turns[None], 0), axis=-1)
@@ -557,22 +532,23 @@
         gain = small[3 * width :].reshape(2, head_dim)
         multiple = jnp.where(is_own, multiple_own, multiple_other)
         given.append(
-            (meta, modul[0], modul[1], modul[2], gain, multiple[..., :256], multiple[..., 256:])
+            (meta, modul[0], modul[1], modul[2], gain, multiple)
         )
-    slices = [columns(weight, j) for j in (1, 3)]
-    wo_own = [paired(columns(weight, 0), wo_across)]
-    wo_other = [shifted(wo_own[0], "segment", 1)]
+    hidden, stale, slices, wo_own, wo_other, given = lax.optimization_barrier(
+        (hidden, stale, slices, wo_own, wo_other, given)
+    )
 
     for section in range(2):
-        if section == 0:
-            blocks, given, slices, wo_other = lax.optimization_barrier(
-                (blocks, given, slices, wo_other)
-            )
-        else:
-            blocks = gather_features(hidden)
-            hidden1, keys0 = hidden.reshape(kv.shape), kv
-        meta, shift, scale, gates, gain, times_own, times_rest = given[section]
-        q_own, kv, *going = project(
+        blocks = gather_features(hidden)
+        begun = meta = given[section][0]
+        if section > 0:
+            hidden1 = hidden.reshape(kv.shape)
+            begun = shifted(hidden[:16, :HEAD_DIM], "segment", 1)
+            early = exchanged(after(kv, begun))
+            blocks, early = lax.optimization_barrier((blocks, early))
+            got_early = shifted(early, "segment", 1)
+        meta, shift, scale, gates, gain, times = given[section]
+        q_own, kv, to_below, to_above, to_far = project(
             meta,
             blocks,
             shift,
@@ -580,35 +556,35 @@
             gain,
             w_own,
             w_other,
-            stale if section > 0 else None,
-            (patches, rows_core, 2 * heads_cols),
+            begun,
+            stale,
         )
-        if section == 0:
-            going = choose_alone(meta, kv, stale)
-        to_below, to_above, to_far = going
         far = along_ring(to_far, seq_size // 2 + 1, patches)
         above = along_ring(to_below, 1, patches)
         below = along_ring(to_above, -1, patches)
         q_other = shifted(q_own, "segment", 1)
         if section == 0:
-            wo_prev, wo_next = after(slices, q_other)
+            wo_prev, wo_next = after(slices, q_other, to_far)
             wo_prev, wo_next = shifted(wo_prev, "tp", 1), shifted(wo_next, "tp", 3)
             far, wo_prev, wo_next = lax.optimization_barrier((far, wo_prev, wo_next))
             wo_own.append(paired(wo_prev, wo_next))
-        before = attend_own(q_own, q_other, kv, times_own)
+        before = attend_own(q_own, q_other, kv, times)
         part_own, part_other = attend_rest(
-            q_own, q_other, below, above, far, times_rest, before
+            q_own, q_other, below, above, far, times, before
         )
         part_back = shifted(part_other, "segment", 1)
         if section == 0:
             wo_other.append(shifted(after(wo_own[1], part_back), "segment", 1))
+        else:
+            part_back, got_early = lax.optimization_barrier((part_back, got_early))
         att = merge(part_own, part_back)
         across = shifted(att, "tp", 2)
         atts = [att, across, shifted(att, "tp", 1), shifted(att, "tp", 3)]
         hidden = output(meta, atts, wo_own, wo_other, hidden, gates)
 
-    home = exchanged(join(hidden1, kv, hidden.reshape(kv.shape), keys0))
-    handed, new_cache = collect(core_scalar, home, shifted(home, "segment", 1))
+    home = exchanged(join(hidden1, kv, hidden.reshape(kv.shape)))
+    got = shifted(home, "segment", 1)
+    handed, new_cache = collect(core_scalar, early, got_early, home, got)
     return (handed[None], new_cache[None])
 
 

time: 212 us -> 217 us (1.024)
  waiting for transfers between devices: 66.7 us -> 75.9 us
  local copies, waits for them, and re-layouts: 15.7 us -> 9.63 us
  blocking collectives: 23.2 us -> 29.1 us
  Pallas kernels: 35.6 us -> 32.5 us
    all_to_all x1 -> x2, blocking collectives: 23.2 us -> 29.1 us  [exchanged(): return lax.all_to_all(tiles, 'seq', 0, 0, axis_index_groups=groups)]
    ppermute x6, starting transfers between devices: 20.3 us -> 15.7 us  [along_ring(): return lax.ppermute(block, 'seq', route)]
    ppermute x26 -> x28, waiting for transfers between devices: 50.1 us -> 54.4 us  [shifted(): return lax.ppermute(block, axis, route)]
    ppermute x26 -> x28, starting transfers between devices: 34.4 us -> 37.7 us  [shifted(): return lax.ppermute(block, axis, route)]
    all_to_all x2, waiting for transfers between devices: 7.88 us -> 11.2 us  [exchanged(): return lax.all_to_all(tiles, 'seq', 0, 0, axis_index_groups=groups)]
    slice x5 -> x2, local copies, waits for them, and re-layouts: 3.19 us -> 0.65 us  [the longest x1 0.65 us: local(): given.append((meta, modul[0], modul[1], modul[2], gain, multiple))]
    unnamed x70 -> x66, local copies, waits for them, and re-layouts: 5.93 us -> 3.77 us
    pallas_call x4 -> x3, Pallas kernels: 16.5 us -> 16.9 us  [the longest x2 15.6 us: project(): pl.pallas_call(project_kernel, in_specs=[SCALARS] + [ANYWHERE] * len(bloc...]
  transfers between devices with their start and end apart: 34 -> 36, of which waited for: 14 -> 16; matrix products, arithmetic and copies ran while one was open for 7% -> 4% of each run, Pallas kernels for 8% -> 3%
where the time goes in v11:
time: 217 us; the launch traced here: 215 us
  waiting for transfers between devices  75.9 us (35%)
  starting transfers between devices  63.7 us (29%)
  Pallas kernels  32.5 us (15%)
  blocking collectives  29.1 us (13%)
  local copies, waits for them, and re-layouts  9.63 us (4%)
  other arithmetic  3.31 us (2%)
    ppermute x28, waiting for transfers between devices, shifted(): return lax.ppermute(block, axis, route)  54.4 us
    ppermute x28, starting transfers between devices, shifted(): return lax.ppermute(block, axis, route)  37.7 us
    all_to_all x2, blocking collectives, exchanged(): return lax.all_to_all(tiles, 'seq', 0, 0, axis_index_groups=groups)  29.1 us
    ppermute x6, starting transfers between devices, along_ring(): return lax.ppermute(block, 'seq', route)  15.7 us
    pallas_call x2, Pallas kernels, project(): pl.pallas_call(project_kernel, in_specs=[SCALARS] + [ANYWHERE] * len(bloc...  15.6 us
    all_to_all x2, waiting for transfers between devices, exchanged(): return lax.all_to_all(tiles, 'seq', 0, 0, axis_index_groups=groups)  11.2 us
    ppermute x6, waiting for transfers between devices, along_ring(): return lax.ppermute(block, 'seq', route)  10.4 us
    all_to_all x2, starting transfers between devices, exchanged(): return lax.all_to_all(tiles, 'seq', 0, 0, axis_index_groups=groups)  10.3 us
  transfers between devices with their start and end apart: 36, of which 16 were waited for; matrix products, arithmetic and copies ran while one was open for 4% of the time, Pallas kernels for 3%

profile of v11, /device:TPU:1, one launch (start us, length us, event | category | flops | bytes accessed | tf_op | source)
XLA Modules:
  0.0 215.2 jit_solution(8115975298307098878)
XLA Ops:
  5.2 5.1 %all-to-all-start = ((bf16[8,32,768]{2,1,0:T(8,128)(2,1)}), bf16[8,32,768]{2,1,0:T(8,128)(2,1)S(1)}, u32[]{:S(2)}, u32[]{:S(2)}) async-start(bf16[8,32,768]{2,1,0:T(8,128)(2,1)} %constant_dynamic-slice_fusion.3), calls=%async_computation | async-start | bytes 786432 | tf_op jit(solution)/shard_map/all_to_all | solution.py:38
  10.3 3.6 %collective-permute-start.1 = (bf16[384,768]{1,0:T(8,128)(2,1)S(1)}, bf16[384,768]{1,0:T(8,128)(2,1)S(1)}, u32[]{:S(2)}, u32[]{:S(2)}) collective-permute-start(bf16[384,768]{1,0:T(8,128)(2,1)S(1)} %dynamic-slice_bitcast_fusion.1), channel_id=1, source_target_pairs={{2,0},{3,1},{0,2},{1,3},{6,4},{7,5},{4,6},{5,7},{10,8},{11,9},{8,1... | collective-permute-start | bytes 1769480 | tf_op jit(solution)/shard_map/ppermute | solution.py:20
  16.5 2.6 %dynamic-slice_bitcast_fusion = (bf16[1,384,768]{2,1,0:T(8,128)(2,1)S(1)}, bf16[384,768]{1,0:T(8,128)(2,1)}, bf16[384,768]{1,0:T(8,128)(2,1)}) fusion(bf16[384,3072]{1,0:T(8,128)(2,1)} %bitcast.75, s32[]{:T(128)S(6)} %select_n.89, s32[]{:T(128)S(6)} %select_n.88, s32[]{:T(128)S(6)} %select_n.87), kind=kLoop, calls=%fused_computation | loop fusion | bytes 3538956 | tf_op jit(solution)/shard_map/broadcast_in_dim | solution.py:448
  19.1 7.9 %collective-permute-done.1 = bf16[384,768]{1,0:T(8,128)(2,1)S(1)} collective-permute-done((bf16[384,768]{1,0:T(8,128)(2,1)S(1)}, bf16[384,768]{1,0:T(8,128)(2,1)S(1)}, u32[]{:S(2)}, u32[]{:S(2)}) %collective-permute-start.1) | collective-permute-done | bytes 589856 | tf_op jit(solution)/shard_map/ppermute | solution.py:20
  30.7 5.1 %all-to-all-start.1 = ((bf16[8,64,768]{2,1,0:T(8,128)(2,1)}), bf16[8,64,768]{2,1,0:T(8,128)(2,1)}, u32[]{:S(2)}, u32[]{:S(2)}) async-start(bf16[8,64,768]{2,1,0:T(8,128)(2,1)} %copy-done.5), calls=%async_computation.1 | async-start | bytes 1572864 | tf_op jit(solution)/shard_map/all_to_all | solution.py:38
  37.8 11.2 %all-to-all-done.1.refs_10_ = bf16[8,64,768]{2,1,0:T(8,128)(2,1)} async-done(((bf16[8,64,768]{2,1,0:T(8,128)(2,1)}), bf16[8,64,768]{2,1,0:T(8,128)(2,1)}, u32[]{:S(2)}, u32[]{:S(2)}) %all-to-all-start.1) | async-done | bytes 786464 | tf_op jit(solution)/shard_map/all_to_all | solution.py:38
  53.5 7.4 %collective-permute-done.7.refs_2_ = bf16[256,768]{1,0:T(8,128)(2,1)S(1)} collective-permute-done((bf16[256,768]{1,0:T(8,128)(2,1)S(1)}, bf16[256,768]{1,0:T(8,128)(2,1)S(1)}, u32[]{:S(2)}, u32[]{:S(2)}) %collective-permute-start.7) | collective-permute-done | bytes 393248 | tf_op jit(solution)/shard_map/ppermute | solution.py:20
  60.9 9.3 %collective-permute-done.5.refs_0_ = bf16[256,768]{1,0:T(8,128)(2,1)S(1)} collective-permute-done((bf16[256,768]{1,0:T(8,128)(2,1)S(1)}, bf16[256,768]{1,0:T(8,128)(2,1)S(1)}, u32[]{:S(2)}, u32[]{:S(2)}) %collective-permute-start.5) | collective-permute-done | bytes 393248 | tf_op jit(solution)/shard_map/ppermute | solution.py:20
  72.2 7.7 %project.2 = (bf16[8,32,384]{2,1,0:T(8,128)(2,1)S(1)}, bf16[8,32,768]{2,1,0:T(8,128)(2,1)S(1)}, bf16[3,32,768]{2,1,0:T(8,128)(2,1)S(1)}, bf16[3,32,768]{2,1,0:T(8,128)(2,1)S(1)}, bf16[8,32,768]{2,1,0:T(8,128)(2,1)S(1)}) custom-call(s32[5]{0:T(128)S(1)} %get-tuple-element.70.meta.refs_9_, bf16[256,768]{1,0:T(8,128)(2,1)S(1)} %collective-permute-done.5.refs_0_, ...), custom_call_target="tpu_custom_call" | custom-call | tf_op jit(solution)/shard_map/project/pallas_call | solution.py:244
  85.5 2.9 %collective-permute-start.12 = (bf16[8,32,768]{2,1,0:T(8,128)(2,1)S(1)}, bf16[8,32,768]{2,1,0:T(8,128)(2,1)S(1)}, u32[]{:S(2)}, u32[]{:S(2)}) collective-permute-start(bf16[8,32,768]{2,1,0:T(8,128)(2,1)S(1)} %get-tuple-element.79), channel_id=1, source_target_pairs={{48,0},{20,32},{52,4},{24,36},{56,8},{28,40},{60,12},{0,44},{32,16... | collective-permute-start | bytes 1179656 | tf_op jit(solution)/shard_map/ppermute | solution.py:46
  88.4 4.8 %collective-permute-start.11 = (bf16[3,32,768]{2,1,0:T(8,128)(2,1)S(1)}, bf16[3,32,768]{2,1,0:T(8,128)(2,1)S(1)}, u32[]{:S(2)}, u32[]{:S(2)}) collective-permute-start(bf16[3,32,768]{2,1,0:T(8,128)(2,1)S(1)} %get-tuple-element.78), channel_id=1, source_target_pairs={{32,0},{4,32},{36,4},{8,36},{40,8},{12,40},{44,12},{16,44},{48,16}... | collective-permute-start | bytes 442376 | tf_op jit(solution)/shard_map/ppermute | solution.py:46
  95.6 7.1 %collective-permute-done.12.far = bf16[8,32,768]{2,1,0:T(8,128)(2,1)S(1)} collective-permute-done((bf16[8,32,768]{2,1,0:T(8,128)(2,1)S(1)}, bf16[8,32,768]{2,1,0:T(8,128)(2,1)S(1)}, u32[]{:S(2)}, u32[]{:S(2)}) %collective-permute-start.12) | collective-permute-done | bytes 393248 | tf_op jit(solution)/shard_map/ppermute | solution.py:46
  111.7 4.0 %collective-permute-done.18.refs_3_ = bf16[256,384]{1,0:T(8,128)(2,1)S(1)} collective-permute-done((bf16[256,384]{1,0:T(8,128)(2,1)S(1)}, bf16[256,384]{1,0:T(8,128)(2,1)S(1)}, u32[]{:S(2)}, u32[]{:S(2)}) %collective-permute-start.18) | collective-permute-done | bytes 196640 | tf_op jit(solution)/shard_map/ppermute | solution.py:20
  115.8 6.2 %collective-permute-done.17.refs_2_ = bf16[256,384]{1,0:T(8,128)(2,1)S(1)} collective-permute-done((bf16[256,384]{1,0:T(8,128)(2,1)S(1)}, bf16[256,384]{1,0:T(8,128)(2,1)S(1)}, u32[]{:S(2)}, u32[]{:S(2)}) %collective-permute-start.17) | collective-permute-done | bytes 196640 | tf_op jit(solution)/shard_map/ppermute | solution.py:20
  124.3 2.7 %collective-permute-start.21 = (bf16[256,768]{1,0:T(8,128)(2,1)S(1)}, bf16[256,768]{1,0:T(8,128)(2,1)S(1)}, u32[]{:S(2)}, u32[]{:S(2)}) collective-permute-start(bf16[256,768]{1,0:T(8,128)(2,1)S(1)} %output.2.refs_3_.refs_8_), channel_id=1, source_target_pairs={{1,0},{2,1},{3,2},{0,3},{5,4},{6,5},{7,6},{4,7},{9,8},{10,9},{11,1... | collective-permute-start | bytes 1179656 | tf_op jit(solution)/shard_map/ppermute | solution.py:20
  129.6 10.9 %all_to_all.20.early = bf16[8,32,768]{2,1,0:T(8,128)(2,1)S(1)} all-to-all(bf16[8,32,768]{2,1,0:T(8,128)(2,1)S(1)} %get-tuple-element.95.own), channel_id=1, replica_groups={{0,4,8,12,16,20,24,28},{32,36,40,44,48,52,56,60},{1,5,9,13,17,21,25,29}..., dimensions={0} | all-to-all | bytes 786432 | tf_op jit(solution)/shard_map/all_to_all | solution.py:38
  142.6 7.9 %project.3 = (bf16[8,32,384]{2,1,0:T(8,128)(2,1)S(1)}, bf16[8,32,768]{2,1,0:T(8,128)(2,1)S(1)}, bf16[3,32,768]{2,1,0:T(8,128)(2,1)S(1)}, bf16[3,32,768]{2,1,0:T(8,128)(2,1)S(1)}, bf16[8,32,768]{2,1,0:T(8,128)(2,1)S(1)}) custom-call(s32[5]{0:T(128)S(1)} %copy-done.18, bf16[256,768]{1,0:T(8,128)(2,1)S(1)} %collective-permute-done.20.refs_0_, ...), custom_call_target="tpu_custom_call" | custom-call | tf_op jit(solution)/shard_map/project/pallas_call | solution.py:244
  150.5 3.2 %collective-permute-start.27 = (bf16[8,32,768]{2,1,0:T(8,128)(2,1)S(1)}, bf16[8,32,768]{2,1,0:T(8,128)(2,1)S(1)}, u32[]{:S(2)}, u32[]{:S(2)}) collective-permute-start(bf16[8,32,768]{2,1,0:T(8,128)(2,1)S(1)} %get-tuple-element.108), channel_id=1, source_target_pairs={{48,0},{20,32},{52,4},{24,36},{56,8},{28,40},{60,12},{0,44},{32,16... | collective-permute-start | bytes 1179656 | tf_op jit(solution)/shard_map/ppermute | solution.py:46
  153.7 4.0 %collective-permute-start.24 = (bf16[8,32,384]{2,1,0:T(8,128)(2,1)S(1)}, bf16[8,32,384]{2,1,0:T(8,128)(2,1)S(1)}, u32[]{:S(2)}, u32[]{:S(2)}) collective-permute-start(bf16[8,32,384]{2,1,0:T(8,128)(2,1)S(1)} %get-tuple-element.105.q_own), channel_id=1, source_target_pairs={{64,0},{0,64},{65,1},{1,65},{66,2},{2,66},{67,3},{3,67},{68,4},{4,... | collective-permute-start | bytes 589832 | tf_op jit(solution)/shard_map/ppermute | solution.py:20
  157.8 4.8 %collective-permute-start.26 = (bf16[3,32,768]{2,1,0:T(8,128)(2,1)S(1)}, bf16[3,32,768]{2,1,0:T(8,128)(2,1)S(1)}, u32[]{:S(2)}, u32[]{:S(2)}) collective-permute-start(bf16[3,32,768]{2,1,0:T(8,128)(2,1)S(1)} %get-tuple-element.107), channel_id=1, source_target_pairs={{32,0},{4,32},{36,4},{8,36},{40,8},{12,40},{44,12},{16,44},{48,16}... | collective-permute-start | bytes 442376 | tf_op jit(solution)/shard_map/ppermute | solution.py:46
  165.0 3.3 %collective-permute-done.25.below = bf16[3,32,768]{2,1,0:T(8,128)(2,1)S(1)} collective-permute-done((bf16[3,32,768]{2,1,0:T(8,128)(2,1)S(1)}, bf16[3,32,768]{2,1,0:T(8,128)(2,1)S(1)}, u32[]{:S(2)}, u32[]{:S(2)}) %collective-permute-start.25) | collective-permute-done | bytes 147488 | tf_op jit(solution)/shard_map/ppermute | solution.py:46
  180.9 7.4 %collective-permute-done.31.refs_2_ = bf16[256,384]{1,0:T(8,128)(2,1)S(1)} collective-permute-done((bf16[256,384]{1,0:T(8,128)(2,1)S(1)}, bf16[256,384]{1,0:T(8,128)(2,1)S(1)}, u32[]{:S(2)}, u32[]{:S(2)}) %collective-permute-start.31) | collective-permute-done | bytes 196640 | tf_op jit(solution)/shard_map/ppermute | solution.py:20
  190.8 18.2 %all_to_all.21.home = bf16[8,96,768]{2,1,0:T(8,128)(2,1)S(1)} all-to-all(bf16[8,96,768]{2,1,0:T(8,128)(2,1)S(1)} %join.7), channel_id=1, replica_groups={{0,4,8,12,16,20,24,28},{32,36,40,44,48,52,56,60},{1,5,9,13,17,21,25,29}..., dimensions={0} | all-to-all | bytes 2359296 | tf_op jit(solution)/shard_map/all_to_all | solution.py:38
  208.9 2.6 %collective-permute-start.33 = (bf16[8,96,768]{2,1,0:T(8,128)(2,1)S(1)}, bf16[8,96,768]{2,1,0:T(8,128)(2,1)S(1)}, u32[]{:S(2)}, u32[]{:S(2)}) collective-permute-start(bf16[8,96,768]{2,1,0:T(8,128)(2,1)S(1)} %all_to_all.21.home), channel_id=1, source_target_pairs={{64,0},{0,64},{65,1},{1,65},{66,2},{2,66},{67,3},{3,67},{68,4},{4,... | collective-permute-start | bytes 3538952 | tf_op jit(solution)/shard_map/ppermute | solution.py:20
  (152 shorter events, 64.3 us)
Async XLA Ops:
  0.7 69.5 %collective-permute-start.8 = (bf16[3,3072,384]{2,1,0:T(8,128)(2,1)}, bf16[3,3072,384]{2,1,0:T(8,128)(2,1)}, u32[]{:S(2)}, u32[]{:S(2)}) collective-permute-start(bf16[3,3072,384]{2,1,0:T(8,128)(2,1)} %bitcast.72), channel_id=1, source_target_pairs={{64,0},{0,64},{65,1},{1,65},{66,2},{2,66},{67,3},{3,67},{68,4},{4,... | collective-permute-start | bytes 21233672 | tf_op jit(solution)/shard_map/ppermute | solution.py:20
  5.2 25.5 %all-to-all-start = ((bf16[8,32,768]{2,1,0:T(8,128)(2,1)}), bf16[8,32,768]{2,1,0:T(8,128)(2,1)S(1)}, u32[]{:S(2)}, u32[]{:S(2)}) async-start(bf16[8,32,768]{2,1,0:T(8,128)(2,1)} %constant_dynamic-slice_fusion.3), calls=%async_computation | async-start | bytes 786432 | tf_op jit(solution)/shard_map/all_to_all | solution.py:38
  10.3 16.7 %collective-permute-start.1 = (bf16[384,768]{1,0:T(8,128)(2,1)S(1)}, bf16[384,768]{1,0:T(8,128)(2,1)S(1)}, u32[]{:S(2)}, u32[]{:S(2)}) collective-permute-start(bf16[384,768]{1,0:T(8,128)(2,1)S(1)} %dynamic-slice_bitcast_fusion.1), channel_id=1, source_target_pairs={{2,0},{3,1},{0,2},{1,3},{6,4},{7,5},{4,6},{5,7},{10,8},{11,9},{8,1... | collective-permute-start | bytes 1769480 | tf_op jit(solution)/shard_map/ppermute | solution.py:20
  14.7 21.1 %collective-permute-start.3 = (f32[9472]{0:T(1024)}, f32[9472]{0:T(1024)}, u32[]{:S(2)}, u32[]{:S(2)}) collective-permute-start(f32[9472]{0:T(1024)} %pad_maximum_fusion), channel_id=1, source_target_pairs={{64,0},{0,64},{65,1},{1,65},{66,2},{2,66},{67,3},{3,67},{68,4},{4,... | collective-permute-start | bytes 113672 | tf_op jit(solution)/shard_map/ppermute | solution.py:20
  16.1 14.0 %collective-permute-start.4 = (f32[8,1,384]{2,1,0:T(1,128)S(1)}, f32[8,1,384]{2,1,0:T(1,128)S(1)}, u32[]{:S(2)}, u32[]{:S(2)}) collective-permute-start(f32[8,1,384]{2,1,0:T(1,128)S(1)} %broadcast_in_dim.50), channel_id=1, source_target_pairs={{64,0},{0,64},{65,1},{1,65},{66,2},{2,66},{67,3},{3,67},{68,4},{4,... | collective-permute-start | bytes 36872 | tf_op jit(solution)/shard_map/ppermute | solution.py:20
  27.2 21.8 %collective-permute-start.2 = (bf16[768,768]{1,0:T(8,128)(2,1)S(1)}, bf16[768,768]{1,0:T(8,128)(2,1)S(1)}, u32[]{:S(2)}, u32[]{:S(2)}) collective-permute-start(bf16[768,768]{1,0:T(8,128)(2,1)S(1)} %bitcast.49), channel_id=1, source_target_pairs={{64,0},{0,64},{65,1},{1,65},{66,2},{2,66},{67,3},{3,67},{68,4},{4,... | collective-permute-start | bytes 3538952 | tf_op jit(solution)/shard_map/ppermute | solution.py:20
  30.7 18.3 %all-to-all-start.1 = ((bf16[8,64,768]{2,1,0:T(8,128)(2,1)}), bf16[8,64,768]{2,1,0:T(8,128)(2,1)}, u32[]{:S(2)}, u32[]{:S(2)}) async-start(bf16[8,64,768]{2,1,0:T(8,128)(2,1)} %copy-done.5), calls=%async_computation.1 | async-start | bytes 1572864 | tf_op jit(solution)/shard_map/all_to_all | solution.py:38
  49.0 11.8 %collective-permute-start.7 = (bf16[256,768]{1,0:T(8,128)(2,1)S(1)}, bf16[256,768]{1,0:T(8,128)(2,1)S(1)}, u32[]{:S(2)}, u32[]{:S(2)}) collective-permute-start(bf16[256,768]{1,0:T(8,128)(2,1)S(1)} %bitcast.56), channel_id=1, source_target_pairs={{3,0},{0,1},{1,2},{2,3},{7,4},{4,5},{5,6},{6,7},{11,8},{8,9},{9,10... | collective-permute-start | bytes 1179656 | tf_op jit(solution)/shard_map/ppermute | solution.py:20
  50.0 10.8 %collective-permute-start.6 = (bf16[256,768]{1,0:T(8,128)(2,1)S(1)}, bf16[256,768]{1,0:T(8,128)(2,1)S(1)}, u32[]{:S(2)}, u32[]{:S(2)}) collective-permute-start(bf16[256,768]{1,0:T(8,128)(2,1)S(1)} %bitcast.57), channel_id=1, source_target_pairs={{1,0},{2,1},{3,2},{0,3},{5,4},{6,5},{7,6},{4,7},{9,8},{10,9},{11,1... | collective-permute-start | bytes 1179656 | tf_op jit(solution)/shard_map/ppermute | solution.py:20
  52.2 17.9 %collective-permute-start.5 = (bf16[256,768]{1,0:T(8,128)(2,1)S(1)}, bf16[256,768]{1,0:T(8,128)(2,1)S(1)}, u32[]{:S(2)}, u32[]{:S(2)}) collective-permute-start(bf16[256,768]{1,0:T(8,128)(2,1)S(1)} %bitcast.58), channel_id=1, source_target_pairs={{2,0},{3,1},{0,2},{1,3},{6,4},{7,5},{4,6},{5,7},{10,8},{11,9},{8,1... | collective-permute-start | bytes 1179656 | tf_op jit(solution)/shard_map/ppermute | solution.py:20
  82.8 19.9 %collective-permute-start.13 = (bf16[384,768]{1,0:T(8,128)(2,1)S(1)}, bf16[384,768]{1,0:T(8,128)(2,1)S(1)}, u32[]{:S(2)}, u32[]{:S(2)}) collective-permute-start(bf16[384,768]{1,0:T(8,128)(2,1)S(1)} %copy-done.22), channel_id=1, source_target_pairs={{3,0},{0,1},{1,2},{2,3},{7,4},{4,5},{5,6},{6,7},{11,8},{8,9},{9,10... | collective-permute-start | bytes 1769480 | tf_op jit(solution)/shard_map/ppermute | solution.py:20
  83.7 19.0 %collective-permute-start.14 = (bf16[384,768]{1,0:T(8,128)(2,1)S(1)}, bf16[384,768]{1,0:T(8,128)(2,1)S(1)}, u32[]{:S(2)}, u32[]{:S(2)}) collective-permute-start(bf16[384,768]{1,0:T(8,128)(2,1)S(1)} %copy-done.21), channel_id=1, source_target_pairs={{1,0},{2,1},{3,2},{0,3},{5,4},{6,5},{7,6},{4,7},{9,8},{10,9},{11,1... | collective-permute-start | bytes 1769480 | tf_op jit(solution)/shard_map/ppermute | solution.py:20
  85.5 17.2 %collective-permute-start.12 = (bf16[8,32,768]{2,1,0:T(8,128)(2,1)S(1)}, bf16[8,32,768]{2,1,0:T(8,128)(2,1)S(1)}, u32[]{:S(2)}, u32[]{:S(2)}) collective-permute-start(bf16[8,32,768]{2,1,0:T(8,128)(2,1)S(1)} %get-tuple-element.79), channel_id=1, source_target_pairs={{48,0},{20,32},{52,4},{24,36},{56,8},{28,40},{60,12},{0,44},{32,16... | collective-permute-start | bytes 1179656 | tf_op jit(solution)/shard_map/ppermute | solution.py:46
  88.4 14.3 %collective-permute-start.10 = (bf16[3,32,768]{2,1,0:T(8,128)(2,1)S(1)}, bf16[3,32,768]{2,1,0:T(8,128)(2,1)S(1)}, u32[]{:S(2)}, u32[]{:S(2)}) collective-permute-start(bf16[3,32,768]{2,1,0:T(8,128)(2,1)S(1)} %get-tuple-element.77), channel_id=1, source_target_pairs={{60,0},{0,32},{32,4},{4,36},{36,8},{8,40},{40,12},{12,44},{44,16},... | collective-permute-start | bytes 442376 | tf_op jit(solution)/shard_map/ppermute | solution.py:46
  88.4 14.3 %collective-permute-start.11 = (bf16[3,32,768]{2,1,0:T(8,128)(2,1)S(1)}, bf16[3,32,768]{2,1,0:T(8,128)(2,1)S(1)}, u32[]{:S(2)}, u32[]{:S(2)}) collective-permute-start(bf16[3,32,768]{2,1,0:T(8,128)(2,1)S(1)} %get-tuple-element.78), channel_id=1, source_target_pairs={{32,0},{4,32},{36,4},{8,36},{40,8},{12,40},{44,12},{16,44},{48,16}... | collective-permute-start | bytes 442376 | tf_op jit(solution)/shard_map/ppermute | solution.py:46
  108.4 13.5 %collective-permute-start.19 = (bf16[768,768]{1,0:T(8,128)(2,1)S(1)}, bf16[768,768]{1,0:T(8,128)(2,1)S(1)}, u32[]{:S(2)}, u32[]{:S(2)}) collective-permute-start(bf16[768,768]{1,0:T(8,128)(2,1)S(1)} %bitcast.52), channel_id=1, source_target_pairs={{64,0},{0,64},{65,1},{1,65},{66,2},{2,66},{67,3},{3,67},{68,4},{4,... | collective-permute-start | bytes 3538952 | tf_op jit(solution)/shard_map/ppermute | solution.py:20
  110.5 11.5 %collective-permute-start.17 = (bf16[256,384]{1,0:T(8,128)(2,1)S(1)}, bf16[256,384]{1,0:T(8,128)(2,1)S(1)}, u32[]{:S(2)}, u32[]{:S(2)}) collective-permute-start(bf16[256,384]{1,0:T(8,128)(2,1)S(1)} %merge.2.refs_0_), channel_id=1, source_target_pairs={{3,0},{0,1},{1,2},{2,3},{7,4},{4,5},{5,6},{6,7},{11,8},{8,9},{9,10... | collective-permute-start | bytes 589832 | tf_op jit(solution)/shard_map/ppermute | solution.py:20
  110.9 11.1 %collective-permute-start.16 = (bf16[256,384]{1,0:T(8,128)(2,1)S(1)}, bf16[256,384]{1,0:T(8,128)(2,1)S(1)}, u32[]{:S(2)}, u32[]{:S(2)}) collective-permute-start(bf16[256,384]{1,0:T(8,128)(2,1)S(1)} %merge.2.refs_0_), channel_id=1, source_target_pairs={{2,0},{3,1},{0,2},{1,3},{6,4},{7,5},{4,6},{5,7},{10,8},{11,9},{8,1... | collective-permute-start | bytes 589832 | tf_op jit(solution)/shard_map/ppermute | solution.py:20
  124.2 16.3 %collective-permute-start.22 = (bf16[256,768]{1,0:T(8,128)(2,1)S(1)}, bf16[256,768]{1,0:T(8,128)(2,1)S(1)}, u32[]{:S(2)}, u32[]{:S(2)}) collective-permute-start(bf16[256,768]{1,0:T(8,128)(2,1)S(1)} %output.2.refs_3_.refs_8_), channel_id=1, source_target_pairs={{3,0},{0,1},{1,2},{2,3},{7,4},{4,5},{5,6},{6,7},{11,8},{8,9},{9,10... | collective-permute-start | bytes 1179656 | tf_op jit(solution)/shard_map/ppermute | solution.py:20
  124.3 16.2 %collective-permute-start.21 = (bf16[256,768]{1,0:T(8,128)(2,1)S(1)}, bf16[256,768]{1,0:T(8,128)(2,1)S(1)}, u32[]{:S(2)}, u32[]{:S(2)}) collective-permute-start(bf16[256,768]{1,0:T(8,128)(2,1)S(1)} %output.2.refs_3_.refs_8_), channel_id=1, source_target_pairs={{1,0},{2,1},{3,2},{0,3},{5,4},{6,5},{7,6},{4,7},{9,8},{10,9},{11,1... | collective-permute-start | bytes 1179656 | tf_op jit(solution)/shard_map/ppermute | solution.py:20
  127.0 15.6 %collective-permute-start.20 = (bf16[256,768]{1,0:T(8,128)(2,1)S(1)}, bf16[256,768]{1,0:T(8,128)(2,1)S(1)}, u32[]{:S(2)}, u32[]{:S(2)}) collective-permute-start(bf16[256,768]{1,0:T(8,128)(2,1)S(1)} %output.2.refs_3_.refs_8_), channel_id=1, source_target_pairs={{2,0},{3,1},{0,2},{1,3},{6,4},{7,5},{4,6},{5,7},{10,8},{11,9},{8,1... | collective-permute-start | bytes 1179656 | tf_op jit(solution)/shard_map/ppermute | solution.py:20
  150.5 17.8 %collective-permute-start.27 = (bf16[8,32,768]{2,1,0:T(8,128)(2,1)S(1)}, bf16[8,32,768]{2,1,0:T(8,128)(2,1)S(1)}, u32[]{:S(2)}, u32[]{:S(2)}) collective-permute-start(bf16[8,32,768]{2,1,0:T(8,128)(2,1)S(1)} %get-tuple-element.108), channel_id=1, source_target_pairs={{48,0},{20,32},{52,4},{24,36},{56,8},{28,40},{60,12},{0,44},{32,16... | collective-permute-start | bytes 1179656 | tf_op jit(solution)/shard_map/ppermute | solution.py:46
  177.1 11.2 %collective-permute-start.31 = (bf16[256,384]{1,0:T(8,128)(2,1)S(1)}, bf16[256,384]{1,0:T(8,128)(2,1)S(1)}, u32[]{:S(2)}, u32[]{:S(2)}) collective-permute-start(bf16[256,384]{1,0:T(8,128)(2,1)S(1)} %merge.3.refs_0_), channel_id=1, source_target_pairs={{3,0},{0,1},{1,2},{2,3},{7,4},{4,5},{5,6},{6,7},{11,8},{8,9},{9,10... | collective-permute-start | bytes 589832 | tf_op jit(solution)/shard_map/ppermute | solution.py:20
  177.1 11.2 %collective-permute-start.30 = (bf16[256,384]{1,0:T(8,128)(2,1)S(1)}, bf16[256,384]{1,0:T(8,128)(2,1)S(1)}, u32[]{:S(2)}, u32[]{:S(2)}) collective-permute-start(bf16[256,384]{1,0:T(8,128)(2,1)S(1)} %merge.3.refs_0_), channel_id=1, source_target_pairs={{2,0},{3,1},{0,2},{1,3},{6,4},{7,5},{4,6},{5,7},{10,8},{11,9},{8,1... | collective-permute-start | bytes 589832 | tf_op jit(solution)/shard_map/ppermute | solution.py:20
  (45 other events, 518.3 us)

commit v12 on v11

--- a/solution.py
+++ b/solution.py
@@ -157,16 +157,34 @@
             out[...] = stale[cut, old]
 
 
+def choose_kernel(meta, kv, stale, lo_out, hi_out, far_out):
+    choose(meta, kv, stale, (lo_out, hi_out, far_out))
+
+
 def payloads(kv_shape):
     edge = struct((REACH,) + kv_shape[1:])
     return [edge, edge, struct(kv_shape)]
 
 
-def project_kernel(meta, *refs):
+def choose_alone(meta, kv, stale):
+    return pl.pallas_call(
+        choose_kernel,
+        in_specs=[SCALARS] + [ON_CHIP] * 2,
+        out_specs=[ON_CHIP] * 3,
+        out_shape=payloads(kv.shape),
+        compiler_params=params(8),
+        name="choose",
+    )(meta, kv, stale)
+
+
+def project_kernel(meta, *refs, with_stale):
     blocks = refs[:4]
     shift, scale, gain, w_own, w_other, _ = refs[4:10]
     refs = refs[10:]
-    stale, q_out, kv_out, *outs = refs[:-4]
+    if with_stale:
+        stale, q_out, kv_out, *outs = refs[:-4]
+    else:
+        q_out, kv_out = refs[:-4]
     xs, modded, weights, sems = refs[-4:]
     _, rows, cols = xs.shape
     tiles, rows_tile, kv_cols = kv_out.shape
@@ -231,23 +249,31 @@
                 q_out[:, :, cut] = vec
             else:
                 kv_out[:, :, cut] = vec
-    choose(meta, kv_out, stale, outs)
-
-
-def project(meta, blocks, shift, scale, gain, w_own, w_other, begun, stale):
+    if with_stale:
+        choose(meta, kv_out, stale, outs)
+
+
+def project(meta, blocks, shift, scale, gain, w_own, w_other, begun, stale, kv_shape):
     rows, cols = blocks[0].shape
-    tiles, rows_tile, kv_cols = stale.shape[0], stale.shape[1] // 2, stale.shape[2]
-    kv_shape = (tiles, rows_tile, kv_cols)
+    tiles, rows_tile, kv_cols = kv_shape
     parts = shift.shape[0]
     heads_cols = kv_cols // 2
-    shapes = [struct((tiles, rows_tile, heads_cols)), struct(kv_shape)] + payloads(kv_shape)
-    return pl.pallas_call(
-        project_kernel,
+    shapes = [struct((tiles, rows_tile, heads_cols)), struct(kv_shape)]
+    extra = []
+    if stale is not None:
+        shapes += payloads(kv_shape)
+        extra = [stale]
+
+    def kernel(*refs):
+        project_kernel(*refs, with_stale=stale is not None)
+
+    return pl.pallas_call(
+        kernel,
         in_specs=[SCALARS]
         + [ANYWHERE] * len(blocks)
         + [ON_CHIP] * 3
         + [ANYWHERE] * 3
-        + [ON_CHIP],
+        + [ON_CHIP] * len(extra),
         out_specs=[ON_CHIP] * len(shapes),
         out_shape=shapes,
         scratch_shapes=[
@@ -258,7 +284,7 @@
         ],
         compiler_params=params(52),
         name="project",
-    )(meta, *blocks, shift, scale, gain, w_own, w_other, begun, stale)
+    )(meta, *blocks, shift, scale, gain, w_own, w_other, begun, *extra)
 
 
 def soften(queries, keys, values, times, floors):
@@ -505,21 +531,26 @@
     stale, stale_send = halve(core_scalar, after(stale_cache[0], mine))
     stale_got = shifted(stale_send, "segment", 1)
     w_other = shifted(w_own, "segment", 1)
-    modulation, qk_gain, kv_tiles, tile_counts, patch_order = after(
-        (modulation, qk_gain, kv_tiles, tile_counts, patch_order), stale_got
+    stale = join(stale, stale_got)
+    kv_tiles, tile_counts = after((kv_tiles, tile_counts), stale_got)
+    multiple_own = count_tiles(kv_tiles[0], tile_counts[0], chip, patches, rows_core)
+    hidden, stale, wo_across, multiple_own = lax.optimization_barrier(
+        (hidden, stale, wo_across, multiple_own)
     )
-    stale = exchanged(join(stale, stale_got))
-    weight = after(w_out[0], stale_got)
+    small_own = jnp.concatenate([modulation[0].reshape(-1), qk_gain[0].reshape(-1)])
+    small_other = shifted(small_own, "segment", 1)
+    blocks = gather_features(hidden)
+    stale, weight, multiple_own, patch_order, small_own, small_other = after(
+        (stale, w_out[0], multiple_own, patch_order, small_own, small_other), blocks[0]
+    )
+    stale = exchanged(stale)
     slices = [columns(weight, j) for j in (1, 3)]
     wo_own = [paired(columns(weight, 0), wo_across)]
     wo_other = [shifted(wo_own[0], "segment", 1)]
-    small_own = jnp.concatenate([modulation[0].reshape(-1), qk_gain[0].reshape(-1)])
-    small_other = shifted(small_own, "segment", 1)
     turns = jnp.arange(patches, dtype=jnp.int32)
     asked = jnp.stack([chip, chip - 1, chip + 1, chip - seq_size // 2 - 1]) % seq_size // share
     ranks = jnp.sum(jnp.where(patch_order[None] == asked[:, None], turns[None], 0), axis=-1)
     fresh = (ranks[0] <= ranks[1:]).astype(jnp.int32)
-    multiple_own = count_tiles(kv_tiles[0], tile_counts[0], chip, patches, rows_core)
     multiple_other = shifted(multiple_own, "segment", 1)
     given = []
     for section in range(2):
@@ -534,21 +565,22 @@
         given.append(
             (meta, modul[0], modul[1], modul[2], gain, multiple)
         )
-    hidden, stale, slices, wo_own, wo_other, given = lax.optimization_barrier(
-        (hidden, stale, slices, wo_own, wo_other, given)
-    )
 
     for section in range(2):
-        blocks = gather_features(hidden)
-        begun = meta = given[section][0]
-        if section > 0:
+        begun = given[section][0]
+        if section == 0:
+            blocks, given, slices, wo_other = lax.optimization_barrier(
+                (blocks, given, slices, wo_other)
+            )
+        else:
+            blocks = gather_features(hidden)
             hidden1 = hidden.reshape(kv.shape)
             begun = shifted(hidden[:16, :HEAD_DIM], "segment", 1)
             early = exchanged(after(kv, begun))
             blocks, early = lax.optimization_barrier((blocks, early))
             got_early = shifted(early, "segment", 1)
         meta, shift, scale, gates, gain, times = given[section]
-        q_own, kv, to_below, to_above, to_far = project(
+        q_own, kv, *going = project(
             meta,
             blocks,
             shift,
@@ -557,8 +589,12 @@
             w_own,
             w_other,
             begun,
-            stale,
+            stale if section > 0 else None,
+            (patches, rows_core, 2 * heads_cols),
         )
+        if section == 0:
+            going = choose_alone(meta, kv, stale)
+        to_below, to_above, to_far = going
         far = along_ring(to_far, seq_size // 2 + 1, patches)
         above = along_ring(to_below, 1, patches)
         below = along_ring(to_above, -1, patches)

time: 217 us -> 203 us (0.935)
  waiting for transfers between devices: 75.9 us -> 51.2 us
  starting transfers between devices: 63.7 us -> 71.8 us
  blocking collectives: 29.1 us -> 31.3 us
  local copies, waits for them, and re-layouts: 9.63 us -> 11.8 us
    ppermute x28, waiting for transfers between devices: 54.4 us -> 39.3 us  [shifted(): return lax.ppermute(block, axis, route)]
    all_to_all x2, waiting for transfers between devices: 11.2 us -> 3.17 us  [exchanged(): return lax.all_to_all(tiles, 'seq', 0, 0, axis_index_groups=groups)]
    ppermute x28, starting transfers between devices: 37.7 us -> 42.3 us  [shifted(): return lax.ppermute(block, axis, route)]
    ppermute x6, starting transfers between devices: 15.7 us -> 19.9 us  [along_ring(): return lax.ppermute(block, 'seq', route)]
    all_to_all x2, blocking collectives: 29.1 us -> 31.3 us  [exchanged(): return lax.all_to_all(tiles, 'seq', 0, 0, axis_index_groups=groups)]
    unnamed x66 -> x72, local copies, waits for them, and re-layouts: 3.77 us -> 4.5 us
    pallas_call x2 -> x3, Pallas kernels: 15.6 us -> 15.5 us  [the longest x2 14.8 us: project(): pl.pallas_call(kernel, in_specs=[SCALARS] + [ANYWHERE] * len(blocks) + [O...]
  transfers between devices with their start and end apart: 36 -> 36, of which waited for: 16 -> 16; matrix products, arithmetic and copies ran while one was open for 4% -> 4% of each run, Pallas kernels for 3% -> 7%
where the time goes in v12:
time: 203 us; the launch traced here: 202 us
  starting transfers between devices  71.8 us (35%)
  waiting for transfers between devices  51.2 us (25%)
  Pallas kernels  33.2 us (16%)
  blocking collectives  31.3 us (15%)
  local copies, waits for them, and re-layouts  11.8 us (6%)
    ppermute x28, starting transfers between devices, shifted(): return lax.ppermute(block, axis, route)  42.3 us
    ppermute x28, waiting for transfers between devices, shifted(): return lax.ppermute(block, axis, route)  39.3 us
    all_to_all x2, blocking collectives, exchanged(): return lax.all_to_all(tiles, 'seq', 0, 0, axis_index_groups=groups)  31.3 us
    ppermute x6, starting transfers between devices, along_ring(): return lax.ppermute(block, 'seq', route)  19.9 us
    pallas_call x2, Pallas kernels, project(): pl.pallas_call(kernel, in_specs=[SCALARS] + [ANYWHERE] * len(blocks) + [O...  14.8 us
    all_to_all x2, starting transfers between devices, exchanged(): return lax.all_to_all(tiles, 'seq', 0, 0, axis_index_groups=groups)  9.59 us
    ppermute x6, waiting for transfers between devices, along_ring(): return lax.ppermute(block, 'seq', route)  8.72 us
    pallas_call x2, Pallas kernels, attend_own(): pl.pallas_call(attend_own_kernel, in_specs=[ON_CHIP] * 4, out_specs=ON_CH...  4.83 us
  transfers between devices with their start and end apart: 36, of which 16 were waited for; matrix products, arithmetic and copies ran while one was open for 4% of the time, Pallas kernels for 7%

profile of v12, /device:TPU:1, one launch (start us, length us, event | category | flops | bytes accessed | tf_op | source)
XLA Modules:
  0.0 202.3 jit_solution(13334139755436084801)
XLA Ops:
  5.3 5.1 %all-to-all-start = ((bf16[8,32,768]{2,1,0:T(8,128)(2,1)}), bf16[8,32,768]{2,1,0:T(8,128)(2,1)S(1)}, u32[]{:S(2)}, u32[]{:S(2)}) async-start(bf16[8,32,768]{2,1,0:T(8,128)(2,1)} %constant_dynamic-slice_fusion.3), calls=%async_computation | async-start | bytes 786432 | tf_op jit(solution)/shard_map/all_to_all | solution.py:38
  10.4 3.6 %collective-permute-start.1 = (bf16[384,768]{1,0:T(8,128)(2,1)}, bf16[384,768]{1,0:T(8,128)(2,1)S(1)}, u32[]{:S(2)}, u32[]{:S(2)}) collective-permute-start(bf16[384,768]{1,0:T(8,128)(2,1)} %dynamic-slice_bitcast_fusion.1), channel_id=1, source_target_pairs={{2,0},{3,1},{0,2},{1,3},{6,4},{7,5},{4,6},{5,7},{10,8},{11,9},{8,1... | collective-permute-start | bytes 1769480 | tf_op jit(solution)/shard_map/ppermute | solution.py:20
  16.1 3.2 %all-to-all-done = bf16[8,32,768]{2,1,0:T(8,128)(2,1)S(1)} async-done(((bf16[8,32,768]{2,1,0:T(8,128)(2,1)}), bf16[8,32,768]{2,1,0:T(8,128)(2,1)S(1)}, u32[]{:S(2)}, u32[]{:S(2)}) %all-to-all-start) | async-done | bytes 393248 | tf_op jit(solution)/shard_map/all_to_all | solution.py:38
  19.2 8.0 %collective-permute-done.1 = bf16[384,768]{1,0:T(8,128)(2,1)S(1)} collective-permute-done((bf16[384,768]{1,0:T(8,128)(2,1)}, bf16[384,768]{1,0:T(8,128)(2,1)S(1)}, u32[]{:S(2)}, u32[]{:S(2)}) %collective-permute-start.1) | collective-permute-done | bytes 589856 | tf_op jit(solution)/shard_map/ppermute | solution.py:20
  27.3 2.6 %collective-permute-start.2 = (bf16[256,768]{1,0:T(8,128)(2,1)S(1)}, bf16[256,768]{1,0:T(8,128)(2,1)S(1)}, u32[]{:S(2)}, u32[]{:S(2)}) collective-permute-start(bf16[256,768]{1,0:T(8,128)(2,1)S(1)} %bitcast.60), channel_id=1, source_target_pairs={{2,0},{3,1},{0,2},{1,3},{6,4},{7,5},{4,6},{5,7},{10,8},{11,9},{8,1... | collective-permute-start | bytes 1179656 | tf_op jit(solution)/shard_map/ppermute | solution.py:20
  34.7 3.5 %collective-permute-done.2.refs_1_ = bf16[256,768]{1,0:T(8,128)(2,1)S(1)} collective-permute-done((bf16[256,768]{1,0:T(8,128)(2,1)S(1)}, bf16[256,768]{1,0:T(8,128)(2,1)S(1)}, u32[]{:S(2)}, u32[]{:S(2)}) %collective-permute-start.2) | collective-permute-done | bytes 393248 | tf_op jit(solution)/shard_map/ppermute | solution.py:20
  38.2 4.5 %all-to-all-start.1 = ((bf16[8,64,768]{2,1,0:T(8,128)(2,1)}), bf16[8,64,768]{2,1,0:T(8,128)(2,1)S(1)}, u32[]{:S(2)}, u32[]{:S(2)}) async-start(bf16[8,64,768]{2,1,0:T(8,128)(2,1)} %join.4), calls=%async_computation.1 | async-start | bytes 1572864 | tf_op jit(solution)/shard_map/all_to_all | solution.py:38
  46.6 4.9 %collective-permute-start.7 = (bf16[768,768]{1,0:T(8,128)(2,1)S(1)}, bf16[768,768]{1,0:T(8,128)(2,1)S(1)}, u32[]{:S(2)}, u32[]{:S(2)}) collective-permute-start(bf16[768,768]{1,0:T(8,128)(2,1)S(1)} %bitcast.53), channel_id=1, source_target_pairs={{64,0},{0,64},{65,1},{1,65},{66,2},{2,66},{67,3},{3,67},{68,4},{4,... | collective-permute-start | bytes 3538952 | tf_op jit(solution)/shard_map/ppermute | solution.py:20
  57.7 6.9 %project.2 = (bf16[8,32,384]{2,1,0:T(8,128)(2,1)S(1)}, bf16[8,32,768]{2,1,0:T(8,128)(2,1)S(1)}) custom-call(s32[5]{0:T(128)S(1)} %get-tuple-element.82.refs_0_.refs_10_.meta, bf16[256,768]{1,0:T(8,128)(2,1)S(1)} %copy-done.12, bf16[256,768]{1,0:T(8,128)(2,1)} %collective-permute-done.3.refs_2_, bf16[256,768]{1,0:T(8,128)(2,1)S(1)} %copy-done.14, ...), custom_call_target="tpu_custom_call" | custom-call | tf_op jit(solution)/shard_map/project/pallas_call | solution.py:270
  69.6 5.3 %collective-permute-start.12 = (bf16[8,32,768]{2,1,0:T(8,128)(2,1)S(1)}, bf16[8,32,768]{2,1,0:T(8,128)(2,1)S(1)}, u32[]{:S(2)}, u32[]{:S(2)}) collective-permute-start(bf16[8,32,768]{2,1,0:T(8,128)(2,1)S(1)} %get-tuple-element.95), channel_id=1, source_target_pairs={{48,0},{20,32},{52,4},{24,36},{56,8},{28,40},{60,12},{0,44},{32,16... | collective-permute-start | bytes 1179656 | tf_op jit(solution)/shard_map/ppermute | solution.py:46
  74.9 4.8 %collective-permute-start.11 = (bf16[3,32,768]{2,1,0:T(8,128)(2,1)S(1)}, bf16[3,32,768]{2,1,0:T(8,128)(2,1)S(1)}, u32[]{:S(2)}, u32[]{:S(2)}) collective-permute-start(bf16[3,32,768]{2,1,0:T(8,128)(2,1)S(1)} %get-tuple-element.94), channel_id=1, source_target_pairs={{32,0},{4,32},{36,4},{8,36},{40,8},{12,40},{44,12},{16,44},{48,16}... | collective-permute-start | bytes 442376 | tf_op jit(solution)/shard_map/ppermute | solution.py:46
  82.1 6.1 %collective-permute-done.12.far = bf16[8,32,768]{2,1,0:T(8,128)(2,1)S(1)} collective-permute-done((bf16[8,32,768]{2,1,0:T(8,128)(2,1)S(1)}, bf16[8,32,768]{2,1,0:T(8,128)(2,1)S(1)}, u32[]{:S(2)}, u32[]{:S(2)}) %collective-permute-start.12) | collective-permute-done | bytes 393248 | tf_op jit(solution)/shard_map/ppermute | solution.py:46
  96.6 3.8 %collective-permute-done.18.refs_3_ = bf16[256,384]{1,0:T(8,128)(2,1)S(1)} collective-permute-done((bf16[256,384]{1,0:T(8,128)(2,1)S(1)}, bf16[256,384]{1,0:T(8,128)(2,1)S(1)}, u32[]{:S(2)}, u32[]{:S(2)}) %collective-permute-start.18) | collective-permute-done | bytes 196640 | tf_op jit(solution)/shard_map/ppermute | solution.py:20
  100.4 6.3 %collective-permute-done.17.refs_2_ = bf16[256,384]{1,0:T(8,128)(2,1)S(1)} collective-permute-done((bf16[256,384]{1,0:T(8,128)(2,1)S(1)}, bf16[256,384]{1,0:T(8,128)(2,1)S(1)}, u32[]{:S(2)}, u32[]{:S(2)}) %collective-permute-start.17) | collective-permute-done | bytes 196640 | tf_op jit(solution)/shard_map/ppermute | solution.py:20
  109.1 2.7 %collective-permute-start.21 = (bf16[256,768]{1,0:T(8,128)(2,1)S(1)}, bf16[256,768]{1,0:T(8,128)(2,1)S(1)}, u32[]{:S(2)}, u32[]{:S(2)}) collective-permute-start(bf16[256,768]{1,0:T(8,128)(2,1)S(1)} %output.2.refs_4_.refs_8_), channel_id=1, source_target_pairs={{1,0},{2,1},{3,2},{0,3},{5,4},{6,5},{7,6},{4,7},{9,8},{10,9},{11,1... | collective-permute-start | bytes 1179656 | tf_op jit(solution)/shard_map/ppermute | solution.py:20
  114.4 12.3 %all_to_all.20.early = bf16[8,32,768]{2,1,0:T(8,128)(2,1)S(1)} all-to-all(bf16[8,32,768]{2,1,0:T(8,128)(2,1)S(1)} %get-tuple-element.109.kv.own), channel_id=1, replica_groups={{0,4,8,12,16,20,24,28},{32,36,40,44,48,52,56,60},{1,5,9,13,17,21,25,29}..., dimensions={0} | all-to-all | bytes 786432 | tf_op jit(solution)/shard_map/all_to_all | solution.py:38
  127.6 7.9 %project.3 = (bf16[8,32,384]{2,1,0:T(8,128)(2,1)S(1)}, bf16[8,32,768]{2,1,0:T(8,128)(2,1)S(1)}, bf16[3,32,768]{2,1,0:T(8,128)(2,1)S(1)}, bf16[3,32,768]{2,1,0:T(8,128)(2,1)S(1)}, bf16[8,32,768]{2,1,0:T(8,128)(2,1)S(1)}) custom-call(s32[5]{0:T(128)S(1)} %copy-done.20, bf16[256,768]{1,0:T(8,128)(2,1)S(1)} %collective-permute-done.20.refs_1_, ...), custom_call_target="tpu_custom_call" | custom-call | tf_op jit(solution)/shard_map/project/pallas_call | solution.py:270
  135.5 5.0 %collective-permute-start.27 = (bf16[8,32,768]{2,1,0:T(8,128)(2,1)S(1)}, bf16[8,32,768]{2,1,0:T(8,128)(2,1)S(1)}, u32[]{:S(2)}, u32[]{:S(2)}) collective-permute-start(bf16[8,32,768]{2,1,0:T(8,128)(2,1)S(1)} %get-tuple-element.122), channel_id=1, source_target_pairs={{48,0},{20,32},{52,4},{24,36},{56,8},{28,40},{60,12},{0,44},{32,16... | collective-permute-start | bytes 1179656 | tf_op jit(solution)/shard_map/ppermute | solution.py:46
  140.6 4.3 %collective-permute-start.24 = (bf16[8,32,384]{2,1,0:T(8,128)(2,1)S(1)}, bf16[8,32,384]{2,1,0:T(8,128)(2,1)S(1)}, u32[]{:S(2)}, u32[]{:S(2)}) collective-permute-start(bf16[8,32,384]{2,1,0:T(8,128)(2,1)S(1)} %get-tuple-element.119.q_own), channel_id=1, source_target_pairs={{64,0},{0,64},{65,1},{1,65},{66,2},{2,66},{67,3},{3,67},{68,4},{4,... | collective-permute-start | bytes 589832 | tf_op jit(solution)/shard_map/ppermute | solution.py:20
  144.9 4.8 %collective-permute-start.26 = (bf16[3,32,768]{2,1,0:T(8,128)(2,1)S(1)}, bf16[3,32,768]{2,1,0:T(8,128)(2,1)S(1)}, u32[]{:S(2)}, u32[]{:S(2)}) collective-permute-start(bf16[3,32,768]{2,1,0:T(8,128)(2,1)S(1)} %get-tuple-element.121), channel_id=1, source_target_pairs={{32,0},{4,32},{36,4},{8,36},{40,8},{12,40},{44,12},{16,44},{48,16}... | collective-permute-start | bytes 442376 | tf_op jit(solution)/shard_map/ppermute | solution.py:46
  152.1 2.6 %collective-permute-done.25.below = bf16[3,32,768]{2,1,0:T(8,128)(2,1)S(1)} collective-permute-done((bf16[3,32,768]{2,1,0:T(8,128)(2,1)S(1)}, bf16[3,32,768]{2,1,0:T(8,128)(2,1)S(1)}, u32[]{:S(2)}, u32[]{:S(2)}) %collective-permute-start.25) | collective-permute-done | bytes 147488 | tf_op jit(solution)/shard_map/ppermute | solution.py:46
  160.7 2.6 %collective-permute-start.32 = (bf16[256,384]{1,0:T(8,128)(2,1)S(1)}, bf16[256,384]{1,0:T(8,128)(2,1)S(1)}, u32[]{:S(2)}, u32[]{:S(2)}) collective-permute-start(bf16[256,384]{1,0:T(8,128)(2,1)S(1)} %merge.3.refs_0_), channel_id=1, source_target_pairs={{1,0},{2,1},{3,2},{0,3},{5,4},{6,5},{7,6},{4,7},{9,8},{10,9},{11,1... | collective-permute-start | bytes 589832 | tf_op jit(solution)/shard_map/ppermute | solution.py:20
  167.1 7.4 %collective-permute-done.31.refs_2_ = bf16[256,384]{1,0:T(8,128)(2,1)S(1)} collective-permute-done((bf16[256,384]{1,0:T(8,128)(2,1)S(1)}, bf16[256,384]{1,0:T(8,128)(2,1)S(1)}, u32[]{:S(2)}, u32[]{:S(2)}) %collective-permute-start.31) | collective-permute-done | bytes 196640 | tf_op jit(solution)/shard_map/ppermute | solution.py:20
  177.0 19.1 %all_to_all.21.home = bf16[8,96,768]{2,1,0:T(8,128)(2,1)S(1)} all-to-all(bf16[8,96,768]{2,1,0:T(8,128)(2,1)S(1)} %join.7), channel_id=1, replica_groups={{0,4,8,12,16,20,24,28},{32,36,40,44,48,52,56,60},{1,5,9,13,17,21,25,29}..., dimensions={0} | all-to-all | bytes 2359296 | tf_op jit(solution)/shard_map/all_to_all | solution.py:38
  (159 shorter events, 63.9 us)
Async XLA Ops:
  0.7 56.1 %collective-permute-start.8 = (bf16[3,3072,384]{2,1,0:T(8,128)(2,1)}, bf16[3,3072,384]{2,1,0:T(8,128)(2,1)}, u32[]{:S(2)}, u32[]{:S(2)}) collective-permute-start(bf16[3,3072,384]{2,1,0:T(8,128)(2,1)} %bitcast.80), channel_id=1, source_target_pairs={{64,0},{0,64},{65,1},{1,65},{66,2},{2,66},{67,3},{3,67},{68,4},{4,... | collective-permute-start | bytes 21233672 | tf_op jit(solution)/shard_map/ppermute | solution.py:20
  5.3 13.9 %all-to-all-start = ((bf16[8,32,768]{2,1,0:T(8,128)(2,1)}), bf16[8,32,768]{2,1,0:T(8,128)(2,1)S(1)}, u32[]{:S(2)}, u32[]{:S(2)}) async-start(bf16[8,32,768]{2,1,0:T(8,128)(2,1)} %constant_dynamic-slice_fusion.3), calls=%async_computation | async-start | bytes 786432 | tf_op jit(solution)/shard_map/all_to_all | solution.py:38
  10.4 16.9 %collective-permute-start.1 = (bf16[384,768]{1,0:T(8,128)(2,1)}, bf16[384,768]{1,0:T(8,128)(2,1)S(1)}, u32[]{:S(2)}, u32[]{:S(2)}) collective-permute-start(bf16[384,768]{1,0:T(8,128)(2,1)} %dynamic-slice_bitcast_fusion.1), channel_id=1, source_target_pairs={{2,0},{3,1},{0,2},{1,3},{6,4},{7,5},{4,6},{5,7},{10,8},{11,9},{8,1... | collective-permute-start | bytes 1769480 | tf_op jit(solution)/shard_map/ppermute | solution.py:20
  27.3 10.9 %collective-permute-start.2 = (bf16[256,768]{1,0:T(8,128)(2,1)S(1)}, bf16[256,768]{1,0:T(8,128)(2,1)S(1)}, u32[]{:S(2)}, u32[]{:S(2)}) collective-permute-start(bf16[256,768]{1,0:T(8,128)(2,1)S(1)} %bitcast.60), channel_id=1, source_target_pairs={{2,0},{3,1},{0,2},{1,3},{6,4},{7,5},{4,6},{5,7},{10,8},{11,9},{8,1... | collective-permute-start | bytes 1179656 | tf_op jit(solution)/shard_map/ppermute | solution.py:20
  32.0 22.9 %collective-permute-start.4 = (bf16[256,768]{1,0:T(8,128)(2,1)S(1)}, bf16[256,768]{1,0:T(8,128)(2,1)S(1)}, u32[]{:S(2)}, u32[]{:S(2)}) collective-permute-start(bf16[256,768]{1,0:T(8,128)(2,1)S(1)} %bitcast.61), channel_id=1, source_target_pairs={{3,0},{0,1},{1,2},{2,3},{7,4},{4,5},{5,6},{6,7},{11,8},{8,9},{9,10... | collective-permute-start | bytes 1179656 | tf_op jit(solution)/shard_map/ppermute | solution.py:20
  32.8 22.9 %collective-permute-start.3 = (bf16[256,768]{1,0:T(8,128)(2,1)S(1)}, bf16[256,768]{1,0:T(8,128)(2,1)}, u32[]{:S(2)}, u32[]{:S(2)}) collective-permute-start(bf16[256,768]{1,0:T(8,128)(2,1)S(1)} %bitcast.62), channel_id=1, source_target_pairs={{1,0},{2,1},{3,2},{0,3},{5,4},{6,5},{7,6},{4,7},{9,8},{10,9},{11,1... | collective-permute-start | bytes 1179656 | tf_op jit(solution)/shard_map/ppermute | solution.py:20
  38.2 26.9 %all-to-all-start.1 = ((bf16[8,64,768]{2,1,0:T(8,128)(2,1)}), bf16[8,64,768]{2,1,0:T(8,128)(2,1)S(1)}, u32[]{:S(2)}, u32[]{:S(2)}) async-start(bf16[8,64,768]{2,1,0:T(8,128)(2,1)} %join.4), calls=%async_computation.1 | async-start | bytes 1572864 | tf_op jit(solution)/shard_map/all_to_all | solution.py:38
  66.2 22.0 %collective-permute-start.13 = (bf16[384,768]{1,0:T(8,128)(2,1)}, bf16[384,768]{1,0:T(8,128)(2,1)S(1)}, u32[]{:S(2)}, u32[]{:S(2)}) collective-permute-start(bf16[384,768]{1,0:T(8,128)(2,1)} %get-tuple-element.98), channel_id=1, source_target_pairs={{3,0},{0,1},{1,2},{2,3},{7,4},{4,5},{5,6},{6,7},{11,8},{8,9},{9,10... | collective-permute-start | bytes 1769480 | tf_op jit(solution)/shard_map/ppermute | solution.py:20
  67.3 20.9 %collective-permute-start.14 = (bf16[384,768]{1,0:T(8,128)(2,1)S(1)}, bf16[384,768]{1,0:T(8,128)(2,1)S(1)}, u32[]{:S(2)}, u32[]{:S(2)}) collective-permute-start(bf16[384,768]{1,0:T(8,128)(2,1)S(1)} %copy-done.22), channel_id=1, source_target_pairs={{1,0},{2,1},{3,2},{0,3},{5,4},{6,5},{7,6},{4,7},{9,8},{10,9},{11,1... | collective-permute-start | bytes 1769480 | tf_op jit(solution)/shard_map/ppermute | solution.py:20
  69.6 18.6 %collective-permute-start.12 = (bf16[8,32,768]{2,1,0:T(8,128)(2,1)S(1)}, bf16[8,32,768]{2,1,0:T(8,128)(2,1)S(1)}, u32[]{:S(2)}, u32[]{:S(2)}) collective-permute-start(bf16[8,32,768]{2,1,0:T(8,128)(2,1)S(1)} %get-tuple-element.95), channel_id=1, source_target_pairs={{48,0},{20,32},{52,4},{24,36},{56,8},{28,40},{60,12},{0,44},{32,16... | collective-permute-start | bytes 1179656 | tf_op jit(solution)/shard_map/ppermute | solution.py:46
  74.9 13.3 %collective-permute-start.10 = (bf16[3,32,768]{2,1,0:T(8,128)(2,1)S(1)}, bf16[3,32,768]{2,1,0:T(8,128)(2,1)S(1)}, u32[]{:S(2)}, u32[]{:S(2)}) collective-permute-start(bf16[3,32,768]{2,1,0:T(8,128)(2,1)S(1)} %get-tuple-element.93), channel_id=1, source_target_pairs={{60,0},{0,32},{32,4},{4,36},{36,8},{8,40},{40,12},{12,44},{44,16},... | collective-permute-start | bytes 442376 | tf_op jit(solution)/shard_map/ppermute | solution.py:46
  74.9 13.3 %collective-permute-start.11 = (bf16[3,32,768]{2,1,0:T(8,128)(2,1)S(1)}, bf16[3,32,768]{2,1,0:T(8,128)(2,1)S(1)}, u32[]{:S(2)}, u32[]{:S(2)}) collective-permute-start(bf16[3,32,768]{2,1,0:T(8,128)(2,1)S(1)} %get-tuple-element.94), channel_id=1, source_target_pairs={{32,0},{4,32},{36,4},{8,36},{40,8},{12,40},{44,12},{16,44},{48,16}... | collective-permute-start | bytes 442376 | tf_op jit(solution)/shard_map/ppermute | solution.py:46
  93.0 13.6 %collective-permute-start.19 = (bf16[768,768]{1,0:T(8,128)(2,1)S(1)}, bf16[768,768]{1,0:T(8,128)(2,1)S(1)}, u32[]{:S(2)}, u32[]{:S(2)}) collective-permute-start(bf16[768,768]{1,0:T(8,128)(2,1)S(1)} %bitcast.56), channel_id=1, source_target_pairs={{64,0},{0,64},{65,1},{1,65},{66,2},{2,66},{67,3},{3,67},{68,4},{4,... | collective-permute-start | bytes 3538952 | tf_op jit(solution)/shard_map/ppermute | solution.py:20
  95.2 11.5 %collective-permute-start.17 = (bf16[256,384]{1,0:T(8,128)(2,1)S(1)}, bf16[256,384]{1,0:T(8,128)(2,1)S(1)}, u32[]{:S(2)}, u32[]{:S(2)}) collective-permute-start(bf16[256,384]{1,0:T(8,128)(2,1)S(1)} %merge.2.refs_0_), channel_id=1, source_target_pairs={{3,0},{0,1},{1,2},{2,3},{7,4},{4,5},{5,6},{6,7},{11,8},{8,9},{9,10... | collective-permute-start | bytes 589832 | tf_op jit(solution)/shard_map/ppermute | solution.py:20
  95.5 11.2 %collective-permute-start.16 = (bf16[256,384]{1,0:T(8,128)(2,1)S(1)}, bf16[256,384]{1,0:T(8,128)(2,1)S(1)}, u32[]{:S(2)}, u32[]{:S(2)}) collective-permute-start(bf16[256,384]{1,0:T(8,128)(2,1)S(1)} %merge.2.refs_0_), channel_id=1, source_target_pairs={{2,0},{3,1},{0,2},{1,3},{6,4},{7,5},{4,6},{5,7},{10,8},{11,9},{8,1... | collective-permute-start | bytes 589832 | tf_op jit(solution)/shard_map/ppermute | solution.py:20
  109.0 17.7 %collective-permute-start.22 = (bf16[256,768]{1,0:T(8,128)(2,1)S(1)}, bf16[256,768]{1,0:T(8,128)(2,1)S(1)}, u32[]{:S(2)}, u32[]{:S(2)}) collective-permute-start(bf16[256,768]{1,0:T(8,128)(2,1)S(1)} %output.2.refs_4_.refs_8_), channel_id=1, source_target_pairs={{3,0},{0,1},{1,2},{2,3},{7,4},{4,5},{5,6},{6,7},{11,8},{8,9},{9,10... | collective-permute-start | bytes 1179656 | tf_op jit(solution)/shard_map/ppermute | solution.py:20
  109.1 17.6 %collective-permute-start.21 = (bf16[256,768]{1,0:T(8,128)(2,1)S(1)}, bf16[256,768]{1,0:T(8,128)(2,1)S(1)}, u32[]{:S(2)}, u32[]{:S(2)}) collective-permute-start(bf16[256,768]{1,0:T(8,128)(2,1)S(1)} %output.2.refs_4_.refs_8_), channel_id=1, source_target_pairs={{1,0},{2,1},{3,2},{0,3},{5,4},{6,5},{7,6},{4,7},{9,8},{10,9},{11,1... | collective-permute-start | bytes 1179656 | tf_op jit(solution)/shard_map/ppermute | solution.py:20
  111.7 15.4 %collective-permute-start.20 = (bf16[256,768]{1,0:T(8,128)(2,1)S(1)}, bf16[256,768]{1,0:T(8,128)(2,1)S(1)}, u32[]{:S(2)}, u32[]{:S(2)}) collective-permute-start(bf16[256,768]{1,0:T(8,128)(2,1)S(1)} %output.2.refs_4_.refs_8_), channel_id=1, source_target_pairs={{2,0},{3,1},{0,2},{1,3},{6,4},{7,5},{4,6},{5,7},{10,8},{11,9},{8,1... | collective-permute-start | bytes 1179656 | tf_op jit(solution)/shard_map/ppermute | solution.py:20
  135.5 19.2 %collective-permute-start.27 = (bf16[8,32,768]{2,1,0:T(8,128)(2,1)S(1)}, bf16[8,32,768]{2,1,0:T(8,128)(2,1)S(1)}, u32[]{:S(2)}, u32[]{:S(2)}) collective-permute-start(bf16[8,32,768]{2,1,0:T(8,128)(2,1)S(1)} %get-tuple-element.122), channel_id=1, source_target_pairs={{48,0},{20,32},{52,4},{24,36},{56,8},{28,40},{60,12},{0,44},{32,16... | collective-permute-start | bytes 1179656 | tf_op jit(solution)/shard_map/ppermute | solution.py:46
  140.6 9.1 %collective-permute-start.24 = (bf16[8,32,384]{2,1,0:T(8,128)(2,1)S(1)}, bf16[8,32,384]{2,1,0:T(8,128)(2,1)S(1)}, u32[]{:S(2)}, u32[]{:S(2)}) collective-permute-start(bf16[8,32,384]{2,1,0:T(8,128)(2,1)S(1)} %get-tuple-element.119.q_own), channel_id=1, source_target_pairs={{64,0},{0,64},{65,1},{1,65},{66,2},{2,66},{67,3},{3,67},{68,4},{4,... | collective-permute-start | bytes 589832 | tf_op jit(solution)/shard_map/ppermute | solution.py:20
  144.9 9.9 %collective-permute-start.25 = (bf16[3,32,768]{2,1,0:T(8,128)(2,1)S(1)}, bf16[3,32,768]{2,1,0:T(8,128)(2,1)S(1)}, u32[]{:S(2)}, u32[]{:S(2)}) collective-permute-start(bf16[3,32,768]{2,1,0:T(8,128)(2,1)S(1)} %get-tuple-element.120), channel_id=1, source_target_pairs={{60,0},{0,32},{32,4},{4,36},{36,8},{8,40},{40,12},{12,44},{44,16},... | collective-permute-start | bytes 442376 | tf_op jit(solution)/shard_map/ppermute | solution.py:46
  144.9 9.9 %collective-permute-start.26 = (bf16[3,32,768]{2,1,0:T(8,128)(2,1)S(1)}, bf16[3,32,768]{2,1,0:T(8,128)(2,1)S(1)}, u32[]{:S(2)}, u32[]{:S(2)}) collective-permute-start(bf16[3,32,768]{2,1,0:T(8,128)(2,1)S(1)} %get-tuple-element.121), channel_id=1, source_target_pairs={{32,0},{4,32},{36,4},{8,36},{40,8},{12,40},{44,12},{16,44},{48,16}... | collective-permute-start | bytes 442376 | tf_op jit(solution)/shard_map/ppermute | solution.py:46
  163.3 11.2 %collective-permute-start.31 = (bf16[256,384]{1,0:T(8,128)(2,1)S(1)}, bf16[256,384]{1,0:T(8,128)(2,1)S(1)}, u32[]{:S(2)}, u32[]{:S(2)}) collective-permute-start(bf16[256,384]{1,0:T(8,128)(2,1)S(1)} %merge.3.refs_0_), channel_id=1, source_target_pairs={{3,0},{0,1},{1,2},{2,3},{7,4},{4,5},{5,6},{6,7},{11,8},{8,9},{9,10... | collective-permute-start | bytes 589832 | tf_op jit(solution)/shard_map/ppermute | solution.py:20
  163.3 11.2 %collective-permute-start.30 = (bf16[256,384]{1,0:T(8,128)(2,1)S(1)}, bf16[256,384]{1,0:T(8,128)(2,1)S(1)}, u32[]{:S(2)}, u32[]{:S(2)}) collective-permute-start(bf16[256,384]{1,0:T(8,128)(2,1)S(1)} %merge.3.refs_0_), channel_id=1, source_target_pairs={{2,0},{3,1},{0,2},{1,3},{6,4},{7,5},{4,6},{5,7},{10,8},{11,9},{8,1... | collective-permute-start | bytes 589832 | tf_op jit(solution)/shard_map/ppermute | solution.py:20
  (48 other events, 533.4 us)

commit v13 on v12

--- a/solution.py
+++ b/solution.py
@@ -532,16 +532,12 @@
     stale_got = shifted(stale_send, "segment", 1)
     w_other = shifted(w_own, "segment", 1)
     stale = join(stale, stale_got)
-    kv_tiles, tile_counts = after((kv_tiles, tile_counts), stale_got)
-    multiple_own = count_tiles(kv_tiles[0], tile_counts[0], chip, patches, rows_core)
-    hidden, stale, wo_across, multiple_own = lax.optimization_barrier(
-        (hidden, stale, wo_across, multiple_own)
-    )
+    hidden, stale, wo_across = lax.optimization_barrier((hidden, stale, wo_across))
     small_own = jnp.concatenate([modulation[0].reshape(-1), qk_gain[0].reshape(-1)])
     small_other = shifted(small_own, "segment", 1)
     blocks = gather_features(hidden)
-    stale, weight, multiple_own, patch_order, small_own, small_other = after(
-        (stale, w_out[0], multiple_own, patch_order, small_own, small_other), blocks[0]
+    stale, weight, kv_tiles, tile_counts, patch_order, small_own, small_other = after(
+        (stale, w_out[0], kv_tiles, tile_counts, patch_order, small_own, small_other), blocks[0]
     )
     stale = exchanged(stale)
     slices = [columns(weight, j) for j in (1, 3)]
@@ -551,6 +547,7 @@
     asked = jnp.stack([chip, chip - 1, chip + 1, chip - seq_size // 2 - 1]) % seq_size // share
     ranks = jnp.sum(jnp.where(patch_order[None] == asked[:, None], turns[None], 0), axis=-1)
     fresh = (ranks[0] <= ranks[1:]).astype(jnp.int32)
+    multiple_own = count_tiles(kv_tiles[0], tile_counts[0], chip, patches, rows_core)
     multiple_other = shifted(multiple_own, "segment", 1)
     given = []
     for section in range(2):

time: 203 us -> 198 us (0.975)
  starting transfers between devices: 71.8 us -> 65.6 us
    ppermute x28, starting transfers between devices: 42.3 us -> 37.1 us  [shifted(): return lax.ppermute(block, axis, route)]
    ppermute x28, waiting for transfers between devices: 39.3 us -> 34.1 us  [shifted(): return lax.ppermute(block, axis, route)]
    all_to_all x2, waiting for transfers between devices: 3.17 us -> 7.87 us  [exchanged(): return lax.all_to_all(tiles, 'seq', 0, 0, axis_index_groups=groups)]
    unnamed x72 -> x74, local copies, waits for them, and re-layouts: 4.5 us -> 4.28 us
  transfers between devices with their start and end apart: 36 -> 36, of which waited for: 16 -> 15; matrix products, arithmetic and copies ran while one was open for 4% -> 5% of each run, Pallas kernels for 7% -> 8%
where the time goes in v13:
time: 198 us; the launch traced here: 197 us
  starting transfers between devices  65.6 us (33%)
  waiting for transfers between devices  50.3 us (25%)
  Pallas kernels  34 us (17%)
  blocking collectives  31.3 us (16%)
  local copies, waits for them, and re-layouts  10.7 us (5%)
  other arithmetic  3.62 us (2%)
    ppermute x28, starting transfers between devices, shifted(): return lax.ppermute(block, axis, route)  37.1 us
    ppermute x28, waiting for transfers between devices, shifted(): return lax.ppermute(block, axis, route)  34.1 us
    all_to_all x2, blocking collectives, exchanged(): return lax.all_to_all(tiles, 'seq', 0, 0, axis_index_groups=groups)  31.3 us
    ppermute x6, starting transfers between devices, along_ring(): return lax.ppermute(block, 'seq', route)  19.9 us
    pallas_call x2, Pallas kernels, project(): pl.pallas_call(kernel, in_specs=[SCALARS] + [ANYWHERE] * len(blocks) + [O...  14.8 us
    all_to_all x2, starting transfers between devices, exchanged(): return lax.all_to_all(tiles, 'seq', 0, 0, axis_index_groups=groups)  8.59 us
    ppermute x6, waiting for transfers between devices, along_ring(): return lax.ppermute(block, 'seq', route)  8.34 us
    all_to_all x2, waiting for transfers between devices, exchanged(): return lax.all_to_all(tiles, 'seq', 0, 0, axis_index_groups=groups)  7.87 us
  transfers between devices with their start and end apart: 36, of which 15 were waited for; matrix products, arithmetic and copies ran while one was open for 5% of the time, Pallas kernels for 8%

profile of v13, /device:TPU:1, one launch (start us, length us, event | category | flops | bytes accessed | tf_op | source)
XLA Modules:
  0.0 196.7 jit_solution(7351167757119472073)
XLA Ops:
  3.3 3.8 %collective-permute-start.1 = (bf16[384,768]{1,0:T(8,128)(2,1)S(1)}, bf16[384,768]{1,0:T(8,128)(2,1)S(1)}, u32[]{:S(2)}, u32[]{:S(2)}) collective-permute-start(bf16[384,768]{1,0:T(8,128)(2,1)S(1)} %dynamic-slice_bitcast_fusion.1), channel_id=1, source_target_pairs={{2,0},{3,1},{0,2},{1,3},{6,4},{7,5},{4,6},{5,7},{10,8},{11,9},{8,1... | collective-permute-start | bytes 1769480 | tf_op jit(solution)/shard_map/ppermute | solution.py:20
  9.2 5.0 %all-to-all-start = ((bf16[8,32,768]{2,1,0:T(8,128)(2,1)}), bf16[8,32,768]{2,1,0:T(8,128)(2,1)S(1)}, u32[]{:S(2)}, u32[]{:S(2)}) async-start(bf16[8,32,768]{2,1,0:T(8,128)(2,1)} %constant_dynamic-slice_fusion.3), calls=%async_computation | async-start | bytes 786432 | tf_op jit(solution)/shard_map/all_to_all | solution.py:38
  15.3 7.9 %all-to-all-done = bf16[8,32,768]{2,1,0:T(8,128)(2,1)S(1)} async-done(((bf16[8,32,768]{2,1,0:T(8,128)(2,1)}), bf16[8,32,768]{2,1,0:T(8,128)(2,1)S(1)}, u32[]{:S(2)}, u32[]{:S(2)}) %all-to-all-start) | async-done | bytes 393248 | tf_op jit(solution)/shard_map/all_to_all | solution.py:38
  29.5 6.0 %collective-permute-done.2.refs_1_ = bf16[256,768]{1,0:T(8,128)(2,1)S(1)} collective-permute-done((bf16[256,768]{1,0:T(8,128)(2,1)S(1)}, bf16[256,768]{1,0:T(8,128)(2,1)S(1)}, u32[]{:S(2)}, u32[]{:S(2)}) %collective-permute-start.2) | collective-permute-done | bytes 393248 | tf_op jit(solution)/shard_map/ppermute | solution.py:20
  35.5 3.5 %all-to-all-start.1 = ((bf16[8,64,768]{2,1,0:T(8,128)(2,1)}), bf16[8,64,768]{2,1,0:T(8,128)(2,1)S(1)}, u32[]{:S(2)}, u32[]{:S(2)}) async-start(bf16[8,64,768]{2,1,0:T(8,128)(2,1)} %join.4), calls=%async_computation.1 | async-start | bytes 1572864 | tf_op jit(solution)/shard_map/all_to_all | solution.py:38
  39.8 2.6 %dynamic-slice_bitcast_fusion = (bf16[1,384,768]{2,1,0:T(8,128)(2,1)S(1)}, bf16[384,768]{1,0:T(8,128)(2,1)}, bf16[384,768]{1,0:T(8,128)(2,1)}) fusion(bf16[384,3072]{1,0:T(8,128)(2,1)} %bitcast.75, s32[]{:T(128)S(6)} %select_n.103, s32[]{:T(128)S(6)} %select_n.102, s32[]{:T(128)S(6)} %select_n.101), kind=kLoop, calls=%fused_computation | loop fusion | bytes 3538956 | tf_op jit(solution)/shard_map/broadcast_in_dim | solution.py:474
  42.8 3.0 %collective-permute-start.7 = (bf16[768,768]{1,0:T(8,128)(2,1)S(1)}, bf16[768,768]{1,0:T(8,128)(2,1)S(1)}, u32[]{:S(2)}, u32[]{:S(2)}) collective-permute-start(bf16[768,768]{1,0:T(8,128)(2,1)S(1)} %bitcast.49), channel_id=1, source_target_pairs={{64,0},{0,64},{65,1},{1,65},{66,2},{2,66},{67,3},{3,67},{68,4},{4,... | collective-permute-start | bytes 3538952 | tf_op jit(solution)/shard_map/ppermute | solution.py:20
  53.0 6.9 %project.2 = (bf16[8,32,384]{2,1,0:T(8,128)(2,1)S(1)}, bf16[8,32,768]{2,1,0:T(8,128)(2,1)S(1)}) custom-call(s32[5]{0:T(128)S(1)} %get-tuple-element.78.refs_0_.refs_10_.meta, bf16[256,768]{1,0:T(8,128)(2,1)S(1)} %copy-done.12, bf16[256,768]{1,0:T(8,128)(2,1)} %collective-permute-done.3.refs_2_, bf16[256,768]{1,0:T(8,128)(2,1)S(1)} %copy-done.14, ...), custom_call_target="tpu_custom_call" | custom-call | tf_op jit(solution)/shard_map/project/pallas_call | solution.py:270
  64.2 5.2 %collective-permute-start.12 = (bf16[8,32,768]{2,1,0:T(8,128)(2,1)S(1)}, bf16[8,32,768]{2,1,0:T(8,128)(2,1)S(1)}, u32[]{:S(2)}, u32[]{:S(2)}) collective-permute-start(bf16[8,32,768]{2,1,0:T(8,128)(2,1)S(1)} %get-tuple-element.91), channel_id=1, source_target_pairs={{48,0},{20,32},{52,4},{24,36},{56,8},{28,40},{60,12},{0,44},{32,16... | collective-permute-start | bytes 1179656 | tf_op jit(solution)/shard_map/ppermute | solution.py:46
  69.4 4.8 %collective-permute-start.11 = (bf16[3,32,768]{2,1,0:T(8,128)(2,1)S(1)}, bf16[3,32,768]{2,1,0:T(8,128)(2,1)S(1)}, u32[]{:S(2)}, u32[]{:S(2)}) collective-permute-start(bf16[3,32,768]{2,1,0:T(8,128)(2,1)S(1)} %get-tuple-element.90), channel_id=1, source_target_pairs={{32,0},{4,32},{36,4},{8,36},{40,8},{12,40},{44,12},{16,44},{48,16}... | collective-permute-start | bytes 442376 | tf_op jit(solution)/shard_map/ppermute | solution.py:46
  76.6 5.7 %collective-permute-done.12.far = bf16[8,32,768]{2,1,0:T(8,128)(2,1)S(1)} collective-permute-done((bf16[8,32,768]{2,1,0:T(8,128)(2,1)S(1)}, bf16[8,32,768]{2,1,0:T(8,128)(2,1)S(1)}, u32[]{:S(2)}, u32[]{:S(2)}) %collective-permute-start.12) | collective-permute-done | bytes 393248 | tf_op jit(solution)/shard_map/ppermute | solution.py:46
  91.0 3.9 %collective-permute-done.18.refs_3_ = bf16[256,384]{1,0:T(8,128)(2,1)S(1)} collective-permute-done((bf16[256,384]{1,0:T(8,128)(2,1)S(1)}, bf16[256,384]{1,0:T(8,128)(2,1)S(1)}, u32[]{:S(2)}, u32[]{:S(2)}) %collective-permute-start.18) | collective-permute-done | bytes 196640 | tf_op jit(solution)/shard_map/ppermute | solution.py:20
  94.9 6.3 %collective-permute-done.17.refs_2_ = bf16[256,384]{1,0:T(8,128)(2,1)S(1)} collective-permute-done((bf16[256,384]{1,0:T(8,128)(2,1)S(1)}, bf16[256,384]{1,0:T(8,128)(2,1)S(1)}, u32[]{:S(2)}, u32[]{:S(2)}) %collective-permute-start.17) | collective-permute-done | bytes 196640 | tf_op jit(solution)/shard_map/ppermute | solution.py:20
  103.5 2.7 %collective-permute-start.21 = (bf16[256,768]{1,0:T(8,128)(2,1)S(1)}, bf16[256,768]{1,0:T(8,128)(2,1)S(1)}, u32[]{:S(2)}, u32[]{:S(2)}) collective-permute-start(bf16[256,768]{1,0:T(8,128)(2,1)S(1)} %output.2.refs_4_.refs_8_), channel_id=1, source_target_pairs={{1,0},{2,1},{3,2},{0,3},{5,4},{6,5},{7,6},{4,7},{9,8},{10,9},{11,1... | collective-permute-start | bytes 1179656 | tf_op jit(solution)/shard_map/ppermute | solution.py:20
  108.8 12.3 %all_to_all.20.early = bf16[8,32,768]{2,1,0:T(8,128)(2,1)S(1)} all-to-all(bf16[8,32,768]{2,1,0:T(8,128)(2,1)S(1)} %get-tuple-element.105.kv.own), channel_id=1, replica_groups={{0,4,8,12,16,20,24,28},{32,36,40,44,48,52,56,60},{1,5,9,13,17,21,25,29}..., dimensions={0} | all-to-all | bytes 786432 | tf_op jit(solution)/shard_map/all_to_all | solution.py:38
  122.1 7.9 %project.3 = (bf16[8,32,384]{2,1,0:T(8,128)(2,1)S(1)}, bf16[8,32,768]{2,1,0:T(8,128)(2,1)S(1)}, bf16[3,32,768]{2,1,0:T(8,128)(2,1)S(1)}, bf16[3,32,768]{2,1,0:T(8,128)(2,1)S(1)}, bf16[8,32,768]{2,1,0:T(8,128)(2,1)S(1)}) custom-call(s32[5]{0:T(128)S(1)} %copy-done.20, bf16[256,768]{1,0:T(8,128)(2,1)S(1)} %collective-permute-done.20.refs_1_, ...), custom_call_target="tpu_custom_call" | custom-call | tf_op jit(solution)/shard_map/project/pallas_call | solution.py:270
  130.0 5.1 %collective-permute-start.27 = (bf16[8,32,768]{2,1,0:T(8,128)(2,1)S(1)}, bf16[8,32,768]{2,1,0:T(8,128)(2,1)S(1)}, u32[]{:S(2)}, u32[]{:S(2)}) collective-permute-start(bf16[8,32,768]{2,1,0:T(8,128)(2,1)S(1)} %get-tuple-element.118), channel_id=1, source_target_pairs={{48,0},{20,32},{52,4},{24,36},{56,8},{28,40},{60,12},{0,44},{32,16... | collective-permute-start | bytes 1179656 | tf_op jit(solution)/shard_map/ppermute | solution.py:46
  135.1 4.1 %collective-permute-start.24 = (bf16[8,32,384]{2,1,0:T(8,128)(2,1)S(1)}, bf16[8,32,384]{2,1,0:T(8,128)(2,1)S(1)}, u32[]{:S(2)}, u32[]{:S(2)}) collective-permute-start(bf16[8,32,384]{2,1,0:T(8,128)(2,1)S(1)} %get-tuple-element.115.q_own), channel_id=1, source_target_pairs={{64,0},{0,64},{65,1},{1,65},{66,2},{2,66},{67,3},{3,67},{68,4},{4,... | collective-permute-start | bytes 589832 | tf_op jit(solution)/shard_map/ppermute | solution.py:20
  139.2 4.8 %collective-permute-start.26 = (bf16[3,32,768]{2,1,0:T(8,128)(2,1)S(1)}, bf16[3,32,768]{2,1,0:T(8,128)(2,1)S(1)}, u32[]{:S(2)}, u32[]{:S(2)}) collective-permute-start(bf16[3,32,768]{2,1,0:T(8,128)(2,1)S(1)} %get-tuple-element.117), channel_id=1, source_target_pairs={{32,0},{4,32},{36,4},{8,36},{40,8},{12,40},{44,12},{16,44},{48,16}... | collective-permute-start | bytes 442376 | tf_op jit(solution)/shard_map/ppermute | solution.py:46
  146.5 2.6 %collective-permute-done.25.below = bf16[3,32,768]{2,1,0:T(8,128)(2,1)S(1)} collective-permute-done((bf16[3,32,768]{2,1,0:T(8,128)(2,1)S(1)}, bf16[3,32,768]{2,1,0:T(8,128)(2,1)S(1)}, u32[]{:S(2)}, u32[]{:S(2)}) %collective-permute-start.25) | collective-permute-done | bytes 147488 | tf_op jit(solution)/shard_map/ppermute | solution.py:46
  155.1 2.6 %collective-permute-start.32 = (bf16[256,384]{1,0:T(8,128)(2,1)S(1)}, bf16[256,384]{1,0:T(8,128)(2,1)S(1)}, u32[]{:S(2)}, u32[]{:S(2)}) collective-permute-start(bf16[256,384]{1,0:T(8,128)(2,1)S(1)} %merge.3.refs_0_), channel_id=1, source_target_pairs={{1,0},{2,1},{3,2},{0,3},{5,4},{6,5},{7,6},{4,7},{9,8},{10,9},{11,1... | collective-permute-start | bytes 589832 | tf_op jit(solution)/shard_map/ppermute | solution.py:20
  161.5 7.4 %collective-permute-done.31.refs_2_ = bf16[256,384]{1,0:T(8,128)(2,1)S(1)} collective-permute-done((bf16[256,384]{1,0:T(8,128)(2,1)S(1)}, bf16[256,384]{1,0:T(8,128)(2,1)S(1)}, u32[]{:S(2)}, u32[]{:S(2)}) %collective-permute-start.31) | collective-permute-done | bytes 196640 | tf_op jit(solution)/shard_map/ppermute | solution.py:20
  171.3 19.0 %all_to_all.21.home = bf16[8,96,768]{2,1,0:T(8,128)(2,1)S(1)} all-to-all(bf16[8,96,768]{2,1,0:T(8,128)(2,1)S(1)} %join.7), channel_id=1, replica_groups={{0,4,8,12,16,20,24,28},{32,36,40,44,48,52,56,60},{1,5,9,13,17,21,25,29}..., dimensions={0} | all-to-all | bytes 2359296 | tf_op jit(solution)/shard_map/all_to_all | solution.py:38
  190.4 2.6 %collective-permute-start.33 = (bf16[8,96,768]{2,1,0:T(8,128)(2,1)S(1)}, bf16[8,96,768]{2,1,0:T(8,128)(2,1)S(1)}, u32[]{:S(2)}, u32[]{:S(2)}) collective-permute-start(bf16[8,96,768]{2,1,0:T(8,128)(2,1)S(1)} %all_to_all.21.home), channel_id=1, source_target_pairs={{64,0},{0,64},{65,1},{1,65},{66,2},{2,66},{67,3},{3,67},{68,4},{4,... | collective-permute-start | bytes 3538952 | tf_op jit(solution)/shard_map/ppermute | solution.py:20
  (161 shorter events, 59.8 us)
Async XLA Ops:
  0.7 51.4 %collective-permute-start.8 = (bf16[3,3072,384]{2,1,0:T(8,128)(2,1)}, bf16[3,3072,384]{2,1,0:T(8,128)(2,1)}, u32[]{:S(2)}, u32[]{:S(2)}) collective-permute-start(bf16[3,3072,384]{2,1,0:T(8,128)(2,1)} %bitcast.72), channel_id=1, source_target_pairs={{64,0},{0,64},{65,1},{1,65},{66,2},{2,66},{67,3},{3,67},{68,4},{4,... | collective-permute-start | bytes 21233672 | tf_op jit(solution)/shard_map/ppermute | solution.py:20
  3.3 19.9 %collective-permute-start.1 = (bf16[384,768]{1,0:T(8,128)(2,1)S(1)}, bf16[384,768]{1,0:T(8,128)(2,1)S(1)}, u32[]{:S(2)}, u32[]{:S(2)}) collective-permute-start(bf16[384,768]{1,0:T(8,128)(2,1)S(1)} %dynamic-slice_bitcast_fusion.1), channel_id=1, source_target_pairs={{2,0},{3,1},{0,2},{1,3},{6,4},{7,5},{4,6},{5,7},{10,8},{11,9},{8,1... | collective-permute-start | bytes 1769480 | tf_op jit(solution)/shard_map/ppermute | solution.py:20
  9.2 13.9 %all-to-all-start = ((bf16[8,32,768]{2,1,0:T(8,128)(2,1)}), bf16[8,32,768]{2,1,0:T(8,128)(2,1)S(1)}, u32[]{:S(2)}, u32[]{:S(2)}) async-start(bf16[8,32,768]{2,1,0:T(8,128)(2,1)} %constant_dynamic-slice_fusion.3), calls=%async_computation | async-start | bytes 786432 | tf_op jit(solution)/shard_map/all_to_all | solution.py:38
  24.0 11.4 %collective-permute-start.2 = (bf16[256,768]{1,0:T(8,128)(2,1)S(1)}, bf16[256,768]{1,0:T(8,128)(2,1)S(1)}, u32[]{:S(2)}, u32[]{:S(2)}) collective-permute-start(bf16[256,768]{1,0:T(8,128)(2,1)S(1)} %bitcast.56), channel_id=1, source_target_pairs={{2,0},{3,1},{0,2},{1,3},{6,4},{7,5},{4,6},{5,7},{10,8},{11,9},{8,1... | collective-permute-start | bytes 1179656 | tf_op jit(solution)/shard_map/ppermute | solution.py:20
  26.7 23.5 %collective-permute-start.4 = (bf16[256,768]{1,0:T(8,128)(2,1)S(1)}, bf16[256,768]{1,0:T(8,128)(2,1)S(1)}, u32[]{:S(2)}, u32[]{:S(2)}) collective-permute-start(bf16[256,768]{1,0:T(8,128)(2,1)S(1)} %bitcast.57), channel_id=1, source_target_pairs={{3,0},{0,1},{1,2},{2,3},{7,4},{4,5},{5,6},{6,7},{11,8},{8,9},{9,10... | collective-permute-start | bytes 1179656 | tf_op jit(solution)/shard_map/ppermute | solution.py:20
  27.4 23.5 %collective-permute-start.3 = (bf16[256,768]{1,0:T(8,128)(2,1)S(1)}, bf16[256,768]{1,0:T(8,128)(2,1)}, u32[]{:S(2)}, u32[]{:S(2)}) collective-permute-start(bf16[256,768]{1,0:T(8,128)(2,1)S(1)} %bitcast.58), channel_id=1, source_target_pairs={{1,0},{2,1},{3,2},{0,3},{5,4},{6,5},{7,6},{4,7},{9,8},{10,9},{11,1... | collective-permute-start | bytes 1179656 | tf_op jit(solution)/shard_map/ppermute | solution.py:20
  35.5 24.8 %all-to-all-start.1 = ((bf16[8,64,768]{2,1,0:T(8,128)(2,1)}), bf16[8,64,768]{2,1,0:T(8,128)(2,1)S(1)}, u32[]{:S(2)}, u32[]{:S(2)}) async-start(bf16[8,64,768]{2,1,0:T(8,128)(2,1)} %join.4), calls=%async_computation.1 | async-start | bytes 1572864 | tf_op jit(solution)/shard_map/all_to_all | solution.py:38
  61.5 20.8 %collective-permute-start.13 = (bf16[384,768]{1,0:T(8,128)(2,1)}, bf16[384,768]{1,0:T(8,128)(2,1)S(1)}, u32[]{:S(2)}, u32[]{:S(2)}) collective-permute-start(bf16[384,768]{1,0:T(8,128)(2,1)} %get-tuple-element.94), channel_id=1, source_target_pairs={{3,0},{0,1},{1,2},{2,3},{7,4},{4,5},{5,6},{6,7},{11,8},{8,9},{9,10... | collective-permute-start | bytes 1769480 | tf_op jit(solution)/shard_map/ppermute | solution.py:20
  62.2 20.1 %collective-permute-start.14 = (bf16[384,768]{1,0:T(8,128)(2,1)S(1)}, bf16[384,768]{1,0:T(8,128)(2,1)S(1)}, u32[]{:S(2)}, u32[]{:S(2)}) collective-permute-start(bf16[384,768]{1,0:T(8,128)(2,1)S(1)} %copy-done.22), channel_id=1, source_target_pairs={{1,0},{2,1},{3,2},{0,3},{5,4},{6,5},{7,6},{4,7},{9,8},{10,9},{11,1... | collective-permute-start | bytes 1769480 | tf_op jit(solution)/shard_map/ppermute | solution.py:20
  64.2 18.1 %collective-permute-start.12 = (bf16[8,32,768]{2,1,0:T(8,128)(2,1)S(1)}, bf16[8,32,768]{2,1,0:T(8,128)(2,1)S(1)}, u32[]{:S(2)}, u32[]{:S(2)}) collective-permute-start(bf16[8,32,768]{2,1,0:T(8,128)(2,1)S(1)} %get-tuple-element.91), channel_id=1, source_target_pairs={{48,0},{20,32},{52,4},{24,36},{56,8},{28,40},{60,12},{0,44},{32,16... | collective-permute-start | bytes 1179656 | tf_op jit(solution)/shard_map/ppermute | solution.py:46
  69.4 12.9 %collective-permute-start.10 = (bf16[3,32,768]{2,1,0:T(8,128)(2,1)S(1)}, bf16[3,32,768]{2,1,0:T(8,128)(2,1)S(1)}, u32[]{:S(2)}, u32[]{:S(2)}) collective-permute-start(bf16[3,32,768]{2,1,0:T(8,128)(2,1)S(1)} %get-tuple-element.89), channel_id=1, source_target_pairs={{60,0},{0,32},{32,4},{4,36},{36,8},{8,40},{40,12},{12,44},{44,16},... | collective-permute-start | bytes 442376 | tf_op jit(solution)/shard_map/ppermute | solution.py:46
  69.4 12.9 %collective-permute-start.11 = (bf16[3,32,768]{2,1,0:T(8,128)(2,1)S(1)}, bf16[3,32,768]{2,1,0:T(8,128)(2,1)S(1)}, u32[]{:S(2)}, u32[]{:S(2)}) collective-permute-start(bf16[3,32,768]{2,1,0:T(8,128)(2,1)S(1)} %get-tuple-element.90), channel_id=1, source_target_pairs={{32,0},{4,32},{36,4},{8,36},{40,8},{12,40},{44,12},{16,44},{48,16}... | collective-permute-start | bytes 442376 | tf_op jit(solution)/shard_map/ppermute | solution.py:46
  87.5 13.6 %collective-permute-start.19 = (bf16[768,768]{1,0:T(8,128)(2,1)S(1)}, bf16[768,768]{1,0:T(8,128)(2,1)S(1)}, u32[]{:S(2)}, u32[]{:S(2)}) collective-permute-start(bf16[768,768]{1,0:T(8,128)(2,1)S(1)} %bitcast.52), channel_id=1, source_target_pairs={{64,0},{0,64},{65,1},{1,65},{66,2},{2,66},{67,3},{3,67},{68,4},{4,... | collective-permute-start | bytes 3538952 | tf_op jit(solution)/shard_map/ppermute | solution.py:20
  89.6 11.5 %collective-permute-start.17 = (bf16[256,384]{1,0:T(8,128)(2,1)S(1)}, bf16[256,384]{1,0:T(8,128)(2,1)S(1)}, u32[]{:S(2)}, u32[]{:S(2)}) collective-permute-start(bf16[256,384]{1,0:T(8,128)(2,1)S(1)} %merge.2.refs_0_), channel_id=1, source_target_pairs={{3,0},{0,1},{1,2},{2,3},{7,4},{4,5},{5,6},{6,7},{11,8},{8,9},{9,10... | collective-permute-start | bytes 589832 | tf_op jit(solution)/shard_map/ppermute | solution.py:20
  90.0 11.2 %collective-permute-start.16 = (bf16[256,384]{1,0:T(8,128)(2,1)S(1)}, bf16[256,384]{1,0:T(8,128)(2,1)S(1)}, u32[]{:S(2)}, u32[]{:S(2)}) collective-permute-start(bf16[256,384]{1,0:T(8,128)(2,1)S(1)} %merge.2.refs_0_), channel_id=1, source_target_pairs={{2,0},{3,1},{0,2},{1,3},{6,4},{7,5},{4,6},{5,7},{10,8},{11,9},{8,1... | collective-permute-start | bytes 589832 | tf_op jit(solution)/shard_map/ppermute | solution.py:20
  103.4 17.7 %collective-permute-start.22 = (bf16[256,768]{1,0:T(8,128)(2,1)S(1)}, bf16[256,768]{1,0:T(8,128)(2,1)S(1)}, u32[]{:S(2)}, u32[]{:S(2)}) collective-permute-start(bf16[256,768]{1,0:T(8,128)(2,1)S(1)} %output.2.refs_4_.refs_8_), channel_id=1, source_target_pairs={{3,0},{0,1},{1,2},{2,3},{7,4},{4,5},{5,6},{6,7},{11,8},{8,9},{9,10... | collective-permute-start | bytes 1179656 | tf_op jit(solution)/shard_map/ppermute | solution.py:20
  103.5 17.6 %collective-permute-start.21 = (bf16[256,768]{1,0:T(8,128)(2,1)S(1)}, bf16[256,768]{1,0:T(8,128)(2,1)S(1)}, u32[]{:S(2)}, u32[]{:S(2)}) collective-permute-start(bf16[256,768]{1,0:T(8,128)(2,1)S(1)} %output.2.refs_4_.refs_8_), channel_id=1, source_target_pairs={{1,0},{2,1},{3,2},{0,3},{5,4},{6,5},{7,6},{4,7},{9,8},{10,9},{11,1... | collective-permute-start | bytes 1179656 | tf_op jit(solution)/shard_map/ppermute | solution.py:20
  106.2 15.5 %collective-permute-start.20 = (bf16[256,768]{1,0:T(8,128)(2,1)S(1)}, bf16[256,768]{1,0:T(8,128)(2,1)S(1)}, u32[]{:S(2)}, u32[]{:S(2)}) collective-permute-start(bf16[256,768]{1,0:T(8,128)(2,1)S(1)} %output.2.refs_4_.refs_8_), channel_id=1, source_target_pairs={{2,0},{3,1},{0,2},{1,3},{6,4},{7,5},{4,6},{5,7},{10,8},{11,9},{8,1... | collective-permute-start | bytes 1179656 | tf_op jit(solution)/shard_map/ppermute | solution.py:20
  130.0 19.1 %collective-permute-start.27 = (bf16[8,32,768]{2,1,0:T(8,128)(2,1)S(1)}, bf16[8,32,768]{2,1,0:T(8,128)(2,1)S(1)}, u32[]{:S(2)}, u32[]{:S(2)}) collective-permute-start(bf16[8,32,768]{2,1,0:T(8,128)(2,1)S(1)} %get-tuple-element.118), channel_id=1, source_target_pairs={{48,0},{20,32},{52,4},{24,36},{56,8},{28,40},{60,12},{0,44},{32,16... | collective-permute-start | bytes 1179656 | tf_op jit(solution)/shard_map/ppermute | solution.py:46
  135.1 8.9 %collective-permute-start.24 = (bf16[8,32,384]{2,1,0:T(8,128)(2,1)S(1)}, bf16[8,32,384]{2,1,0:T(8,128)(2,1)S(1)}, u32[]{:S(2)}, u32[]{:S(2)}) collective-permute-start(bf16[8,32,384]{2,1,0:T(8,128)(2,1)S(1)} %get-tuple-element.115.q_own), channel_id=1, source_target_pairs={{64,0},{0,64},{65,1},{1,65},{66,2},{2,66},{67,3},{3,67},{68,4},{4,... | collective-permute-start | bytes 589832 | tf_op jit(solution)/shard_map/ppermute | solution.py:20
  139.2 9.9 %collective-permute-start.25 = (bf16[3,32,768]{2,1,0:T(8,128)(2,1)S(1)}, bf16[3,32,768]{2,1,0:T(8,128)(2,1)S(1)}, u32[]{:S(2)}, u32[]{:S(2)}) collective-permute-start(bf16[3,32,768]{2,1,0:T(8,128)(2,1)S(1)} %get-tuple-element.116), channel_id=1, source_target_pairs={{60,0},{0,32},{32,4},{4,36},{36,8},{8,40},{40,12},{12,44},{44,16},... | collective-permute-start | bytes 442376 | tf_op jit(solution)/shard_map/ppermute | solution.py:46
  139.2 9.9 %collective-permute-start.26 = (bf16[3,32,768]{2,1,0:T(8,128)(2,1)S(1)}, bf16[3,32,768]{2,1,0:T(8,128)(2,1)S(1)}, u32[]{:S(2)}, u32[]{:S(2)}) collective-permute-start(bf16[3,32,768]{2,1,0:T(8,128)(2,1)S(1)} %get-tuple-element.117), channel_id=1, source_target_pairs={{32,0},{4,32},{36,4},{8,36},{40,8},{12,40},{44,12},{16,44},{48,16}... | collective-permute-start | bytes 442376 | tf_op jit(solution)/shard_map/ppermute | solution.py:46
  157.7 11.2 %collective-permute-start.31 = (bf16[256,384]{1,0:T(8,128)(2,1)S(1)}, bf16[256,384]{1,0:T(8,128)(2,1)S(1)}, u32[]{:S(2)}, u32[]{:S(2)}) collective-permute-start(bf16[256,384]{1,0:T(8,128)(2,1)S(1)} %merge.3.refs_0_), channel_id=1, source_target_pairs={{3,0},{0,1},{1,2},{2,3},{7,4},{4,5},{5,6},{6,7},{11,8},{8,9},{9,10... | collective-permute-start | bytes 589832 | tf_op jit(solution)/shard_map/ppermute | solution.py:20
  157.7 11.2 %collective-permute-start.30 = (bf16[256,384]{1,0:T(8,128)(2,1)S(1)}, bf16[256,384]{1,0:T(8,128)(2,1)S(1)}, u32[]{:S(2)}, u32[]{:S(2)}) collective-permute-start(bf16[256,384]{1,0:T(8,128)(2,1)S(1)} %merge.3.refs_0_), channel_id=1, source_target_pairs={{2,0},{3,1},{0,2},{1,3},{6,4},{7,5},{4,6},{5,7},{10,8},{11,9},{8,1... | collective-permute-start | bytes 589832 | tf_op jit(solution)/shard_map/ppermute | solution.py:20
  (49 other events, 498.0 us)

commit v14 on v13

--- a/solution.py
+++ b/solution.py
@@ -532,16 +532,19 @@
     stale_got = shifted(stale_send, "segment", 1)
     w_other = shifted(w_own, "segment", 1)
     stale = join(stale, stale_got)
-    hidden, stale, wo_across = lax.optimization_barrier((hidden, stale, wo_across))
+    weight = after(w_out[0], stale_got)
+    slices = [columns(weight, j) for j in (0, 1, 3)]
+    hidden, stale, wo_across, slices = lax.optimization_barrier(
+        (hidden, stale, wo_across, slices)
+    )
     small_own = jnp.concatenate([modulation[0].reshape(-1), qk_gain[0].reshape(-1)])
     small_other = shifted(small_own, "segment", 1)
     blocks = gather_features(hidden)
-    stale, weight, kv_tiles, tile_counts, patch_order, small_own, small_other = after(
-        (stale, w_out[0], kv_tiles, tile_counts, patch_order, small_own, small_other), blocks[0]
+    stale, slices, kv_tiles, tile_counts, patch_order, small_own, small_other = after(
+        (stale, slices, kv_tiles, tile_counts, patch_order, small_own, small_other), blocks[0]
     )
     stale = exchanged(stale)
-    slices = [columns(weight, j) for j in (1, 3)]
-    wo_own = [paired(columns(weight, 0), wo_across)]
+    wo_own = [paired(slices[0], wo_across)]
     wo_other = [shifted(wo_own[0], "segment", 1)]
     turns = jnp.arange(patches, dtype=jnp.int32)
     asked = jnp.stack([chip, chip - 1, chip + 1, chip - seq_size // 2 - 1]) % seq_size // share
@@ -597,7 +600,7 @@
         below = along_ring(to_above, -1, patches)
         q_other = shifted(q_own, "segment", 1)
         if section == 0:
-            wo_prev, wo_next = after(slices, q_other, to_far)
+            wo_prev, wo_next = after(slices[1:], q_other, to_far)
             wo_prev, wo_next = shifted(wo_prev, "tp", 1), shifted(wo_next, "tp", 3)
             far, wo_prev, wo_next = lax.optimization_barrier((far, wo_prev, wo_next))
             wo_own.append(paired(wo_prev, wo_next))

time: 198 us -> 197 us (level)
  waiting for transfers between devices: 50.3 us -> 47.6 us
  local copies, waits for them, and re-layouts: 10.7 us -> 12.9 us
    all_to_all x2, waiting for transfers between devices: 7.87 us -> 5.12 us  [exchanged(): return lax.all_to_all(tiles, 'seq', 0, 0, axis_index_groups=groups)]
    dynamic_slice x1 -> x2, local copies, waits for them, and re-layouts: 1.1 us -> 3.83 us  [columns(): return lax.dynamic_slice_in_dim(weight, first, part_cols, 1)]
    broadcast_in_dim x1 -> x0, local copies, waits for them, and re-layouts: 2.61 us -> none  [paired(): return join(first[None], second[None]).reshape(2 * rows, cols)]
    unnamed x74 -> x76, local copies, waits for them, and re-layouts: 4.28 us -> 6.34 us
where the time goes in v14:
time: 197 us; the launch traced here: 196 us
  starting transfers between devices  65.6 us (33%)
  waiting for transfers between devices  47.6 us (24%)
  Pallas kernels  34 us (17%)
  blocking collectives  31.3 us (16%)
  local copies, waits for them, and re-layouts  12.9 us (7%)
  other arithmetic  3.55 us (2%)
    ppermute x28, starting transfers between devices, shifted(): return lax.ppermute(block, axis, route)  37.1 us
    ppermute x28, waiting for transfers between devices, shifted(): return lax.ppermute(block, axis, route)  34.2 us
    all_to_all x2, blocking collectives, exchanged(): return lax.all_to_all(tiles, 'seq', 0, 0, axis_index_groups=groups)  31.3 us
    ppermute x6, starting transfers between devices, along_ring(): return lax.ppermute(block, 'seq', route)  20 us
    pallas_call x2, Pallas kernels, project(): pl.pallas_call(kernel, in_specs=[SCALARS] + [ANYWHERE] * len(blocks) + [O...  14.8 us
    all_to_all x2, starting transfers between devices, exchanged(): return lax.all_to_all(tiles, 'seq', 0, 0, axis_index_groups=groups)  8.59 us
    ppermute x6, waiting for transfers between devices, along_ring(): return lax.ppermute(block, 'seq', route)  8.32 us
    unnamed x76, local copies, waits for them, and re-layouts  6.34 us
  transfers between devices with their start and end apart: 36, of which 15 were waited for; matrix products, arithmetic and copies ran while one was open for 5% of the time, Pallas kernels for 8%

profile of v14, /device:TPU:1, one launch (start us, length us, event | category | flops | bytes accessed | tf_op | source)
XLA Modules:
  0.0 196.1 jit_solution(9223629298817226436)
XLA Ops:
  3.3 3.8 %collective-permute-start.1 = (bf16[384,768]{1,0:T(8,128)(2,1)S(1)}, bf16[384,768]{1,0:T(8,128)(2,1)S(1)}, u32[]{:S(2)}, u32[]{:S(2)}) collective-permute-start(bf16[384,768]{1,0:T(8,128)(2,1)S(1)} %dynamic-slice_bitcast_fusion), channel_id=1, source_target_pairs={{2,0},{3,1},{0,2},{1,3},{6,4},{7,5},{4,6},{5,7},{10,8},{11,9},{8,1... | collective-permute-start | bytes 1769480 | tf_op jit(solution)/shard_map/ppermute | solution.py:20
  9.2 5.0 %all-to-all-start = ((bf16[8,32,768]{2,1,0:T(8,128)(2,1)}), bf16[8,32,768]{2,1,0:T(8,128)(2,1)S(1)}, u32[]{:S(2)}, u32[]{:S(2)}) async-start(bf16[8,32,768]{2,1,0:T(8,128)(2,1)} %constant_dynamic-slice_fusion.4), calls=%async_computation | async-start | bytes 786432 | tf_op jit(solution)/shard_map/all_to_all | solution.py:38
  15.3 2.7 %constant_dynamic-slice_fusion.1 = (bf16[384,768]{1,0:T(8,128)(2,1)}, bf16[384,768]{1,0:T(8,128)(2,1)}, bf16[384,768]{1,0:T(8,128)(2,1)}) fusion(bf16[384,3072]{1,0:T(8,128)(2,1)} %bitcast.75, s32[]{:T(128)S(6)} %select_n.89, s32[]{:T(128)S(6)} %select_n.88, s32[]{:T(128)S(6)} %select_n.87), kind=kLoop, calls=%fused_computation.20 | loop fusion | bytes 3538956 | tf_op jit(solution)/shard_map/dynamic_slice | solution.py:525
  18.0 5.1 %all-to-all-done = bf16[8,32,768]{2,1,0:T(8,128)(2,1)S(1)} async-done(((bf16[8,32,768]{2,1,0:T(8,128)(2,1)}), bf16[8,32,768]{2,1,0:T(8,128)(2,1)S(1)}, u32[]{:S(2)}, u32[]{:S(2)}) %all-to-all-start) | async-done | bytes 393248 | tf_op jit(solution)/shard_map/all_to_all | solution.py:38
  29.5 6.0 %collective-permute-done.2.refs_1_ = bf16[256,768]{1,0:T(8,128)(2,1)S(1)} collective-permute-done((bf16[256,768]{1,0:T(8,128)(2,1)S(1)}, bf16[256,768]{1,0:T(8,128)(2,1)S(1)}, u32[]{:S(2)}, u32[]{:S(2)}) %collective-permute-start.2) | collective-permute-done | bytes 393248 | tf_op jit(solution)/shard_map/ppermute | solution.py:20
  35.5 3.5 %all-to-all-start.1 = ((bf16[8,64,768]{2,1,0:T(8,128)(2,1)}), bf16[8,64,768]{2,1,0:T(8,128)(2,1)S(1)}, u32[]{:S(2)}, u32[]{:S(2)}) async-start(bf16[8,64,768]{2,1,0:T(8,128)(2,1)} %join.4), calls=%async_computation.1 | async-start | bytes 1572864 | tf_op jit(solution)/shard_map/all_to_all | solution.py:38
  42.3 3.0 %collective-permute-start.7 = (bf16[768,768]{1,0:T(8,128)(2,1)S(1)}, bf16[768,768]{1,0:T(8,128)(2,1)S(1)}, u32[]{:S(2)}, u32[]{:S(2)}) collective-permute-start(bf16[768,768]{1,0:T(8,128)(2,1)S(1)} %bitcast.48), channel_id=1, source_target_pairs={{64,0},{0,64},{65,1},{1,65},{66,2},{2,66},{67,3},{3,67},{68,4},{4,... | collective-permute-start | bytes 3538952 | tf_op jit(solution)/shard_map/ppermute | solution.py:20
  52.5 6.9 %project.2 = (bf16[8,32,384]{2,1,0:T(8,128)(2,1)S(1)}, bf16[8,32,768]{2,1,0:T(8,128)(2,1)S(1)}) custom-call(s32[5]{0:T(128)S(1)} %get-tuple-element.90.refs_0_.refs_10_.meta, bf16[256,768]{1,0:T(8,128)(2,1)S(1)} %copy-done.13, bf16[256,768]{1,0:T(8,128)(2,1)} %collective-permute-done.3.refs_2_, bf16[256,768]{1,0:T(8,128)(2,1)S(1)} %copy-done.15, ...), custom_call_target="tpu_custom_call" | custom-call | tf_op jit(solution)/shard_map/project/pallas_call | solution.py:270
  63.6 5.2 %collective-permute-start.12 = (bf16[8,32,768]{2,1,0:T(8,128)(2,1)S(1)}, bf16[8,32,768]{2,1,0:T(8,128)(2,1)S(1)}, u32[]{:S(2)}, u32[]{:S(2)}) collective-permute-start(bf16[8,32,768]{2,1,0:T(8,128)(2,1)S(1)} %get-tuple-element.103), channel_id=1, source_target_pairs={{48,0},{20,32},{52,4},{24,36},{56,8},{28,40},{60,12},{0,44},{32,16... | collective-permute-start | bytes 1179656 | tf_op jit(solution)/shard_map/ppermute | solution.py:46
  68.8 4.8 %collective-permute-start.11 = (bf16[3,32,768]{2,1,0:T(8,128)(2,1)S(1)}, bf16[3,32,768]{2,1,0:T(8,128)(2,1)S(1)}, u32[]{:S(2)}, u32[]{:S(2)}) collective-permute-start(bf16[3,32,768]{2,1,0:T(8,128)(2,1)S(1)} %get-tuple-element.102), channel_id=1, source_target_pairs={{32,0},{4,32},{36,4},{8,36},{40,8},{12,40},{44,12},{16,44},{48,16}... | collective-permute-start | bytes 442376 | tf_op jit(solution)/shard_map/ppermute | solution.py:46
  76.1 5.7 %collective-permute-done.12.far = bf16[8,32,768]{2,1,0:T(8,128)(2,1)S(1)} collective-permute-done((bf16[8,32,768]{2,1,0:T(8,128)(2,1)S(1)}, bf16[8,32,768]{2,1,0:T(8,128)(2,1)S(1)}, u32[]{:S(2)}, u32[]{:S(2)}) %collective-permute-start.12) | collective-permute-done | bytes 393248 | tf_op jit(solution)/shard_map/ppermute | solution.py:46
  90.4 3.9 %collective-permute-done.18.refs_3_ = bf16[256,384]{1,0:T(8,128)(2,1)S(1)} collective-permute-done((bf16[256,384]{1,0:T(8,128)(2,1)S(1)}, bf16[256,384]{1,0:T(8,128)(2,1)S(1)}, u32[]{:S(2)}, u32[]{:S(2)}) %collective-permute-start.18) | collective-permute-done | bytes 196640 | tf_op jit(solution)/shard_map/ppermute | solution.py:20
  94.3 6.2 %collective-permute-done.17.refs_2_ = bf16[256,384]{1,0:T(8,128)(2,1)S(1)} collective-permute-done((bf16[256,384]{1,0:T(8,128)(2,1)S(1)}, bf16[256,384]{1,0:T(8,128)(2,1)S(1)}, u32[]{:S(2)}, u32[]{:S(2)}) %collective-permute-start.17) | collective-permute-done | bytes 196640 | tf_op jit(solution)/shard_map/ppermute | solution.py:20
  102.9 2.7 %collective-permute-start.21 = (bf16[256,768]{1,0:T(8,128)(2,1)S(1)}, bf16[256,768]{1,0:T(8,128)(2,1)S(1)}, u32[]{:S(2)}, u32[]{:S(2)}) collective-permute-start(bf16[256,768]{1,0:T(8,128)(2,1)S(1)} %output.2.refs_4_.refs_8_), channel_id=1, source_target_pairs={{1,0},{2,1},{3,2},{0,3},{5,4},{6,5},{7,6},{4,7},{9,8},{10,9},{11,1... | collective-permute-start | bytes 1179656 | tf_op jit(solution)/shard_map/ppermute | solution.py:20
  108.3 12.3 %all_to_all.20.early = bf16[8,32,768]{2,1,0:T(8,128)(2,1)S(1)} all-to-all(bf16[8,32,768]{2,1,0:T(8,128)(2,1)S(1)} %get-tuple-element.117.kv.own), channel_id=1, replica_groups={{0,4,8,12,16,20,24,28},{32,36,40,44,48,52,56,60},{1,5,9,13,17,21,25,29}..., dimensions={0} | all-to-all | bytes 786432 | tf_op jit(solution)/shard_map/all_to_all | solution.py:38
  121.5 7.9 %project.3 = (bf16[8,32,384]{2,1,0:T(8,128)(2,1)S(1)}, bf16[8,32,768]{2,1,0:T(8,128)(2,1)S(1)}, bf16[3,32,768]{2,1,0:T(8,128)(2,1)S(1)}, bf16[3,32,768]{2,1,0:T(8,128)(2,1)S(1)}, bf16[8,32,768]{2,1,0:T(8,128)(2,1)S(1)}) custom-call(s32[5]{0:T(128)S(1)} %copy-done.21, bf16[256,768]{1,0:T(8,128)(2,1)S(1)} %collective-permute-done.20.refs_1_, ...), custom_call_target="tpu_custom_call" | custom-call | tf_op jit(solution)/shard_map/project/pallas_call | solution.py:270
  129.4 5.2 %collective-permute-start.27 = (bf16[8,32,768]{2,1,0:T(8,128)(2,1)S(1)}, bf16[8,32,768]{2,1,0:T(8,128)(2,1)S(1)}, u32[]{:S(2)}, u32[]{:S(2)}) collective-permute-start(bf16[8,32,768]{2,1,0:T(8,128)(2,1)S(1)} %get-tuple-element.130), channel_id=1, source_target_pairs={{48,0},{20,32},{52,4},{24,36},{56,8},{28,40},{60,12},{0,44},{32,16... | collective-permute-start | bytes 1179656 | tf_op jit(solution)/shard_map/ppermute | solution.py:46
  134.6 4.1 %collective-permute-start.24 = (bf16[8,32,384]{2,1,0:T(8,128)(2,1)S(1)}, bf16[8,32,384]{2,1,0:T(8,128)(2,1)S(1)}, u32[]{:S(2)}, u32[]{:S(2)}) collective-permute-start(bf16[8,32,384]{2,1,0:T(8,128)(2,1)S(1)} %get-tuple-element.127.q_own), channel_id=1, source_target_pairs={{64,0},{0,64},{65,1},{1,65},{66,2},{2,66},{67,3},{3,67},{68,4},{4,... | collective-permute-start | bytes 589832 | tf_op jit(solution)/shard_map/ppermute | solution.py:20
  138.7 4.8 %collective-permute-start.26 = (bf16[3,32,768]{2,1,0:T(8,128)(2,1)S(1)}, bf16[3,32,768]{2,1,0:T(8,128)(2,1)S(1)}, u32[]{:S(2)}, u32[]{:S(2)}) collective-permute-start(bf16[3,32,768]{2,1,0:T(8,128)(2,1)S(1)} %get-tuple-element.129), channel_id=1, source_target_pairs={{32,0},{4,32},{36,4},{8,36},{40,8},{12,40},{44,12},{16,44},{48,16}... | collective-permute-start | bytes 442376 | tf_op jit(solution)/shard_map/ppermute | solution.py:46
  145.9 2.6 %collective-permute-done.25.below = bf16[3,32,768]{2,1,0:T(8,128)(2,1)S(1)} collective-permute-done((bf16[3,32,768]{2,1,0:T(8,128)(2,1)S(1)}, bf16[3,32,768]{2,1,0:T(8,128)(2,1)S(1)}, u32[]{:S(2)}, u32[]{:S(2)}) %collective-permute-start.25) | collective-permute-done | bytes 147488 | tf_op jit(solution)/shard_map/ppermute | solution.py:46
  154.5 2.6 %collective-permute-start.32 = (bf16[256,384]{1,0:T(8,128)(2,1)S(1)}, bf16[256,384]{1,0:T(8,128)(2,1)S(1)}, u32[]{:S(2)}, u32[]{:S(2)}) collective-permute-start(bf16[256,384]{1,0:T(8,128)(2,1)S(1)} %merge.3.refs_0_), channel_id=1, source_target_pairs={{1,0},{2,1},{3,2},{0,3},{5,4},{6,5},{7,6},{4,7},{9,8},{10,9},{11,1... | collective-permute-start | bytes 589832 | tf_op jit(solution)/shard_map/ppermute | solution.py:20
  160.9 7.4 %collective-permute-done.31.refs_2_ = bf16[256,384]{1,0:T(8,128)(2,1)S(1)} collective-permute-done((bf16[256,384]{1,0:T(8,128)(2,1)S(1)}, bf16[256,384]{1,0:T(8,128)(2,1)S(1)}, u32[]{:S(2)}, u32[]{:S(2)}) %collective-permute-start.31) | collective-permute-done | bytes 196640 | tf_op jit(solution)/shard_map/ppermute | solution.py:20
  170.8 19.1 %all_to_all.21.home = bf16[8,96,768]{2,1,0:T(8,128)(2,1)S(1)} all-to-all(bf16[8,96,768]{2,1,0:T(8,128)(2,1)S(1)} %join.7), channel_id=1, replica_groups={{0,4,8,12,16,20,24,28},{32,36,40,44,48,52,56,60},{1,5,9,13,17,21,25,29}..., dimensions={0} | all-to-all | bytes 2359296 | tf_op jit(solution)/shard_map/all_to_all | solution.py:38
  189.8 2.6 %collective-permute-start.33 = (bf16[8,96,768]{2,1,0:T(8,128)(2,1)S(1)}, bf16[8,96,768]{2,1,0:T(8,128)(2,1)S(1)}, u32[]{:S(2)}, u32[]{:S(2)}) collective-permute-start(bf16[8,96,768]{2,1,0:T(8,128)(2,1)S(1)} %all_to_all.21.home), channel_id=1, source_target_pairs={{64,0},{0,64},{65,1},{1,65},{66,2},{2,66},{67,3},{3,67},{68,4},{4,... | collective-permute-start | bytes 3538952 | tf_op jit(solution)/shard_map/ppermute | solution.py:20
  (163 shorter events, 61.9 us)
Async XLA Ops:
  0.7 50.8 %collective-permute-start.8 = (bf16[3,3072,384]{2,1,0:T(8,128)(2,1)}, bf16[3,3072,384]{2,1,0:T(8,128)(2,1)}, u32[]{:S(2)}, u32[]{:S(2)}) collective-permute-start(bf16[3,3072,384]{2,1,0:T(8,128)(2,1)} %bitcast.72), channel_id=1, source_target_pairs={{64,0},{0,64},{65,1},{1,65},{66,2},{2,66},{67,3},{3,67},{68,4},{4,... | collective-permute-start | bytes 21233672 | tf_op jit(solution)/shard_map/ppermute | solution.py:20
  3.3 19.9 %collective-permute-start.1 = (bf16[384,768]{1,0:T(8,128)(2,1)S(1)}, bf16[384,768]{1,0:T(8,128)(2,1)S(1)}, u32[]{:S(2)}, u32[]{:S(2)}) collective-permute-start(bf16[384,768]{1,0:T(8,128)(2,1)S(1)} %dynamic-slice_bitcast_fusion), channel_id=1, source_target_pairs={{2,0},{3,1},{0,2},{1,3},{6,4},{7,5},{4,6},{5,7},{10,8},{11,9},{8,1... | collective-permute-start | bytes 1769480 | tf_op jit(solution)/shard_map/ppermute | solution.py:20
  9.2 13.9 %all-to-all-start = ((bf16[8,32,768]{2,1,0:T(8,128)(2,1)}), bf16[8,32,768]{2,1,0:T(8,128)(2,1)S(1)}, u32[]{:S(2)}, u32[]{:S(2)}) async-start(bf16[8,32,768]{2,1,0:T(8,128)(2,1)} %constant_dynamic-slice_fusion.4), calls=%async_computation | async-start | bytes 786432 | tf_op jit(solution)/shard_map/all_to_all | solution.py:38
  24.1 11.4 %collective-permute-start.2 = (bf16[256,768]{1,0:T(8,128)(2,1)S(1)}, bf16[256,768]{1,0:T(8,128)(2,1)S(1)}, u32[]{:S(2)}, u32[]{:S(2)}) collective-permute-start(bf16[256,768]{1,0:T(8,128)(2,1)S(1)} %bitcast.55), channel_id=1, source_target_pairs={{2,0},{3,1},{0,2},{1,3},{6,4},{7,5},{4,6},{5,7},{10,8},{11,9},{8,1... | collective-permute-start | bytes 1179656 | tf_op jit(solution)/shard_map/ppermute | solution.py:20
  26.6 23.0 %collective-permute-start.4 = (bf16[256,768]{1,0:T(8,128)(2,1)S(1)}, bf16[256,768]{1,0:T(8,128)(2,1)S(1)}, u32[]{:S(2)}, u32[]{:S(2)}) collective-permute-start(bf16[256,768]{1,0:T(8,128)(2,1)S(1)} %bitcast.56), channel_id=1, source_target_pairs={{3,0},{0,1},{1,2},{2,3},{7,4},{4,5},{5,6},{6,7},{11,8},{8,9},{9,10... | collective-permute-start | bytes 1179656 | tf_op jit(solution)/shard_map/ppermute | solution.py:20
  27.4 23.0 %collective-permute-start.3 = (bf16[256,768]{1,0:T(8,128)(2,1)S(1)}, bf16[256,768]{1,0:T(8,128)(2,1)}, u32[]{:S(2)}, u32[]{:S(2)}) collective-permute-start(bf16[256,768]{1,0:T(8,128)(2,1)S(1)} %bitcast.57), channel_id=1, source_target_pairs={{1,0},{2,1},{3,2},{0,3},{5,4},{6,5},{7,6},{4,7},{9,8},{10,9},{11,1... | collective-permute-start | bytes 1179656 | tf_op jit(solution)/shard_map/ppermute | solution.py:20
  35.5 24.3 %all-to-all-start.1 = ((bf16[8,64,768]{2,1,0:T(8,128)(2,1)}), bf16[8,64,768]{2,1,0:T(8,128)(2,1)S(1)}, u32[]{:S(2)}, u32[]{:S(2)}) async-start(bf16[8,64,768]{2,1,0:T(8,128)(2,1)} %join.4), calls=%async_computation.1 | async-start | bytes 1572864 | tf_op jit(solution)/shard_map/all_to_all | solution.py:38
  61.0 20.8 %collective-permute-start.13 = (bf16[384,768]{1,0:T(8,128)(2,1)}, bf16[384,768]{1,0:T(8,128)(2,1)S(1)}, u32[]{:S(2)}, u32[]{:S(2)}) collective-permute-start(bf16[384,768]{1,0:T(8,128)(2,1)} %get-tuple-element.106), channel_id=1, source_target_pairs={{3,0},{0,1},{1,2},{2,3},{7,4},{4,5},{5,6},{6,7},{11,8},{8,9},{9,10... | collective-permute-start | bytes 1769480 | tf_op jit(solution)/shard_map/ppermute | solution.py:20
  61.7 20.1 %collective-permute-start.14 = (bf16[384,768]{1,0:T(8,128)(2,1)S(1)}, bf16[384,768]{1,0:T(8,128)(2,1)S(1)}, u32[]{:S(2)}, u32[]{:S(2)}) collective-permute-start(bf16[384,768]{1,0:T(8,128)(2,1)S(1)} %copy-done.23), channel_id=1, source_target_pairs={{1,0},{2,1},{3,2},{0,3},{5,4},{6,5},{7,6},{4,7},{9,8},{10,9},{11,1... | collective-permute-start | bytes 1769480 | tf_op jit(solution)/shard_map/ppermute | solution.py:20
  63.6 18.1 %collective-permute-start.12 = (bf16[8,32,768]{2,1,0:T(8,128)(2,1)S(1)}, bf16[8,32,768]{2,1,0:T(8,128)(2,1)S(1)}, u32[]{:S(2)}, u32[]{:S(2)}) collective-permute-start(bf16[8,32,768]{2,1,0:T(8,128)(2,1)S(1)} %get-tuple-element.103), channel_id=1, source_target_pairs={{48,0},{20,32},{52,4},{24,36},{56,8},{28,40},{60,12},{0,44},{32,16... | collective-permute-start | bytes 1179656 | tf_op jit(solution)/shard_map/ppermute | solution.py:46
  68.8 12.9 %collective-permute-start.10 = (bf16[3,32,768]{2,1,0:T(8,128)(2,1)S(1)}, bf16[3,32,768]{2,1,0:T(8,128)(2,1)S(1)}, u32[]{:S(2)}, u32[]{:S(2)}) collective-permute-start(bf16[3,32,768]{2,1,0:T(8,128)(2,1)S(1)} %get-tuple-element.101), channel_id=1, source_target_pairs={{60,0},{0,32},{32,4},{4,36},{36,8},{8,40},{40,12},{12,44},{44,16},... | collective-permute-start | bytes 442376 | tf_op jit(solution)/shard_map/ppermute | solution.py:46
  68.8 12.9 %collective-permute-start.11 = (bf16[3,32,768]{2,1,0:T(8,128)(2,1)S(1)}, bf16[3,32,768]{2,1,0:T(8,128)(2,1)S(1)}, u32[]{:S(2)}, u32[]{:S(2)}) collective-permute-start(bf16[3,32,768]{2,1,0:T(8,128)(2,1)S(1)} %get-tuple-element.102), channel_id=1, source_target_pairs={{32,0},{4,32},{36,4},{8,36},{40,8},{12,40},{44,12},{16,44},{48,16}... | collective-permute-start | bytes 442376 | tf_op jit(solution)/shard_map/ppermute | solution.py:46
  87.0 13.6 %collective-permute-start.19 = (bf16[768,768]{1,0:T(8,128)(2,1)S(1)}, bf16[768,768]{1,0:T(8,128)(2,1)S(1)}, u32[]{:S(2)}, u32[]{:S(2)}) collective-permute-start(bf16[768,768]{1,0:T(8,128)(2,1)S(1)} %bitcast.51), channel_id=1, source_target_pairs={{64,0},{0,64},{65,1},{1,65},{66,2},{2,66},{67,3},{3,67},{68,4},{4,... | collective-permute-start | bytes 3538952 | tf_op jit(solution)/shard_map/ppermute | solution.py:20
  89.1 11.5 %collective-permute-start.17 = (bf16[256,384]{1,0:T(8,128)(2,1)S(1)}, bf16[256,384]{1,0:T(8,128)(2,1)S(1)}, u32[]{:S(2)}, u32[]{:S(2)}) collective-permute-start(bf16[256,384]{1,0:T(8,128)(2,1)S(1)} %merge.2.refs_0_), channel_id=1, source_target_pairs={{3,0},{0,1},{1,2},{2,3},{7,4},{4,5},{5,6},{6,7},{11,8},{8,9},{9,10... | collective-permute-start | bytes 589832 | tf_op jit(solution)/shard_map/ppermute | solution.py:20
  89.4 11.1 %collective-permute-start.16 = (bf16[256,384]{1,0:T(8,128)(2,1)S(1)}, bf16[256,384]{1,0:T(8,128)(2,1)S(1)}, u32[]{:S(2)}, u32[]{:S(2)}) collective-permute-start(bf16[256,384]{1,0:T(8,128)(2,1)S(1)} %merge.2.refs_0_), channel_id=1, source_target_pairs={{2,0},{3,1},{0,2},{1,3},{6,4},{7,5},{4,6},{5,7},{10,8},{11,9},{8,1... | collective-permute-start | bytes 589832 | tf_op jit(solution)/shard_map/ppermute | solution.py:20
  102.9 17.7 %collective-permute-start.22 = (bf16[256,768]{1,0:T(8,128)(2,1)S(1)}, bf16[256,768]{1,0:T(8,128)(2,1)S(1)}, u32[]{:S(2)}, u32[]{:S(2)}) collective-permute-start(bf16[256,768]{1,0:T(8,128)(2,1)S(1)} %output.2.refs_4_.refs_8_), channel_id=1, source_target_pairs={{3,0},{0,1},{1,2},{2,3},{7,4},{4,5},{5,6},{6,7},{11,8},{8,9},{9,10... | collective-permute-start | bytes 1179656 | tf_op jit(solution)/shard_map/ppermute | solution.py:20
  102.9 17.6 %collective-permute-start.21 = (bf16[256,768]{1,0:T(8,128)(2,1)S(1)}, bf16[256,768]{1,0:T(8,128)(2,1)S(1)}, u32[]{:S(2)}, u32[]{:S(2)}) collective-permute-start(bf16[256,768]{1,0:T(8,128)(2,1)S(1)} %output.2.refs_4_.refs_8_), channel_id=1, source_target_pairs={{1,0},{2,1},{3,2},{0,3},{5,4},{6,5},{7,6},{4,7},{9,8},{10,9},{11,1... | collective-permute-start | bytes 1179656 | tf_op jit(solution)/shard_map/ppermute | solution.py:20
  105.6 15.5 %collective-permute-start.20 = (bf16[256,768]{1,0:T(8,128)(2,1)S(1)}, bf16[256,768]{1,0:T(8,128)(2,1)S(1)}, u32[]{:S(2)}, u32[]{:S(2)}) collective-permute-start(bf16[256,768]{1,0:T(8,128)(2,1)S(1)} %output.2.refs_4_.refs_8_), channel_id=1, source_target_pairs={{2,0},{3,1},{0,2},{1,3},{6,4},{7,5},{4,6},{5,7},{10,8},{11,9},{8,1... | collective-permute-start | bytes 1179656 | tf_op jit(solution)/shard_map/ppermute | solution.py:20
  129.4 19.1 %collective-permute-start.27 = (bf16[8,32,768]{2,1,0:T(8,128)(2,1)S(1)}, bf16[8,32,768]{2,1,0:T(8,128)(2,1)S(1)}, u32[]{:S(2)}, u32[]{:S(2)}) collective-permute-start(bf16[8,32,768]{2,1,0:T(8,128)(2,1)S(1)} %get-tuple-element.130), channel_id=1, source_target_pairs={{48,0},{20,32},{52,4},{24,36},{56,8},{28,40},{60,12},{0,44},{32,16... | collective-permute-start | bytes 1179656 | tf_op jit(solution)/shard_map/ppermute | solution.py:46
  134.6 8.9 %collective-permute-start.24 = (bf16[8,32,384]{2,1,0:T(8,128)(2,1)S(1)}, bf16[8,32,384]{2,1,0:T(8,128)(2,1)S(1)}, u32[]{:S(2)}, u32[]{:S(2)}) collective-permute-start(bf16[8,32,384]{2,1,0:T(8,128)(2,1)S(1)} %get-tuple-element.127.q_own), channel_id=1, source_target_pairs={{64,0},{0,64},{65,1},{1,65},{66,2},{2,66},{67,3},{3,67},{68,4},{4,... | collective-permute-start | bytes 589832 | tf_op jit(solution)/shard_map/ppermute | solution.py:20
  138.7 9.9 %collective-permute-start.25 = (bf16[3,32,768]{2,1,0:T(8,128)(2,1)S(1)}, bf16[3,32,768]{2,1,0:T(8,128)(2,1)S(1)}, u32[]{:S(2)}, u32[]{:S(2)}) collective-permute-start(bf16[3,32,768]{2,1,0:T(8,128)(2,1)S(1)} %get-tuple-element.128), channel_id=1, source_target_pairs={{60,0},{0,32},{32,4},{4,36},{36,8},{8,40},{40,12},{12,44},{44,16},... | collective-permute-start | bytes 442376 | tf_op jit(solution)/shard_map/ppermute | solution.py:46
  138.7 9.9 %collective-permute-start.26 = (bf16[3,32,768]{2,1,0:T(8,128)(2,1)S(1)}, bf16[3,32,768]{2,1,0:T(8,128)(2,1)S(1)}, u32[]{:S(2)}, u32[]{:S(2)}) collective-permute-start(bf16[3,32,768]{2,1,0:T(8,128)(2,1)S(1)} %get-tuple-element.129), channel_id=1, source_target_pairs={{32,0},{4,32},{36,4},{8,36},{40,8},{12,40},{44,12},{16,44},{48,16}... | collective-permute-start | bytes 442376 | tf_op jit(solution)/shard_map/ppermute | solution.py:46
  157.1 11.2 %collective-permute-start.31 = (bf16[256,384]{1,0:T(8,128)(2,1)S(1)}, bf16[256,384]{1,0:T(8,128)(2,1)S(1)}, u32[]{:S(2)}, u32[]{:S(2)}) collective-permute-start(bf16[256,384]{1,0:T(8,128)(2,1)S(1)} %merge.3.refs_0_), channel_id=1, source_target_pairs={{3,0},{0,1},{1,2},{2,3},{7,4},{4,5},{5,6},{6,7},{11,8},{8,9},{9,10... | collective-permute-start | bytes 589832 | tf_op jit(solution)/shard_map/ppermute | solution.py:20
  157.1 11.2 %collective-permute-start.30 = (bf16[256,384]{1,0:T(8,128)(2,1)S(1)}, bf16[256,384]{1,0:T(8,128)(2,1)S(1)}, u32[]{:S(2)}, u32[]{:S(2)}) collective-permute-start(bf16[256,384]{1,0:T(8,128)(2,1)S(1)} %merge.3.refs_0_), channel_id=1, source_target_pairs={{2,0},{3,1},{0,2},{1,3},{6,4},{7,5},{4,6},{5,7},{10,8},{11,9},{8,1... | collective-permute-start | bytes 589832 | tf_op jit(solution)/shard_map/ppermute | solution.py:20
  (50 other events, 473.3 us)

commit v15 on v14

--- a/solution.py
+++ b/solution.py
@@ -602,14 +602,14 @@
         if section == 0:
             wo_prev, wo_next = after(slices[1:], q_other, to_far)
             wo_prev, wo_next = shifted(wo_prev, "tp", 1), shifted(wo_next, "tp", 3)
-            far, wo_prev, wo_next = lax.optimization_barrier((far, wo_prev, wo_next))
-            wo_own.append(paired(wo_prev, wo_next))
         before = attend_own(q_own, q_other, kv, times)
         part_own, part_other = attend_rest(
             q_own, q_other, below, above, far, times, before
         )
         part_back = shifted(part_other, "segment", 1)
         if section == 0:
+            part_back, wo_prev, wo_next = lax.optimization_barrier((part_back, wo_prev, wo_next))
+            wo_own.append(paired(wo_prev, wo_next))
             wo_other.append(shifted(after(wo_own[1], part_back), "segment", 1))
         else:
             part_back, got_early = lax.optimization_barrier((part_back, got_early))

time: 197 us -> 197 us (level)
  blocking collectives: 31.3 us -> 28.8 us
  waiting for transfers between devices: 47.6 us -> 49.7 us
    ppermute x28, waiting for transfers between devices: 34.2 us -> 38.8 us  [shifted(): return lax.ppermute(block, axis, route)]
    ppermute x28, starting transfers between devices: 37.1 us -> 41.2 us  [shifted(): return lax.ppermute(block, axis, route)]
    ppermute x6, starting transfers between devices: 20 us -> 16.4 us  [along_ring(): return lax.ppermute(block, 'seq', route)]
    all_to_all x2, blocking collectives: 31.3 us -> 28.8 us  [exchanged(): return lax.all_to_all(tiles, 'seq', 0, 0, axis_index_groups=groups)]
    ppermute x6, waiting for transfers between devices: 8.32 us -> 5.85 us  [along_ring(): return lax.ppermute(block, 'seq', route)]
where the time goes in v15:
time: 197 us; the launch traced here: 196 us
  starting transfers between devices  66.2 us (34%)
  waiting for transfers between devices  49.7 us (25%)
  Pallas kernels  33.9 us (17%)
  blocking collectives  28.8 us (15%)
  local copies, waits for them, and re-layouts  12.6 us (6%)
  other arithmetic  3.54 us (2%)
    ppermute x28, starting transfers between devices, shifted(): return lax.ppermute(block, axis, route)  41.2 us
    ppermute x28, waiting for transfers between devices, shifted(): return lax.ppermute(block, axis, route)  38.8 us
    all_to_all x2, blocking collectives, exchanged(): return lax.all_to_all(tiles, 'seq', 0, 0, axis_index_groups=groups)  28.8 us
    ppermute x6, starting transfers between devices, along_ring(): return lax.ppermute(block, 'seq', route)  16.4 us
    pallas_call x2, Pallas kernels, project(): pl.pallas_call(kernel, in_specs=[SCALARS] + [ANYWHERE] * len(blocks) + [O...  14.8 us
    all_to_all x2, starting transfers between devices, exchanged(): return lax.all_to_all(tiles, 'seq', 0, 0, axis_index_groups=groups)  8.59 us
    unnamed x76, local copies, waits for them, and re-layouts  6.02 us
    ppermute x6, waiting for transfers between devices, along_ring(): return lax.ppermute(block, 'seq', route)  5.85 us
  transfers between devices with their start and end apart: 36, of which 15 were waited for; matrix products, arithmetic and copies ran while one was open for 5% of the time, Pallas kernels for 8%

profile of v15, /device:TPU:1, one launch (start us, length us, event | category | flops | bytes accessed | tf_op | source)
XLA Modules:
  0.0 196.0 jit_solution(9530160350185727577)
XLA Ops:
  3.3 3.8 %collective-permute-start.1 = (bf16[384,768]{1,0:T(8,128)(2,1)S(1)}, bf16[384,768]{1,0:T(8,128)(2,1)S(1)}, u32[]{:S(2)}, u32[]{:S(2)}) collective-permute-start(bf16[384,768]{1,0:T(8,128)(2,1)S(1)} %dynamic-slice_bitcast_fusion), channel_id=1, source_target_pairs={{2,0},{3,1},{0,2},{1,3},{6,4},{7,5},{4,6},{5,7},{10,8},{11,9},{8,1... | collective-permute-start | bytes 1769480 | tf_op jit(solution)/shard_map/ppermute | solution.py:20
  9.2 5.0 %all-to-all-start = ((bf16[8,32,768]{2,1,0:T(8,128)(2,1)}), bf16[8,32,768]{2,1,0:T(8,128)(2,1)S(1)}, u32[]{:S(2)}, u32[]{:S(2)}) async-start(bf16[8,32,768]{2,1,0:T(8,128)(2,1)} %constant_dynamic-slice_fusion.4), calls=%async_computation | async-start | bytes 786432 | tf_op jit(solution)/shard_map/all_to_all | solution.py:38
  15.3 2.7 %constant_dynamic-slice_fusion.1 = (bf16[384,768]{1,0:T(8,128)(2,1)}, bf16[384,768]{1,0:T(8,128)(2,1)}, bf16[384,768]{1,0:T(8,128)(2,1)}) fusion(bf16[384,3072]{1,0:T(8,128)(2,1)} %bitcast.75, s32[]{:T(128)S(6)} %select_n.89, s32[]{:T(128)S(6)} %select_n.88, s32[]{:T(128)S(6)} %select_n.87), kind=kLoop, calls=%fused_computation.20 | loop fusion | bytes 3538956 | tf_op jit(solution)/shard_map/dynamic_slice | solution.py:525
  18.0 5.1 %all-to-all-done = bf16[8,32,768]{2,1,0:T(8,128)(2,1)S(1)} async-done(((bf16[8,32,768]{2,1,0:T(8,128)(2,1)}), bf16[8,32,768]{2,1,0:T(8,128)(2,1)S(1)}, u32[]{:S(2)}, u32[]{:S(2)}) %all-to-all-start) | async-done | bytes 393248 | tf_op jit(solution)/shard_map/all_to_all | solution.py:38
  29.5 6.0 %collective-permute-done.2.refs_1_ = bf16[256,768]{1,0:T(8,128)(2,1)S(1)} collective-permute-done((bf16[256,768]{1,0:T(8,128)(2,1)S(1)}, bf16[256,768]{1,0:T(8,128)(2,1)S(1)}, u32[]{:S(2)}, u32[]{:S(2)}) %collective-permute-start.2) | collective-permute-done | bytes 393248 | tf_op jit(solution)/shard_map/ppermute | solution.py:20
  35.5 3.5 %all-to-all-start.1 = ((bf16[8,64,768]{2,1,0:T(8,128)(2,1)}), bf16[8,64,768]{2,1,0:T(8,128)(2,1)S(1)}, u32[]{:S(2)}, u32[]{:S(2)}) async-start(bf16[8,64,768]{2,1,0:T(8,128)(2,1)} %join.4), calls=%async_computation.1 | async-start | bytes 1572864 | tf_op jit(solution)/shard_map/all_to_all | solution.py:38
  42.3 3.0 %collective-permute-start.7 = (bf16[768,768]{1,0:T(8,128)(2,1)S(1)}, bf16[768,768]{1,0:T(8,128)(2,1)S(1)}, u32[]{:S(2)}, u32[]{:S(2)}) collective-permute-start(bf16[768,768]{1,0:T(8,128)(2,1)S(1)} %bitcast.48), channel_id=1, source_target_pairs={{64,0},{0,64},{65,1},{1,65},{66,2},{2,66},{67,3},{3,67},{68,4},{4,... | collective-permute-start | bytes 3538952 | tf_op jit(solution)/shard_map/ppermute | solution.py:20
  52.5 6.9 %project.2 = (bf16[8,32,384]{2,1,0:T(8,128)(2,1)S(1)}, bf16[8,32,768]{2,1,0:T(8,128)(2,1)S(1)}) custom-call(s32[5]{0:T(128)S(1)} %get-tuple-element.90.refs_0_.refs_10_.meta, bf16[256,768]{1,0:T(8,128)(2,1)S(1)} %copy-done.13, bf16[256,768]{1,0:T(8,128)(2,1)} %collective-permute-done.3.refs_2_, bf16[256,768]{1,0:T(8,128)(2,1)S(1)} %copy-done.15, ...), custom_call_target="tpu_custom_call" | custom-call | tf_op jit(solution)/shard_map/project/pallas_call | solution.py:270
  60.1 5.3 %collective-permute-start.12 = (bf16[8,32,768]{2,1,0:T(8,128)(2,1)S(1)}, bf16[8,32,768]{2,1,0:T(8,128)(2,1)S(1)}, u32[]{:S(2)}, u32[]{:S(2)}) collective-permute-start(bf16[8,32,768]{2,1,0:T(8,128)(2,1)S(1)} %get-tuple-element.103), channel_id=1, source_target_pairs={{48,0},{20,32},{52,4},{24,36},{56,8},{28,40},{60,12},{0,44},{32,16... | collective-permute-start | bytes 1179656 | tf_op jit(solution)/shard_map/ppermute | solution.py:46
  65.9 4.8 %collective-permute-start.11 = (bf16[3,32,768]{2,1,0:T(8,128)(2,1)S(1)}, bf16[3,32,768]{2,1,0:T(8,128)(2,1)S(1)}, u32[]{:S(2)}, u32[]{:S(2)}) collective-permute-start(bf16[3,32,768]{2,1,0:T(8,128)(2,1)S(1)} %get-tuple-element.102), channel_id=1, source_target_pairs={{32,0},{4,32},{36,4},{8,36},{40,8},{12,40},{44,12},{16,44},{48,16}... | collective-permute-start | bytes 442376 | tf_op jit(solution)/shard_map/ppermute | solution.py:46
  82.0 4.5 %collective-permute-done.14 = bf16[384,768]{1,0:T(8,128)(2,1)S(1)} collective-permute-done((bf16[384,768]{1,0:T(8,128)(2,1)}, bf16[384,768]{1,0:T(8,128)(2,1)S(1)}, u32[]{:S(2)}, u32[]{:S(2)}) %collective-permute-start.14) | collective-permute-done | bytes 589856 | tf_op jit(solution)/shard_map/ppermute | solution.py:20
  92.5 7.1 %collective-permute-done.18.refs_3_ = bf16[256,384]{1,0:T(8,128)(2,1)S(1)} collective-permute-done((bf16[256,384]{1,0:T(8,128)(2,1)S(1)}, bf16[256,384]{1,0:T(8,128)(2,1)S(1)}, u32[]{:S(2)}, u32[]{:S(2)}) %collective-permute-start.18) | collective-permute-done | bytes 196640 | tf_op jit(solution)/shard_map/ppermute | solution.py:20
  99.7 3.2 %collective-permute-done.17.refs_2_ = bf16[256,384]{1,0:T(8,128)(2,1)S(1)} collective-permute-done((bf16[256,384]{1,0:T(8,128)(2,1)S(1)}, bf16[256,384]{1,0:T(8,128)(2,1)S(1)}, u32[]{:S(2)}, u32[]{:S(2)}) %collective-permute-start.17) | collective-permute-done | bytes 196640 | tf_op jit(solution)/shard_map/ppermute | solution.py:20
  105.3 2.7 %collective-permute-start.21 = (bf16[256,768]{1,0:T(8,128)(2,1)S(1)}, bf16[256,768]{1,0:T(8,128)(2,1)S(1)}, u32[]{:S(2)}, u32[]{:S(2)}) collective-permute-start(bf16[256,768]{1,0:T(8,128)(2,1)S(1)} %output.2.refs_4_.refs_8_), channel_id=1, source_target_pairs={{1,0},{2,1},{3,2},{0,3},{5,4},{6,5},{7,6},{4,7},{9,8},{10,9},{11,1... | collective-permute-start | bytes 1179656 | tf_op jit(solution)/shard_map/ppermute | solution.py:20
  110.4 10.9 %all_to_all.20.early = bf16[8,32,768]{2,1,0:T(8,128)(2,1)S(1)} all-to-all(bf16[8,32,768]{2,1,0:T(8,128)(2,1)S(1)} %get-tuple-element.117.kv.own), channel_id=1, replica_groups={{0,4,8,12,16,20,24,28},{32,36,40,44,48,52,56,60},{1,5,9,13,17,21,25,29}..., dimensions={0} | all-to-all | bytes 786432 | tf_op jit(solution)/shard_map/all_to_all | solution.py:38
  123.7 7.9 %project.3 = (bf16[8,32,384]{2,1,0:T(8,128)(2,1)S(1)}, bf16[8,32,768]{2,1,0:T(8,128)(2,1)S(1)}, bf16[3,32,768]{2,1,0:T(8,128)(2,1)S(1)}, bf16[3,32,768]{2,1,0:T(8,128)(2,1)S(1)}, bf16[8,32,768]{2,1,0:T(8,128)(2,1)S(1)}) custom-call(s32[5]{0:T(128)S(1)} %copy-done.21, bf16[256,768]{1,0:T(8,128)(2,1)S(1)} %collective-permute-done.20.refs_1_, ...), custom_call_target="tpu_custom_call" | custom-call | tf_op jit(solution)/shard_map/project/pallas_call | solution.py:270
  133.1 4.1 %collective-permute-start.24 = (bf16[8,32,384]{2,1,0:T(8,128)(2,1)S(1)}, bf16[8,32,384]{2,1,0:T(8,128)(2,1)S(1)}, u32[]{:S(2)}, u32[]{:S(2)}) collective-permute-start(bf16[8,32,384]{2,1,0:T(8,128)(2,1)S(1)} %get-tuple-element.127.q_own), channel_id=1, source_target_pairs={{64,0},{0,64},{65,1},{1,65},{66,2},{2,66},{67,3},{3,67},{68,4},{4,... | collective-permute-start | bytes 589832 | tf_op jit(solution)/shard_map/ppermute | solution.py:20
  137.3 4.8 %collective-permute-start.26 = (bf16[3,32,768]{2,1,0:T(8,128)(2,1)S(1)}, bf16[3,32,768]{2,1,0:T(8,128)(2,1)S(1)}, u32[]{:S(2)}, u32[]{:S(2)}) collective-permute-start(bf16[3,32,768]{2,1,0:T(8,128)(2,1)S(1)} %get-tuple-element.129), channel_id=1, source_target_pairs={{32,0},{4,32},{36,4},{8,36},{40,8},{12,40},{44,12},{16,44},{48,16}... | collective-permute-start | bytes 442376 | tf_op jit(solution)/shard_map/ppermute | solution.py:46
  144.5 2.7 %collective-permute-done.25.below = bf16[3,32,768]{2,1,0:T(8,128)(2,1)S(1)} collective-permute-done((bf16[3,32,768]{2,1,0:T(8,128)(2,1)S(1)}, bf16[3,32,768]{2,1,0:T(8,128)(2,1)S(1)}, u32[]{:S(2)}, u32[]{:S(2)}) %collective-permute-start.25) | collective-permute-done | bytes 147488 | tf_op jit(solution)/shard_map/ppermute | solution.py:46
  149.5 3.5 %collective-permute-start.28 = (f32[8,32,512]{2,1,0:T(8,128)S(1)}, f32[8,32,512]{2,1,0:T(8,128)S(1)}, u32[]{:S(2)}, u32[]{:S(2)}) collective-permute-start(f32[8,32,512]{2,1,0:T(8,128)S(1)} %get-tuple-element.133), channel_id=1, source_target_pairs={{64,0},{0,64},{65,1},{1,65},{66,2},{2,66},{67,3},{3,67},{68,4},{4,... | collective-permute-start | bytes 1572872 | tf_op jit(solution)/shard_map/ppermute | solution.py:20
  155.6 2.6 %collective-permute-start.32 = (bf16[256,384]{1,0:T(8,128)(2,1)S(1)}, bf16[256,384]{1,0:T(8,128)(2,1)S(1)}, u32[]{:S(2)}, u32[]{:S(2)}) collective-permute-start(bf16[256,384]{1,0:T(8,128)(2,1)S(1)} %merge.3.refs_0_), channel_id=1, source_target_pairs={{1,0},{2,1},{3,2},{0,3},{5,4},{6,5},{7,6},{4,7},{9,8},{10,9},{11,1... | collective-permute-start | bytes 589832 | tf_op jit(solution)/shard_map/ppermute | solution.py:20
  161.9 7.4 %collective-permute-done.31.refs_2_ = bf16[256,384]{1,0:T(8,128)(2,1)S(1)} collective-permute-done((bf16[256,384]{1,0:T(8,128)(2,1)S(1)}, bf16[256,384]{1,0:T(8,128)(2,1)S(1)}, u32[]{:S(2)}, u32[]{:S(2)}) %collective-permute-start.31) | collective-permute-done | bytes 196640 | tf_op jit(solution)/shard_map/ppermute | solution.py:20
  171.8 17.9 %all_to_all.21.home = bf16[8,96,768]{2,1,0:T(8,128)(2,1)S(1)} all-to-all(bf16[8,96,768]{2,1,0:T(8,128)(2,1)S(1)} %join.7), channel_id=1, replica_groups={{0,4,8,12,16,20,24,28},{32,36,40,44,48,52,56,60},{1,5,9,13,17,21,25,29}..., dimensions={0} | all-to-all | bytes 2359296 | tf_op jit(solution)/shard_map/all_to_all | solution.py:38
  189.7 2.5 %collective-permute-start.33 = (bf16[8,96,768]{2,1,0:T(8,128)(2,1)S(1)}, bf16[8,96,768]{2,1,0:T(8,128)(2,1)S(1)}, u32[]{:S(2)}, u32[]{:S(2)}) collective-permute-start(bf16[8,96,768]{2,1,0:T(8,128)(2,1)S(1)} %all_to_all.21.home), channel_id=1, source_target_pairs={{64,0},{0,64},{65,1},{1,65},{66,2},{2,66},{67,3},{3,67},{68,4},{4,... | collective-permute-start | bytes 3538952 | tf_op jit(solution)/shard_map/ppermute | solution.py:20
  (163 shorter events, 66.7 us)
Async XLA Ops:
  0.7 50.8 %collective-permute-start.8 = (bf16[3,3072,384]{2,1,0:T(8,128)(2,1)}, bf16[3,3072,384]{2,1,0:T(8,128)(2,1)}, u32[]{:S(2)}, u32[]{:S(2)}) collective-permute-start(bf16[3,3072,384]{2,1,0:T(8,128)(2,1)} %bitcast.72), channel_id=1, source_target_pairs={{64,0},{0,64},{65,1},{1,65},{66,2},{2,66},{67,3},{3,67},{68,4},{4,... | collective-permute-start | bytes 21233672 | tf_op jit(solution)/shard_map/ppermute | solution.py:20
  3.3 19.9 %collective-permute-start.1 = (bf16[384,768]{1,0:T(8,128)(2,1)S(1)}, bf16[384,768]{1,0:T(8,128)(2,1)S(1)}, u32[]{:S(2)}, u32[]{:S(2)}) collective-permute-start(bf16[384,768]{1,0:T(8,128)(2,1)S(1)} %dynamic-slice_bitcast_fusion), channel_id=1, source_target_pairs={{2,0},{3,1},{0,2},{1,3},{6,4},{7,5},{4,6},{5,7},{10,8},{11,9},{8,1... | collective-permute-start | bytes 1769480 | tf_op jit(solution)/shard_map/ppermute | solution.py:20
  9.2 13.9 %all-to-all-start = ((bf16[8,32,768]{2,1,0:T(8,128)(2,1)}), bf16[8,32,768]{2,1,0:T(8,128)(2,1)S(1)}, u32[]{:S(2)}, u32[]{:S(2)}) async-start(bf16[8,32,768]{2,1,0:T(8,128)(2,1)} %constant_dynamic-slice_fusion.4), calls=%async_computation | async-start | bytes 786432 | tf_op jit(solution)/shard_map/all_to_all | solution.py:38
  24.1 11.4 %collective-permute-start.2 = (bf16[256,768]{1,0:T(8,128)(2,1)S(1)}, bf16[256,768]{1,0:T(8,128)(2,1)S(1)}, u32[]{:S(2)}, u32[]{:S(2)}) collective-permute-start(bf16[256,768]{1,0:T(8,128)(2,1)S(1)} %bitcast.55), channel_id=1, source_target_pairs={{2,0},{3,1},{0,2},{1,3},{6,4},{7,5},{4,6},{5,7},{10,8},{11,9},{8,1... | collective-permute-start | bytes 1179656 | tf_op jit(solution)/shard_map/ppermute | solution.py:20
  26.6 23.0 %collective-permute-start.4 = (bf16[256,768]{1,0:T(8,128)(2,1)S(1)}, bf16[256,768]{1,0:T(8,128)(2,1)S(1)}, u32[]{:S(2)}, u32[]{:S(2)}) collective-permute-start(bf16[256,768]{1,0:T(8,128)(2,1)S(1)} %bitcast.56), channel_id=1, source_target_pairs={{3,0},{0,1},{1,2},{2,3},{7,4},{4,5},{5,6},{6,7},{11,8},{8,9},{9,10... | collective-permute-start | bytes 1179656 | tf_op jit(solution)/shard_map/ppermute | solution.py:20
  27.4 23.0 %collective-permute-start.3 = (bf16[256,768]{1,0:T(8,128)(2,1)S(1)}, bf16[256,768]{1,0:T(8,128)(2,1)}, u32[]{:S(2)}, u32[]{:S(2)}) collective-permute-start(bf16[256,768]{1,0:T(8,128)(2,1)S(1)} %bitcast.57), channel_id=1, source_target_pairs={{1,0},{2,1},{3,2},{0,3},{5,4},{6,5},{7,6},{4,7},{9,8},{10,9},{11,1... | collective-permute-start | bytes 1179656 | tf_op jit(solution)/shard_map/ppermute | solution.py:20
  35.5 24.0 %all-to-all-start.1 = ((bf16[8,64,768]{2,1,0:T(8,128)(2,1)}), bf16[8,64,768]{2,1,0:T(8,128)(2,1)S(1)}, u32[]{:S(2)}, u32[]{:S(2)}) async-start(bf16[8,64,768]{2,1,0:T(8,128)(2,1)} %join.4), calls=%async_computation.1 | async-start | bytes 1572864 | tf_op jit(solution)/shard_map/all_to_all | solution.py:38
  60.1 18.8 %collective-permute-start.12 = (bf16[8,32,768]{2,1,0:T(8,128)(2,1)S(1)}, bf16[8,32,768]{2,1,0:T(8,128)(2,1)S(1)}, u32[]{:S(2)}, u32[]{:S(2)}) collective-permute-start(bf16[8,32,768]{2,1,0:T(8,128)(2,1)S(1)} %get-tuple-element.103), channel_id=1, source_target_pairs={{48,0},{20,32},{52,4},{24,36},{56,8},{28,40},{60,12},{0,44},{32,16... | collective-permute-start | bytes 1179656 | tf_op jit(solution)/shard_map/ppermute | solution.py:46
  65.9 10.0 %collective-permute-start.10 = (bf16[3,32,768]{2,1,0:T(8,128)(2,1)S(1)}, bf16[3,32,768]{2,1,0:T(8,128)(2,1)S(1)}, u32[]{:S(2)}, u32[]{:S(2)}) collective-permute-start(bf16[3,32,768]{2,1,0:T(8,128)(2,1)S(1)} %get-tuple-element.101), channel_id=1, source_target_pairs={{60,0},{0,32},{32,4},{4,36},{36,8},{8,40},{40,12},{12,44},{44,16},... | collective-permute-start | bytes 442376 | tf_op jit(solution)/shard_map/ppermute | solution.py:46
  65.9 11.0 %collective-permute-start.11 = (bf16[3,32,768]{2,1,0:T(8,128)(2,1)S(1)}, bf16[3,32,768]{2,1,0:T(8,128)(2,1)S(1)}, u32[]{:S(2)}, u32[]{:S(2)}) collective-permute-start(bf16[3,32,768]{2,1,0:T(8,128)(2,1)S(1)} %get-tuple-element.102), channel_id=1, source_target_pairs={{32,0},{4,32},{36,4},{8,36},{40,8},{12,40},{44,12},{16,44},{48,16}... | collective-permute-start | bytes 442376 | tf_op jit(solution)/shard_map/ppermute | solution.py:46
  70.7 15.7 %collective-permute-start.14 = (bf16[384,768]{1,0:T(8,128)(2,1)}, bf16[384,768]{1,0:T(8,128)(2,1)S(1)}, u32[]{:S(2)}, u32[]{:S(2)}) collective-permute-start(bf16[384,768]{1,0:T(8,128)(2,1)} %get-tuple-element.109), channel_id=1, source_target_pairs={{3,0},{0,1},{1,2},{2,3},{7,4},{4,5},{5,6},{6,7},{11,8},{8,9},{9,10... | collective-permute-start | bytes 1769480 | tf_op jit(solution)/shard_map/ppermute | solution.py:20
  71.4 15.0 %collective-permute-start.15 = (bf16[384,768]{1,0:T(8,128)(2,1)S(1)}, bf16[384,768]{1,0:T(8,128)(2,1)S(1)}, u32[]{:S(2)}, u32[]{:S(2)}) collective-permute-start(bf16[384,768]{1,0:T(8,128)(2,1)S(1)} %copy-done.23), channel_id=1, source_target_pairs={{1,0},{2,1},{3,2},{0,3},{5,4},{6,5},{7,6},{4,7},{9,8},{10,9},{11,1... | collective-permute-start | bytes 1769480 | tf_op jit(solution)/shard_map/ppermute | solution.py:20
  86.7 16.2 %collective-permute-start.19 = (bf16[768,768]{1,0:T(8,128)(2,1)S(1)}, bf16[768,768]{1,0:T(8,128)(2,1)S(1)}, u32[]{:S(2)}, u32[]{:S(2)}) collective-permute-start(bf16[768,768]{1,0:T(8,128)(2,1)S(1)} %bitcast.51), channel_id=1, source_target_pairs={{64,0},{0,64},{65,1},{1,65},{66,2},{2,66},{67,3},{3,67},{68,4},{4,... | collective-permute-start | bytes 3538952 | tf_op jit(solution)/shard_map/ppermute | solution.py:20
  88.7 10.9 %collective-permute-start.18 = (bf16[256,384]{1,0:T(8,128)(2,1)S(1)}, bf16[256,384]{1,0:T(8,128)(2,1)S(1)}, u32[]{:S(2)}, u32[]{:S(2)}) collective-permute-start(bf16[256,384]{1,0:T(8,128)(2,1)S(1)} %merge.2.refs_0_), channel_id=1, source_target_pairs={{1,0},{2,1},{3,2},{0,3},{5,4},{6,5},{7,6},{4,7},{9,8},{10,9},{11,1... | collective-permute-start | bytes 589832 | tf_op jit(solution)/shard_map/ppermute | solution.py:20
  91.3 11.6 %collective-permute-start.17 = (bf16[256,384]{1,0:T(8,128)(2,1)S(1)}, bf16[256,384]{1,0:T(8,128)(2,1)S(1)}, u32[]{:S(2)}, u32[]{:S(2)}) collective-permute-start(bf16[256,384]{1,0:T(8,128)(2,1)S(1)} %merge.2.refs_0_), channel_id=1, source_target_pairs={{3,0},{0,1},{1,2},{2,3},{7,4},{4,5},{5,6},{6,7},{11,8},{8,9},{9,10... | collective-permute-start | bytes 589832 | tf_op jit(solution)/shard_map/ppermute | solution.py:20
  91.3 11.6 %collective-permute-start.16 = (bf16[256,384]{1,0:T(8,128)(2,1)S(1)}, bf16[256,384]{1,0:T(8,128)(2,1)S(1)}, u32[]{:S(2)}, u32[]{:S(2)}) collective-permute-start(bf16[256,384]{1,0:T(8,128)(2,1)S(1)} %merge.2.refs_0_), channel_id=1, source_target_pairs={{2,0},{3,1},{0,2},{1,3},{6,4},{7,5},{4,6},{5,7},{10,8},{11,9},{8,1... | collective-permute-start | bytes 589832 | tf_op jit(solution)/shard_map/ppermute | solution.py:20
  105.2 16.2 %collective-permute-start.22 = (bf16[256,768]{1,0:T(8,128)(2,1)S(1)}, bf16[256,768]{1,0:T(8,128)(2,1)S(1)}, u32[]{:S(2)}, u32[]{:S(2)}) collective-permute-start(bf16[256,768]{1,0:T(8,128)(2,1)S(1)} %output.2.refs_4_.refs_8_), channel_id=1, source_target_pairs={{3,0},{0,1},{1,2},{2,3},{7,4},{4,5},{5,6},{6,7},{11,8},{8,9},{9,10... | collective-permute-start | bytes 1179656 | tf_op jit(solution)/shard_map/ppermute | solution.py:20
  105.3 16.1 %collective-permute-start.21 = (bf16[256,768]{1,0:T(8,128)(2,1)S(1)}, bf16[256,768]{1,0:T(8,128)(2,1)S(1)}, u32[]{:S(2)}, u32[]{:S(2)}) collective-permute-start(bf16[256,768]{1,0:T(8,128)(2,1)S(1)} %output.2.refs_4_.refs_8_), channel_id=1, source_target_pairs={{1,0},{2,1},{3,2},{0,3},{5,4},{6,5},{7,6},{4,7},{9,8},{10,9},{11,1... | collective-permute-start | bytes 1179656 | tf_op jit(solution)/shard_map/ppermute | solution.py:20
  107.9 15.7 %collective-permute-start.20 = (bf16[256,768]{1,0:T(8,128)(2,1)S(1)}, bf16[256,768]{1,0:T(8,128)(2,1)S(1)}, u32[]{:S(2)}, u32[]{:S(2)}) collective-permute-start(bf16[256,768]{1,0:T(8,128)(2,1)S(1)} %output.2.refs_4_.refs_8_), channel_id=1, source_target_pairs={{2,0},{3,1},{0,2},{1,3},{6,4},{7,5},{4,6},{5,7},{10,8},{11,9},{8,1... | collective-permute-start | bytes 1179656 | tf_op jit(solution)/shard_map/ppermute | solution.py:20
  131.6 15.7 %collective-permute-start.27 = (bf16[8,32,768]{2,1,0:T(8,128)(2,1)S(1)}, bf16[8,32,768]{2,1,0:T(8,128)(2,1)S(1)}, u32[]{:S(2)}, u32[]{:S(2)}) collective-permute-start(bf16[8,32,768]{2,1,0:T(8,128)(2,1)S(1)} %get-tuple-element.130), channel_id=1, source_target_pairs={{48,0},{20,32},{52,4},{24,36},{56,8},{28,40},{60,12},{0,44},{32,16... | collective-permute-start | bytes 1179656 | tf_op jit(solution)/shard_map/ppermute | solution.py:46
  137.3 10.0 %collective-permute-start.25 = (bf16[3,32,768]{2,1,0:T(8,128)(2,1)S(1)}, bf16[3,32,768]{2,1,0:T(8,128)(2,1)S(1)}, u32[]{:S(2)}, u32[]{:S(2)}) collective-permute-start(bf16[3,32,768]{2,1,0:T(8,128)(2,1)S(1)} %get-tuple-element.128), channel_id=1, source_target_pairs={{60,0},{0,32},{32,4},{4,36},{36,8},{8,40},{40,12},{12,44},{44,16},... | collective-permute-start | bytes 442376 | tf_op jit(solution)/shard_map/ppermute | solution.py:46
  137.3 10.0 %collective-permute-start.26 = (bf16[3,32,768]{2,1,0:T(8,128)(2,1)S(1)}, bf16[3,32,768]{2,1,0:T(8,128)(2,1)S(1)}, u32[]{:S(2)}, u32[]{:S(2)}) collective-permute-start(bf16[3,32,768]{2,1,0:T(8,128)(2,1)S(1)} %get-tuple-element.129), channel_id=1, source_target_pairs={{32,0},{4,32},{36,4},{8,36},{40,8},{12,40},{44,12},{16,44},{48,16}... | collective-permute-start | bytes 442376 | tf_op jit(solution)/shard_map/ppermute | solution.py:46
  158.2 11.2 %collective-permute-start.31 = (bf16[256,384]{1,0:T(8,128)(2,1)S(1)}, bf16[256,384]{1,0:T(8,128)(2,1)S(1)}, u32[]{:S(2)}, u32[]{:S(2)}) collective-permute-start(bf16[256,384]{1,0:T(8,128)(2,1)S(1)} %merge.3.refs_0_), channel_id=1, source_target_pairs={{3,0},{0,1},{1,2},{2,3},{7,4},{4,5},{5,6},{6,7},{11,8},{8,9},{9,10... | collective-permute-start | bytes 589832 | tf_op jit(solution)/shard_map/ppermute | solution.py:20
  158.2 11.2 %collective-permute-start.30 = (bf16[256,384]{1,0:T(8,128)(2,1)S(1)}, bf16[256,384]{1,0:T(8,128)(2,1)S(1)}, u32[]{:S(2)}, u32[]{:S(2)}) collective-permute-start(bf16[256,384]{1,0:T(8,128)(2,1)S(1)} %merge.3.refs_0_), channel_id=1, source_target_pairs={{2,0},{3,1},{0,2},{1,3},{6,4},{7,5},{4,6},{5,7},{10,8},{11,9},{8,1... | collective-permute-start | bytes 589832 | tf_op jit(solution)/shard_map/ppermute | solution.py:20
  (50 other events, 511.3 us)
